TPU v7x, 32 devices: a whole 2x2x4 slice. The times are simulated.
32 devices in a mesh: frame: 4 (over y, x), seq: 8 (over z, core).
Axes of the slice: x: 2, y: 2, z: 4, core: 2. Of those that a mesh axis runs over, the one named last changes fastest.
Arguments:
- tokens: bfloat16 [4, 256, 5120], P('frame', 'seq'), may hold values from -6 to 6
- query_rows: bfloat16 [4, 256, 4096], P('frame', 'seq'), may hold values from -40 to 40
- key_rows: bfloat16 [4, 256, 4096], P('frame', 'seq'), may hold values from -40 to 40
- value_rows: bfloat16 [4, 256, 4096], P('frame', 'seq'), may hold values from -6 to 6
- gain_query: float32 [4096], replicated, may hold values from 0.5 to 2.5
- gain_key: float32 [4096], replicated, may hold values from 0.5 to 2.5
- out_weight: bfloat16 [4096, 5120], P('seq'), may hold values from -0.09375 to 0.09375
- out_bias: bfloat16 [5120], replicated, may hold values from -3 to 3
- gate_table: bfloat16 [64, 5120], replicated, may hold values from -12 to 12
- noise_level: int32 [4], replicated, may hold values from 0 to 63
- slot_order: int32 [4], replicated, may hold values from 0 to 255, as said below
Outputs:
- updated: bfloat16 [4, 256, 5120], P('frame', 'seq')
Inputs may be any that keep to these rules, and one draw needn't show every extreme that they name: `slot_order`: all 4 stamps are distinct.
All inputs are finite; a program needn't handle non-finite values.
Results may differ from a plain program's by a relative error of at most 0.013.
Values may be sent and summed in bfloat16 or wider, within the bound.
No kernel may reach another device: no remote copies, remote signals or barrier semaphores. Data moves between devices by JAX's collectives and lax.ppermute only.
A program may use at most 64 MiB of HBM per device.

v0:
```python
import jax
import jax.numpy as jnp
from jax import lax
from jax.sharding import PartitionSpec as P

HD = 128


epsilon = 1e-06


def normalize(rows, gain):
    values = rows.astype(jnp.float32)
    inverse = lax.rsqrt(jnp.mean(values * values, axis=-1, keepdims=True) + epsilon)
    return (values * inverse * gain).astype(jnp.bfloat16)


def update_half(current, query_half, half_rank, key_piece, value_piece, key_rank):
    score_scale = HD ** (-0.5)

    def compute(running):
        run_max, run_sum, run_acc = running
        scores = (
            jnp.einsum("qhd,khd->qhk", query_half, key_piece, preferred_element_type=jnp.float32)
            * score_scale
        )
        visible = (key_rank <= half_rank)[None, None, :]
        masked = jnp.where(visible, scores, -1e30)
        new_max = jnp.maximum(run_max, jnp.max(masked, axis=-1))
        exponent = jnp.where(visible, jnp.exp(masked - new_max[..., None]), 0.0)
        new_sum = jnp.sum(exponent, axis=-1)
        summed = jnp.einsum(
            "qhk,khd->qhd",
            exponent.astype(jnp.bfloat16),
            value_piece,
            preferred_element_type=jnp.float32,
        )
        return (new_max, new_sum, summed)

    def keep(running):
        return running

    return lax.cond(jnp.min(key_rank) <= half_rank, compute, keep, current)


def finish(running):
    run_max, run_sum, run_acc = running
    result = run_acc / run_sum[..., None]
    return result.reshape(result.shape[0], -1).astype(jnp.bfloat16)


def shards(
    tokens,
    query_rows,
    key_rows,
    value_rows,
    gain_query,
    gain_key,
    out_weight,
    out_bias,
    gate_table,
    noise_level,
    slot_order,
):
    normed_query = normalize(query_rows, gain_query)
    normed_key = normalize(key_rows, gain_key)
    query_heads, key_heads, value_heads = (
        lax.all_to_all(normed_query, "seq", split_axis=2, concat_axis=1, tiled=True),
        lax.all_to_all(normed_key, "seq", split_axis=2, concat_axis=1, tiled=True),
        lax.all_to_all(value_rows, "seq", split_axis=2, concat_axis=1, tiled=True),
    )
    query_heads = query_heads[0]
    key_heads = key_heads[0]
    value_heads = value_heads[0]
    frame_tokens = query_heads.shape[0]
    half_rows = frame_tokens // 2
    heads_here = query_heads.shape[1] // HD
    frame_count = lax.axis_size("frame")
    my_slot = lax.axis_index("frame")
    slot_ids = jnp.arange(frame_count, dtype=jnp.int32)
    my_rank = jnp.sum(jnp.where(slot_ids == my_slot, slot_order, 0))
    first_half = query_heads[:half_rows]
    second_half = query_heads[half_rows:]
    first_half = first_half.reshape(half_rows, heads_here, HD)
    second_half = second_half.reshape(half_rows, heads_here, HD)

    def start_state():
        return (
            jnp.full((half_rows, heads_here), -1e30, jnp.float32),
            jnp.zeros((half_rows, heads_here), jnp.float32),
            jnp.zeros((half_rows, heads_here, HD), jnp.float32),
        )

    key_piece = lax.all_gather(key_heads, "frame", axis=0, tiled=True)
    value_piece = lax.all_gather(value_heads, "frame", axis=0, tiled=True)
    row_total = key_piece.shape[0]
    frame_of = jnp.arange(row_total, dtype=jnp.int32) // frame_tokens
    key_rank = jnp.sum(
        jnp.where(frame_of[:, None] == slot_ids[None, :], slot_order[None, :], 0), axis=1
    )
    key_piece = key_piece.reshape(row_total, heads_here, HD)
    value_piece = value_piece.reshape(row_total, heads_here, HD)
    first_state = update_half(start_state(), first_half, my_rank, key_piece, value_piece, key_rank)
    second_state = update_half(
        start_state(), second_half, my_rank, key_piece, value_piece, key_rank
    )
    first_done = finish(first_state)
    second_done = finish(second_state)
    attended = jnp.concatenate([first_done, second_done], axis=0)
    projected = lax.psum_scatter(
        jnp.dot(attended, out_weight, preferred_element_type=jnp.float32).astype(jnp.bfloat16),
        "seq",
        scatter_dimension=0,
        tiled=True,
    ).astype(jnp.float32)
    my_level = jnp.sum(jnp.where(slot_ids == my_slot, noise_level, 0))
    level_hot = (jnp.arange(gate_table.shape[0], dtype=jnp.int32) == my_level).astype(jnp.bfloat16)
    gate_row = jnp.dot(level_hot[None, :], gate_table, preferred_element_type=jnp.float32)[0]
    mixed = tokens[0].astype(jnp.float32) + gate_row[None, :] * (
        projected + out_bias.astype(jnp.float32)[None, :]
    )
    return mixed.astype(jnp.bfloat16)[None]


def solution(mesh):
    placed = (
        P("frame", "seq", None),
        P("frame", "seq", None),
        P("frame", "seq", None),
        P("frame", "seq", None),
        P(),
        P(),
        P("seq", None),
        P(),
        P(),
        P(),
        P(),
    )
    return jax.shard_map(
        shards, mesh=mesh, in_specs=placed, out_specs=P("frame", "seq", None), check_vma=False
    )
```

profile of v0, /device:TPU:0, one launch (start us, length us, event | category | flops | bytes accessed | tf_op | source)
XLA Modules:
  0.0 212.1 jit_solution(108757552606103359)
XLA Ops:
  8.8 2.8 %copy.100 = bf16[1,32,4096]{1,0,2:T(2,128)(2,1)S(1)} copy(bf16[1,32,4096]{2,1,0:T(8,128)(2,1)S(1)} %fusion.38) | data formatting | bytes 524288 | tf_op jit(solution)/shard_map/convert_element_type | solution.py:15
  12.1 23.3 %reduce.3 = bf16[4096,32]{1,0:T(8,128)(2,1)} reduce(bf16[4096,1,32]{2,1,0:T(2,128)(2,1)S(1)} %bitcast.88, bf16[]{:T(256)} %broadcast.134), dimensions={1}, to_apply=%bitcast.70.reduce_sub_computation | reduce | bytes 524290
  35.4 2.5 %reshape.95 = bf16[8,2,8192]{2,1,0:T(2,128)(2,1)S(1)} reshape(bf16[4096,32]{1,0:T(8,128)(2,1)} %reduce.3) | data formatting | bytes 524288
  37.9 15.9 %all_to_all.45 = bf16[8,2,8192]{2,1,0:T(2,128)(2,1)S(1)} all-to-all(bf16[8,2,8192]{2,1,0:T(2,128)(2,1)S(1)} %reshape.95), channel_id=1, replica_groups=mesh['frame'=4,'seq'=8] {'seq'}, dimensions={0} | all-to-all | bytes 524288 | tf_op jit(solution)/shard_map/all_to_all | solution.py:69
  55.1 2.1 copy.101
  58.2 2.8 %copy.104 = bf16[1,32,4096]{1,0,2:T(2,128)(2,1)S(1)} copy(bf16[1,32,4096]{2,1,0:T(8,128)(2,1)S(1)} %copy-done.3) | data formatting | bytes 524288 | tf_op args[3]
  60.9 23.4 %reduce.4 = bf16[4096,32]{1,0:T(8,128)(2,1)} reduce(bf16[4096,1,32]{2,1,0:T(2,128)(2,1)S(1)} %bitcast.90, bf16[]{:T(256)} %broadcast.134), dimensions={1}, to_apply=%bitcast.72.reduce_sub_computation | reduce | bytes 524290
  84.3 3.1 %reshape.97 = bf16[8,2,8192]{2,1,0:T(2,128)(2,1)} reshape(bf16[4096,32]{1,0:T(8,128)(2,1)} %reduce.4) | data formatting | bytes 524288
  87.4 3.4 %all-to-all-start.2 = ((bf16[8,2,8192]{2,1,0:T(2,128)(2,1)}), bf16[8,2,8192]{2,1,0:T(2,128)(2,1)S(1)}, u32[]{:S(2)}, u32[]{:S(2)}) async-start(bf16[8,2,8192]{2,1,0:T(2,128)(2,1)} %reshape.97), calls=%async_computation.2 | async-start | bytes 524288 | tf_op jit(solution)/shard_map/all_to_all | solution.py:70
  91.3 9.2 %all-to-all-done.2 = bf16[8,2,8192]{2,1,0:T(2,128)(2,1)S(1)} async-done(((bf16[8,2,8192]{2,1,0:T(2,128)(2,1)}), bf16[8,2,8192]{2,1,0:T(2,128)(2,1)S(1)}, u32[]{:S(2)}, u32[]{:S(2)}) %all-to-all-start.2) | async-done | bytes 262176 | tf_op jit(solution)/shard_map/all_to_all | solution.py:70
  101.9 2.1 copy.105
  105.0 2.8 %copy.98 = bf16[1,32,4096]{1,0,2:T(2,128)(2,1)S(1)} copy(bf16[1,32,4096]{2,1,0:T(8,128)(2,1)S(1)} %fusion.35) | data formatting | bytes 524288 | tf_op jit(solution)/shard_map/convert_element_type | solution.py:15
  107.8 23.3 %reduce.2 = bf16[4096,32]{1,0:T(8,128)(2,1)} reduce(bf16[4096,1,32]{2,1,0:T(2,128)(2,1)S(1)} %bitcast.89, bf16[]{:T(256)} %broadcast.134), dimensions={1}, to_apply=%bitcast.68.reduce_sub_computation | reduce | bytes 524290
  131.1 3.1 %reshape.93 = bf16[8,2,8192]{2,1,0:T(2,128)(2,1)} reshape(bf16[4096,32]{1,0:T(8,128)(2,1)} %reduce.2) | data formatting | bytes 524288
  134.2 3.4 %all-to-all-start = ((bf16[8,2,8192]{2,1,0:T(2,128)(2,1)}), bf16[8,2,8192]{2,1,0:T(2,128)(2,1)S(1)}, u32[]{:S(2)}, u32[]{:S(2)}) async-start(bf16[8,2,8192]{2,1,0:T(2,128)(2,1)} %reshape.93), calls=%async_computation | async-start | bytes 524288 | tf_op jit(solution)/shard_map/all_to_all | solution.py:68
  140.3 7.0 %all-to-all-done = bf16[8,2,8192]{2,1,0:T(2,128)(2,1)S(1)} async-done(((bf16[8,2,8192]{2,1,0:T(2,128)(2,1)}), bf16[8,2,8192]{2,1,0:T(2,128)(2,1)S(1)}, u32[]{:S(2)}, u32[]{:S(2)}) %all-to-all-start) | async-done | bytes 262176 | tf_op jit(solution)/shard_map/all_to_all | solution.py:68
  148.6 2.1 copy.99
  150.9 1.5 copy.103
  152.4 1.5 copy.107
  153.9 3.7 %conditional.3 = (f32[128,4]{0,1:T(4,128)S(1)}, f32[128,4,128]{0,2,1:T(8,128)S(1)}) conditional(s32[]{:T(128)} %convert_element_type.55, () %tuple.23, (s32[]{:T(128)}, s32[1024]{0:T(1024)S(1)}, bf16[1,8,32,512]{3,1,2,0:T(8,128)(2,1)S(1)}, bf16[1024,4,128]{0,2,1:T(8,128)(2,1)S(1)}, bf16[1024,4,128]{0,2,1:T(8,128)(2,1)S(1)}) %tuple.52), branch_computations={%region_10.11_spmd, %region_11.14_spmd} | conditional | flops 275251712 | bytes 10375188 | solution.py:43
  157.6 4.0 %conditional.2 = (f32[128,4]{0,1:T(4,128)S(1)}, f32[128,4,128]{0,2,1:T(8,128)S(1)}) conditional(s32[]{:T(128)} %convert_element_type.55, () %tuple.21, (s32[]{:T(128)}, s32[1024]{0:T(1024)S(1)}, bf16[1,8,32,512]{3,1,2,0:T(8,128)(2,1)S(1)}, bf16[1024,4,128]{0,2,1:T(8,128)(2,1)S(1)}, bf16[1024,4,128]{0,2,1:T(8,128)(2,1)S(1)}) %tuple.53), branch_computations={%region_6.7_spmd, %region_7.10_spmd} | conditional | flops 275251712 | bytes 10375188 | solution.py:43
  161.7 5.5 %convolution_convert_fusion = bf16[256,5120]{1,0:T(8,128)(2,1)} fusion(bf16[512,5120]{1,0:T(8,128)(2,1)} %param.21, bf16[128,512]{0,1:T(8,128)(2,1)S(1)} %bitcast.101, bf16[128,512]{0,1:T(8,128)(2,1)S(1)} %bitcast.102), kind=kOutput, calls=%fused_computation.42 | convolution fusion | flops 1344012288 | bytes 8126464 | tf_op jit(solution)/shard_map/dot_general | solution.py:111
  169.4 34.3 %reduce-scatter.2.cloned.1.call-done = bf16[32,5120]{1,0:T(8,128)(2,1)} async-done(((bf16[256,5120]{1,0:T(8,128)(2,1)}), bf16[32,5120]{1,0:T(8,128)(2,1)}) %reduce-scatter.2.cloned.1.call-update) | async-done | bytes 327696 | tf_op jit(solution)/shard_map/reduce_scatter | solution.py:110
  203.7 1.8 fusion.39
  (69 shorter events, 20.4 us)
Async XLA Ops:
  6.5 162.0 %copy-start = (bf16[64,5120]{1,0:T(8,128)(2,1)S(1)}, bf16[64,5120]{1,0:T(8,128)(2,1)}, u32[]{:S(2)}) copy-start(bf16[64,5120]{1,0:T(8,128)(2,1)} %param.23) | copy-start | bytes 1966084
  6.5 144.3 %all-gather.3.cloned.1.call-start = ((), (), s32[]{:S(2)}) async-start(), calls=%async_computation.4 | async-start | bytes 1310720 | tf_op jit(solution)/shard_map/all_gather | solution.py:94
  55.1 3.0 %copy-start.3 = (bf16[1,32,4096]{2,1,0:T(8,128)(2,1)S(1)}, bf16[1,32,4096]{2,1,0:T(8,128)(2,1)}, u32[]{:S(2)}) copy-start(bf16[1,32,4096]{2,1,0:T(8,128)(2,1)} %param.18) | copy-start | bytes 786436
  60.9 30.2 %copy-start.1 = (bf16[1,32,4096]{2,1,0:T(8,128)(2,1)S(1)}, bf16[1,32,4096]{2,1,0:T(8,128)(2,1)}, u32[]{:S(2)}) copy-start(bf16[1,32,4096]{2,1,0:T(8,128)(2,1)} %param.16) | copy-start | bytes 786436
  87.4 13.1 %all-to-all-start.2 = ((bf16[8,2,8192]{2,1,0:T(2,128)(2,1)}), bf16[8,2,8192]{2,1,0:T(2,128)(2,1)S(1)}, u32[]{:S(2)}, u32[]{:S(2)}) async-start(bf16[8,2,8192]{2,1,0:T(2,128)(2,1)} %reshape.97), calls=%async_computation.2 | async-start | bytes 524288 | tf_op jit(solution)/shard_map/all_to_all | solution.py:70
  90.8 61.6 %all-gather.5.cloned.1.call-start = ((), (), s32[]{:S(2)}) async-start(), calls=%async_computation.5 | async-start | bytes 1310720 | tf_op jit(solution)/shard_map/all_gather | solution.py:95
  101.9 3.0 %copy-start.4 = (f32[4096]{0:T(1024)S(1)}, f32[4096]{0:T(1024)}, u32[]{:S(2)}) copy-start(f32[4096]{0:T(1024)} %param.19) | copy-start | bytes 49156
  107.8 29.9 %copy-start.6 = (s32[4]{0:T(128)S(1)}, s32[4]{0:T(128)}, u32[]{:S(2)}) copy-start(s32[4]{0:T(128)} %param.25) | copy-start | bytes 52
  134.2 13.1 %all-to-all-start = ((bf16[8,2,8192]{2,1,0:T(2,128)(2,1)}), bf16[8,2,8192]{2,1,0:T(2,128)(2,1)S(1)}, u32[]{:S(2)}, u32[]{:S(2)}) async-start(bf16[8,2,8192]{2,1,0:T(2,128)(2,1)} %reshape.93), calls=%async_computation | async-start | bytes 524288 | tf_op jit(solution)/shard_map/all_to_all | solution.py:68
  137.6 66.1 %reduce-scatter.2.cloned.1.call-start = ((), (), s32[]{:S(2)}) async-start(), calls=%async_computation.6 | async-start | bytes 2949120 | tf_op jit(solution)/shard_map/reduce_scatter | solution.py:110
  167.2 0.7 copy-start.5
  167.2 0.7 copy-start.7
  167.2 36.5 %copy-start.2 = (bf16[1,32,5120]{2,1,0:T(8,128)(2,1)S(1)}, bf16[1,32,5120]{2,1,0:T(8,128)(2,1)}, u32[]{:S(2)}) copy-start(bf16[1,32,5120]{2,1,0:T(8,128)(2,1)} %param.15) | copy-start | bytes 983044
Sparse Core Ops, SparseCore 0:
  58.3 25.5 all-gather.2
  105.0 25.5 all-gather.4
  167.4 36.2 reduce-scatter.1
where the time goes:
time: 213 us; the launch traced here: 212 us
  other arithmetic  79.5 us (37%)
  waiting for transfers between devices  50.6 us (24%)
  local copies, waits for them, and re-layouts  33.8 us (16%)
  blocking collectives  15.9 us (7%)
  between operations  14.6 us (7%)
  matrix products  10.2 us (5%)
  starting transfers between devices  7.13 us (3%)
    unnamed x3, other arithmetic  70 us
    reduce_scatter x1, waiting for transfers between devices, shards(): lax.psum_scatter(jnp.dot(attended, out_weight, preferred_element_type=jnp...  34.3 us
    unnamed x27, local copies, waits for them, and re-layouts  16.9 us
    all_to_all x1, blocking collectives, shards(): lax.all_to_all(normed_key, 'seq', split_axis=2, concat_axis=1, tiled=True)  15.9 us
    all_to_all x1, waiting for transfers between devices, shards(): lax.all_to_all(value_rows, 'seq', split_axis=2, concat_axis=1, tiled=True)  9.2 us
    all_to_all x1, waiting for transfers between devices, shards(): lax.all_to_all(normed_query, 'seq', split_axis=2, concat_axis=1, tiled=True)  6.97 us
    dot_general x1, matrix products, shards(): jnp.dot(attended, out_weight, preferred_element_type=jnp.float32)  5.55 us
    convert_element_type x2, local copies, waits for them, and re-layouts, normalize(): return (values * inverse * gain).astype(jnp.bfloat16)  5.5 us
  transfers between devices with their start and end apart: 5, of which 3 were waited for; matrix products, arithmetic and copies ran while one was open for 33% of the time, Pallas kernels for 0%

commit v1 on v0

v1 whole, which is shorter than its diff:
```python
import functools

import jax
import jax.numpy as jnp
from jax import lax
from jax.experimental import pallas as pl
from jax.experimental.pallas import tpu as pltpu
from jax.sharding import PartitionSpec as P

HD = 128
EPS = 1e-06
LOG2E = 1.4426950408889634
VMEM = pltpu.VMEM
SMEM = pltpu.SMEM


def inverse_rms(rows):
    values = rows.astype(jnp.float32)
    return lax.rsqrt(jnp.mean(values * values, axis=-1, keepdims=True) + EPS)


def key_value_kernel(n, me_ref, key_ref, value_ref, gain_ref, *outs):
    width = key_ref.shape[1] // n
    inverse = inverse_rms(key_ref[...])
    me = me_ref[0]
    for j in range(n):
        cols = pl.ds(pl.multiple_of((me ^ j) * width, width), width)
        normed = key_ref[:, cols].astype(jnp.float32) * inverse * gain_ref[:, cols]
        outs[j][:, :width] = normed.astype(jnp.bfloat16)
        outs[j][:, width:] = value_ref[:, cols]


def query_kernel(n, me_ref, query_ref, gain_ref, *outs):
    width = query_ref.shape[1] // n
    inverse = inverse_rms(query_ref[...])
    me = me_ref[0]
    for j in range(n):
        cols = pl.ds(pl.multiple_of((me ^ j) * width, width), width)
        normed = query_ref[:, cols].astype(jnp.float32) * inverse * gain_ref[:, cols]
        outs[j][...] = normed.astype(jnp.bfloat16)


def attention_kernel(n, frames, units, slot_ref, order_ref, *refs):
    queries = refs[:n]
    pieces = refs[n : n + frames * units]
    even_ref, odd_ref = refs[n + frames * units :]
    width = queries[0].shape[1]
    rows = queries[0].shape[0]
    piece_rows = pieces[0].shape[0]
    heads = width // HD
    slot = slot_ref[0]
    my_rank = order_ref[slot]
    factor = (HD ** (-0.5)) * LOG2E
    group = max(1, min(n // 2, 128 // rows))
    for h in range(heads):
        cols = slice(h * HD, (h + 1) * HD)
        value_cols = slice(width + h * HD, width + (h + 1) * HD)
        for start in range(0, n, 2 * group):
            for parity, out_ref in ((0, even_ref), (1, odd_ref)):
                picked = [start + 2 * i + parity for i in range(group)]
                query = jnp.concatenate([queries[j][:, cols] for j in picked], axis=0)
                scores = []
                for f in range(frames):
                    hidden = jnp.where(order_ref[slot ^ f] <= my_rank, 0.0, -1e30)
                    for u in range(units):
                        score = lax.dot_general(
                            query,
                            pieces[f * units + u][:, cols],
                            (((1,), (1,)), ((), ())),
                            preferred_element_type=jnp.float32,
                        )
                        scores.append(score + hidden)
                scores = jnp.concatenate(scores, axis=1)
                top = jnp.max(scores, axis=1, keepdims=True)
                exponent = jnp.exp2((scores - top) * factor)
                total = jnp.sum(exponent, axis=1, keepdims=True)
                weights = exponent.astype(jnp.bfloat16)
                values = jnp.concatenate([piece[:, value_cols] for piece in pieces], axis=0)
                summed = jnp.dot(weights, values, preferred_element_type=jnp.float32)
                first = (start // 2) * rows
                out_ref[first : first + group * rows, cols] = (summed / total).astype(jnp.bfloat16)


def projection_kernel(chunks, mine_ref, theirs_ref, own_ref, other_ref, *outs):
    rows = mine_ref.shape[0] // chunks
    result = jnp.dot(mine_ref[...], own_ref[...], preferred_element_type=jnp.float32)
    result += jnp.dot(theirs_ref[...], other_ref[...], preferred_element_type=jnp.float32)
    for j in range(chunks):
        outs[j][...] = result[j * rows : (j + 1) * rows].astype(outs[j].dtype)


def shards(
    tokens,
    query_rows,
    key_rows,
    value_rows,
    gain_query,
    gain_key,
    out_weight,
    out_bias,
    gate_table,
    noise_level,
    slot_order,
):
    n = lax.axis_size("seq")
    frames = lax.axis_size("frame")
    rows, features = query_rows.shape[1:]
    width = features // n
    model = out_weight.shape[1]
    me = lax.axis_index("seq").astype(jnp.int32)
    slot = lax.axis_index("frame").astype(jnp.int32)
    me_array = me.reshape(1)
    slot_array = slot.reshape(1)

    def across(value, axis, distance):
        size = n if axis == "seq" else frames
        return lax.ppermute(value, axis, [(i, i ^ distance) for i in range(size)])

    smem = pl.BlockSpec(memory_space=SMEM)
    vmem = pl.BlockSpec(memory_space=VMEM)

    other_weight = across(out_weight, "seq", 1)

    kv = pl.pallas_call(
        functools.partial(key_value_kernel, n),
        out_shape=[jax.ShapeDtypeStruct((rows, 2 * width), jnp.bfloat16)] * n,
        in_specs=[smem, vmem, vmem, vmem],
        out_specs=[vmem] * n,
        cost_estimate=pl.CostEstimate(
            flops=8 * rows * features, bytes_accessed=8 * rows * features, transcendentals=0
        ),
        name="key_value_norm",
    )(me_array, key_rows[0], value_rows[0], gain_key.reshape(1, features))
    kv = [kv[0]] + [across(kv[j], "seq", j) for j in range(1, n)]

    queries = pl.pallas_call(
        functools.partial(query_kernel, n),
        out_shape=[jax.ShapeDtypeStruct((rows, width), jnp.bfloat16)] * n,
        in_specs=[smem, vmem, vmem],
        out_specs=[vmem] * n,
        cost_estimate=pl.CostEstimate(
            flops=8 * rows * features, bytes_accessed=4 * rows * features, transcendentals=0
        ),
        name="query_norm",
    )(me_array, query_rows[0], gain_query.reshape(1, features))
    queries = [queries[0]] + [across(queries[j], "seq", j) for j in range(1, n)]

    bits = [1 << b for b in range(frames.bit_length() - 1)]
    halves = [jnp.concatenate(kv[: n // 2], axis=0), jnp.concatenate(kv[n // 2 :], axis=0)]
    held = []
    for half, order in zip(halves, (bits, bits[::-1])):
        found = {0: half}
        for bit in order:
            found.update({f ^ bit: across(piece, "frame", bit) for f, piece in found.items()})
        held.append(found)
    pieces = [held[u][f] for f in range(frames) for u in range(2)]

    frame_rows = n * rows
    even, odd = pl.pallas_call(
        functools.partial(attention_kernel, n, frames, 2),
        out_shape=[jax.ShapeDtypeStruct((frame_rows // 2, width), jnp.bfloat16)] * 2,
        in_specs=[smem, smem] + [vmem] * (n + 2 * frames),
        out_specs=[vmem] * 2,
        compiler_params=pltpu.CompilerParams(vmem_limit_bytes=40 * 2**20),
        cost_estimate=pl.CostEstimate(
            flops=4 * frame_rows * frame_rows * frames * width,
            bytes_accessed=4 * frame_rows * frames * width,
            transcendentals=frame_rows * frame_rows * frames * (width // HD),
        ),
        name="attention",
    )(slot_array, slot_order, *queries, *pieces)
    theirs = across(odd, "seq", 1)

    chunks = n // 2
    tile = model // 4
    partial_sums = pl.pallas_call(
        functools.partial(projection_kernel, chunks),
        grid=(model // tile,),
        out_shape=[
            jax.ShapeDtypeStruct((rows, model), jnp.bfloat16 if j % 2 else jnp.float32)
            for j in range(chunks)
        ],
        in_specs=[
            pl.BlockSpec((frame_rows // 2, width), lambda i: (0, 0)),
            pl.BlockSpec((frame_rows // 2, width), lambda i: (0, 0)),
            pl.BlockSpec((width, tile), lambda i: (0, i)),
            pl.BlockSpec((width, tile), lambda i: (0, i)),
        ],
        out_specs=[pl.BlockSpec((rows, tile), lambda i: (0, i))] * chunks,
        compiler_params=pltpu.CompilerParams(vmem_limit_bytes=24 * 2**20),
        cost_estimate=pl.CostEstimate(
            flops=2 * frame_rows * width * model,
            bytes_accessed=4 * width * model + 8 * rows * model,
            transcendentals=0,
        ),
        name="projection",
    )(even, theirs, out_weight, other_weight)

    sums = {j: part for j, part in enumerate(partial_sums)}
    bit = 1
    while bit < chunks:
        leaving = sorted((j for j in sums if j & bit), reverse=True)
        for j in leaving:
            arrived = across(sums.pop(j).astype(jnp.bfloat16), "seq", 2 * bit)
            sums[j ^ bit] = sums[j ^ bit].astype(jnp.float32) + arrived.astype(jnp.float32)
        bit *= 2
    projected = sums[0]

    level = lax.dynamic_index_in_dim(noise_level, slot, keepdims=False)
    gate_row = lax.dynamic_index_in_dim(gate_table, level, keepdims=True).astype(jnp.float32)
    bias = out_bias.astype(jnp.float32)[None, :]
    mixed = tokens[0].astype(jnp.float32) + gate_row * (projected + bias)
    return mixed.astype(jnp.bfloat16)[None]


def solution(mesh):
    placed = (
        P("frame", "seq", None),
        P("frame", "seq", None),
        P("frame", "seq", None),
        P("frame", "seq", None),
        P(),
        P(),
        P("seq", None),
        P(),
        P(),
        P(),
        P(),
    )
    return jax.shard_map(
        shards, mesh=mesh, in_specs=placed, out_specs=P("frame", "seq", None), check_vma=False
    )
```

time: 213 us -> 98.5 us (0.46)
  other arithmetic: 79.5 us -> 1.88 us
  local copies, waits for them, and re-layouts: 33.8 us -> 5.38 us
  starting transfers between devices: 7.13 us -> 31.2 us
  blocking collectives: 15.9 us -> 0 us
  Pallas kernels: 0 us -> 12.8 us
  between operations: 14.6 us -> 2.07 us
  matrix products: 10.2 us -> 0 us
  waiting for transfers between devices: 50.6 us -> 44.7 us
    unnamed x3 -> x0, other arithmetic: 70 us -> none
    ppermute x0 -> x25, waiting for transfers between devices: none -> 44.7 us  [across(): return lax.ppermute(value, axis, [(i, i ^ distance) for i in range(size)])]
    reduce_scatter x1 -> x0, waiting for transfers between devices: 34.3 us -> none  [shards(): lax.psum_scatter(jnp.dot(attended, out_weight, preferred_element_type=jnp...]
    ppermute x0 -> x25, starting transfers between devices: none -> 31.2 us  [across(): return lax.ppermute(value, axis, [(i, i ^ distance) for i in range(size)])]
    all_to_all x2 -> x0, waiting for transfers between devices: 16.2 us -> none  [the longest x1 9.2 us: shards(): lax.all_to_all(value_rows, 'seq', split_axis=2, concat_axis=1, tiled=True)]
    all_to_all x1 -> x0, blocking collectives: 15.9 us -> none  [shards(): lax.all_to_all(normed_key, 'seq', split_axis=2, concat_axis=1, tiled=True)]
    pallas_call x0 -> x4, Pallas kernels: none -> 12.8 us  [the longest x1 4.71 us: shards(): pl.pallas_call(functools.partial(projection_kernel, chunks), grid=(model...]
    unnamed x27 -> x18, local copies, waits for them, and re-layouts: 16.9 us -> 4.78 us
  transfers between devices with their start and end apart: 5 -> 25, of which waited for: 3 -> 14; matrix products, arithmetic and copies ran while one was open for 33% -> 2% of each run, Pallas kernels for 0% -> 8%
where the time goes in v1:
time: 98.5 us; the launch traced here: 98 us
  waiting for transfers between devices  44.7 us (45%)
  starting transfers between devices  31.2 us (32%)
  Pallas kernels  12.8 us (13%)
  local copies, waits for them, and re-layouts  5.38 us (5%)
  between operations  2.07 us (2%)
  other arithmetic  1.88 us (2%)
    ppermute x25, waiting for transfers between devices, across(): return lax.ppermute(value, axis, [(i, i ^ distance) for i in range(size)])  44.7 us
    ppermute x25, starting transfers between devices, across(): return lax.ppermute(value, axis, [(i, i ^ distance) for i in range(size)])  31.2 us
    unnamed x18, local copies, waits for them, and re-layouts  4.78 us
    pallas_call x1, Pallas kernels, shards(): pl.pallas_call(functools.partial(projection_kernel, chunks), grid=(model...  4.71 us
    pallas_call x1, Pallas kernels, shards(): pl.pallas_call(functools.partial(attention_kernel, n, frames, 2), out_sha...  4.34 us
    pallas_call x1, Pallas kernels, shards(): pl.pallas_call(functools.partial(key_value_kernel, n), out_shape=[jax.Sha...  1.99 us
  transfers between devices with their start and end apart: 25, of which 14 were waited for; matrix products, arithmetic and copies ran while one was open for 2% of the time, Pallas kernels for 8%

profile of v1, /device:TPU:0, one launch (start us, length us, event | category | flops | bytes accessed | tf_op | source)
XLA Modules:
  0.0 98.0 jit_solution(12123913679744652079)
XLA Ops:
  0.5 2.0 %key_value_norm.1 = (bf16[32,1024]{1,0:T(8,128)(2,1)}, bf16[32,1024]{1,0:T(8,128)(2,1)}, bf16[32,1024]{1,0:T(8,128)(2,1)}, bf16[32,1024]{1,0:T(8,128)(2,1)}, bf1...) custom-call(s32[1]{0:T(128)} %bitcast.4.me_ref, ...), custom_call_target="tpu_custom_call" | custom-call | flops 1048576 | bytes 1048576 | tf_op jit(solution)/shard_map/key_value_norm/pallas_call | solution.py:124
  2.4 3.6 %collective-permute-start.10 = (bf16[32,1024]{1,0:T(8,128)(2,1)}, bf16[32,1024]{1,0:T(8,128)(2,1)S(1)}, u32[]{:S(2)}, u32[]{:S(2)}) collective-permute-start(bf16[32,1024]{1,0:T(8,128)(2,1)} %get-tuple-element.39), channel_id=1, source_target_pairs={{0,4},{1,5},{2,6},{3,7},{4,0},{5,1},{6,2},{7,3},{8,12},{9,13},{10,... | collective-permute-start | bytes 196616 | tf_op jit(solution)/shard_map/ppermute | solution.py:117
  6.2 3.6 %collective-permute-start.12 = (bf16[32,1024]{1,0:T(8,128)(2,1)}, bf16[32,1024]{1,0:T(8,128)(2,1)S(1)}, u32[]{:S(2)}, u32[]{:S(2)}) collective-permute-start(bf16[32,1024]{1,0:T(8,128)(2,1)} %get-tuple-element.41), channel_id=1, source_target_pairs={{0,6},{1,7},{2,4},{3,5},{4,2},{5,3},{6,0},{7,1},{8,14},{9,15},{10,... | collective-permute-start | bytes 196616 | tf_op jit(solution)/shard_map/ppermute | solution.py:117
  11.0 3.4 %collective-permute-done.11 = bf16[32,1024]{1,0:T(8,128)(2,1)S(1)} collective-permute-done((bf16[32,1024]{1,0:T(8,128)(2,1)}, bf16[32,1024]{1,0:T(8,128)(2,1)S(1)}, u32[]{:S(2)}, u32[]{:S(2)}) %collective-permute-start.11) | collective-permute-done | bytes 65568 | tf_op jit(solution)/shard_map/ppermute | solution.py:117
  14.4 2.5 %collective-permute-start.8 = (bf16[32,1024]{1,0:T(8,128)(2,1)}, bf16[32,1024]{1,0:T(8,128)(2,1)S(1)}, u32[]{:S(2)}, u32[]{:S(2)}) collective-permute-start(bf16[32,1024]{1,0:T(8,128)(2,1)} %get-tuple-element.37), channel_id=1, source_target_pairs={{0,2},{1,3},{2,0},{3,1},{4,6},{5,7},{6,4},{7,5},{8,10},{9,11},{10,... | collective-permute-start | bytes 196616 | tf_op jit(solution)/shard_map/ppermute | solution.py:117
  18.0 1.6 %collective-permute-start.17 = (bf16[128,1024]{1,0:T(8,128)(2,1)S(1)}, bf16[128,1024]{1,0:T(8,128)(2,1)S(1)}, u32[]{:S(2)}, u32[]{:S(2)}) collective-permute-start(bf16[128,1024]{1,0:T(8,128)(2,1)S(1)} %constant_dynamic-update-slice_fusion.4.refs_9_), channel_id=1, source_target_pairs={{0,16},{8,24},{16,0},{24,8},{1,17},{9,25},{17,1},{25,9},{2,18},{10... | collective-permute-start | bytes 786440 | tf_op jit(solution)/shard_map/ppermute | solution.py:117
  19.6 1.9 %collective-permute-done.9 = bf16[32,1024]{1,0:T(8,128)(2,1)S(1)} collective-permute-done((bf16[32,1024]{1,0:T(8,128)(2,1)}, bf16[32,1024]{1,0:T(8,128)(2,1)S(1)}, u32[]{:S(2)}, u32[]{:S(2)}) %collective-permute-start.9) | collective-permute-done | bytes 65568 | tf_op jit(solution)/shard_map/ppermute | solution.py:117
  23.0 1.8 %query_norm.1 = (bf16[32,512]{1,0:T(8,128)(2,1)}, bf16[32,512]{1,0:T(8,128)(2,1)}, bf16[32,512]{1,0:T(8,128)(2,1)}, bf16[32,512]{1,0:T(8,128)(2,1)}, bf16[32,512...) custom-call(s32[1]{0:T(128)} %bitcast.4.me_ref, ...), custom_call_target="tpu_custom_call" | custom-call | flops 1048576 | bytes 524288 | tf_op jit(solution)/shard_map/query_norm/pallas_call | solution.py:136
  27.2 1.8 %collective-permute-done.1.refs_2_ = bf16[32,512]{1,0:T(8,128)(2,1)S(1)} collective-permute-done((bf16[32,512]{1,0:T(8,128)(2,1)}, bf16[32,512]{1,0:T(8,128)(2,1)S(1)}, u32[]{:S(2)}, u32[]{:S(2)}) %collective-permute-start.1) | collective-permute-done | bytes 32800 | tf_op jit(solution)/shard_map/ppermute | solution.py:117
  29.0 3.1 %collective-permute-start.3 = (bf16[32,512]{1,0:T(8,128)(2,1)}, bf16[32,512]{1,0:T(8,128)(2,1)S(1)}, u32[]{:S(2)}, u32[]{:S(2)}) collective-permute-start(bf16[32,512]{1,0:T(8,128)(2,1)} %get-tuple-element.31), channel_id=1, source_target_pairs={{0,4},{1,5},{2,6},{3,7},{4,0},{5,1},{6,2},{7,3},{8,12},{9,13},{10,... | collective-permute-start | bytes 98312 | tf_op jit(solution)/shard_map/ppermute | solution.py:117
  32.7 1.5 %collective-permute-done.3.refs_4_ = bf16[32,512]{1,0:T(8,128)(2,1)S(1)} collective-permute-done((bf16[32,512]{1,0:T(8,128)(2,1)}, bf16[32,512]{1,0:T(8,128)(2,1)S(1)}, u32[]{:S(2)}, u32[]{:S(2)}) %collective-permute-start.3) | collective-permute-done | bytes 32800 | tf_op jit(solution)/shard_map/ppermute | solution.py:117
  34.2 4.7 %collective-permute-start.5 = (bf16[32,512]{1,0:T(8,128)(2,1)}, bf16[32,512]{1,0:T(8,128)(2,1)S(1)}, u32[]{:S(2)}, u32[]{:S(2)}) collective-permute-start(bf16[32,512]{1,0:T(8,128)(2,1)} %get-tuple-element.33), channel_id=1, source_target_pairs={{0,6},{1,7},{2,4},{3,5},{4,2},{5,3},{6,0},{7,1},{8,14},{9,15},{10,... | collective-permute-start | bytes 98312 | tf_op jit(solution)/shard_map/ppermute | solution.py:117
  38.9 2.2 %collective-permute-done.5.refs_6_ = bf16[32,512]{1,0:T(8,128)(2,1)S(1)} collective-permute-done((bf16[32,512]{1,0:T(8,128)(2,1)}, bf16[32,512]{1,0:T(8,128)(2,1)S(1)}, u32[]{:S(2)}, u32[]{:S(2)}) %collective-permute-start.5) | collective-permute-done | bytes 32800 | tf_op jit(solution)/shard_map/ppermute | solution.py:117
  41.2 3.1 %collective-permute-done.6.refs_7_ = bf16[32,512]{1,0:T(8,128)(2,1)S(1)} collective-permute-done((bf16[32,512]{1,0:T(8,128)(2,1)}, bf16[32,512]{1,0:T(8,128)(2,1)S(1)}, u32[]{:S(2)}, u32[]{:S(2)}) %collective-permute-start.6) | collective-permute-done | bytes 32800 | tf_op jit(solution)/shard_map/ppermute | solution.py:117
  46.4 2.5 %collective-permute-done.15.refs_11_ = bf16[128,1024]{1,0:T(8,128)(2,1)S(1)} collective-permute-done((bf16[128,1024]{1,0:T(8,128)(2,1)S(1)}, bf16[128,1024]{1,0:T(8,128)(2,1)S(1)}, u32[]{:S(2)}, u32[]{:S(2)}) %collective-permute-start.15) | collective-permute-done | bytes 262176 | tf_op jit(solution)/shard_map/ppermute | solution.py:117
  49.0 4.1 %collective-permute-done.16.refs_12_ = bf16[128,1024]{1,0:T(8,128)(2,1)S(1)} collective-permute-done((bf16[128,1024]{1,0:T(8,128)(2,1)S(1)}, bf16[128,1024]{1,0:T(8,128)(2,1)S(1)}, u32[]{:S(2)}, u32[]{:S(2)}) %collective-permute-start.16) | collective-permute-done | bytes 262176 | tf_op jit(solution)/shard_map/ppermute | solution.py:117
  53.1 2.8 %collective-permute-done.18.refs_14_ = bf16[128,1024]{1,0:T(8,128)(2,1)S(1)} collective-permute-done((bf16[128,1024]{1,0:T(8,128)(2,1)S(1)}, bf16[128,1024]{1,0:T(8,128)(2,1)S(1)}, u32[]{:S(2)}, u32[]{:S(2)}) %collective-permute-start.18) | collective-permute-done | bytes 262176 | tf_op jit(solution)/shard_map/ppermute | solution.py:117
  57.3 4.3 %attention.1 = (bf16[128,512]{1,0:T(8,128)(2,1)S(1)}, bf16[128,512]{1,0:T(8,128)(2,1)S(1)}) custom-call(s32[1]{0:T(128)} %bitcast.3.slot_ref, s32[4]{0:T(128)S(1)} %copy-done.2, bf16[32,512]{1,0:T(8,128)(2,1)S(1)} %copy-done.1, bf16[32,512]{1,0:T(8,128)(2,1)S(1)} %collective-permute-done.refs_1_, bf16[32,512]{1,0:T(8,128)(2,1)S(1)} %collective-permute-done.1.refs_2_, ...), custom_call_target="tpu_custom_call" | custom-call | flops 536870912 | bytes 2097152 | tf_op jit(solution)/shard_map/attention/pallas_call | solution.py:159
  63.1 2.5 %copy-done = bf16[512,5120]{1,0:T(8,128)(2,1)S(1)} copy-done((bf16[512,5120]{1,0:T(8,128)(2,1)S(1)}, bf16[512,5120]{1,0:T(8,128)(2,1)}, u32[]{:S(2)}) %copy-start) | copy-done | bytes 5242904
  65.6 4.7 %projection.1 = (f32[32,5120]{1,0:T(8,128)S(1)}, bf16[32,5120]{1,0:T(8,128)(2,1)S(1)}, f32[32,5120]{1,0:T(8,128)S(1)}, bf16[32,5120]{1,0:T(8,128)(2,1)S(1)}) custom-call(bf16[128,512]{1,0:T(8,128)(2,1)S(1)} %get-tuple-element.43.mine_ref, bf16[128,512]{1,0:T(8,128)(2,1)S(1)} %collective-permute-done.20.theirs_ref, bf16[512,5120]{1,0:T(8,128)(2,1)S(1)} %copy-done, ...), custom_call_target="tpu_custom_call" | custom-call | flops 1342177280 | bytes 11796480 | tf_op jit(solution)/shard_map/projection/pallas_call | solution.py:176
  72.9 2.1 %collective-permute-start.22 = (bf16[32,5120]{1,0:T(8,128)(2,1)S(1)}, bf16[32,5120]{1,0:T(8,128)(2,1)S(1)}, u32[]{:S(2)}, u32[]{:S(2)}) collective-permute-start(bf16[32,5120]{1,0:T(8,128)(2,1)S(1)} %get-tuple-element.46), channel_id=1, source_target_pairs={{0,2},{1,3},{2,0},{3,1},{4,6},{5,7},{6,4},{7,5},{8,10},{9,11},{10,... | collective-permute-start | bytes 983048 | tf_op jit(solution)/shard_map/ppermute | solution.py:117
  75.0 5.9 %collective-permute-done.23 = bf16[32,5120]{1,0:T(8,128)(2,1)S(1)} collective-permute-done((bf16[32,5120]{1,0:T(8,128)(2,1)S(1)}, bf16[32,5120]{1,0:T(8,128)(2,1)S(1)}, u32[]{:S(2)}, u32[]{:S(2)}) %collective-permute-start.23) | collective-permute-done | bytes 327712 | tf_op jit(solution)/shard_map/ppermute | solution.py:117
  83.3 9.1 %collective-permute-done.22 = bf16[32,5120]{1,0:T(8,128)(2,1)S(1)} collective-permute-done((bf16[32,5120]{1,0:T(8,128)(2,1)S(1)}, bf16[32,5120]{1,0:T(8,128)(2,1)S(1)}, u32[]{:S(2)}, u32[]{:S(2)}) %collective-permute-start.22) | collective-permute-done | bytes 327712 | tf_op jit(solution)/shard_map/ppermute | solution.py:117
  92.4 4.7 %collective-permute-done.24 = bf16[32,5120]{1,0:T(8,128)(2,1)S(1)} collective-permute-done((bf16[32,5120]{1,0:T(8,128)(2,1)S(1)}, bf16[32,5120]{1,0:T(8,128)(2,1)S(1)}, u32[]{:S(2)}, u32[]{:S(2)}) %collective-permute-start.24) | collective-permute-done | bytes 327712 | tf_op jit(solution)/shard_map/ppermute | solution.py:117
  (55 shorter events, 16.4 us)
Async XLA Ops:
  0.0 63.1 %collective-permute-start.21 = (bf16[512,5120]{1,0:T(8,128)(2,1)}, bf16[512,5120]{1,0:T(8,128)(2,1)}, u32[]{:S(2)}, u32[]{:S(2)}) collective-permute-start(bf16[512,5120]{1,0:T(8,128)(2,1)} %own_ref.1), channel_id=1, source_target_pairs={{0,1},{1,0},{2,3},{3,2},{4,5},{5,4},{6,7},{7,6},{8,9},{9,8},{10,11... | collective-permute-start | bytes 15728648 | tf_op jit(solution)/shard_map/ppermute | solution.py:117
  2.4 8.2 %collective-permute-start.10 = (bf16[32,1024]{1,0:T(8,128)(2,1)}, bf16[32,1024]{1,0:T(8,128)(2,1)S(1)}, u32[]{:S(2)}, u32[]{:S(2)}) collective-permute-start(bf16[32,1024]{1,0:T(8,128)(2,1)} %get-tuple-element.39), channel_id=1, source_target_pairs={{0,4},{1,5},{2,6},{3,7},{4,0},{5,1},{6,2},{7,3},{8,12},{9,13},{10,... | collective-permute-start | bytes 196616 | tf_op jit(solution)/shard_map/ppermute | solution.py:117
  6.0 8.4 %collective-permute-start.11 = (bf16[32,1024]{1,0:T(8,128)(2,1)}, bf16[32,1024]{1,0:T(8,128)(2,1)S(1)}, u32[]{:S(2)}, u32[]{:S(2)}) collective-permute-start(bf16[32,1024]{1,0:T(8,128)(2,1)} %get-tuple-element.40), channel_id=1, source_target_pairs={{0,5},{1,4},{2,7},{3,6},{4,1},{5,0},{6,3},{7,2},{8,13},{9,12},{10,... | collective-permute-start | bytes 196616 | tf_op jit(solution)/shard_map/ppermute | solution.py:117
  6.2 10.7 %collective-permute-start.12 = (bf16[32,1024]{1,0:T(8,128)(2,1)}, bf16[32,1024]{1,0:T(8,128)(2,1)S(1)}, u32[]{:S(2)}, u32[]{:S(2)}) collective-permute-start(bf16[32,1024]{1,0:T(8,128)(2,1)} %get-tuple-element.41), channel_id=1, source_target_pairs={{0,6},{1,7},{2,4},{3,5},{4,2},{5,3},{6,0},{7,1},{8,14},{9,15},{10,... | collective-permute-start | bytes 196616 | tf_op jit(solution)/shard_map/ppermute | solution.py:117
  9.8 8.1 %collective-permute-start.13 = (bf16[32,1024]{1,0:T(8,128)(2,1)}, bf16[32,1024]{1,0:T(8,128)(2,1)S(1)}, u32[]{:S(2)}, u32[]{:S(2)}) collective-permute-start(bf16[32,1024]{1,0:T(8,128)(2,1)} %get-tuple-element.42), channel_id=1, source_target_pairs={{0,7},{1,6},{2,5},{3,4},{4,3},{5,2},{6,1},{7,0},{8,15},{9,14},{10,... | collective-permute-start | bytes 196616 | tf_op jit(solution)/shard_map/ppermute | solution.py:117
  10.6 8.9 %collective-permute-start.7 = (bf16[32,1024]{1,0:T(8,128)(2,1)}, bf16[32,1024]{1,0:T(8,128)(2,1)S(1)}, u32[]{:S(2)}, u32[]{:S(2)}) collective-permute-start(bf16[32,1024]{1,0:T(8,128)(2,1)} %get-tuple-element.36), channel_id=1, source_target_pairs={{0,1},{1,0},{2,3},{3,2},{4,5},{5,4},{6,7},{7,6},{8,9},{9,8},{10,11... | collective-permute-start | bytes 196616 | tf_op jit(solution)/shard_map/ppermute | solution.py:117
  14.4 5.1 %collective-permute-start.8 = (bf16[32,1024]{1,0:T(8,128)(2,1)}, bf16[32,1024]{1,0:T(8,128)(2,1)S(1)}, u32[]{:S(2)}, u32[]{:S(2)}) collective-permute-start(bf16[32,1024]{1,0:T(8,128)(2,1)} %get-tuple-element.37), channel_id=1, source_target_pairs={{0,2},{1,3},{2,0},{3,1},{4,6},{5,7},{6,4},{7,5},{8,10},{9,11},{10,... | collective-permute-start | bytes 196616 | tf_op jit(solution)/shard_map/ppermute | solution.py:117
  16.9 4.6 %collective-permute-start.9 = (bf16[32,1024]{1,0:T(8,128)(2,1)}, bf16[32,1024]{1,0:T(8,128)(2,1)S(1)}, u32[]{:S(2)}, u32[]{:S(2)}) collective-permute-start(bf16[32,1024]{1,0:T(8,128)(2,1)} %get-tuple-element.38), channel_id=1, source_target_pairs={{0,3},{1,2},{2,1},{3,0},{4,7},{5,6},{6,5},{7,4},{8,11},{9,10},{10,... | collective-permute-start | bytes 196616 | tf_op jit(solution)/shard_map/ppermute | solution.py:117
  18.0 27.8 %collective-permute-start.17 = (bf16[128,1024]{1,0:T(8,128)(2,1)S(1)}, bf16[128,1024]{1,0:T(8,128)(2,1)S(1)}, u32[]{:S(2)}, u32[]{:S(2)}) collective-permute-start(bf16[128,1024]{1,0:T(8,128)(2,1)S(1)} %constant_dynamic-update-slice_fusion.4.refs_9_), channel_id=1, source_target_pairs={{0,16},{8,24},{16,0},{24,8},{1,17},{9,25},{17,1},{25,9},{2,18},{10... | collective-permute-start | bytes 786440 | tf_op jit(solution)/shard_map/ppermute | solution.py:117
  21.5 24.4 %collective-permute-start.14 = (bf16[128,1024]{1,0:T(8,128)(2,1)S(1)}, bf16[128,1024]{1,0:T(8,128)(2,1)S(1)}, u32[]{:S(2)}, u32[]{:S(2)}) collective-permute-start(bf16[128,1024]{1,0:T(8,128)(2,1)S(1)} %constant_dynamic-update-slice_fusion.refs_8_), channel_id=1, source_target_pairs={{0,8},{8,0},{16,24},{24,16},{1,9},{9,1},{17,25},{25,17},{2,10},{10... | collective-permute-start | bytes 786440 | tf_op jit(solution)/shard_map/ppermute | solution.py:117
  24.8 1.4 %collective-permute-start = (bf16[32,512]{1,0:T(8,128)(2,1)}, bf16[32,512]{1,0:T(8,128)(2,1)S(1)}, u32[]{:S(2)}, u32[]{:S(2)}) collective-permute-start(bf16[32,512]{1,0:T(8,128)(2,1)} %get-tuple-element.28), channel_id=1, source_target_pairs={{0,1},{1,0},{2,3},{3,2},{4,5},{5,4},{6,7},{7,6},{8,9},{9,8},{10,11... | collective-permute-start | bytes 98312 | tf_op jit(solution)/shard_map/ppermute | solution.py:117
  24.8 4.2 %collective-permute-start.1 = (bf16[32,512]{1,0:T(8,128)(2,1)}, bf16[32,512]{1,0:T(8,128)(2,1)S(1)}, u32[]{:S(2)}, u32[]{:S(2)}) collective-permute-start(bf16[32,512]{1,0:T(8,128)(2,1)} %get-tuple-element.29), channel_id=1, source_target_pairs={{0,2},{1,3},{2,0},{3,1},{4,6},{5,7},{6,4},{7,5},{8,10},{9,11},{10,... | collective-permute-start | bytes 98312 | tf_op jit(solution)/shard_map/ppermute | solution.py:117
  26.2 5.9 %collective-permute-start.2 = (bf16[32,512]{1,0:T(8,128)(2,1)}, bf16[32,512]{1,0:T(8,128)(2,1)S(1)}, u32[]{:S(2)}, u32[]{:S(2)}) collective-permute-start(bf16[32,512]{1,0:T(8,128)(2,1)} %get-tuple-element.30), channel_id=1, source_target_pairs={{0,3},{1,2},{2,1},{3,0},{4,7},{5,6},{6,5},{7,4},{8,11},{9,10},{10,... | collective-permute-start | bytes 98312 | tf_op jit(solution)/shard_map/ppermute | solution.py:117
  29.0 5.2 %collective-permute-start.3 = (bf16[32,512]{1,0:T(8,128)(2,1)}, bf16[32,512]{1,0:T(8,128)(2,1)S(1)}, u32[]{:S(2)}, u32[]{:S(2)}) collective-permute-start(bf16[32,512]{1,0:T(8,128)(2,1)} %get-tuple-element.31), channel_id=1, source_target_pairs={{0,4},{1,5},{2,6},{3,7},{4,0},{5,1},{6,2},{7,3},{8,12},{9,13},{10,... | collective-permute-start | bytes 98312 | tf_op jit(solution)/shard_map/ppermute | solution.py:117
  32.1 6.8 %collective-permute-start.4 = (bf16[32,512]{1,0:T(8,128)(2,1)}, bf16[32,512]{1,0:T(8,128)(2,1)S(1)}, u32[]{:S(2)}, u32[]{:S(2)}) collective-permute-start(bf16[32,512]{1,0:T(8,128)(2,1)} %get-tuple-element.32), channel_id=1, source_target_pairs={{0,5},{1,4},{2,7},{3,6},{4,1},{5,0},{6,3},{7,2},{8,13},{9,12},{10,... | collective-permute-start | bytes 98312 | tf_op jit(solution)/shard_map/ppermute | solution.py:117
  34.2 6.9 %collective-permute-start.5 = (bf16[32,512]{1,0:T(8,128)(2,1)}, bf16[32,512]{1,0:T(8,128)(2,1)S(1)}, u32[]{:S(2)}, u32[]{:S(2)}) collective-permute-start(bf16[32,512]{1,0:T(8,128)(2,1)} %get-tuple-element.33), channel_id=1, source_target_pairs={{0,6},{1,7},{2,4},{3,5},{4,2},{5,3},{6,0},{7,1},{8,14},{9,15},{10,... | collective-permute-start | bytes 98312 | tf_op jit(solution)/shard_map/ppermute | solution.py:117
  38.9 5.3 %collective-permute-start.6 = (bf16[32,512]{1,0:T(8,128)(2,1)}, bf16[32,512]{1,0:T(8,128)(2,1)S(1)}, u32[]{:S(2)}, u32[]{:S(2)}) collective-permute-start(bf16[32,512]{1,0:T(8,128)(2,1)} %get-tuple-element.34), channel_id=1, source_target_pairs={{0,7},{1,6},{2,5},{3,4},{4,3},{5,2},{6,1},{7,0},{8,15},{9,14},{10,... | collective-permute-start | bytes 98312 | tf_op jit(solution)/shard_map/ppermute | solution.py:117
  41.1 7.9 %collective-permute-start.15 = (bf16[128,1024]{1,0:T(8,128)(2,1)S(1)}, bf16[128,1024]{1,0:T(8,128)(2,1)S(1)}, u32[]{:S(2)}, u32[]{:S(2)}) collective-permute-start(bf16[128,1024]{1,0:T(8,128)(2,1)S(1)} %constant_dynamic-update-slice_fusion.4.refs_9_), channel_id=1, source_target_pairs={{0,8},{8,0},{16,24},{24,16},{1,9},{9,1},{17,25},{25,17},{2,10},{10... | collective-permute-start | bytes 786440 | tf_op jit(solution)/shard_map/ppermute | solution.py:117
  44.2 8.9 %collective-permute-start.16 = (bf16[128,1024]{1,0:T(8,128)(2,1)S(1)}, bf16[128,1024]{1,0:T(8,128)(2,1)S(1)}, u32[]{:S(2)}, u32[]{:S(2)}) collective-permute-start(bf16[128,1024]{1,0:T(8,128)(2,1)S(1)} %constant_dynamic-update-slice_fusion.refs_8_), channel_id=1, source_target_pairs={{0,16},{8,24},{16,0},{24,8},{1,17},{9,25},{17,1},{25,9},{2,18},{10... | collective-permute-start | bytes 786440 | tf_op jit(solution)/shard_map/ppermute | solution.py:117
  45.7 7.3 %collective-permute-start.19 = (bf16[128,1024]{1,0:T(8,128)(2,1)S(1)}, bf16[128,1024]{1,0:T(8,128)(2,1)S(1)}, u32[]{:S(2)}, u32[]{:S(2)}) collective-permute-start(bf16[128,1024]{1,0:T(8,128)(2,1)S(1)} %collective-permute-done.17.refs_13_), channel_id=1, source_target_pairs={{0,8},{8,0},{16,24},{24,16},{1,9},{9,1},{17,25},{25,17},{2,10},{10... | collective-permute-start | bytes 786440 | tf_op jit(solution)/shard_map/ppermute | solution.py:117
  45.9 10.0 %collective-permute-start.18 = (bf16[128,1024]{1,0:T(8,128)(2,1)S(1)}, bf16[128,1024]{1,0:T(8,128)(2,1)S(1)}, u32[]{:S(2)}, u32[]{:S(2)}) collective-permute-start(bf16[128,1024]{1,0:T(8,128)(2,1)S(1)} %collective-permute-done.14.refs_10_), channel_id=1, source_target_pairs={{0,16},{8,24},{16,0},{24,8},{1,17},{9,25},{17,1},{25,9},{2,18},{10... | collective-permute-start | bytes 786440 | tf_op jit(solution)/shard_map/ppermute | solution.py:117
  70.3 10.6 %collective-permute-start.23 = (bf16[32,5120]{1,0:T(8,128)(2,1)S(1)}, bf16[32,5120]{1,0:T(8,128)(2,1)S(1)}, u32[]{:S(2)}, u32[]{:S(2)}) collective-permute-start(bf16[32,5120]{1,0:T(8,128)(2,1)S(1)} %get-tuple-element.48), channel_id=1, source_target_pairs={{0,2},{1,3},{2,0},{3,1},{4,6},{5,7},{6,4},{7,5},{8,10},{9,11},{10,... | collective-permute-start | bytes 983048 | tf_op jit(solution)/shard_map/ppermute | solution.py:117
  72.9 19.5 %collective-permute-start.22 = (bf16[32,5120]{1,0:T(8,128)(2,1)S(1)}, bf16[32,5120]{1,0:T(8,128)(2,1)S(1)}, u32[]{:S(2)}, u32[]{:S(2)}) collective-permute-start(bf16[32,5120]{1,0:T(8,128)(2,1)S(1)} %get-tuple-element.46), channel_id=1, source_target_pairs={{0,2},{1,3},{2,0},{3,1},{4,6},{5,7},{6,4},{7,5},{8,10},{9,11},{10,... | collective-permute-start | bytes 983048 | tf_op jit(solution)/shard_map/ppermute | solution.py:117
  81.0 16.2 %collective-permute-start.24 = (bf16[32,5120]{1,0:T(8,128)(2,1)S(1)}, bf16[32,5120]{1,0:T(8,128)(2,1)S(1)}, u32[]{:S(2)}, u32[]{:S(2)}) collective-permute-start(bf16[32,5120]{1,0:T(8,128)(2,1)S(1)} %add_convert_fusion), channel_id=1, source_target_pairs={{0,4},{1,5},{2,6},{3,7},{4,0},{5,1},{6,2},{7,3},{8,12},{9,13},{10,... | collective-permute-start | bytes 983048 | tf_op jit(solution)/shard_map/ppermute | solution.py:117
  (7 other events, 48.4 us)

commit v2 on v1

v2 whole, which is shorter than its diff:
```python
import functools

import jax
import jax.numpy as jnp
from jax import lax
from jax.experimental import pallas as pl
from jax.experimental.pallas import tpu as pltpu
from jax.sharding import PartitionSpec as P

HD = 128
EPS = 1e-06
LOG2E = 1.4426950408889634
VMEM = pltpu.VMEM
SMEM = pltpu.SMEM


def inverse_rms(rows):
    values = rows.astype(jnp.float32)
    return lax.rsqrt(jnp.mean(values * values, axis=-1, keepdims=True) + EPS)


def key_value_kernel(chips, me_ref, key_ref, gain_ref, value_ref, *outs):
    rows = key_ref.shape[0]
    width = key_ref.shape[1] // (2 * chips)
    inverse = inverse_rms(key_ref[...])
    me = me_ref[0]
    for r in range(chips):
        for parity in range(2):
            here = slice(parity * rows, (parity + 1) * rows)
            cols = pl.ds(pl.multiple_of((me ^ (2 * r + parity)) * width, width), width)
            normed = key_ref[:, cols].astype(jnp.float32) * inverse * gain_ref[:, cols]
            outs[r][here, :width] = normed.astype(jnp.bfloat16)
            outs[r][here, width:] = value_ref[:, cols]


def query_kernel(chips, me_ref, rows_ref, gain_ref, own_ref, cross_ref):
    rows = rows_ref.shape[0]
    width = rows_ref.shape[1] // (2 * chips)
    inverse = inverse_rms(rows_ref[...])
    me = me_ref[0]
    for r in range(chips):
        here = slice(r * rows, (r + 1) * rows)
        for parity, out_ref in ((1, cross_ref), (0, own_ref)):
            cols = pl.ds(pl.multiple_of((me ^ (2 * r + parity)) * width, width), width)
            normed = rows_ref[:, cols].astype(jnp.float32) * inverse * gain_ref[:, cols]
            out_ref[here] = normed.astype(jnp.bfloat16)


def pair_kernel(chips, own_ref, got_ref, *refs):
    outs = refs[-chips:]
    rows = own_ref.shape[0] // chips
    for r in range(chips):
        here = slice(r * rows, (r + 1) * rows)
        outs[r][:rows] = own_ref[here]
        outs[r][rows:] = got_ref[here]


def attention_kernel(count, frames, slot_ref, order_ref, *refs):
    queries = refs[:count]
    pieces = refs[count:-2]
    even_ref, odd_ref = refs[-2:]
    width = queries[0].shape[1]
    rows = queries[0].shape[0] // 2
    key_rows = sum(piece.shape[0] for piece in pieces) // frames
    slot = slot_ref[0]
    my_rank = order_ref[slot]
    factor = (HD ** (-0.5)) * LOG2E
    hidden = jnp.concatenate(
        [
            jnp.full((1, key_rows), jnp.where(order_ref[slot ^ f] <= my_rank, 0.0, -1e30), jnp.float32)
            for f in range(frames)
        ],
        axis=1,
    )
    step = max(1, min(count, 128 // rows))
    for h in range(width // HD):
        cols = slice(h * HD, (h + 1) * HD)
        value_cols = slice(width + h * HD, width + (h + 1) * HD)
        keys = jnp.concatenate([piece[:, cols] for piece in pieces], axis=0)
        values = jnp.concatenate([piece[:, value_cols] for piece in pieces], axis=0)
        for parity, out_ref in ((1, odd_ref), (0, even_ref)):
            for start in range(0, count, step):
                here = slice(start * rows, (start + step) * rows)
                query = jnp.concatenate(
                    [block[parity * rows : (parity + 1) * rows, cols] for block in queries[start : start + step]],
                    axis=0,
                )
                scores = lax.dot_general(
                    query,
                    keys,
                    (((1,), (1,)), ((), ())),
                    preferred_element_type=jnp.float32,
                )
                scores = scores + hidden
                top = jnp.max(scores, axis=1, keepdims=True)
                exponent = jnp.exp2((scores - top) * factor)
                total = jnp.sum(exponent, axis=1, keepdims=True)
                summed = jnp.dot(
                    exponent.astype(jnp.bfloat16), values, preferred_element_type=jnp.float32
                )
                out_ref[here, cols] = (summed / total).astype(jnp.bfloat16)


def projection_kernel(chunks, mine_ref, theirs_ref, own_ref, other_ref, *outs):
    rows = mine_ref.shape[0] // chunks
    result = jnp.dot(mine_ref[...], own_ref[...], preferred_element_type=jnp.float32)
    result += jnp.dot(theirs_ref[...], other_ref[...], preferred_element_type=jnp.float32)
    for j in range(chunks):
        outs[j][...] = result[j * rows : (j + 1) * rows].astype(outs[j].dtype)


def shards(
    tokens,
    query_rows,
    key_rows,
    value_rows,
    gain_query,
    gain_key,
    out_weight,
    out_bias,
    gate_table,
    noise_level,
    slot_order,
):
    n = lax.axis_size("seq")
    frames = lax.axis_size("frame")
    chips = n // 2
    rows, features = query_rows.shape[1:]
    width = features // n
    model = out_weight.shape[1]
    me = lax.axis_index("seq").astype(jnp.int32)
    slot = lax.axis_index("frame").astype(jnp.int32)
    me_array = me.reshape(1)
    slot_array = slot.reshape(1)

    def across(value, axis, distance):
        size = n if axis == "seq" else frames
        return lax.ppermute(value, axis, [(i, i ^ distance) for i in range(size)])

    def after(value, *earlier):
        return lax.optimization_barrier((value, *earlier))[0]

    smem = pl.BlockSpec(memory_space=SMEM)
    vmem = pl.BlockSpec(memory_space=VMEM)

    other_weight = across(out_weight, "seq", 1)
    sends = pl.pallas_call(
        functools.partial(key_value_kernel, chips),
        out_shape=[jax.ShapeDtypeStruct((2 * rows, 2 * width), jnp.bfloat16)] * chips,
        in_specs=[smem, vmem, vmem, vmem],
        out_specs=[vmem] * chips,
        cost_estimate=pl.CostEstimate(
            flops=8 * rows * features, bytes_accessed=8 * rows * features, transcendentals=0
        ),
        name="key_value_norm",
    )(me_array, key_rows[0], gain_key.reshape(1, features), value_rows[0])
    query_own, query_cross = pl.pallas_call(
        functools.partial(query_kernel, chips),
        out_shape=[jax.ShapeDtypeStruct((chips * rows, width), jnp.bfloat16)] * 2,
        in_specs=[smem, vmem, vmem],
        out_specs=[vmem] * 2,
        cost_estimate=pl.CostEstimate(
            flops=8 * rows * features, bytes_accessed=4 * rows * features, transcendentals=0
        ),
        name="query_norm",
    )(me_array, query_rows[0], gain_query.reshape(1, features))
    query_sends = pl.pallas_call(
        functools.partial(pair_kernel, chips),
        out_shape=[jax.ShapeDtypeStruct((2 * rows, width), jnp.bfloat16)] * chips,
        in_specs=[vmem, vmem],
        out_specs=[vmem] * chips,
        cost_estimate=pl.CostEstimate(
            flops=0, bytes_accessed=8 * chips * rows * width, transcendentals=0
        ),
        name="query_pair",
    )(query_own, across(query_cross, "seq", 1))

    blocks = [sends[0]] + [across(sends[r], "seq", 2 * r) for r in range(1, chips)]
    mine = jnp.concatenate([block[:rows] for block in blocks], axis=0)
    given = jnp.concatenate([block[rows:] for block in blocks], axis=0)
    halves = mine, across(after(given, *query_sends), "seq", 1)

    bits = [1 << b for b in range(frames.bit_length() - 1)]
    held = []
    for half, order in zip(halves, (bits, bits[::-1])):
        found = {0: half}
        for bit in order:
            found.update({f ^ bit: across(piece, "frame", bit) for f, piece in found.items()})
        held.append(found)
    pieces = [held[u][f] for f in range(frames) for u in range(2)]

    queries = [query_sends[0]] + [
        across(after(query_sends[r], held[0][bits[0]], other_weight), "seq", 2 * r) for r in range(1, chips)
    ]
    frame_rows = n * rows
    keys = frame_rows * frames
    even, odd = pl.pallas_call(
        functools.partial(attention_kernel, chips, frames),
        out_shape=[jax.ShapeDtypeStruct((frame_rows // 2, width), jnp.bfloat16)] * 2,
        in_specs=[smem, smem] + [vmem] * (chips + len(pieces)),
        out_specs=[vmem] * 2,
        compiler_params=pltpu.CompilerParams(vmem_limit_bytes=8 * 2**20 + 6 * 128 * keys * 4),
        cost_estimate=pl.CostEstimate(
            flops=4 * frame_rows * keys * width,
            bytes_accessed=4 * keys * width,
            transcendentals=frame_rows * keys * (width // HD),
        ),
        name="attention",
    )(slot_array, slot_order, *queries, *pieces)
    theirs = across(odd, "seq", 1)

    tile = model // 4
    partial_sums = pl.pallas_call(
        functools.partial(projection_kernel, chips),
        grid=(model // tile,),
        out_shape=[
            jax.ShapeDtypeStruct((rows, model), jnp.bfloat16 if j % 2 else jnp.float32)
            for j in range(chips)
        ],
        in_specs=[
            pl.BlockSpec((frame_rows // 2, width), lambda i: (0, 0)),
            pl.BlockSpec((frame_rows // 2, width), lambda i: (0, 0)),
            pl.BlockSpec((width, tile), lambda i: (0, i)),
            pl.BlockSpec((width, tile), lambda i: (0, i)),
        ],
        out_specs=[pl.BlockSpec((rows, tile), lambda i: (0, i))] * chips,
        compiler_params=pltpu.CompilerParams(vmem_limit_bytes=16 * 2**20),
        cost_estimate=pl.CostEstimate(
            flops=2 * frame_rows * width * model,
            bytes_accessed=4 * width * model + 8 * rows * model,
            transcendentals=0,
        ),
        name="projection",
    )(even, theirs, out_weight, other_weight)

    sums = {j: part for j, part in enumerate(partial_sums)}
    bit = 1
    while bit < chips:
        leaving = sorted((j for j in sums if j & bit), reverse=True)
        earlier = ()
        for j in leaving:
            leaves = after(sums.pop(j).astype(jnp.bfloat16), *earlier)
            arrived = across(leaves, "seq", 2 * bit)
            sums[j ^ bit] = sums[j ^ bit].astype(jnp.float32) + arrived.astype(jnp.float32)
            earlier = (arrived,)
        bit *= 2
    projected = sums[0]

    level = lax.dynamic_index_in_dim(noise_level, slot, keepdims=False)
    gate_row = lax.dynamic_index_in_dim(gate_table, level, keepdims=True).astype(jnp.float32)
    bias = out_bias.astype(jnp.float32)[None, :]
    mixed = tokens[0].astype(jnp.float32) + gate_row * (projected + bias)
    return mixed.astype(jnp.bfloat16)[None]


def solution(mesh):
    placed = (
        P("frame", "seq", None),
        P("frame", "seq", None),
        P("frame", "seq", None),
        P("frame", "seq", None),
        P(),
        P(),
        P("seq", None),
        P(),
        P(),
        P(),
        P(),
    )
    return jax.shard_map(
        shards, mesh=mesh, in_specs=placed, out_specs=P("frame", "seq", None), check_vma=False
    )
```

time: 98.5 us -> 85 us (0.86)
  starting transfers between devices: 31.2 us -> 22.6 us
  waiting for transfers between devices: 44.7 us -> 38.1 us
  Pallas kernels: 12.8 us -> 13.8 us
    ppermute x25 -> x19, starting transfers between devices: 31.2 us -> 22.6 us  [across(): return lax.ppermute(value, axis, [(i, i ^ distance) for i in range(size)])]
    ppermute x25 -> x19, waiting for transfers between devices: 44.7 us -> 38.1 us  [across(): return lax.ppermute(value, axis, [(i, i ^ distance) for i in range(size)])]
    pallas_call x4 -> x5, Pallas kernels: 12.8 us -> 13.8 us  [the longest x1 4.71 us: shards(): pl.pallas_call(functools.partial(projection_kernel, chips), grid=(model /...]
    unnamed x18 -> x14, local copies, waits for them, and re-layouts: 4.78 us -> 4.65 us
  transfers between devices with their start and end apart: 25 -> 19, of which waited for: 14 -> 11; matrix products, arithmetic and copies ran while one was open for 2% -> 3% of each run, Pallas kernels for 8% -> 7%
where the time goes in v2:
time: 85 us; the launch traced here: 84.6 us
  waiting for transfers between devices  38.1 us (45%)
  starting transfers between devices  22.6 us (27%)
  Pallas kernels  13.8 us (16%)
  local copies, waits for them, and re-layouts  6.14 us (7%)
  between operations  2.07 us (2%)
  other arithmetic  1.92 us (2%)
    ppermute x19, waiting for transfers between devices, across(): return lax.ppermute(value, axis, [(i, i ^ distance) for i in range(size)])  38.1 us
    ppermute x19, starting transfers between devices, across(): return lax.ppermute(value, axis, [(i, i ^ distance) for i in range(size)])  22.6 us
    pallas_call x1, Pallas kernels, shards(): pl.pallas_call(functools.partial(projection_kernel, chips), grid=(model /...  4.71 us
    unnamed x14, local copies, waits for them, and re-layouts  4.65 us
    pallas_call x1, Pallas kernels, shards(): pl.pallas_call(functools.partial(attention_kernel, chips, frames), out_sh...  3.51 us
    pallas_call x1, Pallas kernels, shards(): pl.pallas_call(functools.partial(key_value_kernel, chips), out_shape=[jax...  2.02 us
    pallas_call x1, Pallas kernels, shards(): pl.pallas_call(functools.partial(query_kernel, chips), out_shape=[jax.Sha...  1.83 us
  transfers between devices with their start and end apart: 19, of which 11 were waited for; matrix products, arithmetic and copies ran while one was open for 3% of the time, Pallas kernels for 7%

profile of v2, /device:TPU:0, one launch (start us, length us, event | category | flops | bytes accessed | tf_op | source)
XLA Modules:
  0.0 84.6 jit_solution(18322093363725670904)
XLA Ops:
  0.5 2.0 %key_value_norm.1 = (bf16[64,1024]{1,0:T(8,128)(2,1)}, bf16[64,1024]{1,0:T(8,128)(2,1)}, bf16[64,1024]{1,0:T(8,128)(2,1)}, bf16[64,1024]{1,0:T(8,128)(2,1)}) custom-call(s32[1]{0:T(128)} %bitcast.4.me_ref, bf16[32,4096]{1,0:T(8,128)(2,1)} %bitcast.14, f32[1,4096]{1,0:T(1,128)} %bitcast.18, bf16[32,4096]{1,0:T(8,128)(2,1)} %bitcast.15), custom_call_target="tpu_custom_call" | custom-call | flops 1048576 | bytes 1048576 | tf_op jit(solution)/shard_map/key_value_norm/pallas_call | solution.py:147
  2.5 2.6 %collective-permute-start.1 = (bf16[64,1024]{1,0:T(8,128)(2,1)}, bf16[64,1024]{1,0:T(8,128)(2,1)S(1)}, u32[]{:S(2)}, u32[]{:S(2)}) collective-permute-start(bf16[64,1024]{1,0:T(8,128)(2,1)} %get-tuple-element.31), channel_id=1, source_target_pairs={{0,2},{1,3},{2,0},{3,1},{4,6},{5,7},{6,4},{7,5},{8,10},{9,11},{10,... | collective-permute-start | bytes 393224 | tf_op jit(solution)/shard_map/ppermute | solution.py:138
  5.0 2.6 %collective-permute-start.2 = (bf16[64,1024]{1,0:T(8,128)(2,1)}, bf16[64,1024]{1,0:T(8,128)(2,1)S(1)}, u32[]{:S(2)}, u32[]{:S(2)}) collective-permute-start(bf16[64,1024]{1,0:T(8,128)(2,1)} %get-tuple-element.32), channel_id=1, source_target_pairs={{0,4},{1,5},{2,6},{3,7},{4,0},{5,1},{6,2},{7,3},{8,12},{9,13},{10,... | collective-permute-start | bytes 393224 | tf_op jit(solution)/shard_map/ppermute | solution.py:138
  7.6 1.8 %query_norm.1 = (bf16[128,512]{1,0:T(8,128)(2,1)}, bf16[128,512]{1,0:T(8,128)(2,1)}) custom-call(s32[1]{0:T(128)} %bitcast.4.me_ref, bf16[32,4096]{1,0:T(8,128)(2,1)} %bitcast.16, f32[1,4096]{1,0:T(1,128)} %bitcast.19), custom_call_target="tpu_custom_call" | custom-call | flops 1048576 | bytes 524288 | tf_op jit(solution)/shard_map/query_norm/pallas_call | solution.py:157
  11.7 1.7 %query_pair.1 = (bf16[64,512]{1,0:T(8,128)(2,1)}, bf16[64,512]{1,0:T(8,128)(2,1)}, bf16[64,512]{1,0:T(8,128)(2,1)}, bf16[64,512]{1,0:T(8,128)(2,1)}) custom-call(bf16[128,512]{1,0:T(8,128)(2,1)} %get-tuple-element.26.own_ref, bf16[128,512]{1,0:T(8,128)(2,1)} %copy-done.4), custom_call_target="tpu_custom_call" | custom-call | bytes 524288 | tf_op jit(solution)/shard_map/query_pair/pallas_call | solution.py:167
  13.4 4.8 %collective-permute-done.2 = bf16[64,1024]{1,0:T(8,128)(2,1)S(1)} collective-permute-done((bf16[64,1024]{1,0:T(8,128)(2,1)}, bf16[64,1024]{1,0:T(8,128)(2,1)S(1)}, u32[]{:S(2)}, u32[]{:S(2)}) %collective-permute-start.2) | collective-permute-done | bytes 131104 | tf_op jit(solution)/shard_map/ppermute | solution.py:138
  18.3 1.6 %collective-permute-start.4 = (bf16[128,1024]{1,0:T(8,128)(2,1)S(1)}, bf16[128,1024]{1,0:T(8,128)(2,1)S(1)}, u32[]{:S(2)}, u32[]{:S(2)}) collective-permute-start(bf16[128,1024]{1,0:T(8,128)(2,1)S(1)} %pad_maximum_fusion.refs_4_), channel_id=1, source_target_pairs={{0,8},{8,0},{16,24},{24,16},{1,9},{9,1},{17,25},{25,17},{2,10},{10... | collective-permute-start | bytes 786440 | tf_op jit(solution)/shard_map/ppermute | solution.py:138
  19.9 1.5 %collective-permute-start.12 = (bf16[128,1024]{1,0:T(8,128)(2,1)S(1)}, bf16[128,1024]{1,0:T(8,128)(2,1)S(1)}, u32[]{:S(2)}, u32[]{:S(2)}) collective-permute-start(bf16[128,1024]{1,0:T(8,128)(2,1)S(1)} %collective-permute-done.9.refs_5_), channel_id=1, source_target_pairs={{0,16},{8,24},{16,0},{24,8},{1,17},{9,25},{17,1},{25,9},{2,18},{10... | collective-permute-start | bytes 786440 | tf_op jit(solution)/shard_map/ppermute | solution.py:138
  21.9 1.4 %collective-permute-start.10 = (bf16[128,1024]{1,0:T(8,128)(2,1)S(1)}, bf16[128,1024]{1,0:T(8,128)(2,1)S(1)}, u32[]{:S(2)}, u32[]{:S(2)}) collective-permute-start(bf16[128,1024]{1,0:T(8,128)(2,1)S(1)} %collective-permute-done.9.refs_5_), channel_id=1, source_target_pairs={{0,8},{8,0},{16,24},{24,16},{1,9},{9,1},{17,25},{25,17},{2,10},{10... | collective-permute-start | bytes 786440 | tf_op jit(solution)/shard_map/ppermute | solution.py:138
  23.3 4.2 %collective-permute-done.4.refs_6_ = bf16[128,1024]{1,0:T(8,128)(2,1)S(1)} collective-permute-done((bf16[128,1024]{1,0:T(8,128)(2,1)S(1)}, bf16[128,1024]{1,0:T(8,128)(2,1)S(1)}, u32[]{:S(2)}, u32[]{:S(2)}) %collective-permute-start.4) | collective-permute-done | bytes 262176 | tf_op jit(solution)/shard_map/ppermute | solution.py:138
  27.5 1.5 %collective-permute-start.13 = (bf16[128,1024]{1,0:T(8,128)(2,1)S(1)}, bf16[128,1024]{1,0:T(8,128)(2,1)S(1)}, u32[]{:S(2)}, u32[]{:S(2)}) collective-permute-start(bf16[128,1024]{1,0:T(8,128)(2,1)S(1)} %collective-permute-done.4.refs_6_), channel_id=1, source_target_pairs={{0,16},{8,24},{16,0},{24,8},{1,17},{9,25},{17,1},{25,9},{2,18},{10... | collective-permute-start | bytes 786440 | tf_op jit(solution)/shard_map/ppermute | solution.py:138
  29.0 1.5 %collective-permute-start.14 = (bf16[128,1024]{1,0:T(8,128)(2,1)S(1)}, bf16[128,1024]{1,0:T(8,128)(2,1)S(1)}, u32[]{:S(2)}, u32[]{:S(2)}) collective-permute-start(bf16[128,1024]{1,0:T(8,128)(2,1)S(1)} %collective-permute-done.12.refs_9_), channel_id=1, source_target_pairs={{0,8},{8,0},{16,24},{24,16},{1,9},{9,1},{17,25},{25,17},{2,10},{10... | collective-permute-start | bytes 786440 | tf_op jit(solution)/shard_map/ppermute | solution.py:138
  30.5 2.5 %collective-permute-start.8 = (bf16[64,512]{1,0:T(8,128)(2,1)}, bf16[64,512]{1,0:T(8,128)(2,1)S(1)}, u32[]{:S(2)}, u32[]{:S(2)}) collective-permute-start(bf16[64,512]{1,0:T(8,128)(2,1)} %get-tuple-element.38), channel_id=1, source_target_pairs={{0,6},{1,7},{2,4},{3,5},{4,2},{5,3},{6,0},{7,1},{8,14},{9,15},{10,... | collective-permute-start | bytes 196616 | tf_op jit(solution)/shard_map/ppermute | solution.py:138
  33.0 1.7 %collective-permute-done.11.refs_8_ = bf16[128,1024]{1,0:T(8,128)(2,1)S(1)} collective-permute-done((bf16[128,1024]{1,0:T(8,128)(2,1)S(1)}, bf16[128,1024]{1,0:T(8,128)(2,1)S(1)}, u32[]{:S(2)}, u32[]{:S(2)}) %collective-permute-start.11) | collective-permute-done | bytes 262176 | tf_op jit(solution)/shard_map/ppermute | solution.py:138
  34.6 3.6 %collective-permute-start.7 = (bf16[64,512]{1,0:T(8,128)(2,1)}, bf16[64,512]{1,0:T(8,128)(2,1)S(1)}, u32[]{:S(2)}, u32[]{:S(2)}) collective-permute-start(bf16[64,512]{1,0:T(8,128)(2,1)} %get-tuple-element.36), channel_id=1, source_target_pairs={{0,4},{1,5},{2,6},{3,7},{4,0},{5,1},{6,2},{7,3},{8,12},{9,13},{10,... | collective-permute-start | bytes 196616 | tf_op jit(solution)/shard_map/ppermute | solution.py:138
  39.6 1.3 %collective-permute-done.7.refs_2_ = bf16[64,512]{1,0:T(8,128)(2,1)S(1)} collective-permute-done((bf16[64,512]{1,0:T(8,128)(2,1)}, bf16[64,512]{1,0:T(8,128)(2,1)S(1)}, u32[]{:S(2)}, u32[]{:S(2)}) %collective-permute-start.7) | collective-permute-done | bytes 65568 | tf_op jit(solution)/shard_map/ppermute | solution.py:138
  40.9 1.9 %collective-permute-done.6.refs_1_ = bf16[64,512]{1,0:T(8,128)(2,1)S(1)} collective-permute-done((bf16[64,512]{1,0:T(8,128)(2,1)}, bf16[64,512]{1,0:T(8,128)(2,1)S(1)}, u32[]{:S(2)}, u32[]{:S(2)}) %collective-permute-start.6) | collective-permute-done | bytes 65568 | tf_op jit(solution)/shard_map/ppermute | solution.py:138
  44.3 3.5 %attention.1 = (bf16[128,512]{1,0:T(8,128)(2,1)S(1)}, bf16[128,512]{1,0:T(8,128)(2,1)S(1)}) custom-call(s32[1]{0:T(128)} %bitcast.3.slot_ref, s32[4]{0:T(128)S(1)} %copy-done.2, bf16[64,512]{1,0:T(8,128)(2,1)S(1)} %copy-done.1, bf16[64,512]{1,0:T(8,128)(2,1)S(1)} %collective-permute-done.6.refs_1_, bf16[64,512]{1,0:T(8,128)(2,1)S(1)} %collective-permute-done.7.refs_2_, ...), custom_call_target="tpu_custom_call" | custom-call | flops 536870912 | bytes 2097152 | tf_op jit(solution)/shard_map/attention/pallas_call | solution.py:197
  47.9 1.3 %collective-permute-done.15.theirs_ref = bf16[128,512]{1,0:T(8,128)(2,1)S(1)} collective-permute-done((bf16[128,512]{1,0:T(8,128)(2,1)S(1)}, bf16[128,512]{1,0:T(8,128)(2,1)S(1)}, u32[]{:S(2)}, u32[]{:S(2)}) %collective-permute-start.15) | collective-permute-done | bytes 131104 | tf_op jit(solution)/shard_map/ppermute | solution.py:138
  49.2 2.5 %copy-done = bf16[512,5120]{1,0:T(8,128)(2,1)S(1)} copy-done((bf16[512,5120]{1,0:T(8,128)(2,1)S(1)}, bf16[512,5120]{1,0:T(8,128)(2,1)}, u32[]{:S(2)}) %copy-start) | copy-done | bytes 5242904
  51.7 4.7 %projection.1 = (f32[32,5120]{1,0:T(8,128)S(1)}, bf16[32,5120]{1,0:T(8,128)(2,1)S(1)}, f32[32,5120]{1,0:T(8,128)S(1)}, bf16[32,5120]{1,0:T(8,128)(2,1)S(1)}) custom-call(bf16[128,512]{1,0:T(8,128)(2,1)S(1)} %get-tuple-element.40.mine_ref, bf16[128,512]{1,0:T(8,128)(2,1)S(1)} %collective-permute-done.15.theirs_ref, bf16[512,5120]{1,0:T(8,128)(2,1)S(1)} %copy-done, ...), custom_call_target="tpu_custom_call" | custom-call | flops 1342177280 | bytes 11796480 | tf_op jit(solution)/shard_map/projection/pallas_call | solution.py:213
  59.7 6.5 %collective-permute-done.16 = bf16[32,5120]{1,0:T(8,128)(2,1)S(1)} collective-permute-done((bf16[32,5120]{1,0:T(8,128)(2,1)S(1)}, bf16[32,5120]{1,0:T(8,128)(2,1)S(1)}, u32[]{:S(2)}, u32[]{:S(2)}) %collective-permute-start.16) | collective-permute-done | bytes 327712 | tf_op jit(solution)/shard_map/ppermute | solution.py:138
  69.2 12.0 %collective-permute-done.17 = bf16[32,5120]{1,0:T(8,128)(2,1)S(1)} collective-permute-done((bf16[32,5120]{1,0:T(8,128)(2,1)S(1)}, bf16[32,5120]{1,0:T(8,128)(2,1)S(1)}, u32[]{:S(2)}, u32[]{:S(2)}) %collective-permute-start.17) | collective-permute-done | bytes 327712 | tf_op jit(solution)/shard_map/ppermute | solution.py:138
  81.2 2.5 %collective-permute-done.18 = bf16[32,5120]{1,0:T(8,128)(2,1)S(1)} collective-permute-done((bf16[32,5120]{1,0:T(8,128)(2,1)S(1)}, bf16[32,5120]{1,0:T(8,128)(2,1)S(1)}, u32[]{:S(2)}, u32[]{:S(2)}) %collective-permute-start.18) | collective-permute-done | bytes 327712 | tf_op jit(solution)/shard_map/ppermute | solution.py:138
  (44 shorter events, 11.4 us)
Async XLA Ops:
  0.0 30.5 %collective-permute-start.5 = (bf16[512,5120]{1,0:T(8,128)(2,1)}, bf16[512,5120]{1,0:T(8,128)(2,1)}, u32[]{:S(2)}, u32[]{:S(2)}) collective-permute-start(bf16[512,5120]{1,0:T(8,128)(2,1)} %own_ref.1), channel_id=1, source_target_pairs={{0,1},{1,0},{2,3},{3,2},{4,5},{5,4},{6,7},{7,6},{8,9},{9,8},{10,11... | collective-permute-start | bytes 15728648 | tf_op jit(solution)/shard_map/ppermute | solution.py:138
  2.5 10.9 %collective-permute-start.1 = (bf16[64,1024]{1,0:T(8,128)(2,1)}, bf16[64,1024]{1,0:T(8,128)(2,1)S(1)}, u32[]{:S(2)}, u32[]{:S(2)}) collective-permute-start(bf16[64,1024]{1,0:T(8,128)(2,1)} %get-tuple-element.31), channel_id=1, source_target_pairs={{0,2},{1,3},{2,0},{3,1},{4,6},{5,7},{6,4},{7,5},{8,10},{9,11},{10,... | collective-permute-start | bytes 393224 | tf_op jit(solution)/shard_map/ppermute | solution.py:138
  5.0 13.1 %collective-permute-start.2 = (bf16[64,1024]{1,0:T(8,128)(2,1)}, bf16[64,1024]{1,0:T(8,128)(2,1)S(1)}, u32[]{:S(2)}, u32[]{:S(2)}) collective-permute-start(bf16[64,1024]{1,0:T(8,128)(2,1)} %get-tuple-element.32), channel_id=1, source_target_pairs={{0,4},{1,5},{2,6},{3,7},{4,0},{5,1},{6,2},{7,3},{8,12},{9,13},{10,... | collective-permute-start | bytes 393224 | tf_op jit(solution)/shard_map/ppermute | solution.py:138
  7.6 10.5 %collective-permute-start.3 = (bf16[64,1024]{1,0:T(8,128)(2,1)}, bf16[64,1024]{1,0:T(8,128)(2,1)S(1)}, u32[]{:S(2)}, u32[]{:S(2)}) collective-permute-start(bf16[64,1024]{1,0:T(8,128)(2,1)} %get-tuple-element.33), channel_id=1, source_target_pairs={{0,6},{1,7},{2,4},{3,5},{4,2},{5,3},{6,0},{7,1},{8,14},{9,15},{10,... | collective-permute-start | bytes 393224 | tf_op jit(solution)/shard_map/ppermute | solution.py:138
  9.5 1.6 %collective-permute-start = (bf16[128,512]{1,0:T(8,128)(2,1)}, bf16[128,512]{1,0:T(8,128)(2,1)S(1)}, u32[]{:S(2)}, u32[]{:S(2)}) collective-permute-start(bf16[128,512]{1,0:T(8,128)(2,1)} %get-tuple-element.27), channel_id=1, source_target_pairs={{0,1},{1,0},{2,3},{3,2},{4,5},{5,4},{6,7},{7,6},{8,9},{9,8},{10,11... | collective-permute-start | bytes 393224 | tf_op jit(solution)/shard_map/ppermute | solution.py:138
  18.2 1.7 %collective-permute-start.9 = (bf16[128,1024]{1,0:T(8,128)(2,1)S(1)}, bf16[128,1024]{1,0:T(8,128)(2,1)S(1)}, u32[]{:S(2)}, u32[]{:S(2)}) collective-permute-start(bf16[128,1024]{1,0:T(8,128)(2,1)S(1)} %pad_maximum_fusion.1), channel_id=1, source_target_pairs={{0,1},{1,0},{2,3},{3,2},{4,5},{5,4},{6,7},{7,6},{8,9},{9,8},{10,11... | collective-permute-start | bytes 786440 | tf_op jit(solution)/shard_map/ppermute | solution.py:138
  18.3 9.2 %collective-permute-start.4 = (bf16[128,1024]{1,0:T(8,128)(2,1)S(1)}, bf16[128,1024]{1,0:T(8,128)(2,1)S(1)}, u32[]{:S(2)}, u32[]{:S(2)}) collective-permute-start(bf16[128,1024]{1,0:T(8,128)(2,1)S(1)} %pad_maximum_fusion.refs_4_), channel_id=1, source_target_pairs={{0,8},{8,0},{16,24},{24,16},{1,9},{9,1},{17,25},{25,17},{2,10},{10... | collective-permute-start | bytes 786440 | tf_op jit(solution)/shard_map/ppermute | solution.py:138
  19.9 9.1 %collective-permute-start.12 = (bf16[128,1024]{1,0:T(8,128)(2,1)S(1)}, bf16[128,1024]{1,0:T(8,128)(2,1)S(1)}, u32[]{:S(2)}, u32[]{:S(2)}) collective-permute-start(bf16[128,1024]{1,0:T(8,128)(2,1)S(1)} %collective-permute-done.9.refs_5_), channel_id=1, source_target_pairs={{0,16},{8,24},{16,0},{24,8},{1,17},{9,25},{17,1},{25,9},{2,18},{10... | collective-permute-start | bytes 786440 | tf_op jit(solution)/shard_map/ppermute | solution.py:138
  21.4 13.2 %collective-permute-start.11 = (bf16[128,1024]{1,0:T(8,128)(2,1)S(1)}, bf16[128,1024]{1,0:T(8,128)(2,1)S(1)}, u32[]{:S(2)}, u32[]{:S(2)}) collective-permute-start(bf16[128,1024]{1,0:T(8,128)(2,1)S(1)} %pad_maximum_fusion.refs_4_), channel_id=1, source_target_pairs={{0,16},{8,24},{16,0},{24,8},{1,17},{9,25},{17,1},{25,9},{2,18},{10... | collective-permute-start | bytes 786440 | tf_op jit(solution)/shard_map/ppermute | solution.py:138
  21.9 16.4 %collective-permute-start.10 = (bf16[128,1024]{1,0:T(8,128)(2,1)S(1)}, bf16[128,1024]{1,0:T(8,128)(2,1)S(1)}, u32[]{:S(2)}, u32[]{:S(2)}) collective-permute-start(bf16[128,1024]{1,0:T(8,128)(2,1)S(1)} %collective-permute-done.9.refs_5_), channel_id=1, source_target_pairs={{0,8},{8,0},{16,24},{24,16},{1,9},{9,1},{17,25},{25,17},{2,10},{10... | collective-permute-start | bytes 786440 | tf_op jit(solution)/shard_map/ppermute | solution.py:138
  27.5 12.1 %collective-permute-start.13 = (bf16[128,1024]{1,0:T(8,128)(2,1)S(1)}, bf16[128,1024]{1,0:T(8,128)(2,1)S(1)}, u32[]{:S(2)}, u32[]{:S(2)}) collective-permute-start(bf16[128,1024]{1,0:T(8,128)(2,1)S(1)} %collective-permute-done.4.refs_6_), channel_id=1, source_target_pairs={{0,16},{8,24},{16,0},{24,8},{1,17},{9,25},{17,1},{25,9},{2,18},{10... | collective-permute-start | bytes 786440 | tf_op jit(solution)/shard_map/ppermute | solution.py:138
  29.0 10.5 %collective-permute-start.14 = (bf16[128,1024]{1,0:T(8,128)(2,1)S(1)}, bf16[128,1024]{1,0:T(8,128)(2,1)S(1)}, u32[]{:S(2)}, u32[]{:S(2)}) collective-permute-start(bf16[128,1024]{1,0:T(8,128)(2,1)S(1)} %collective-permute-done.12.refs_9_), channel_id=1, source_target_pairs={{0,8},{8,0},{16,24},{24,16},{1,9},{9,1},{17,25},{25,17},{2,10},{10... | collective-permute-start | bytes 786440 | tf_op jit(solution)/shard_map/ppermute | solution.py:138
  30.5 9.0 %collective-permute-start.8 = (bf16[64,512]{1,0:T(8,128)(2,1)}, bf16[64,512]{1,0:T(8,128)(2,1)S(1)}, u32[]{:S(2)}, u32[]{:S(2)}) collective-permute-start(bf16[64,512]{1,0:T(8,128)(2,1)} %get-tuple-element.38), channel_id=1, source_target_pairs={{0,6},{1,7},{2,4},{3,5},{4,2},{5,3},{6,0},{7,1},{8,14},{9,15},{10,... | collective-permute-start | bytes 196616 | tf_op jit(solution)/shard_map/ppermute | solution.py:138
  34.6 6.2 %collective-permute-start.7 = (bf16[64,512]{1,0:T(8,128)(2,1)}, bf16[64,512]{1,0:T(8,128)(2,1)S(1)}, u32[]{:S(2)}, u32[]{:S(2)}) collective-permute-start(bf16[64,512]{1,0:T(8,128)(2,1)} %get-tuple-element.36), channel_id=1, source_target_pairs={{0,4},{1,5},{2,6},{3,7},{4,0},{5,1},{6,2},{7,3},{8,12},{9,13},{10,... | collective-permute-start | bytes 196616 | tf_op jit(solution)/shard_map/ppermute | solution.py:138
  38.3 4.5 %collective-permute-start.6 = (bf16[64,512]{1,0:T(8,128)(2,1)}, bf16[64,512]{1,0:T(8,128)(2,1)S(1)}, u32[]{:S(2)}, u32[]{:S(2)}) collective-permute-start(bf16[64,512]{1,0:T(8,128)(2,1)} %get-tuple-element.34), channel_id=1, source_target_pairs={{0,2},{1,3},{2,0},{3,1},{4,6},{5,7},{6,4},{7,5},{8,10},{9,11},{10,... | collective-permute-start | bytes 196616 | tf_op jit(solution)/shard_map/ppermute | solution.py:138
  42.8 0.8 copy-start.1
  47.8 1.4 %collective-permute-start.15 = (bf16[128,512]{1,0:T(8,128)(2,1)S(1)}, bf16[128,512]{1,0:T(8,128)(2,1)S(1)}, u32[]{:S(2)}, u32[]{:S(2)}) collective-permute-start(bf16[128,512]{1,0:T(8,128)(2,1)S(1)} %get-tuple-element.41), channel_id=1, source_target_pairs={{0,1},{1,0},{2,3},{3,2},{4,5},{5,4},{6,7},{7,6},{8,9},{9,8},{10,11... | collective-permute-start | bytes 393224 | tf_op jit(solution)/shard_map/ppermute | solution.py:138
  49.2 2.5 %copy-start = (bf16[512,5120]{1,0:T(8,128)(2,1)S(1)}, bf16[512,5120]{1,0:T(8,128)(2,1)}, u32[]{:S(2)}) copy-start(bf16[512,5120]{1,0:T(8,128)(2,1)} %own_ref.1) | copy-start | bytes 15728644
  51.7 5.5 %copy-start.6 = (s32[4]{0:T(128)S(1)}, s32[4]{0:T(128)}, u32[]{:S(2)}) copy-start(s32[4]{0:T(128)} %param.20) | copy-start | bytes 52
  51.7 7.4 %copy-start.5 = (bf16[5120]{0:T(1024)(128)(2,1)S(1)}, bf16[5120]{0:T(1024)(128)(2,1)}, u32[]{:S(2)}) copy-start(bf16[5120]{0:T(1024)(128)(2,1)} %param.18) | copy-start | bytes 30724
  51.7 32.0 %copy-start.3 = (bf16[1,32,5120]{2,1,0:T(8,128)(2,1)S(1)}, bf16[1,32,5120]{2,1,0:T(8,128)(2,1)}, u32[]{:S(2)}) copy-start(bf16[1,32,5120]{2,1,0:T(8,128)(2,1)} %param.11) | copy-start | bytes 983044
  56.4 9.8 %collective-permute-start.16 = (bf16[32,5120]{1,0:T(8,128)(2,1)S(1)}, bf16[32,5120]{1,0:T(8,128)(2,1)S(1)}, u32[]{:S(2)}, u32[]{:S(2)}) collective-permute-start(bf16[32,5120]{1,0:T(8,128)(2,1)S(1)} %get-tuple-element.44), channel_id=1, source_target_pairs={{0,2},{1,3},{2,0},{3,1},{4,6},{5,7},{6,4},{7,5},{8,10},{9,11},{10,... | collective-permute-start | bytes 983048 | tf_op jit(solution)/shard_map/ppermute | solution.py:138
  66.2 14.9 %collective-permute-start.17 = (bf16[32,5120]{1,0:T(8,128)(2,1)S(1)}, bf16[32,5120]{1,0:T(8,128)(2,1)S(1)}, u32[]{:S(2)}, u32[]{:S(2)}) collective-permute-start(bf16[32,5120]{1,0:T(8,128)(2,1)S(1)} %get-tuple-element.45), channel_id=1, source_target_pairs={{0,2},{1,3},{2,0},{3,1},{4,6},{5,7},{6,4},{7,5},{8,10},{9,11},{10,... | collective-permute-start | bytes 983048 | tf_op jit(solution)/shard_map/ppermute | solution.py:138
  67.0 16.7 %collective-permute-start.18 = (bf16[32,5120]{1,0:T(8,128)(2,1)S(1)}, bf16[32,5120]{1,0:T(8,128)(2,1)S(1)}, u32[]{:S(2)}, u32[]{:S(2)}) collective-permute-start(bf16[32,5120]{1,0:T(8,128)(2,1)S(1)} %add_convert_fusion), channel_id=1, source_target_pairs={{0,4},{1,5},{2,6},{3,7},{4,0},{5,1},{6,2},{7,3},{8,12},{9,13},{10,... | collective-permute-start | bytes 983048 | tf_op jit(solution)/shard_map/ppermute | solution.py:138
  (2 other events, 1.3 us)

commit v3 on v2

--- a/solution.py
+++ b/solution.py
@@ -101,12 +101,214 @@
                 out_ref[here, cols] = (summed / total).astype(jnp.bfloat16)
 
 
-def projection_kernel(chunks, mine_ref, theirs_ref, own_ref, other_ref, *outs):
-    rows = mine_ref.shape[0] // chunks
-    result = jnp.dot(mine_ref[...], own_ref[...], preferred_element_type=jnp.float32)
-    result += jnp.dot(theirs_ref[...], other_ref[...], preferred_element_type=jnp.float32)
-    for j in range(chunks):
+def projection_kernel(chips, index_ref, rows_ref, own_ref, other_ref, *outs):
+    shift = index_ref[0]
+    core = index_ref[1]
+    sources, half, _ = rows_ref.shape
+    rows = half // chips
+
+    def gathered(parity):
+        return jnp.concatenate(
+            [
+                jnp.concatenate(
+                    [
+                        rows_ref[2 * i + (core ^ parity), pl.ds(pl.multiple_of((shift ^ j) * rows, rows), rows), :]
+                        for j in range(chips)
+                    ],
+                    axis=0,
+                )
+                for i in range(sources // 2)
+            ],
+            axis=1,
+        )
+
+    result = jnp.dot(gathered(0), own_ref[...], preferred_element_type=jnp.float32)
+    result += jnp.dot(gathered(1), other_ref[...], preferred_element_type=jnp.float32)
+    for j in range(chips):
         outs[j][...] = result[j * rows : (j + 1) * rows].astype(outs[j].dtype)
+
+
+def spread_norm_kernel(n, frames, query_ref, key_ref, value_ref, gain_query_ref, gain_key_ref, out_ref):
+    features = query_ref.shape[1]
+    part = features // (n * frames)
+    query_inverse = inverse_rms(query_ref[...])
+    key_inverse = inverse_rms(key_ref[...])
+    for s in range(n):
+        for f in range(frames):
+            first = (s * frames + f) * part
+            cols = slice(first, first + part)
+            query = query_ref[:, cols].astype(jnp.float32) * query_inverse * gain_query_ref[:, cols]
+            key = key_ref[:, cols].astype(jnp.float32) * key_inverse * gain_key_ref[:, cols]
+            out_ref[f * n + s, :, :part] = query.astype(jnp.bfloat16)
+            out_ref[f * n + s, :, part : 2 * part] = key.astype(jnp.bfloat16)
+            out_ref[f * n + s, :, 2 * part :] = value_ref[:, cols]
+
+
+def spread_attention_kernel(n, frames, order_ref, rows_ref, out_ref):
+    rows = rows_ref.shape[1]
+    part = out_ref.shape[2]
+    frame_rows = n * rows
+    tokens = rows_ref[...].reshape(frames * frame_rows, 3 * part)
+    factor = (HD ** (-0.5)) * LOG2E
+    step = min(frame_rows, 128)
+    for h in range(part // HD):
+        cols = slice(h * HD, (h + 1) * HD)
+        query = tokens[:, h * HD : (h + 1) * HD]
+        keys = tokens[:, part + h * HD : part + (h + 1) * HD]
+        values = tokens[:, 2 * part + h * HD : 2 * part + (h + 1) * HD]
+        for g in range(frames):
+            hidden = jnp.concatenate(
+                [
+                    jnp.full((1, frame_rows), jnp.where(order_ref[f] <= order_ref[g], 0.0, -1e30), jnp.float32)
+                    for f in range(frames)
+                ],
+                axis=1,
+            )
+            for start in range(0, frame_rows, step):
+                scores = lax.dot_general(
+                    query[g * frame_rows + start : g * frame_rows + start + step],
+                    keys,
+                    (((1,), (1,)), ((), ())),
+                    preferred_element_type=jnp.float32,
+                )
+                scores = scores + hidden
+                top = jnp.max(scores, axis=1, keepdims=True)
+                exponent = jnp.exp2((scores - top) * factor)
+                total = jnp.sum(exponent, axis=1, keepdims=True)
+                summed = jnp.dot(
+                    exponent.astype(jnp.bfloat16), values, preferred_element_type=jnp.float32
+                )
+                done = (summed / total).astype(jnp.bfloat16)
+                for i in range(step // rows):
+                    s = start // rows + i
+                    z = s // 2
+                    out_ref[2 * g + s % 2, z * rows : (z + 1) * rows, cols] = done[
+                        i * rows : (i + 1) * rows
+                    ]
+
+
+def spread_attention(query_rows, key_rows, value_rows, gain_query, gain_key, slot_order):
+    n = lax.axis_size("seq")
+    frames = lax.axis_size("frame")
+    rows, features = query_rows.shape
+    part = features // (n * frames)
+    chips = n // 2
+    frame_rows = n * rows
+    vmem = pl.BlockSpec(memory_space=VMEM)
+    smem = pl.BlockSpec(memory_space=SMEM)
+    sends = pl.pallas_call(
+        functools.partial(spread_norm_kernel, n, frames),
+        out_shape=jax.ShapeDtypeStruct((n * frames, rows, 3 * part), jnp.bfloat16),
+        in_specs=[vmem] * 5,
+        out_specs=vmem,
+        name="norm",
+    )(query_rows, key_rows, value_rows, gain_query.reshape(1, features), gain_key.reshape(1, features))
+    held = lax.all_to_all(sends, ("frame", "seq"), split_axis=0, concat_axis=0, tiled=True)
+    keys = frames * frame_rows
+    done = pl.pallas_call(
+        functools.partial(spread_attention_kernel, n, frames),
+        out_shape=jax.ShapeDtypeStruct((2 * frames, frame_rows // 2, part), jnp.bfloat16),
+        in_specs=[smem, vmem],
+        out_specs=vmem,
+        compiler_params=pltpu.CompilerParams(vmem_limit_bytes=8 * 2**20 + 6 * 128 * keys * 4),
+        cost_estimate=pl.CostEstimate(
+            flops=4 * keys * keys * part,
+            bytes_accessed=8 * keys * part,
+            transcendentals=keys * keys * (part // HD),
+        ),
+        name="attention",
+    )(slot_order, held)
+    planes = [[f * n + 2 * z + c for f in range(frames) for c in range(2)] for z in range(chips)]
+    return lax.all_to_all(
+        done, ("frame", "seq"), split_axis=0, concat_axis=0, axis_index_groups=planes, tiled=True
+    )
+
+
+def gathered_attention(query_rows, key_rows, value_rows, gain_query, gain_key, slot_order):
+    n = lax.axis_size("seq")
+    frames = lax.axis_size("frame")
+    chips = n // 2
+    rows, features = query_rows.shape
+    width = features // n
+    me = lax.axis_index("seq").astype(jnp.int32)
+    slot = lax.axis_index("frame").astype(jnp.int32)
+    me_array = me.reshape(1)
+    slot_array = slot.reshape(1)
+
+    def across(value, axis, distance):
+        size = n if axis == "seq" else frames
+        return lax.ppermute(value, axis, [(i, i ^ distance) for i in range(size)])
+
+    def after(value, *earlier):
+        return lax.optimization_barrier((value, *earlier))[0]
+
+    smem = pl.BlockSpec(memory_space=SMEM)
+    vmem = pl.BlockSpec(memory_space=VMEM)
+
+    sends = pl.pallas_call(
+        functools.partial(key_value_kernel, chips),
+        out_shape=[jax.ShapeDtypeStruct((2 * rows, 2 * width), jnp.bfloat16)] * chips,
+        in_specs=[smem, vmem, vmem, vmem],
+        out_specs=[vmem] * chips,
+        cost_estimate=pl.CostEstimate(
+            flops=8 * rows * features, bytes_accessed=8 * rows * features, transcendentals=0
+        ),
+        name="key_value_norm",
+    )(me_array, key_rows, gain_key.reshape(1, features), value_rows)
+    query_own, query_cross = pl.pallas_call(
+        functools.partial(query_kernel, chips),
+        out_shape=[jax.ShapeDtypeStruct((chips * rows, width), jnp.bfloat16)] * 2,
+        in_specs=[smem, vmem, vmem],
+        out_specs=[vmem] * 2,
+        cost_estimate=pl.CostEstimate(
+            flops=8 * rows * features, bytes_accessed=4 * rows * features, transcendentals=0
+        ),
+        name="query_norm",
+    )(me_array, query_rows, gain_query.reshape(1, features))
+    query_sends = pl.pallas_call(
+        functools.partial(pair_kernel, chips),
+        out_shape=[jax.ShapeDtypeStruct((2 * rows, width), jnp.bfloat16)] * chips,
+        in_specs=[vmem, vmem],
+        out_specs=[vmem] * chips,
+        cost_estimate=pl.CostEstimate(
+            flops=0, bytes_accessed=8 * chips * rows * width, transcendentals=0
+        ),
+        name="query_pair",
+    )(query_own, across(query_cross, "seq", 1))
+
+    blocks = [sends[0]] + [across(sends[r], "seq", 2 * r) for r in range(1, chips)]
+    mine = jnp.concatenate([block[:rows] for block in blocks], axis=0)
+    given = jnp.concatenate([block[rows:] for block in blocks], axis=0)
+    halves = mine, across(after(given, *query_sends), "seq", 1)
+
+    bits = [1 << b for b in range(frames.bit_length() - 1)]
+    held = []
+    for half, order in zip(halves, (bits, bits[::-1])):
+        found = {0: half}
+        for bit in order:
+            found.update({f ^ bit: across(piece, "frame", bit) for f, piece in found.items()})
+        held.append(found)
+    pieces = [held[u][f] for f in range(frames) for u in range(2)]
+
+    queries = [query_sends[0]] + [
+        across(after(query_sends[r], held[0][bits[0]]), "seq", 2 * r) for r in range(1, chips)
+    ]
+    frame_rows = n * rows
+    keys = frame_rows * frames
+    even, odd = pl.pallas_call(
+        functools.partial(attention_kernel, chips, frames),
+        out_shape=[jax.ShapeDtypeStruct((frame_rows // 2, width), jnp.bfloat16)] * 2,
+        in_specs=[smem, smem] + [vmem] * (chips + len(pieces)),
+        out_specs=[vmem] * 2,
+        compiler_params=pltpu.CompilerParams(vmem_limit_bytes=8 * 2**20 + 6 * 128 * keys * 4),
+        cost_estimate=pl.CostEstimate(
+            flops=4 * frame_rows * keys * width,
+            bytes_accessed=4 * keys * width,
+            transcendentals=frame_rows * keys * (width // HD),
+        ),
+        name="attention",
+    )(slot_array, slot_order, *queries, *pieces)
+    return jnp.stack([even, across(odd, "seq", 1)])
 
 
 def shards(
@@ -128,86 +330,22 @@
     rows, features = query_rows.shape[1:]
     width = features // n
     model = out_weight.shape[1]
+    half = chips * rows
     me = lax.axis_index("seq").astype(jnp.int32)
     slot = lax.axis_index("frame").astype(jnp.int32)
-    me_array = me.reshape(1)
-    slot_array = slot.reshape(1)
 
     def across(value, axis, distance):
-        size = n if axis == "seq" else frames
-        return lax.ppermute(value, axis, [(i, i ^ distance) for i in range(size)])
+        return lax.ppermute(value, axis, [(i, i ^ distance) for i in range(n)])
 
     def after(value, *earlier):
         return lax.optimization_barrier((value, *earlier))[0]
 
-    smem = pl.BlockSpec(memory_space=SMEM)
-    vmem = pl.BlockSpec(memory_space=VMEM)
-
     other_weight = across(out_weight, "seq", 1)
-    sends = pl.pallas_call(
-        functools.partial(key_value_kernel, chips),
-        out_shape=[jax.ShapeDtypeStruct((2 * rows, 2 * width), jnp.bfloat16)] * chips,
-        in_specs=[smem, vmem, vmem, vmem],
-        out_specs=[vmem] * chips,
-        cost_estimate=pl.CostEstimate(
-            flops=8 * rows * features, bytes_accessed=8 * rows * features, transcendentals=0
-        ),
-        name="key_value_norm",
-    )(me_array, key_rows[0], gain_key.reshape(1, features), value_rows[0])
-    query_own, query_cross = pl.pallas_call(
-        functools.partial(query_kernel, chips),
-        out_shape=[jax.ShapeDtypeStruct((chips * rows, width), jnp.bfloat16)] * 2,
-        in_specs=[smem, vmem, vmem],
-        out_specs=[vmem] * 2,
-        cost_estimate=pl.CostEstimate(
-            flops=8 * rows * features, bytes_accessed=4 * rows * features, transcendentals=0
-        ),
-        name="query_norm",
-    )(me_array, query_rows[0], gain_query.reshape(1, features))
-    query_sends = pl.pallas_call(
-        functools.partial(pair_kernel, chips),
-        out_shape=[jax.ShapeDtypeStruct((2 * rows, width), jnp.bfloat16)] * chips,
-        in_specs=[vmem, vmem],
-        out_specs=[vmem] * chips,
-        cost_estimate=pl.CostEstimate(
-            flops=0, bytes_accessed=8 * chips * rows * width, transcendentals=0
-        ),
-        name="query_pair",
-    )(query_own, across(query_cross, "seq", 1))
-
-    blocks = [sends[0]] + [across(sends[r], "seq", 2 * r) for r in range(1, chips)]
-    mine = jnp.concatenate([block[:rows] for block in blocks], axis=0)
-    given = jnp.concatenate([block[rows:] for block in blocks], axis=0)
-    halves = mine, across(after(given, *query_sends), "seq", 1)
-
-    bits = [1 << b for b in range(frames.bit_length() - 1)]
-    held = []
-    for half, order in zip(halves, (bits, bits[::-1])):
-        found = {0: half}
-        for bit in order:
-            found.update({f ^ bit: across(piece, "frame", bit) for f, piece in found.items()})
-        held.append(found)
-    pieces = [held[u][f] for f in range(frames) for u in range(2)]
-
-    queries = [query_sends[0]] + [
-        across(after(query_sends[r], held[0][bits[0]], other_weight), "seq", 2 * r) for r in range(1, chips)
-    ]
-    frame_rows = n * rows
-    keys = frame_rows * frames
-    even, odd = pl.pallas_call(
-        functools.partial(attention_kernel, chips, frames),
-        out_shape=[jax.ShapeDtypeStruct((frame_rows // 2, width), jnp.bfloat16)] * 2,
-        in_specs=[smem, smem] + [vmem] * (chips + len(pieces)),
-        out_specs=[vmem] * 2,
-        compiler_params=pltpu.CompilerParams(vmem_limit_bytes=8 * 2**20 + 6 * 128 * keys * 4),
-        cost_estimate=pl.CostEstimate(
-            flops=4 * frame_rows * keys * width,
-            bytes_accessed=4 * keys * width,
-            transcendentals=frame_rows * keys * (width // HD),
-        ),
-        name="attention",
-    )(slot_array, slot_order, *queries, *pieces)
-    theirs = across(odd, "seq", 1)
+    spread = (width // HD) % frames == 0
+    attended = (spread_attention if spread else gathered_attention)(
+        query_rows[0], key_rows[0], value_rows[0], gain_query, gain_key, slot_order
+    )
+    index = jnp.stack([me // 2, me % 2]) if spread else jnp.zeros((2,), jnp.int32)
 
     tile = model // 4
     partial_sums = pl.pallas_call(
@@ -218,20 +356,20 @@
             for j in range(chips)
         ],
         in_specs=[
-            pl.BlockSpec((frame_rows // 2, width), lambda i: (0, 0)),
-            pl.BlockSpec((frame_rows // 2, width), lambda i: (0, 0)),
+            pl.BlockSpec(memory_space=SMEM),
+            pl.BlockSpec(attended.shape, lambda i: (0, 0, 0)),
             pl.BlockSpec((width, tile), lambda i: (0, i)),
             pl.BlockSpec((width, tile), lambda i: (0, i)),
         ],
         out_specs=[pl.BlockSpec((rows, tile), lambda i: (0, i))] * chips,
-        compiler_params=pltpu.CompilerParams(vmem_limit_bytes=16 * 2**20),
-        cost_estimate=pl.CostEstimate(
-            flops=2 * frame_rows * width * model,
+        compiler_params=pltpu.CompilerParams(vmem_limit_bytes=48 * 2**20),
+        cost_estimate=pl.CostEstimate(
+            flops=4 * half * width * model,
             bytes_accessed=4 * width * model + 8 * rows * model,
             transcendentals=0,
         ),
         name="projection",
-    )(even, theirs, out_weight, other_weight)
+    )(index, attended, out_weight, other_weight)
 
     sums = {j: part for j, part in enumerate(partial_sums)}
     bit = 1

time: 85 us -> 78.9 us (0.928)
  blocking collectives: 0 us -> 28.9 us
  starting transfers between devices: 22.6 us -> 4.91 us
  waiting for transfers between devices: 38.1 us -> 27.3 us
  local copies, waits for them, and re-layouts: 6.14 us -> 1.25 us
  Pallas kernels: 13.8 us -> 12.1 us
    all_to_all x0 -> x1, blocking collectives: none -> 28.9 us  [spread_attention(): lax.all_to_all(sends, ('frame', 'seq'), split_axis=0, concat_axis=0, tile...]
    ppermute x19 -> x4, starting transfers between devices: 22.6 us -> 1.5 us  [across(): return lax.ppermute(value, axis, [(i, i ^ distance) for i in range(n)])]
    ppermute x19 -> x4, waiting for transfers between devices: 38.1 us -> 20.5 us  [across(): return lax.ppermute(value, axis, [(i, i ^ distance) for i in range(n)])]
    all_to_all x0 -> x1, waiting for transfers between devices: none -> 6.76 us  [spread_attention(): lax.all_to_all(done, ('frame', 'seq'), split_axis=0, concat_axis=0, axis_...]
    unnamed x14 -> x8, local copies, waits for them, and re-layouts: 4.65 us -> 0.67 us
    all_to_all x0 -> x1, starting transfers between devices: none -> 3.41 us  [spread_attention(): lax.all_to_all(done, ('frame', 'seq'), split_axis=0, concat_axis=0, axis_...]
    pallas_call x4 -> x2, Pallas kernels: 9.05 us -> 6.49 us  [the longest x1 4.17 us: spread_attention(): pl.pallas_call(functools.partial(spread_attention_kernel, n, frames), out...]
    slice x4 -> x0, local copies, waits for them, and re-layouts: 0.91 us -> none  [shards(): given = jnp.concatenate([block[rows:] for block in blocks], axis=0)]
  transfers between devices with their start and end apart: 19 -> 5, of which waited for: 11 -> 4; matrix products, arithmetic and copies ran while one was open for 3% -> 2% of each run, Pallas kernels for 7% -> 8%
where the time goes in v3:
time: 78.9 us; the launch traced here: 78.5 us
  blocking collectives  28.9 us (37%)
  waiting for transfers between devices  27.3 us (35%)
  Pallas kernels  12.1 us (15%)
  starting transfers between devices  4.91 us (6%)
  between operations  2.03 us (3%)
  other arithmetic  1.96 us (2%)
  local copies, waits for them, and re-layouts  1.25 us (2%)
    all_to_all x1, blocking collectives, spread_attention(): lax.all_to_all(sends, ('frame', 'seq'), split_axis=0, concat_axis=0, tile...  28.9 us
    ppermute x4, waiting for transfers between devices, across(): return lax.ppermute(value, axis, [(i, i ^ distance) for i in range(n)])  20.5 us
    all_to_all x1, waiting for transfers between devices, spread_attention(): lax.all_to_all(done, ('frame', 'seq'), split_axis=0, concat_axis=0, axis_...  6.76 us
    pallas_call x1, Pallas kernels, shards(): pl.pallas_call(functools.partial(projection_kernel, chips), grid=(model /...  5.57 us
    pallas_call x1, Pallas kernels, spread_attention(): pl.pallas_call(functools.partial(spread_attention_kernel, n, frames), out...  4.17 us
    all_to_all x1, starting transfers between devices, spread_attention(): lax.all_to_all(done, ('frame', 'seq'), split_axis=0, concat_axis=0, axis_...  3.41 us
    pallas_call x1, Pallas kernels, spread_attention(): pl.pallas_call(functools.partial(spread_norm_kernel, n, frames), out_shap...  2.32 us
  transfers between devices with their start and end apart: 5, of which 4 were waited for; matrix products, arithmetic and copies ran while one was open for 2% of the time, Pallas kernels for 8%

profile of v3, /device:TPU:0, one launch (start us, length us, event | category | flops | bytes accessed | tf_op | source)
XLA Modules:
  0.0 78.5 jit_solution(2515311745245326852)
XLA Ops:
  0.0 0.5 collective-permute-start
  0.5 2.3 %norm.1 = bf16[32,32,384]{2,1,0:T(8,128)(2,1)} custom-call(bf16[32,4096]{1,0:T(8,128)(2,1)} %bitcast.14, bf16[32,4096]{1,0:T(8,128)(2,1)} %bitcast.15, bf16[32,4096]{1,0:T(8,128)(2,1)} %bitcast.16, f32[1,4096]{1,0:T(1,128)} %bitcast.18, f32[1,4096]{1,0:T(1,128)} %bitcast.19), custom_call_target="tpu_custom_call" | custom-call | tf_op jit(solution)/shard_map/norm/pallas_call | solution.py:199
  2.8 28.9 %all_to_all.10.rows_ref = bf16[32,32,384]{2,1,0:T(8,128)(2,1)S(1)} all-to-all(bf16[32,32,384]{2,1,0:T(8,128)(2,1)} %norm.1), channel_id=1, replica_groups=mesh['frame'=4,'seq'=8] {'frame','seq'}, dimensions={0} | all-to-all | bytes 1572864 | tf_op jit(solution)/shard_map/all_to_all | solution.py:206
  31.7 0.0 copy-start
  31.7 0.7 copy-done
  32.4 4.2 %attention.1 = bf16[8,128,128]{2,1,0:T(8,128)(2,1)} custom-call(s32[4]{0:T(128)S(1)} %copy-done, bf16[32,32,384]{2,1,0:T(8,128)(2,1)S(1)} %all_to_all.10.rows_ref), custom_call_target="tpu_custom_call" | custom-call | flops 536870912 | bytes 1048576 | tf_op jit(solution)/shard_map/attention/pallas_call | solution.py:208
  36.5 3.4 %all-to-all-start.1 = ((bf16[8,128,128]{2,1,0:T(8,128)(2,1)}), bf16[8,128,128]{2,1,0:T(8,128)(2,1)S(1)}, u32[]{:S(2)}, u32[]{:S(2)}) async-start(bf16[8,128,128]{2,1,0:T(8,128)(2,1)} %attention.1), calls=%async_computation.1 | async-start | bytes 524288 | tf_op jit(solution)/shard_map/all_to_all | solution.py:222
  40.0 0.1 pad_add_fusion.index_ref
  40.1 6.8 %all-to-all-done.1.rows_ref = bf16[8,128,128]{2,1,0:T(8,128)(2,1)S(1)} async-done(((bf16[8,128,128]{2,1,0:T(8,128)(2,1)}), bf16[8,128,128]{2,1,0:T(8,128)(2,1)S(1)}, u32[]{:S(2)}, u32[]{:S(2)}) %all-to-all-start.1) | async-done | bytes 262176 | tf_op jit(solution)/shard_map/all_to_all | solution.py:222
  46.8 0.0 collective-permute-done.other_ref
  46.8 5.6 %projection.1 = (f32[32,5120]{1,0:T(8,128)S(1)}, bf16[32,5120]{1,0:T(8,128)(2,1)S(1)}, f32[32,5120]{1,0:T(8,128)S(1)}, bf16[32,5120]{1,0:T(8,128)(2,1)S(1)}) custom-call(s32[2]{0:T(128)S(1)} %pad_add_fusion.index_ref, bf16[8,128,128]{2,1,0:T(8,128)(2,1)S(1)} %all-to-all-done.1.rows_ref, bf16[512,5120]{1,0:T(8,128)(2,1)} %own_ref.1, ...), custom_call_target="tpu_custom_call" | custom-call | flops 1342177280 | bytes 11796480 | tf_op jit(solution)/shard_map/projection/pallas_call | solution.py:351
  52.4 0.1 collective-permute-start.1
  52.5 0.0 copy-done.3
  52.5 0.6 dynamic_slice.8
  54.4 0.0 copy-done.2
  55.1 6.2 %collective-permute-done.1 = bf16[32,5120]{1,0:T(8,128)(2,1)S(1)} collective-permute-done((bf16[32,5120]{1,0:T(8,128)(2,1)S(1)}, bf16[32,5120]{1,0:T(8,128)(2,1)S(1)}, u32[]{:S(2)}, u32[]{:S(2)}) %collective-permute-start.1) | collective-permute-done | bytes 327712 | tf_op jit(solution)/shard_map/ppermute | solution.py:338
  61.3 0.3 collective-permute-start.2
  61.6 0.1 add_convert_fusion
  61.6 0.7 collective-permute-start.3
  62.3 0.9 %dynamic-slice_convert_fusion = f32[1,5120]{1,0:T(1,128)S(1)} fusion(bf16[64,5120]{1,0:T(8,128)(2,1)} %param.19, s32[]{:T(128)S(6)} %select_n.20), kind=kLoop, calls=%fused_computation.4 | loop fusion | flops 5120 | bytes 30724 | tf_op jit(solution)/shard_map/mul | solution.py:390
  63.2 10.4 %collective-permute-done.2 = bf16[32,5120]{1,0:T(8,128)(2,1)S(1)} collective-permute-done((bf16[32,5120]{1,0:T(8,128)(2,1)S(1)}, bf16[32,5120]{1,0:T(8,128)(2,1)S(1)}, u32[]{:S(2)}, u32[]{:S(2)}) %collective-permute-start.2) | collective-permute-done | bytes 327712 | tf_op jit(solution)/shard_map/ppermute | solution.py:338
  73.6 3.9 %collective-permute-done.3 = bf16[32,5120]{1,0:T(8,128)(2,1)S(1)} collective-permute-done((bf16[32,5120]{1,0:T(8,128)(2,1)S(1)}, bf16[32,5120]{1,0:T(8,128)(2,1)S(1)}, u32[]{:S(2)}, u32[]{:S(2)}) %collective-permute-start.3) | collective-permute-done | bytes 327712 | tf_op jit(solution)/shard_map/ppermute | solution.py:338
  77.5 0.0 copy-done.1
  77.5 0.9 %fusion.1 = bf16[1,32,5120]{2,1,0:T(8,128)(2,1)} fusion(bf16[32,5120]{1,0:T(8,128)(2,1)S(1)} %collective-permute-done.3, f32[32,5120]{1,0:T(8,128)S(1)} %get-tuple-element.10, bf16[32,5120]{1,0:T(8,128)(2,1)S(1)} %collective-permute-done.2, bf16[1,32,5120]{2,1,0:T(8,128)(2,1)S(1)} %copy-done.1, f32[5120]{0:T(1024)S(1)} %convert_element_type.31, ...), kind=kLoop, calls=%fused_computation.3 | loop fusion | flops 1474560 | bytes 2007040 | tf_op jit(solution)/shard_map/broadcast_in_dim | solution.py:391
  (4 shorter events, 0.0 us)
Async XLA Ops:
  0.0 46.8 %collective-permute-start = (bf16[512,5120]{1,0:T(8,128)(2,1)}, bf16[512,5120]{1,0:T(8,128)(2,1)}, u32[]{:S(2)}, u32[]{:S(2)}) collective-permute-start(bf16[512,5120]{1,0:T(8,128)(2,1)} %own_ref.1), channel_id=1, source_target_pairs={{0,1},{1,0},{2,3},{3,2},{4,5},{5,4},{6,7},{7,6},{8,9},{9,8},{10,11... | collective-permute-start | bytes 15728648 | tf_op jit(solution)/shard_map/ppermute | solution.py:338
  31.7 0.7 copy-start
  36.5 10.3 %all-to-all-start.1 = ((bf16[8,128,128]{2,1,0:T(8,128)(2,1)}), bf16[8,128,128]{2,1,0:T(8,128)(2,1)S(1)}, u32[]{:S(2)}, u32[]{:S(2)}) async-start(bf16[8,128,128]{2,1,0:T(8,128)(2,1)} %attention.1), calls=%async_computation.1 | async-start | bytes 524288 | tf_op jit(solution)/shard_map/all_to_all | solution.py:222
  40.1 12.4 %copy-start.3 = (s32[4]{0:T(128)S(1)}, s32[4]{0:T(128)}, u32[]{:S(2)}) copy-start(s32[4]{0:T(128)} %param.20) | copy-start | bytes 52
  40.1 14.3 %copy-start.2 = (bf16[5120]{0:T(1024)(128)(2,1)S(1)}, bf16[5120]{0:T(1024)(128)(2,1)}, u32[]{:S(2)}) copy-start(bf16[5120]{0:T(1024)(128)(2,1)} %param.18) | copy-start | bytes 30724
  40.1 37.5 %copy-start.1 = (bf16[1,32,5120]{2,1,0:T(8,128)(2,1)S(1)}, bf16[1,32,5120]{2,1,0:T(8,128)(2,1)}, u32[]{:S(2)}) copy-start(bf16[1,32,5120]{2,1,0:T(8,128)(2,1)} %param.11) | copy-start | bytes 983044
  52.4 8.9 %collective-permute-start.1 = (bf16[32,5120]{1,0:T(8,128)(2,1)S(1)}, bf16[32,5120]{1,0:T(8,128)(2,1)S(1)}, u32[]{:S(2)}, u32[]{:S(2)}) collective-permute-start(bf16[32,5120]{1,0:T(8,128)(2,1)S(1)} %get-tuple-element.12), channel_id=1, source_target_pairs={{0,2},{1,3},{2,0},{3,1},{4,6},{5,7},{6,4},{7,5},{8,10},{9,11},{10,... | collective-permute-start | bytes 983048 | tf_op jit(solution)/shard_map/ppermute | solution.py:338
  61.3 12.3 %collective-permute-start.2 = (bf16[32,5120]{1,0:T(8,128)(2,1)S(1)}, bf16[32,5120]{1,0:T(8,128)(2,1)S(1)}, u32[]{:S(2)}, u32[]{:S(2)}) collective-permute-start(bf16[32,5120]{1,0:T(8,128)(2,1)S(1)} %get-tuple-element.13), channel_id=1, source_target_pairs={{0,2},{1,3},{2,0},{3,1},{4,6},{5,7},{6,4},{7,5},{8,10},{9,11},{10,... | collective-permute-start | bytes 983048 | tf_op jit(solution)/shard_map/ppermute | solution.py:338
  61.6 15.9 %collective-permute-start.3 = (bf16[32,5120]{1,0:T(8,128)(2,1)S(1)}, bf16[32,5120]{1,0:T(8,128)(2,1)S(1)}, u32[]{:S(2)}, u32[]{:S(2)}) collective-permute-start(bf16[32,5120]{1,0:T(8,128)(2,1)S(1)} %add_convert_fusion), channel_id=1, source_target_pairs={{0,4},{1,5},{2,6},{3,7},{4,0},{5,1},{6,2},{7,3},{8,12},{9,13},{10,... | collective-permute-start | bytes 983048 | tf_op jit(solution)/shard_map/ppermute | solution.py:338

commit v4 on v3

--- a/solution.py
+++ b/solution.py
@@ -101,29 +101,37 @@
                 out_ref[here, cols] = (summed / total).astype(jnp.bfloat16)
 
 
-def projection_kernel(chips, index_ref, rows_ref, own_ref, other_ref, *outs):
+def ordered(index_ref, rows_ref, chips):
     shift = index_ref[0]
-    core = index_ref[1]
-    sources, half, _ = rows_ref.shape
+    slot = index_ref[1]
+    blocks, half, _ = rows_ref.shape
     rows = half // chips
-
-    def gathered(parity):
-        return jnp.concatenate(
-            [
-                jnp.concatenate(
-                    [
-                        rows_ref[2 * i + (core ^ parity), pl.ds(pl.multiple_of((shift ^ j) * rows, rows), rows), :]
-                        for j in range(chips)
-                    ],
-                    axis=0,
-                )
-                for i in range(sources // 2)
-            ],
-            axis=1,
-        )
-
-    result = jnp.dot(gathered(0), own_ref[...], preferred_element_type=jnp.float32)
-    result += jnp.dot(gathered(1), other_ref[...], preferred_element_type=jnp.float32)
+    return jnp.concatenate(
+        [
+            jnp.concatenate(
+                [
+                    rows_ref[slot ^ i, pl.ds(pl.multiple_of((shift ^ j) * rows, rows), rows), :]
+                    for j in range(chips)
+                ],
+                axis=0,
+            )
+            for i in range(blocks)
+        ],
+        axis=1,
+    )
+
+
+def own_projection_kernel(chips, index_ref, rows_ref, weight_ref, out_ref):
+    out_ref[...] = jnp.dot(
+        ordered(index_ref, rows_ref, chips), weight_ref[...], preferred_element_type=jnp.float32
+    )
+
+
+def projection_kernel(chips, index_ref, rows_ref, weight_ref, start_ref, *outs):
+    rows = rows_ref.shape[1] // chips
+    result = start_ref[...] + jnp.dot(
+        ordered(index_ref, rows_ref, chips), weight_ref[...], preferred_element_type=jnp.float32
+    )
     for j in range(chips):
         outs[j][...] = result[j * rows : (j + 1) * rows].astype(outs[j].dtype)
 
@@ -144,29 +152,32 @@
             out_ref[f * n + s, :, 2 * part :] = value_ref[:, cols]
 
 
-def spread_attention_kernel(n, frames, order_ref, rows_ref, out_ref):
+def spread_attention_kernel(n, frames, picked, index_ref, order_ref, rows_ref, *outs):
+    slot = index_ref[0]
+    core = index_ref[1]
     rows = rows_ref.shape[1]
-    part = out_ref.shape[2]
+    part = outs[0].shape[2]
     frame_rows = n * rows
-    tokens = rows_ref[...].reshape(frames * frame_rows, 3 * part)
     factor = (HD ** (-0.5)) * LOG2E
     step = min(frame_rows, 128)
     for h in range(part // HD):
         cols = slice(h * HD, (h + 1) * HD)
-        query = tokens[:, h * HD : (h + 1) * HD]
-        keys = tokens[:, part + h * HD : part + (h + 1) * HD]
-        values = tokens[:, 2 * part + h * HD : 2 * part + (h + 1) * HD]
-        for g in range(frames):
+        keys = rows_ref[:, :, part + h * HD : part + (h + 1) * HD].reshape(-1, HD)
+        values = rows_ref[:, :, 2 * part + h * HD : 2 * part + (h + 1) * HD].reshape(-1, HD)
+        for distance, out_ref in zip(picked, outs):
+            frame = slot ^ distance
+            rank = order_ref[frame]
             hidden = jnp.concatenate(
                 [
-                    jnp.full((1, frame_rows), jnp.where(order_ref[f] <= order_ref[g], 0.0, -1e30), jnp.float32)
+                    jnp.full((1, frame_rows), jnp.where(order_ref[f] <= rank, 0.0, -1e30), jnp.float32)
                     for f in range(frames)
                 ],
                 axis=1,
             )
             for start in range(0, frame_rows, step):
+                query = rows_ref[pl.ds(frame * n + start // rows, step // rows), :, cols]
                 scores = lax.dot_general(
-                    query[g * frame_rows + start : g * frame_rows + start + step],
+                    query.reshape(step, HD),
                     keys,
                     (((1,), (1,)), ((), ())),
                     preferred_element_type=jnp.float32,
@@ -182,7 +193,7 @@
                 for i in range(step // rows):
                     s = start // rows + i
                     z = s // 2
-                    out_ref[2 * g + s % 2, z * rows : (z + 1) * rows, cols] = done[
+                    out_ref[(s % 2) ^ core, z * rows : (z + 1) * rows, cols] = done[
                         i * rows : (i + 1) * rows
                     ]
 
@@ -205,23 +216,35 @@
     )(query_rows, key_rows, value_rows, gain_query.reshape(1, features), gain_key.reshape(1, features))
     held = lax.all_to_all(sends, ("frame", "seq"), split_axis=0, concat_axis=0, tiled=True)
     keys = frames * frame_rows
-    done = pl.pallas_call(
-        functools.partial(spread_attention_kernel, n, frames),
-        out_shape=jax.ShapeDtypeStruct((2 * frames, frame_rows // 2, part), jnp.bfloat16),
-        in_specs=[smem, vmem],
-        out_specs=vmem,
-        compiler_params=pltpu.CompilerParams(vmem_limit_bytes=8 * 2**20 + 6 * 128 * keys * 4),
-        cost_estimate=pl.CostEstimate(
-            flops=4 * keys * keys * part,
-            bytes_accessed=8 * keys * part,
-            transcendentals=keys * keys * (part // HD),
-        ),
-        name="attention",
-    )(slot_order, held)
-    planes = [[f * n + 2 * z + c for f in range(frames) for c in range(2)] for z in range(chips)]
-    return lax.all_to_all(
-        done, ("frame", "seq"), split_axis=0, concat_axis=0, axis_index_groups=planes, tiled=True
-    )
+    me = lax.axis_index("seq").astype(jnp.int32)
+    slot = lax.axis_index("frame").astype(jnp.int32)
+    index = jnp.stack([slot, me % 2])
+
+    def attend(picked, name):
+        count = len(picked)
+        return pl.pallas_call(
+            functools.partial(spread_attention_kernel, n, frames, picked),
+            out_shape=[jax.ShapeDtypeStruct((2, frame_rows // 2, part), jnp.bfloat16)] * count,
+            in_specs=[smem, smem, vmem],
+            out_specs=[vmem] * count,
+            compiler_params=pltpu.CompilerParams(vmem_limit_bytes=8 * 2**20 + 6 * 128 * keys * 4),
+            cost_estimate=pl.CostEstimate(
+                flops=4 * count * frame_rows * keys * part,
+                bytes_accessed=8 * keys * part,
+                transcendentals=count * frame_rows * keys * (part // HD),
+            ),
+            name=name,
+        )(index, slot_order, held)
+
+    far = list(range(frames - 1, 0, -1))
+    done = {
+        d: lax.ppermute(block, "frame", [(i, i ^ d) for i in range(frames)])
+        for d, block in zip(far, attend(far, "attention_far"))
+    }
+    done[0] = attend([0], "attention_near")[0]
+    mine = jnp.stack([done[d][0] for d in range(frames)])
+    given = jnp.stack([done[d][1] for d in range(frames)])
+    return mine, lax.ppermute(given, "seq", [(i, i ^ 1) for i in range(n)])
 
 
 def gathered_attention(query_rows, key_rows, value_rows, gain_query, gain_key, slot_order):
@@ -308,7 +331,7 @@
         ),
         name="attention",
     )(slot_array, slot_order, *queries, *pieces)
-    return jnp.stack([even, across(odd, "seq", 1)])
+    return even[None], across(odd, "seq", 1)[None]
 
 
 def shards(
@@ -342,34 +365,44 @@
 
     other_weight = across(out_weight, "seq", 1)
     spread = (width // HD) % frames == 0
-    attended = (spread_attention if spread else gathered_attention)(
+    mine, theirs = (spread_attention if spread else gathered_attention)(
         query_rows[0], key_rows[0], value_rows[0], gain_query, gain_key, slot_order
     )
-    index = jnp.stack([me // 2, me % 2]) if spread else jnp.zeros((2,), jnp.int32)
+    index = jnp.stack([me // 2, slot]) if spread else jnp.zeros((2,), jnp.int32)
 
     tile = model // 4
+    rows_spec = pl.BlockSpec(mine.shape, lambda i: (0, 0, 0))
+    weight_spec = pl.BlockSpec((width, tile), lambda i: (0, i))
+    wide_spec = pl.BlockSpec((half, tile), lambda i: (0, i))
+    projecting = dict(
+        grid=(model // tile,),
+        compiler_params=pltpu.CompilerParams(vmem_limit_bytes=32 * 2**20),
+        cost_estimate=pl.CostEstimate(
+            flops=2 * half * width * model,
+            bytes_accessed=2 * width * model + 4 * half * model,
+            transcendentals=0,
+        ),
+    )
+    smem = pl.BlockSpec(memory_space=SMEM)
+    own_part = pl.pallas_call(
+        functools.partial(own_projection_kernel, chips),
+        out_shape=jax.ShapeDtypeStruct((half, model), jnp.float32),
+        in_specs=[smem, rows_spec, weight_spec],
+        out_specs=wide_spec,
+        name="own_projection",
+        **projecting,
+    )(index, mine, out_weight)
     partial_sums = pl.pallas_call(
         functools.partial(projection_kernel, chips),
-        grid=(model // tile,),
         out_shape=[
             jax.ShapeDtypeStruct((rows, model), jnp.bfloat16 if j % 2 else jnp.float32)
             for j in range(chips)
         ],
-        in_specs=[
-            pl.BlockSpec(memory_space=SMEM),
-            pl.BlockSpec(attended.shape, lambda i: (0, 0, 0)),
-            pl.BlockSpec((width, tile), lambda i: (0, i)),
-            pl.BlockSpec((width, tile), lambda i: (0, i)),
-        ],
+        in_specs=[smem, rows_spec, weight_spec, wide_spec],
         out_specs=[pl.BlockSpec((rows, tile), lambda i: (0, i))] * chips,
-        compiler_params=pltpu.CompilerParams(vmem_limit_bytes=48 * 2**20),
-        cost_estimate=pl.CostEstimate(
-            flops=4 * half * width * model,
-            bytes_accessed=4 * width * model + 8 * rows * model,
-            transcendentals=0,
-        ),
         name="projection",
-    )(index, attended, out_weight, other_weight)
+        **projecting,
+    )(index, theirs, other_weight, own_part)
 
     sums = {j: part for j, part in enumerate(partial_sums)}
     bit = 1

time: 78.9 us -> 79.8 us (1.011)
  blocking collectives: 28.9 us -> 0 us
  waiting for transfers between devices: 27.3 us -> 44.7 us
  starting transfers between devices: 4.91 us -> 13.7 us
  local copies, waits for them, and re-layouts: 1.25 us -> 3.76 us
  Pallas kernels: 12.1 us -> 13 us
    all_to_all x1 -> x0, blocking collectives: 28.9 us -> none  [spread_attention(): lax.all_to_all(sends, ('frame', 'seq'), split_axis=0, concat_axis=0, tile...]
    all_to_all x1, waiting for transfers between devices: 6.76 us -> 21.8 us  [spread_attention(): lax.all_to_all(sends, ('frame', 'seq'), split_axis=0, concat_axis=0, tile...]
    ppermute x0 -> x4, starting transfers between devices: none -> 3.62 us  [the longest x3 3.55 us: spread_attention(): lax.ppermute(block, 'frame', [(i, i ^ d) for i in range(frames)])]
    all_to_all x1, starting transfers between devices: 3.41 us -> 6.96 us  [spread_attention(): lax.all_to_all(sends, ('frame', 'seq'), split_axis=0, concat_axis=0, tile...]
    unnamed x8 -> x10, local copies, waits for them, and re-layouts: 0.67 us -> 3.16 us
    ppermute x4, starting transfers between devices: 1.5 us -> 3.11 us  [across(): return lax.ppermute(value, axis, [(i, i ^ distance) for i in range(n)])]
    ppermute x0 -> x4, waiting for transfers between devices: none -> 1.34 us  [the longest x3 1.34 us: spread_attention(): lax.ppermute(block, 'frame', [(i, i ^ d) for i in range(frames)])]
    ppermute x4, waiting for transfers between devices: 20.5 us -> 21.6 us  [across(): return lax.ppermute(value, axis, [(i, i ^ distance) for i in range(n)])]
  transfers between devices with their start and end apart: 5 -> 9, of which waited for: 4 -> 6; matrix products, arithmetic and copies ran while one was open for 2% -> 2% of each run, Pallas kernels for 8% -> 11%
where the time goes in v4:
time: 79.8 us; the launch traced here: 79.4 us
  waiting for transfers between devices  44.7 us (56%)
  starting transfers between devices  13.7 us (17%)
  Pallas kernels  13 us (16%)
  local copies, waits for them, and re-layouts  3.76 us (5%)
  between operations  2.14 us (3%)
  other arithmetic  2.08 us (3%)
    all_to_all x1, waiting for transfers between devices, spread_attention(): lax.all_to_all(sends, ('frame', 'seq'), split_axis=0, concat_axis=0, tile...  21.8 us
    ppermute x4, waiting for transfers between devices, across(): return lax.ppermute(value, axis, [(i, i ^ distance) for i in range(n)])  21.6 us
    all_to_all x1, starting transfers between devices, spread_attention(): lax.all_to_all(sends, ('frame', 'seq'), split_axis=0, concat_axis=0, tile...  6.96 us
    pallas_call x2, Pallas kernels, attend(): pl.pallas_call(functools.partial(spread_attention_kernel, n, frames, pick...  4.16 us
    pallas_call x1, Pallas kernels, shards(): pl.pallas_call(functools.partial(projection_kernel, chips), out_shape=[ja...  4.11 us
    ppermute x3, starting transfers between devices, spread_attention(): lax.ppermute(block, 'frame', [(i, i ^ d) for i in range(frames)])  3.55 us
    unnamed x10, local copies, waits for them, and re-layouts  3.16 us
    ppermute x4, starting transfers between devices, across(): return lax.ppermute(value, axis, [(i, i ^ distance) for i in range(n)])  3.11 us
  transfers between devices with their start and end apart: 9, of which 6 were waited for; matrix products, arithmetic and copies ran while one was open for 2% of the time, Pallas kernels for 11%

profile of v4, /device:TPU:0, one launch (start us, length us, event | category | flops | bytes accessed | tf_op | source)
XLA Modules:
  0.0 79.4 jit_solution(701259096261423307)
XLA Ops:
  0.0 0.5 collective-permute-start.4
  0.5 2.3 %norm.1 = bf16[32,32,384]{2,1,0:T(8,128)(2,1)} custom-call(bf16[32,4096]{1,0:T(8,128)(2,1)} %bitcast.15, bf16[32,4096]{1,0:T(8,128)(2,1)} %bitcast.16, bf16[32,4096]{1,0:T(8,128)(2,1)} %bitcast.17, f32[1,4096]{1,0:T(1,128)} %bitcast.19, f32[1,4096]{1,0:T(1,128)} %bitcast.20), custom_call_target="tpu_custom_call" | custom-call | tf_op jit(solution)/shard_map/norm/pallas_call | solution.py:210
  2.8 7.0 %all-to-all-start = ((bf16[32,32,384]{2,1,0:T(8,128)(2,1)}), bf16[32,32,384]{2,1,0:T(8,128)(2,1)S(1)}, u32[]{:S(2)}, u32[]{:S(2)}) async-start(bf16[32,32,384]{2,1,0:T(8,128)(2,1)} %norm.1), calls=%async_computation | async-start | bytes 1572864 | tf_op jit(solution)/shard_map/all_to_all | solution.py:217
  9.8 0.1 pad_add_fusion.1.index_ref
  9.9 21.8 %all-to-all-done.rows_ref = bf16[32,32,384]{2,1,0:T(8,128)(2,1)S(1)} async-done(((bf16[32,32,384]{2,1,0:T(8,128)(2,1)}), bf16[32,32,384]{2,1,0:T(8,128)(2,1)S(1)}, u32[]{:S(2)}, u32[]{:S(2)}) %all-to-all-start) | async-done | bytes 786464 | tf_op jit(solution)/shard_map/all_to_all | solution.py:217
  31.7 0.7 copy-done.1
  32.4 2.8 %attention_far.1 = (bf16[2,128,128]{2,1,0:T(8,128)(2,1)S(1)}, bf16[2,128,128]{2,1,0:T(8,128)(2,1)S(1)}, bf16[2,128,128]{2,1,0:T(8,128)(2,1)S(1)}) custom-call(s32[2]{0:T(128)S(1)} %pad_add_fusion.1.index_ref, s32[4]{0:T(128)S(1)} %copy-done.1, bf16[32,32,384]{2,1,0:T(8,128)(2,1)S(1)} %all-to-all-done.rows_ref), custom_call_target="tpu_custom_call" | custom-call | flops 402653184 | bytes 1048576 | tf_op jit(solution)/shard_map/attention_far/pallas_call | solution.py:225
  35.2 1.1 %collective-permute-start.1 = (bf16[2,128,128]{2,1,0:T(8,128)(2,1)S(1)}, bf16[2,128,128]{2,1,0:T(8,128)(2,1)S(1)}, u32[]{:S(2)}, u32[]{:S(2)}) collective-permute-start(bf16[2,128,128]{2,1,0:T(8,128)(2,1)S(1)} %get-tuple-element.14), channel_id=1, source_target_pairs={{0,16},{8,24},{16,0},{24,8},{1,17},{9,25},{17,1},{25,9},{2,18},{10... | collective-permute-start | bytes 196616 | tf_op jit(solution)/shard_map/ppermute | solution.py:241
  36.3 2.4 %collective-permute-start.2 = (bf16[2,128,128]{2,1,0:T(8,128)(2,1)S(1)}, bf16[2,128,128]{2,1,0:T(8,128)(2,1)S(1)}, u32[]{:S(2)}, u32[]{:S(2)}) collective-permute-start(bf16[2,128,128]{2,1,0:T(8,128)(2,1)S(1)} %get-tuple-element.15), channel_id=1, source_target_pairs={{0,24},{8,16},{16,8},{24,0},{1,25},{9,17},{17,9},{25,1},{2,26},{10... | collective-permute-start | bytes 196616 | tf_op jit(solution)/shard_map/ppermute | solution.py:241
  38.7 1.4 %attention_near.1 = bf16[2,128,128]{2,1,0:T(8,128)(2,1)S(1)} custom-call(s32[2]{0:T(128)S(1)} %pad_add_fusion.1.index_ref, s32[4]{0:T(128)S(1)} %copy-done.1, bf16[32,32,384]{2,1,0:T(8,128)(2,1)S(1)} %all-to-all-done.rows_ref), custom_call_target="tpu_custom_call" | custom-call | flops 134217728 | bytes 1048576 | tf_op jit(solution)/shard_map/attention_near/pallas_call | solution.py:225
  40.1 0.3 collective-permute-done.1
  40.5 1.0 %collective-permute-done.2 = bf16[2,128,128]{2,1,0:T(8,128)(2,1)S(1)} collective-permute-done((bf16[2,128,128]{2,1,0:T(8,128)(2,1)S(1)}, bf16[2,128,128]{2,1,0:T(8,128)(2,1)S(1)}, u32[]{:S(2)}, u32[]{:S(2)}) %collective-permute-start.2) | collective-permute-done | bytes 65568 | tf_op jit(solution)/shard_map/ppermute | solution.py:241
  41.6 2.5 %copy-done = bf16[512,5120]{1,0:T(8,128)(2,1)S(1)} copy-done((bf16[512,5120]{1,0:T(8,128)(2,1)S(1)}, bf16[512,5120]{1,0:T(8,128)(2,1)}, u32[]{:S(2)}) %copy-start) | copy-done | bytes 5242904
  44.1 2.5 %own_projection.1.start_ref = f32[128,5120]{1,0:T(8,128)S(1)} custom-call(s32[2]{0:T(128)S(1)} %pad_add_fusion.index_ref, bf16[4,128,128]{2,1,0:T(8,128)(2,1)S(1)} %pad_maximum_fusion.1.rows_ref, bf16[512,5120]{1,0:T(8,128)(2,1)S(1)} %copy-done), custom_call_target="tpu_custom_call" | custom-call | flops 671088640 | bytes 7864320 | tf_op jit(solution)/shard_map/own_projection/pallas_call | solution.py:387
  46.6 4.1 %projection.1 = (f32[32,5120]{1,0:T(8,128)S(1)}, bf16[32,5120]{1,0:T(8,128)(2,1)S(1)}, f32[32,5120]{1,0:T(8,128)S(1)}, bf16[32,5120]{1,0:T(8,128)(2,1)S(1)}) custom-call(s32[2]{0:T(128)S(1)} %pad_add_fusion.index_ref, bf16[4,128,128]{2,1,0:T(8,128)(2,1)S(1)} %collective-permute-done.3.rows_ref, bf16[512,5120]{1,0:T(8,128)(2,1)} %collective-permute-done.4.weight_ref, ...), custom_call_target="tpu_custom_call" | custom-call | flops 671088640 | bytes 7864320 | tf_op jit(solution)/shard_map/projection/pallas_call | solution.py:395
  50.7 0.1 collective-permute-start.5
  50.9 0.6 dynamic_slice.8
  53.4 7.5 %collective-permute-done.5 = bf16[32,5120]{1,0:T(8,128)(2,1)S(1)} collective-permute-done((bf16[32,5120]{1,0:T(8,128)(2,1)S(1)}, bf16[32,5120]{1,0:T(8,128)(2,1)S(1)}, u32[]{:S(2)}, u32[]{:S(2)}) %collective-permute-start.5) | collective-permute-done | bytes 327712 | tf_op jit(solution)/shard_map/ppermute | solution.py:361
  60.9 0.3 collective-permute-start.6
  61.3 2.3 %collective-permute-start.7 = (bf16[32,5120]{1,0:T(8,128)(2,1)S(1)}, bf16[32,5120]{1,0:T(8,128)(2,1)S(1)}, u32[]{:S(2)}, u32[]{:S(2)}) collective-permute-start(bf16[32,5120]{1,0:T(8,128)(2,1)S(1)} %add_convert_fusion), channel_id=1, source_target_pairs={{0,4},{1,5},{2,6},{3,7},{4,0},{5,1},{6,2},{7,3},{8,12},{9,13},{10,... | collective-permute-start | bytes 983048 | tf_op jit(solution)/shard_map/ppermute | solution.py:361
  63.5 0.9 %dynamic-slice_convert_fusion = f32[1,5120]{1,0:T(1,128)S(1)} fusion(bf16[64,5120]{1,0:T(8,128)(2,1)} %param.19, s32[]{:T(128)S(6)} %select_n.20), kind=kLoop, calls=%fused_computation.6 | loop fusion | flops 5120 | bytes 30724 | tf_op jit(solution)/shard_map/mul | solution.py:423
  64.4 12.1 %collective-permute-done.6 = bf16[32,5120]{1,0:T(8,128)(2,1)S(1)} collective-permute-done((bf16[32,5120]{1,0:T(8,128)(2,1)S(1)}, bf16[32,5120]{1,0:T(8,128)(2,1)S(1)}, u32[]{:S(2)}, u32[]{:S(2)}) %collective-permute-start.6) | collective-permute-done | bytes 327712 | tf_op jit(solution)/shard_map/ppermute | solution.py:361
  76.5 2.0 %collective-permute-done.7 = bf16[32,5120]{1,0:T(8,128)(2,1)S(1)} collective-permute-done((bf16[32,5120]{1,0:T(8,128)(2,1)S(1)}, bf16[32,5120]{1,0:T(8,128)(2,1)S(1)}, u32[]{:S(2)}, u32[]{:S(2)}) %collective-permute-start.7) | collective-permute-done | bytes 327712 | tf_op jit(solution)/shard_map/ppermute | solution.py:361
  78.5 0.9 %fusion.1 = bf16[1,32,5120]{2,1,0:T(8,128)(2,1)} fusion(bf16[32,5120]{1,0:T(8,128)(2,1)S(1)} %collective-permute-done.7, f32[32,5120]{1,0:T(8,128)S(1)} %get-tuple-element.16, bf16[32,5120]{1,0:T(8,128)(2,1)S(1)} %collective-permute-done.6, bf16[1,32,5120]{2,1,0:T(8,128)(2,1)S(1)} %copy-done.2, f32[5120]{0:T(1024)S(1)} %convert_element_type.31, ...), kind=kLoop, calls=%fused_computation.3 | loop fusion | flops 1474560 | bytes 2007040 | tf_op jit(solution)/shard_map/broadcast_in_dim | solution.py:424
  (22 shorter events, 0.4 us)
Async XLA Ops:
  0.0 46.6 %collective-permute-start.4 = (bf16[512,5120]{1,0:T(8,128)(2,1)}, bf16[512,5120]{1,0:T(8,128)(2,1)}, u32[]{:S(2)}, u32[]{:S(2)}) collective-permute-start(bf16[512,5120]{1,0:T(8,128)(2,1)} %weight_ref.1), channel_id=1, source_target_pairs={{0,1},{1,0},{2,3},{3,2},{4,5},{5,4},{6,7},{7,6},{8,9},{9,8},{10,11... | collective-permute-start | bytes 15728648 | tf_op jit(solution)/shard_map/ppermute | solution.py:361
  2.8 28.9 %all-to-all-start = ((bf16[32,32,384]{2,1,0:T(8,128)(2,1)}), bf16[32,32,384]{2,1,0:T(8,128)(2,1)S(1)}, u32[]{:S(2)}, u32[]{:S(2)}) async-start(bf16[32,32,384]{2,1,0:T(8,128)(2,1)} %norm.1), calls=%async_computation | async-start | bytes 1572864 | tf_op jit(solution)/shard_map/all_to_all | solution.py:217
  31.7 0.7 copy-start.1
  35.1 5.0 %collective-permute-start = (bf16[2,128,128]{2,1,0:T(8,128)(2,1)S(1)}, bf16[2,128,128]{2,1,0:T(8,128)(2,1)S(1)}, u32[]{:S(2)}, u32[]{:S(2)}) collective-permute-start(bf16[2,128,128]{2,1,0:T(8,128)(2,1)S(1)} %get-tuple-element.13), channel_id=1, source_target_pairs={{0,8},{8,0},{16,24},{24,16},{1,9},{9,1},{17,25},{25,17},{2,10},{10... | collective-permute-start | bytes 196616 | tf_op jit(solution)/shard_map/ppermute | solution.py:241
  35.2 5.3 %collective-permute-start.1 = (bf16[2,128,128]{2,1,0:T(8,128)(2,1)S(1)}, bf16[2,128,128]{2,1,0:T(8,128)(2,1)S(1)}, u32[]{:S(2)}, u32[]{:S(2)}) collective-permute-start(bf16[2,128,128]{2,1,0:T(8,128)(2,1)S(1)} %get-tuple-element.14), channel_id=1, source_target_pairs={{0,16},{8,24},{16,0},{24,8},{1,17},{9,25},{17,1},{25,9},{2,18},{10... | collective-permute-start | bytes 196616 | tf_op jit(solution)/shard_map/ppermute | solution.py:241
  36.3 5.2 %collective-permute-start.2 = (bf16[2,128,128]{2,1,0:T(8,128)(2,1)S(1)}, bf16[2,128,128]{2,1,0:T(8,128)(2,1)S(1)}, u32[]{:S(2)}, u32[]{:S(2)}) collective-permute-start(bf16[2,128,128]{2,1,0:T(8,128)(2,1)S(1)} %get-tuple-element.15), channel_id=1, source_target_pairs={{0,24},{8,16},{16,8},{24,0},{1,25},{9,17},{17,9},{25,1},{2,26},{10... | collective-permute-start | bytes 196616 | tf_op jit(solution)/shard_map/ppermute | solution.py:241
  41.5 5.1 %collective-permute-start.3 = (bf16[4,128,128]{2,1,0:T(8,128)(2,1)S(1)}, bf16[4,128,128]{2,1,0:T(8,128)(2,1)S(1)}, u32[]{:S(2)}, u32[]{:S(2)}) collective-permute-start(bf16[4,128,128]{2,1,0:T(8,128)(2,1)S(1)} %pad_maximum_fusion), channel_id=1, source_target_pairs={{0,1},{1,0},{2,3},{3,2},{4,5},{5,4},{6,7},{7,6},{8,9},{9,8},{10,11... | collective-permute-start | bytes 393224 | tf_op jit(solution)/shard_map/ppermute | solution.py:247
  41.6 2.5 %copy-start = (bf16[512,5120]{1,0:T(8,128)(2,1)S(1)}, bf16[512,5120]{1,0:T(8,128)(2,1)}, u32[]{:S(2)}) copy-start(bf16[512,5120]{1,0:T(8,128)(2,1)} %weight_ref.1) | copy-start | bytes 15728644
  46.6 4.3 %copy-start.4 = (s32[4]{0:T(128)S(1)}, s32[4]{0:T(128)}, u32[]{:S(2)}) copy-start(s32[4]{0:T(128)} %param.20) | copy-start | bytes 52
  46.6 6.2 %copy-start.3 = (bf16[5120]{0:T(1024)(128)(2,1)S(1)}, bf16[5120]{0:T(1024)(128)(2,1)}, u32[]{:S(2)}) copy-start(bf16[5120]{0:T(1024)(128)(2,1)} %param.18) | copy-start | bytes 30724
  46.6 31.9 %copy-start.2 = (bf16[1,32,5120]{2,1,0:T(8,128)(2,1)S(1)}, bf16[1,32,5120]{2,1,0:T(8,128)(2,1)}, u32[]{:S(2)}) copy-start(bf16[1,32,5120]{2,1,0:T(8,128)(2,1)} %param.11) | copy-start | bytes 983044
  50.7 10.2 %collective-permute-start.5 = (bf16[32,5120]{1,0:T(8,128)(2,1)S(1)}, bf16[32,5120]{1,0:T(8,128)(2,1)S(1)}, u32[]{:S(2)}, u32[]{:S(2)}) collective-permute-start(bf16[32,5120]{1,0:T(8,128)(2,1)S(1)} %get-tuple-element.18), channel_id=1, source_target_pairs={{0,2},{1,3},{2,0},{3,1},{4,6},{5,7},{6,4},{7,5},{8,10},{9,11},{10,... | collective-permute-start | bytes 983048 | tf_op jit(solution)/shard_map/ppermute | solution.py:361
  60.9 15.6 %collective-permute-start.6 = (bf16[32,5120]{1,0:T(8,128)(2,1)S(1)}, bf16[32,5120]{1,0:T(8,128)(2,1)S(1)}, u32[]{:S(2)}, u32[]{:S(2)}) collective-permute-start(bf16[32,5120]{1,0:T(8,128)(2,1)S(1)} %get-tuple-element.19), channel_id=1, source_target_pairs={{0,2},{1,3},{2,0},{3,1},{4,6},{5,7},{6,4},{7,5},{8,10},{9,11},{10,... | collective-permute-start | bytes 983048 | tf_op jit(solution)/shard_map/ppermute | solution.py:361
  61.3 17.2 %collective-permute-start.7 = (bf16[32,5120]{1,0:T(8,128)(2,1)S(1)}, bf16[32,5120]{1,0:T(8,128)(2,1)S(1)}, u32[]{:S(2)}, u32[]{:S(2)}) collective-permute-start(bf16[32,5120]{1,0:T(8,128)(2,1)S(1)} %add_convert_fusion), channel_id=1, source_target_pairs={{0,4},{1,5},{2,6},{3,7},{4,0},{5,1},{6,2},{7,3},{8,12},{9,13},{10,... | collective-permute-start | bytes 983048 | tf_op jit(solution)/shard_map/ppermute | solution.py:361

commit v5 on v4

--- a/solution.py
+++ b/solution.py
@@ -101,37 +101,27 @@
                 out_ref[here, cols] = (summed / total).astype(jnp.bfloat16)
 
 
-def ordered(index_ref, rows_ref, chips):
+def projection_kernel(chips, sources, index_ref, *refs):
+    own_ref, other_ref = refs[sources : sources + 2]
+    outs = refs[sources + 2 : -1]
+    gathered_ref = refs[-1]
     shift = index_ref[0]
     slot = index_ref[1]
-    blocks, half, _ = rows_ref.shape
+    _, half, part = refs[0].shape
     rows = half // chips
-    return jnp.concatenate(
-        [
-            jnp.concatenate(
-                [
-                    rows_ref[slot ^ i, pl.ds(pl.multiple_of((shift ^ j) * rows, rows), rows), :]
-                    for j in range(chips)
-                ],
-                axis=0,
-            )
-            for i in range(blocks)
-        ],
-        axis=1,
-    )
-
-
-def own_projection_kernel(chips, index_ref, rows_ref, weight_ref, out_ref):
-    out_ref[...] = jnp.dot(
-        ordered(index_ref, rows_ref, chips), weight_ref[...], preferred_element_type=jnp.float32
-    )
-
-
-def projection_kernel(chips, index_ref, rows_ref, weight_ref, start_ref, *outs):
-    rows = rows_ref.shape[1] // chips
-    result = start_ref[...] + jnp.dot(
-        ordered(index_ref, rows_ref, chips), weight_ref[...], preferred_element_type=jnp.float32
-    )
+    width = own_ref.shape[0]
+
+    @pl.when(pl.program_id(0) == 0)
+    def _():
+        for d in range(sources):
+            for parity in range(2):
+                first = pl.multiple_of(parity * width + (slot ^ d) * part, part)
+                for j in range(chips):
+                    here = pl.ds(pl.multiple_of((shift ^ j) * rows, rows), rows)
+                    gathered_ref[j * rows : (j + 1) * rows, pl.ds(first, part)] = refs[d][parity, here, :]
+
+    result = jnp.dot(gathered_ref[:, :width], own_ref[...], preferred_element_type=jnp.float32)
+    result += jnp.dot(gathered_ref[:, width:], other_ref[...], preferred_element_type=jnp.float32)
     for j in range(chips):
         outs[j][...] = result[j * rows : (j + 1) * rows].astype(outs[j].dtype)
 
@@ -152,11 +142,11 @@
             out_ref[f * n + s, :, 2 * part :] = value_ref[:, cols]
 
 
-def spread_attention_kernel(n, frames, picked, index_ref, order_ref, rows_ref, *outs):
+def spread_attention_kernel(n, frames, picked, index_ref, order_ref, rows_ref, mine_ref, given_ref, both):
     slot = index_ref[0]
     core = index_ref[1]
     rows = rows_ref.shape[1]
-    part = outs[0].shape[2]
+    part = mine_ref.shape[2]
     frame_rows = n * rows
     factor = (HD ** (-0.5)) * LOG2E
     step = min(frame_rows, 128)
@@ -164,7 +154,7 @@
         cols = slice(h * HD, (h + 1) * HD)
         keys = rows_ref[:, :, part + h * HD : part + (h + 1) * HD].reshape(-1, HD)
         values = rows_ref[:, :, 2 * part + h * HD : 2 * part + (h + 1) * HD].reshape(-1, HD)
-        for distance, out_ref in zip(picked, outs):
+        for place, distance in enumerate(picked):
             frame = slot ^ distance
             rank = order_ref[frame]
             hidden = jnp.concatenate(
@@ -193,9 +183,9 @@
                 for i in range(step // rows):
                     s = start // rows + i
                     z = s // 2
-                    out_ref[(s % 2) ^ core, z * rows : (z + 1) * rows, cols] = done[
-                        i * rows : (i + 1) * rows
-                    ]
+                    both[s % 2, place, z * rows : (z + 1) * rows, cols] = done[i * rows : (i + 1) * rows]
+    mine_ref[...] = both[core]
+    given_ref[...] = both[core ^ 1]
 
 
 def spread_attention(query_rows, key_rows, value_rows, gain_query, gain_key, slot_order):
@@ -224,9 +214,10 @@
         count = len(picked)
         return pl.pallas_call(
             functools.partial(spread_attention_kernel, n, frames, picked),
-            out_shape=[jax.ShapeDtypeStruct((2, frame_rows // 2, part), jnp.bfloat16)] * count,
+            out_shape=[jax.ShapeDtypeStruct((count, frame_rows // 2, part), jnp.bfloat16)] * 2,
             in_specs=[smem, smem, vmem],
-            out_specs=[vmem] * count,
+            out_specs=[vmem] * 2,
+            scratch_shapes=[pltpu.VMEM((2, count, frame_rows // 2, part), jnp.bfloat16)],
             compiler_params=pltpu.CompilerParams(vmem_limit_bytes=8 * 2**20 + 6 * 128 * keys * 4),
             cost_estimate=pl.CostEstimate(
                 flops=4 * count * frame_rows * keys * part,
@@ -236,15 +227,19 @@
             name=name,
         )(index, slot_order, held)
 
+    def across(value, axis, distance):
+        size = n if axis == "seq" else frames
+        return lax.ppermute(value, axis, [(i, i ^ distance) for i in range(size)])
+
     far = list(range(frames - 1, 0, -1))
-    done = {
-        d: lax.ppermute(block, "frame", [(i, i ^ d) for i in range(frames)])
-        for d, block in zip(far, attend(far, "attention_far"))
-    }
-    done[0] = attend([0], "attention_near")[0]
-    mine = jnp.stack([done[d][0] for d in range(frames)])
-    given = jnp.stack([done[d][1] for d in range(frames)])
-    return mine, lax.ppermute(given, "seq", [(i, i ^ 1) for i in range(n)])
+    far_mine, far_given = attend(far, "attention_far")
+    far_got = across(far_given, "seq", 1)
+    near_mine, near_given = attend([0], "attention_near")
+    near_got = across(near_given, "seq", 1)
+    found = {0: jnp.concatenate([near_mine, near_got], axis=0)}
+    for place, d in enumerate(far):
+        found[d] = across(jnp.stack([far_mine[place], far_got[place]]), "frame", d)
+    return [found[d] for d in range(frames)]
 
 
 def gathered_attention(query_rows, key_rows, value_rows, gain_query, gain_key, slot_order):
@@ -331,7 +326,7 @@
         ),
         name="attention",
     )(slot_array, slot_order, *queries, *pieces)
-    return even[None], across(odd, "seq", 1)[None]
+    return [jnp.stack([even, across(odd, "seq", 1)])]
 
 
 def shards(
@@ -365,57 +360,51 @@
 
     other_weight = across(out_weight, "seq", 1)
     spread = (width // HD) % frames == 0
-    mine, theirs = (spread_attention if spread else gathered_attention)(
+    attended = (spread_attention if spread else gathered_attention)(
         query_rows[0], key_rows[0], value_rows[0], gain_query, gain_key, slot_order
     )
     index = jnp.stack([me // 2, slot]) if spread else jnp.zeros((2,), jnp.int32)
 
-    tile = model // 4
-    rows_spec = pl.BlockSpec(mine.shape, lambda i: (0, 0, 0))
-    weight_spec = pl.BlockSpec((width, tile), lambda i: (0, i))
-    wide_spec = pl.BlockSpec((half, tile), lambda i: (0, i))
-    projecting = dict(
-        grid=(model // tile,),
-        compiler_params=pltpu.CompilerParams(vmem_limit_bytes=32 * 2**20),
-        cost_estimate=pl.CostEstimate(
-            flops=2 * half * width * model,
-            bytes_accessed=2 * width * model + 4 * half * model,
-            transcendentals=0,
-        ),
-    )
-    smem = pl.BlockSpec(memory_space=SMEM)
-    own_part = pl.pallas_call(
-        functools.partial(own_projection_kernel, chips),
-        out_shape=jax.ShapeDtypeStruct((half, model), jnp.float32),
-        in_specs=[smem, rows_spec, weight_spec],
-        out_specs=wide_spec,
-        name="own_projection",
-        **projecting,
-    )(index, mine, out_weight)
-    partial_sums = pl.pallas_call(
-        functools.partial(projection_kernel, chips),
-        out_shape=[
-            jax.ShapeDtypeStruct((rows, model), jnp.bfloat16 if j % 2 else jnp.float32)
-            for j in range(chips)
-        ],
-        in_specs=[smem, rows_spec, weight_spec, wide_spec],
-        out_specs=[pl.BlockSpec((rows, tile), lambda i: (0, i))] * chips,
-        name="projection",
-        **projecting,
-    )(index, theirs, other_weight, own_part)
-
-    sums = {j: part for j, part in enumerate(partial_sums)}
-    bit = 1
-    while bit < chips:
-        leaving = sorted((j for j in sums if j & bit), reverse=True)
-        earlier = ()
-        for j in leaving:
-            leaves = after(sums.pop(j).astype(jnp.bfloat16), *earlier)
-            arrived = across(leaves, "seq", 2 * bit)
-            sums[j ^ bit] = sums[j ^ bit].astype(jnp.float32) + arrived.astype(jnp.float32)
-            earlier = (arrived,)
-        bit *= 2
-    projected = sums[0]
+    cuts = 2
+    columns = model // cuts
+    tile = columns // 2
+    sources = len(attended)
+    halves = []
+    for cut in range(cuts):
+        weight_spec = pl.BlockSpec((width, tile), lambda i, first=2 * cut: (0, first + i))
+        partial_sums = pl.pallas_call(
+            functools.partial(projection_kernel, chips, sources),
+            grid=(columns // tile,),
+            out_shape=[
+                jax.ShapeDtypeStruct((rows, columns), jnp.bfloat16 if j % 2 else jnp.float32)
+                for j in range(chips)
+            ],
+            in_specs=[pl.BlockSpec(memory_space=SMEM)]
+            + [pl.BlockSpec(block.shape, lambda i: (0, 0, 0)) for block in attended]
+            + [weight_spec, weight_spec],
+            out_specs=[pl.BlockSpec((rows, tile), lambda i: (0, i))] * chips,
+            scratch_shapes=[pltpu.VMEM((half, 2 * width), jnp.bfloat16)],
+            compiler_params=pltpu.CompilerParams(vmem_limit_bytes=48 * 2**20),
+            cost_estimate=pl.CostEstimate(
+                flops=4 * half * width * columns,
+                bytes_accessed=4 * width * columns + 8 * rows * columns,
+                transcendentals=0,
+            ),
+            name=f"projection_{cut}",
+        )(index, *attended, out_weight, other_weight)
+        sums = {j: part for j, part in enumerate(partial_sums)}
+        bit = 1
+        while bit < chips:
+            leaving = sorted((j for j in sums if j & bit), reverse=True)
+            earlier = ()
+            for j in leaving:
+                leaves = after(sums.pop(j).astype(jnp.bfloat16), *earlier)
+                arrived = across(leaves, "seq", 2 * bit)
+                sums[j ^ bit] = sums[j ^ bit].astype(jnp.float32) + arrived.astype(jnp.float32)
+                earlier = (arrived,)
+            bit *= 2
+        halves.append(sums[0])
+    projected = jnp.concatenate(halves, axis=1)
 
     level = lax.dynamic_index_in_dim(noise_level, slot, keepdims=False)
     gate_row = lax.dynamic_index_in_dim(gate_table, level, keepdims=True).astype(jnp.float32)

time: 79.8 us -> 72.9 us (0.914)
  waiting for transfers between devices: 44.7 us -> 36 us
  starting transfers between devices: 13.7 us -> 17.7 us
  local copies, waits for them, and re-layouts: 3.76 us -> 1.95 us
    ppermute x4 -> x7, waiting for transfers between devices: 21.6 us -> 14.8 us  [across(): return lax.ppermute(value, axis, [(i, i ^ distance) for i in range(n)])]
    ppermute x4 -> x7, starting transfers between devices: 3.11 us -> 6.45 us  [across(): return lax.ppermute(value, axis, [(i, i ^ distance) for i in range(n)])]
    all_to_all x1, waiting for transfers between devices: 21.8 us -> 18.7 us  [spread_attention(): lax.all_to_all(sends, ('frame', 'seq'), split_axis=0, concat_axis=0, tile...]
    unnamed x10 -> x7, local copies, waits for them, and re-layouts: 3.16 us -> 0.67 us
    ppermute x4 -> x5, waiting for transfers between devices: 1.34 us -> 2.59 us  [across(): return lax.ppermute(value, axis, [(i, i ^ distance) for i in range(size)])]
    broadcast_in_dim x1 -> x0, other arithmetic: 0.93 us -> none  [shards(): return mixed.astype(jnp.bfloat16)[None]]
    convert_element_type x0 -> x1, other arithmetic: none -> 0.83 us  [shards(): return mixed.astype(jnp.bfloat16)[None]]
    ppermute x4 -> x5, starting transfers between devices: 3.62 us -> 4.32 us  [across(): return lax.ppermute(value, axis, [(i, i ^ distance) for i in range(size)])]
  transfers between devices with their start and end apart: 9 -> 13, of which waited for: 6 -> 8; matrix products, arithmetic and copies ran while one was open for 2% -> 3% of each run, Pallas kernels for 11% -> 13%
where the time goes in v5:
time: 72.9 us; the launch traced here: 72.6 us
  waiting for transfers between devices  36 us (49%)
  starting transfers between devices  17.7 us (24%)
  Pallas kernels  12.8 us (18%)
  other arithmetic  2.1 us (3%)
  between operations  2.04 us (3%)
  local copies, waits for them, and re-layouts  1.95 us (3%)
    all_to_all x1, waiting for transfers between devices, spread_attention(): lax.all_to_all(sends, ('frame', 'seq'), split_axis=0, concat_axis=0, tile...  18.7 us
    ppermute x7, waiting for transfers between devices, across(): return lax.ppermute(value, axis, [(i, i ^ distance) for i in range(n)])  14.8 us
    all_to_all x1, starting transfers between devices, spread_attention(): lax.all_to_all(sends, ('frame', 'seq'), split_axis=0, concat_axis=0, tile...  6.96 us
    ppermute x7, starting transfers between devices, across(): return lax.ppermute(value, axis, [(i, i ^ distance) for i in range(n)])  6.45 us
    pallas_call x2, Pallas kernels, shards(): pl.pallas_call(functools.partial(projection_kernel, chips, sources), grid...  6.29 us
    ppermute x5, starting transfers between devices, across(): return lax.ppermute(value, axis, [(i, i ^ distance) for i in range(size)])  4.32 us
    pallas_call x2, Pallas kernels, attend(): pl.pallas_call(functools.partial(spread_attention_kernel, n, frames, pick...  4.18 us
    ppermute x5, waiting for transfers between devices, across(): return lax.ppermute(value, axis, [(i, i ^ distance) for i in range(size)])  2.59 us
  transfers between devices with their start and end apart: 13, of which 8 were waited for; matrix products, arithmetic and copies ran while one was open for 3% of the time, Pallas kernels for 13%

profile of v5, /device:TPU:0, one launch (start us, length us, event | category | flops | bytes accessed | tf_op | source)
XLA Modules:
  0.0 72.6 jit_solution(11987804860669723221)
XLA Ops:
  0.0 0.5 collective-permute-start.5
  0.5 2.3 %norm.1 = bf16[32,32,384]{2,1,0:T(8,128)(2,1)} custom-call(bf16[32,4096]{1,0:T(8,128)(2,1)} %bitcast.14, bf16[32,4096]{1,0:T(8,128)(2,1)} %bitcast.15, bf16[32,4096]{1,0:T(8,128)(2,1)} %bitcast.16, f32[1,4096]{1,0:T(1,128)} %bitcast.18, f32[1,4096]{1,0:T(1,128)} %bitcast.19), custom_call_target="tpu_custom_call" | custom-call | tf_op jit(solution)/shard_map/norm/pallas_call | solution.py:200
  2.8 7.0 %all-to-all-start = ((bf16[32,32,384]{2,1,0:T(8,128)(2,1)}), bf16[32,32,384]{2,1,0:T(8,128)(2,1)S(1)}, u32[]{:S(2)}, u32[]{:S(2)}) async-start(bf16[32,32,384]{2,1,0:T(8,128)(2,1)} %norm.1), calls=%async_computation | async-start | bytes 1572864 | tf_op jit(solution)/shard_map/all_to_all | solution.py:207
  9.7 1.3 %dynamic_slice.8 = s32[1]{0:T(128)} dynamic-slice(s32[4]{0:T(128)} %param.20, s32[]{:T(128)S(6)} %select_n.19), dynamic_slice_sizes={1} | dynamic-slice | bytes 12 | tf_op jit(solution)/shard_map/jit(dynamic_index_in_dim)/dynamic_slice | solution.py:409
  13.0 18.7 %all-to-all-done.rows_ref = bf16[32,32,384]{2,1,0:T(8,128)(2,1)S(1)} async-done(((bf16[32,32,384]{2,1,0:T(8,128)(2,1)}), bf16[32,32,384]{2,1,0:T(8,128)(2,1)S(1)}, u32[]{:S(2)}, u32[]{:S(2)}) %all-to-all-start) | async-done | bytes 786464 | tf_op jit(solution)/shard_map/all_to_all | solution.py:207
  31.7 0.7 copy-done
  32.3 2.8 %attention_far.1 = (bf16[3,128,128]{2,1,0:T(8,128)(2,1)S(1)}, bf16[3,128,128]{2,1,0:T(8,128)(2,1)S(1)}) custom-call(s32[2]{0:T(128)S(1)} %pad_add_fusion.1.index_ref, s32[4]{0:T(128)S(1)} %copy-done, bf16[32,32,384]{2,1,0:T(8,128)(2,1)S(1)} %all-to-all-done.rows_ref), custom_call_target="tpu_custom_call" | custom-call | flops 402653184 | bytes 1048576 | tf_op jit(solution)/shard_map/attention_far/pallas_call | solution.py:215
  35.2 1.4 %attention_near.1 = (bf16[1,128,128]{2,1,0:T(8,128)(2,1)S(1)}, bf16[1,128,128]{2,1,0:T(8,128)(2,1)S(1)}) custom-call(s32[2]{0:T(128)S(1)} %pad_add_fusion.1.index_ref, s32[4]{0:T(128)S(1)} %copy-done, bf16[32,32,384]{2,1,0:T(8,128)(2,1)S(1)} %all-to-all-done.rows_ref), custom_call_target="tpu_custom_call" | custom-call | flops 134217728 | bytes 1048576 | tf_op jit(solution)/shard_map/attention_near/pallas_call | solution.py:215
  36.6 0.6 collective-permute-start
  37.2 0.6 collective-permute-start.4
  37.9 1.3 %collective-permute-start.3 = (bf16[2,128,128]{2,1,0:T(8,128)(2,1)S(1)}, bf16[2,128,128]{2,1,0:T(8,128)(2,1)S(1)}, u32[]{:S(2)}, u32[]{:S(2)}) collective-permute-start(bf16[2,128,128]{2,1,0:T(8,128)(2,1)S(1)} %pad_maximum_fusion.1), channel_id=1, source_target_pairs={{0,16},{8,24},{16,0},{24,8},{1,17},{9,25},{17,1},{25,9},{2,18},{10... | collective-permute-start | bytes 196616 | tf_op jit(solution)/shard_map/ppermute | solution.py:232
  39.2 1.7 %collective-permute-start.2 = (bf16[2,128,128]{2,1,0:T(8,128)(2,1)S(1)}, bf16[2,128,128]{2,1,0:T(8,128)(2,1)S(1)}, u32[]{:S(2)}, u32[]{:S(2)}) collective-permute-start(bf16[2,128,128]{2,1,0:T(8,128)(2,1)S(1)} %pad_maximum_fusion), channel_id=1, source_target_pairs={{0,8},{8,0},{16,24},{24,16},{1,9},{9,1},{17,25},{25,17},{2,10},{10... | collective-permute-start | bytes 196616 | tf_op jit(solution)/shard_map/ppermute | solution.py:232
  41.0 2.2 %collective-permute-done.4.refs_3_ = bf16[2,128,128]{2,1,0:T(8,128)(2,1)S(1)} collective-permute-done((bf16[2,128,128]{2,1,0:T(8,128)(2,1)S(1)}, bf16[2,128,128]{2,1,0:T(8,128)(2,1)S(1)}, u32[]{:S(2)}, u32[]{:S(2)}) %collective-permute-start.4) | collective-permute-done | bytes 65568 | tf_op jit(solution)/shard_map/ppermute | solution.py:232
  43.5 3.1 %projection_0.1 = (f32[32,2560]{1,0:T(8,128)S(1)}, bf16[32,2560]{1,0:T(8,128)(2,1)S(1)}, f32[32,2560]{1,0:T(8,128)S(1)}, bf16[32,2560]{1,0:T(8,128)(2,1)S(1)}) custom-call(s32[2]{0:T(128)S(1)} %pad_add_fusion.index_ref, bf16[2,128,128]{2,1,0:T(8,128)(2,1)S(1)} %constant_dynamic-update-slice_fusion.refs_0_, ...), custom_call_target="tpu_custom_call" | custom-call | flops 671088640 | bytes 5898240 | tf_op jit(solution)/shard_map/projection_0/pallas_call | solution.py:375
  47.0 0.9 %dynamic-slice_convert_fusion = f32[1,5120]{1,0:T(1,128)S(1)} fusion(bf16[64,5120]{1,0:T(8,128)(2,1)} %param.19, s32[]{:T(128)S(6)} %select_n.20), kind=kLoop, calls=%fused_computation.11 | loop fusion | flops 5120 | bytes 30724 | tf_op jit(solution)/shard_map/mul | solution.py:412
  47.9 3.2 %projection_1.1 = (f32[32,2560]{1,0:T(8,128)S(1)}, bf16[32,2560]{1,0:T(8,128)(2,1)S(1)}, f32[32,2560]{1,0:T(8,128)S(1)}, bf16[32,2560]{1,0:T(8,128)(2,1)S(1)}) custom-call(s32[2]{0:T(128)S(1)} %pad_add_fusion.index_ref, bf16[2,128,128]{2,1,0:T(8,128)(2,1)S(1)} %constant_dynamic-update-slice_fusion.refs_0_, ...), custom_call_target="tpu_custom_call" | custom-call | flops 671088640 | bytes 5898240 | tf_op jit(solution)/shard_map/projection_1/pallas_call | solution.py:375
  51.1 1.9 %collective-permute-start.9 = (bf16[32,2560]{1,0:T(8,128)(2,1)S(1)}, bf16[32,2560]{1,0:T(8,128)(2,1)S(1)}, u32[]{:S(2)}, u32[]{:S(2)}) collective-permute-start(bf16[32,2560]{1,0:T(8,128)(2,1)S(1)} %get-tuple-element.30), channel_id=1, source_target_pairs={{0,2},{1,3},{2,0},{3,1},{4,6},{5,7},{6,4},{7,5},{8,10},{9,11},{10,... | collective-permute-start | bytes 491528 | tf_op jit(solution)/shard_map/ppermute | solution.py:356
  53.2 1.6 %collective-permute-start.8 = (bf16[32,2560]{1,0:T(8,128)(2,1)S(1)}, bf16[32,2560]{1,0:T(8,128)(2,1)S(1)}, u32[]{:S(2)}, u32[]{:S(2)}) collective-permute-start(bf16[32,2560]{1,0:T(8,128)(2,1)S(1)} %add_convert_fusion.1), channel_id=1, source_target_pairs={{0,4},{1,5},{2,6},{3,7},{4,0},{5,1},{6,2},{7,3},{8,12},{9,13},{10,... | collective-permute-start | bytes 491528 | tf_op jit(solution)/shard_map/ppermute | solution.py:356
  54.8 8.8 %collective-permute-done.9 = bf16[32,2560]{1,0:T(8,128)(2,1)S(1)} collective-permute-done((bf16[32,2560]{1,0:T(8,128)(2,1)S(1)}, bf16[32,2560]{1,0:T(8,128)(2,1)S(1)}, u32[]{:S(2)}, u32[]{:S(2)}) %collective-permute-start.9) | collective-permute-done | bytes 163872 | tf_op jit(solution)/shard_map/ppermute | solution.py:356
  63.6 2.1 %collective-permute-start.11 = (bf16[32,2560]{1,0:T(8,128)(2,1)S(1)}, bf16[32,2560]{1,0:T(8,128)(2,1)S(1)}, u32[]{:S(2)}, u32[]{:S(2)}) collective-permute-start(bf16[32,2560]{1,0:T(8,128)(2,1)S(1)} %add_convert_fusion), channel_id=1, source_target_pairs={{0,4},{1,5},{2,6},{3,7},{4,0},{5,1},{6,2},{7,3},{8,12},{9,13},{10,... | collective-permute-start | bytes 491528 | tf_op jit(solution)/shard_map/ppermute | solution.py:356
  65.7 1.2 %collective-permute-done.7 = bf16[32,2560]{1,0:T(8,128)(2,1)S(1)} collective-permute-done((bf16[32,2560]{1,0:T(8,128)(2,1)S(1)}, bf16[32,2560]{1,0:T(8,128)(2,1)S(1)}, u32[]{:S(2)}, u32[]{:S(2)}) %collective-permute-start.7) | collective-permute-done | bytes 163872 | tf_op jit(solution)/shard_map/ppermute | solution.py:356
  66.9 3.5 %collective-permute-done.10 = bf16[32,2560]{1,0:T(8,128)(2,1)S(1)} collective-permute-done((bf16[32,2560]{1,0:T(8,128)(2,1)S(1)}, bf16[32,2560]{1,0:T(8,128)(2,1)S(1)}, u32[]{:S(2)}, u32[]{:S(2)}) %collective-permute-start.10) | collective-permute-done | bytes 163872 | tf_op jit(solution)/shard_map/ppermute | solution.py:356
  70.4 1.3 %collective-permute-done.11 = bf16[32,2560]{1,0:T(8,128)(2,1)S(1)} collective-permute-done((bf16[32,2560]{1,0:T(8,128)(2,1)S(1)}, bf16[32,2560]{1,0:T(8,128)(2,1)S(1)}, u32[]{:S(2)}, u32[]{:S(2)}) %collective-permute-start.11) | collective-permute-done | bytes 163872 | tf_op jit(solution)/shard_map/ppermute | solution.py:356
  71.8 0.8 %fusion.2 = bf16[1,32,5120]{2,1,0:T(8,128)(2,1)} fusion(f32[1,32,2560]{2,1,0:T(8,128)S(1)} %add_bitcast_fusion, f32[1,32,2560]{2,1,0:T(8,128)S(1)} %add_bitcast_fusion.1, bf16[1,32,5120]{2,1,0:T(8,128)(2,1)S(1)} %copy-done.1, f32[5120]{0:T(1024)S(1)} %convert_element_type.45, f32[5120]{0:T(1024)S(1)} %bitcast.17), kind=kLoop, calls=%fused_computation.3 | loop fusion | flops 983040 | bytes 1351680 | tf_op jit(solution)/shard_map/convert_element_type | solution.py:413
  (30 shorter events, 1.4 us)
Async XLA Ops:
  0.0 43.5 %collective-permute-start.5 = (bf16[512,5120]{1,0:T(8,128)(2,1)}, bf16[512,5120]{1,0:T(8,128)(2,1)}, u32[]{:S(2)}, u32[]{:S(2)}) collective-permute-start(bf16[512,5120]{1,0:T(8,128)(2,1)} %refs_4_.3), channel_id=1, source_target_pairs={{0,1},{1,0},{2,3},{3,2},{4,5},{5,4},{6,7},{7,6},{8,9},{9,8},{10,11... | collective-permute-start | bytes 15728648 | tf_op jit(solution)/shard_map/ppermute | solution.py:356
  2.8 28.9 %all-to-all-start = ((bf16[32,32,384]{2,1,0:T(8,128)(2,1)}), bf16[32,32,384]{2,1,0:T(8,128)(2,1)S(1)}, u32[]{:S(2)}, u32[]{:S(2)}) async-start(bf16[32,32,384]{2,1,0:T(8,128)(2,1)} %norm.1), calls=%async_computation | async-start | bytes 1572864 | tf_op jit(solution)/shard_map/all_to_all | solution.py:207
  31.7 0.7 copy-start
  35.1 2.1 %collective-permute-start.1 = (bf16[3,128,128]{2,1,0:T(8,128)(2,1)S(1)}, bf16[3,128,128]{2,1,0:T(8,128)(2,1)S(1)}, u32[]{:S(2)}, u32[]{:S(2)}) collective-permute-start(bf16[3,128,128]{2,1,0:T(8,128)(2,1)S(1)} %get-tuple-element.22), channel_id=1, source_target_pairs={{0,1},{1,0},{2,3},{3,2},{4,5},{5,4},{6,7},{7,6},{8,9},{9,8},{10,11... | collective-permute-start | bytes 294920 | tf_op jit(solution)/shard_map/ppermute | solution.py:232
  36.6 4.3 %collective-permute-start = (bf16[1,128,128]{2,1,0:T(8,128)(2,1)S(1)}, bf16[1,128,128]{2,1,0:T(8,128)(2,1)S(1)}, u32[]{:S(2)}, u32[]{:S(2)}) collective-permute-start(bf16[1,128,128]{2,1,0:T(8,128)(2,1)S(1)} %get-tuple-element.20), channel_id=1, source_target_pairs={{0,1},{1,0},{2,3},{3,2},{4,5},{5,4},{6,7},{7,6},{8,9},{9,8},{10,11... | collective-permute-start | bytes 98312 | tf_op jit(solution)/shard_map/ppermute | solution.py:232
  37.2 5.9 %collective-permute-start.4 = (bf16[2,128,128]{2,1,0:T(8,128)(2,1)S(1)}, bf16[2,128,128]{2,1,0:T(8,128)(2,1)S(1)}, u32[]{:S(2)}, u32[]{:S(2)}) collective-permute-start(bf16[2,128,128]{2,1,0:T(8,128)(2,1)S(1)} %pad_maximum_fusion.2), channel_id=1, source_target_pairs={{0,24},{8,16},{16,8},{24,0},{1,25},{9,17},{17,9},{25,1},{2,26},{10... | collective-permute-start | bytes 196616 | tf_op jit(solution)/shard_map/ppermute | solution.py:232
  37.9 5.5 %collective-permute-start.3 = (bf16[2,128,128]{2,1,0:T(8,128)(2,1)S(1)}, bf16[2,128,128]{2,1,0:T(8,128)(2,1)S(1)}, u32[]{:S(2)}, u32[]{:S(2)}) collective-permute-start(bf16[2,128,128]{2,1,0:T(8,128)(2,1)S(1)} %pad_maximum_fusion.1), channel_id=1, source_target_pairs={{0,16},{8,24},{16,0},{24,8},{1,17},{9,25},{17,1},{25,9},{2,18},{10... | collective-permute-start | bytes 196616 | tf_op jit(solution)/shard_map/ppermute | solution.py:232
  39.2 4.3 %collective-permute-start.2 = (bf16[2,128,128]{2,1,0:T(8,128)(2,1)S(1)}, bf16[2,128,128]{2,1,0:T(8,128)(2,1)S(1)}, u32[]{:S(2)}, u32[]{:S(2)}) collective-permute-start(bf16[2,128,128]{2,1,0:T(8,128)(2,1)S(1)} %pad_maximum_fusion), channel_id=1, source_target_pairs={{0,8},{8,0},{16,24},{24,16},{1,9},{9,1},{17,25},{25,17},{2,10},{10... | collective-permute-start | bytes 196616 | tf_op jit(solution)/shard_map/ppermute | solution.py:232
  40.9 6.9 %copy-start.2 = (bf16[5120]{0:T(1024)(128)(2,1)S(1)}, bf16[5120]{0:T(1024)(128)(2,1)}, u32[]{:S(2)}) copy-start(bf16[5120]{0:T(1024)(128)(2,1)} %param.18) | copy-start | bytes 30724
  46.7 6.3 %collective-permute-start.6 = (bf16[32,2560]{1,0:T(8,128)(2,1)S(1)}, bf16[32,2560]{1,0:T(8,128)(2,1)S(1)}, u32[]{:S(2)}, u32[]{:S(2)}) collective-permute-start(bf16[32,2560]{1,0:T(8,128)(2,1)S(1)} %get-tuple-element.25), channel_id=1, source_target_pairs={{0,2},{1,3},{2,0},{3,1},{4,6},{5,7},{6,4},{7,5},{8,10},{9,11},{10,... | collective-permute-start | bytes 491528 | tf_op jit(solution)/shard_map/ppermute | solution.py:356
  47.9 23.9 %copy-start.1 = (bf16[1,32,5120]{2,1,0:T(8,128)(2,1)S(1)}, bf16[1,32,5120]{2,1,0:T(8,128)(2,1)}, u32[]{:S(2)}) copy-start(bf16[1,32,5120]{2,1,0:T(8,128)(2,1)} %param.11) | copy-start | bytes 983044
  51.1 12.5 %collective-permute-start.9 = (bf16[32,2560]{1,0:T(8,128)(2,1)S(1)}, bf16[32,2560]{1,0:T(8,128)(2,1)S(1)}, u32[]{:S(2)}, u32[]{:S(2)}) collective-permute-start(bf16[32,2560]{1,0:T(8,128)(2,1)S(1)} %get-tuple-element.30), channel_id=1, source_target_pairs={{0,2},{1,3},{2,0},{3,1},{4,6},{5,7},{6,4},{7,5},{8,10},{9,11},{10,... | collective-permute-start | bytes 491528 | tf_op jit(solution)/shard_map/ppermute | solution.py:356
  53.0 13.9 %collective-permute-start.7 = (bf16[32,2560]{1,0:T(8,128)(2,1)S(1)}, bf16[32,2560]{1,0:T(8,128)(2,1)S(1)}, u32[]{:S(2)}, u32[]{:S(2)}) collective-permute-start(bf16[32,2560]{1,0:T(8,128)(2,1)S(1)} %get-tuple-element.26), channel_id=1, source_target_pairs={{0,2},{1,3},{2,0},{3,1},{4,6},{5,7},{6,4},{7,5},{8,10},{9,11},{10,... | collective-permute-start | bytes 491528 | tf_op jit(solution)/shard_map/ppermute | solution.py:356
  53.2 13.6 %collective-permute-start.8 = (bf16[32,2560]{1,0:T(8,128)(2,1)S(1)}, bf16[32,2560]{1,0:T(8,128)(2,1)S(1)}, u32[]{:S(2)}, u32[]{:S(2)}) collective-permute-start(bf16[32,2560]{1,0:T(8,128)(2,1)S(1)} %add_convert_fusion.1), channel_id=1, source_target_pairs={{0,4},{1,5},{2,6},{3,7},{4,0},{5,1},{6,2},{7,3},{8,12},{9,13},{10,... | collective-permute-start | bytes 491528 | tf_op jit(solution)/shard_map/ppermute | solution.py:356
  63.6 6.8 %collective-permute-start.10 = (bf16[32,2560]{1,0:T(8,128)(2,1)S(1)}, bf16[32,2560]{1,0:T(8,128)(2,1)S(1)}, u32[]{:S(2)}, u32[]{:S(2)}) collective-permute-start(bf16[32,2560]{1,0:T(8,128)(2,1)S(1)} %get-tuple-element.31), channel_id=1, source_target_pairs={{0,2},{1,3},{2,0},{3,1},{4,6},{5,7},{6,4},{7,5},{8,10},{9,11},{10,... | collective-permute-start | bytes 491528 | tf_op jit(solution)/shard_map/ppermute | solution.py:356
  63.6 8.1 %collective-permute-start.11 = (bf16[32,2560]{1,0:T(8,128)(2,1)S(1)}, bf16[32,2560]{1,0:T(8,128)(2,1)S(1)}, u32[]{:S(2)}, u32[]{:S(2)}) collective-permute-start(bf16[32,2560]{1,0:T(8,128)(2,1)S(1)} %add_convert_fusion), channel_id=1, source_target_pairs={{0,4},{1,5},{2,6},{3,7},{4,0},{5,1},{6,2},{7,3},{8,12},{9,13},{10,... | collective-permute-start | bytes 491528 | tf_op jit(solution)/shard_map/ppermute | solution.py:356

commit v6 on v5

--- a/solution.py
+++ b/solution.py
@@ -142,7 +142,7 @@
             out_ref[f * n + s, :, 2 * part :] = value_ref[:, cols]
 
 
-def spread_attention_kernel(n, frames, picked, index_ref, order_ref, rows_ref, mine_ref, given_ref, both):
+def spread_attention_kernel(n, frames, near, index_ref, order_ref, rows_ref, mine_ref, given_ref, both):
     slot = index_ref[0]
     core = index_ref[1]
     rows = rows_ref.shape[1]
@@ -150,40 +150,47 @@
     frame_rows = n * rows
     factor = (HD ** (-0.5)) * LOG2E
     step = min(frame_rows, 128)
-    for h in range(part // HD):
-        cols = slice(h * HD, (h + 1) * HD)
-        keys = rows_ref[:, :, part + h * HD : part + (h + 1) * HD].reshape(-1, HD)
-        values = rows_ref[:, :, 2 * part + h * HD : 2 * part + (h + 1) * HD].reshape(-1, HD)
-        for place, distance in enumerate(picked):
-            frame = slot ^ distance
-            rank = order_ref[frame]
-            hidden = jnp.concatenate(
-                [
-                    jnp.full((1, frame_rows), jnp.where(order_ref[f] <= rank, 0.0, -1e30), jnp.float32)
-                    for f in range(frames)
-                ],
-                axis=1,
-            )
-            for start in range(0, frame_rows, step):
-                query = rows_ref[pl.ds(frame * n + start // rows, step // rows), :, cols]
-                scores = lax.dot_general(
-                    query.reshape(step, HD),
-                    keys,
-                    (((1,), (1,)), ((), ())),
-                    preferred_element_type=jnp.float32,
-                )
-                scores = scores + hidden
-                top = jnp.max(scores, axis=1, keepdims=True)
-                exponent = jnp.exp2((scores - top) * factor)
-                total = jnp.sum(exponent, axis=1, keepdims=True)
-                summed = jnp.dot(
-                    exponent.astype(jnp.bfloat16), values, preferred_element_type=jnp.float32
-                )
-                done = (summed / total).astype(jnp.bfloat16)
-                for i in range(step // rows):
-                    s = start // rows + i
-                    z = s // 2
-                    both[s % 2, place, z * rows : (z + 1) * rows, cols] = done[i * rows : (i + 1) * rows]
+    stamps = [order_ref[f] for f in range(frames)]
+    ranks = [
+        sum((stamps[e] < stamps[f]).astype(jnp.int32) for e in range(frames)) for f in range(frames)
+    ]
+    at_rank = [sum(jnp.where(ranks[f] == r, f, 0) for f in range(frames)) for r in range(frames)]
+
+    def tokens(frame, first):
+        return rows_ref[pl.ds(frame * n, n), :, first : first + HD].reshape(frame_rows, HD)
+
+    for rank, frame in enumerate(at_rank):
+
+        @pl.when(frame == slot if near else frame != slot)
+        def _(rank=rank, frame=frame):
+            place = 0 if near else frames - 1 - (slot ^ frame)
+            for h in range(part // HD):
+                cols = slice(h * HD, (h + 1) * HD)
+                seen = at_rank[: rank + 1]
+                keys = jnp.concatenate([tokens(f, part + h * HD) for f in seen], axis=0)
+                values = jnp.concatenate([tokens(f, 2 * part + h * HD) for f in seen], axis=0)
+                for start in range(0, frame_rows, step):
+                    query = rows_ref[pl.ds(frame * n + start // rows, step // rows), :, cols]
+                    scores = lax.dot_general(
+                        query.reshape(step, HD),
+                        keys,
+                        (((1,), (1,)), ((), ())),
+                        preferred_element_type=jnp.float32,
+                    )
+                    top = jnp.max(scores, axis=1, keepdims=True)
+                    exponent = jnp.exp2((scores - top) * factor)
+                    total = jnp.sum(exponent, axis=1, keepdims=True)
+                    summed = jnp.dot(
+                        exponent.astype(jnp.bfloat16), values, preferred_element_type=jnp.float32
+                    )
+                    done = (summed / total).astype(jnp.bfloat16)
+                    for i in range(step // rows):
+                        s = start // rows + i
+                        z = s // 2
+                        both[s % 2, place, z * rows : (z + 1) * rows, cols] = done[
+                            i * rows : (i + 1) * rows
+                        ]
+
     mine_ref[...] = both[core]
     given_ref[...] = both[core ^ 1]
 
@@ -213,7 +220,7 @@
     def attend(picked, name):
         count = len(picked)
         return pl.pallas_call(
-            functools.partial(spread_attention_kernel, n, frames, picked),
+            functools.partial(spread_attention_kernel, n, frames, picked == [0]),
             out_shape=[jax.ShapeDtypeStruct((count, frame_rows // 2, part), jnp.bfloat16)] * 2,
             in_specs=[smem, smem, vmem],
             out_specs=[vmem] * 2,
@@ -239,7 +246,7 @@
     found = {0: jnp.concatenate([near_mine, near_got], axis=0)}
     for place, d in enumerate(far):
         found[d] = across(jnp.stack([far_mine[place], far_got[place]]), "frame", d)
-    return [found[d] for d in range(frames)]
+    return [found[d] for d in range(frames)], held
 
 
 def gathered_attention(query_rows, key_rows, value_rows, gain_query, gain_key, slot_order):
@@ -326,7 +333,7 @@
         ),
         name="attention",
     )(slot_array, slot_order, *queries, *pieces)
-    return [jnp.stack([even, across(odd, "seq", 1)])]
+    return [jnp.stack([even, across(odd, "seq", 1)])], halves[1]
 
 
 def shards(
@@ -358,20 +365,20 @@
     def after(value, *earlier):
         return lax.optimization_barrier((value, *earlier))[0]
 
-    other_weight = across(out_weight, "seq", 1)
     spread = (width // HD) % frames == 0
-    attended = (spread_attention if spread else gathered_attention)(
+    attended, travelled = (spread_attention if spread else gathered_attention)(
         query_rows[0], key_rows[0], value_rows[0], gain_query, gain_key, slot_order
     )
+    other_weight = across(after(out_weight, travelled), "seq", 1)
     index = jnp.stack([me // 2, slot]) if spread else jnp.zeros((2,), jnp.int32)
 
     cuts = 2
     columns = model // cuts
-    tile = columns // 2
+    tile = columns // 5
     sources = len(attended)
     halves = []
     for cut in range(cuts):
-        weight_spec = pl.BlockSpec((width, tile), lambda i, first=2 * cut: (0, first + i))
+        weight_spec = pl.BlockSpec((width, tile), lambda i, first=5 * cut: (0, first + i))
         partial_sums = pl.pallas_call(
             functools.partial(projection_kernel, chips, sources),
             grid=(columns // tile,),

time: 72.9 us -> 79.8 us (1.095)
  blocking collectives: 0 us -> 29.3 us
  waiting for transfers between devices: 36 us -> 17.9 us
  starting transfers between devices: 17.7 us -> 10.1 us
  Pallas kernels: 12.8 us -> 16.1 us
    all_to_all x0 -> x1, blocking collectives: none -> 29.3 us  [spread_attention(): lax.all_to_all(sends, ('frame', 'seq'), split_axis=0, concat_axis=0, tile...]
    all_to_all x1 -> x0, waiting for transfers between devices: 18.7 us -> none  [spread_attention(): lax.all_to_all(sends, ('frame', 'seq'), split_axis=0, concat_axis=0, tile...]
    all_to_all x1 -> x0, starting transfers between devices: 6.96 us -> none  [spread_attention(): lax.all_to_all(sends, ('frame', 'seq'), split_axis=0, concat_axis=0, tile...]
    pallas_call x2, Pallas kernels: 6.29 us -> 9.68 us  [shards(): pl.pallas_call(functools.partial(projection_kernel, chips, sources), grid...]
  transfers between devices with their start and end apart: 13 -> 12, of which waited for: 8 -> 7; matrix products, arithmetic and copies ran while one was open for 3% -> 3% of each run, Pallas kernels for 13% -> 11%
where the time goes in v6:
time: 79.8 us; the launch traced here: 79.4 us
  blocking collectives  29.3 us (37%)
  waiting for transfers between devices  17.9 us (22%)
  Pallas kernels  16.1 us (20%)
  starting transfers between devices  10.1 us (13%)
  other arithmetic  2.09 us (3%)
  between operations  2.02 us (3%)
  local copies, waits for them, and re-layouts  1.94 us (2%)
    all_to_all x1, blocking collectives, spread_attention(): lax.all_to_all(sends, ('frame', 'seq'), split_axis=0, concat_axis=0, tile...  29.3 us
    ppermute x7, waiting for transfers between devices, across(): return lax.ppermute(value, axis, [(i, i ^ distance) for i in range(n)])  14.8 us
    pallas_call x2, Pallas kernels, shards(): pl.pallas_call(functools.partial(projection_kernel, chips, sources), grid...  9.68 us
    ppermute x7, starting transfers between devices, across(): return lax.ppermute(value, axis, [(i, i ^ distance) for i in range(n)])  5.72 us
    ppermute x5, starting transfers between devices, across(): return lax.ppermute(value, axis, [(i, i ^ distance) for i in range(size)])  4.33 us
    pallas_call x2, Pallas kernels, attend(): pl.pallas_call(functools.partial(spread_attention_kernel, n, frames, pick...  4.13 us
    ppermute x5, waiting for transfers between devices, across(): return lax.ppermute(value, axis, [(i, i ^ distance) for i in range(size)])  3.06 us
    pallas_call x1, Pallas kernels, spread_attention(): pl.pallas_call(functools.partial(spread_norm_kernel, n, frames), out_shap...  2.29 us
  transfers between devices with their start and end apart: 12, of which 7 were waited for; matrix products, arithmetic and copies ran while one was open for 3% of the time, Pallas kernels for 11%

profile of v6, /device:TPU:0, one launch (start us, length us, event | category | flops | bytes accessed | tf_op | source)
XLA Modules:
  0.0 79.4 jit_solution(5104779180642393104)
XLA Ops:
  0.0 2.3 %norm.1 = bf16[32,32,384]{2,1,0:T(8,128)(2,1)} custom-call(bf16[32,4096]{1,0:T(8,128)(2,1)} %bitcast.14, bf16[32,4096]{1,0:T(8,128)(2,1)} %bitcast.15, bf16[32,4096]{1,0:T(8,128)(2,1)} %bitcast.16, f32[1,4096]{1,0:T(1,128)} %bitcast.18, f32[1,4096]{1,0:T(1,128)} %bitcast.19), custom_call_target="tpu_custom_call" | custom-call | tf_op jit(solution)/shard_map/norm/pallas_call | solution.py:207
  2.3 29.3 %all_to_all.5.rows_ref = bf16[32,32,384]{2,1,0:T(8,128)(2,1)S(1)} all-to-all(bf16[32,32,384]{2,1,0:T(8,128)(2,1)} %norm.1), channel_id=1, replica_groups=mesh['frame'=4,'seq'=8] {'frame','seq'}, dimensions={0} | all-to-all | bytes 1572864 | tf_op jit(solution)/shard_map/all_to_all | solution.py:214
  31.6 1.2 %dynamic_slice.8 = s32[1]{0:T(128)} dynamic-slice(s32[4]{0:T(128)} %param.20, s32[]{:T(128)S(6)} %select_n.19), dynamic_slice_sizes={1} | dynamic-slice | bytes 12 | tf_op jit(solution)/shard_map/jit(dynamic_index_in_dim)/dynamic_slice | solution.py:416
  34.8 0.7 copy-done
  35.5 2.9 %attention_far.1 = (bf16[3,128,128]{2,1,0:T(8,128)(2,1)S(1)}, bf16[3,128,128]{2,1,0:T(8,128)(2,1)S(1)}) custom-call(s32[2]{0:T(128)S(1)} %pad_add_fusion.1.index_ref, s32[4]{0:T(128)S(1)} %copy-done, bf16[32,32,384]{2,1,0:T(8,128)(2,1)S(1)} %all_to_all.5.rows_ref), custom_call_target="tpu_custom_call" | custom-call | flops 402653184 | bytes 1048576 | tf_op jit(solution)/shard_map/attention_far/pallas_call | solution.py:222
  38.4 0.6 collective-permute-start.1
  39.0 1.3 %attention_near.1 = (bf16[1,128,128]{2,1,0:T(8,128)(2,1)S(1)}, bf16[1,128,128]{2,1,0:T(8,128)(2,1)S(1)}) custom-call(s32[2]{0:T(128)S(1)} %pad_add_fusion.1.index_ref, s32[4]{0:T(128)S(1)} %copy-done, bf16[32,32,384]{2,1,0:T(8,128)(2,1)S(1)} %all_to_all.5.rows_ref), custom_call_target="tpu_custom_call" | custom-call | flops 134217728 | bytes 1048576 | tf_op jit(solution)/shard_map/attention_near/pallas_call | solution.py:222
  40.4 0.9 %collective-permute-start.4 = (bf16[2,128,128]{2,1,0:T(8,128)(2,1)S(1)}, bf16[2,128,128]{2,1,0:T(8,128)(2,1)S(1)}, u32[]{:S(2)}, u32[]{:S(2)}) collective-permute-start(bf16[2,128,128]{2,1,0:T(8,128)(2,1)S(1)} %pad_maximum_fusion.2), channel_id=1, source_target_pairs={{0,24},{8,16},{16,8},{24,0},{1,25},{9,17},{17,9},{25,1},{2,26},{10... | collective-permute-start | bytes 196616 | tf_op jit(solution)/shard_map/ppermute | solution.py:239
  41.3 1.5 %collective-permute-start.3 = (bf16[2,128,128]{2,1,0:T(8,128)(2,1)S(1)}, bf16[2,128,128]{2,1,0:T(8,128)(2,1)S(1)}, u32[]{:S(2)}, u32[]{:S(2)}) collective-permute-start(bf16[2,128,128]{2,1,0:T(8,128)(2,1)S(1)} %pad_maximum_fusion.1), channel_id=1, source_target_pairs={{0,16},{8,24},{16,0},{24,8},{1,17},{9,25},{17,1},{25,9},{2,18},{10... | collective-permute-start | bytes 196616 | tf_op jit(solution)/shard_map/ppermute | solution.py:239
  42.8 1.3 %collective-permute-start.2 = (bf16[2,128,128]{2,1,0:T(8,128)(2,1)S(1)}, bf16[2,128,128]{2,1,0:T(8,128)(2,1)S(1)}, u32[]{:S(2)}, u32[]{:S(2)}) collective-permute-start(bf16[2,128,128]{2,1,0:T(8,128)(2,1)S(1)} %pad_maximum_fusion), channel_id=1, source_target_pairs={{0,8},{8,0},{16,24},{24,16},{1,9},{9,1},{17,25},{25,17},{2,10},{10... | collective-permute-start | bytes 196616 | tf_op jit(solution)/shard_map/ppermute | solution.py:239
  44.1 2.2 %collective-permute-done.4.refs_3_ = bf16[2,128,128]{2,1,0:T(8,128)(2,1)S(1)} collective-permute-done((bf16[2,128,128]{2,1,0:T(8,128)(2,1)S(1)}, bf16[2,128,128]{2,1,0:T(8,128)(2,1)S(1)}, u32[]{:S(2)}, u32[]{:S(2)}) %collective-permute-start.4) | collective-permute-done | bytes 65568 | tf_op jit(solution)/shard_map/ppermute | solution.py:239
  46.3 0.4 collective-permute-done.3.refs_2_
  46.7 0.5 collective-permute-done.2.refs_1_
  47.1 4.8 %projection_0.1 = (f32[32,2560]{1,0:T(8,128)S(1)}, bf16[32,2560]{1,0:T(8,128)(2,1)S(1)}, f32[32,2560]{1,0:T(8,128)S(1)}, bf16[32,2560]{1,0:T(8,128)(2,1)S(1)}) custom-call(s32[2]{0:T(128)S(1)} %pad_add_fusion.index_ref, bf16[2,128,128]{2,1,0:T(8,128)(2,1)S(1)} %constant_dynamic-update-slice_fusion.refs_0_, ...), custom_call_target="tpu_custom_call" | custom-call | flops 671088640 | bytes 5898240 | tf_op jit(solution)/shard_map/projection_0/pallas_call | solution.py:382
  52.0 0.9 %dynamic-slice_convert_fusion = f32[1,5120]{1,0:T(1,128)S(1)} fusion(bf16[64,5120]{1,0:T(8,128)(2,1)} %param.19, s32[]{:T(128)S(6)} %select_n.20), kind=kLoop, calls=%fused_computation.11 | loop fusion | flops 5120 | bytes 30724 | tf_op jit(solution)/shard_map/mul | solution.py:419
  53.0 4.9 %projection_1.1 = (f32[32,2560]{1,0:T(8,128)S(1)}, bf16[32,2560]{1,0:T(8,128)(2,1)S(1)}, f32[32,2560]{1,0:T(8,128)S(1)}, bf16[32,2560]{1,0:T(8,128)(2,1)S(1)}) custom-call(s32[2]{0:T(128)S(1)} %pad_add_fusion.index_ref, bf16[2,128,128]{2,1,0:T(8,128)(2,1)S(1)} %constant_dynamic-update-slice_fusion.refs_0_, ...), custom_call_target="tpu_custom_call" | custom-call | flops 671088640 | bytes 5898240 | tf_op jit(solution)/shard_map/projection_1/pallas_call | solution.py:382
  57.9 2.1 %collective-permute-start.9 = (bf16[32,2560]{1,0:T(8,128)(2,1)S(1)}, bf16[32,2560]{1,0:T(8,128)(2,1)S(1)}, u32[]{:S(2)}, u32[]{:S(2)}) collective-permute-start(bf16[32,2560]{1,0:T(8,128)(2,1)S(1)} %get-tuple-element.32), channel_id=1, source_target_pairs={{0,2},{1,3},{2,0},{3,1},{4,6},{5,7},{6,4},{7,5},{8,10},{9,11},{10,... | collective-permute-start | bytes 491528 | tf_op jit(solution)/shard_map/ppermute | solution.py:363
  60.1 1.5 %collective-permute-start.8 = (bf16[32,2560]{1,0:T(8,128)(2,1)S(1)}, bf16[32,2560]{1,0:T(8,128)(2,1)S(1)}, u32[]{:S(2)}, u32[]{:S(2)}) collective-permute-start(bf16[32,2560]{1,0:T(8,128)(2,1)S(1)} %add_convert_fusion.1), channel_id=1, source_target_pairs={{0,4},{1,5},{2,6},{3,7},{4,0},{5,1},{6,2},{7,3},{8,12},{9,13},{10,... | collective-permute-start | bytes 491528 | tf_op jit(solution)/shard_map/ppermute | solution.py:363
  61.5 8.8 %collective-permute-done.9 = bf16[32,2560]{1,0:T(8,128)(2,1)S(1)} collective-permute-done((bf16[32,2560]{1,0:T(8,128)(2,1)S(1)}, bf16[32,2560]{1,0:T(8,128)(2,1)S(1)}, u32[]{:S(2)}, u32[]{:S(2)}) %collective-permute-start.9) | collective-permute-done | bytes 163872 | tf_op jit(solution)/shard_map/ppermute | solution.py:363
  70.4 2.0 %collective-permute-start.11 = (bf16[32,2560]{1,0:T(8,128)(2,1)S(1)}, bf16[32,2560]{1,0:T(8,128)(2,1)S(1)}, u32[]{:S(2)}, u32[]{:S(2)}) collective-permute-start(bf16[32,2560]{1,0:T(8,128)(2,1)S(1)} %add_convert_fusion), channel_id=1, source_target_pairs={{0,4},{1,5},{2,6},{3,7},{4,0},{5,1},{6,2},{7,3},{8,12},{9,13},{10,... | collective-permute-start | bytes 491528 | tf_op jit(solution)/shard_map/ppermute | solution.py:363
  72.4 1.1 %collective-permute-done.7 = bf16[32,2560]{1,0:T(8,128)(2,1)S(1)} collective-permute-done((bf16[32,2560]{1,0:T(8,128)(2,1)S(1)}, bf16[32,2560]{1,0:T(8,128)(2,1)S(1)}, u32[]{:S(2)}, u32[]{:S(2)}) %collective-permute-start.7) | collective-permute-done | bytes 163872 | tf_op jit(solution)/shard_map/ppermute | solution.py:363
  73.6 3.6 %collective-permute-done.10 = bf16[32,2560]{1,0:T(8,128)(2,1)S(1)} collective-permute-done((bf16[32,2560]{1,0:T(8,128)(2,1)S(1)}, bf16[32,2560]{1,0:T(8,128)(2,1)S(1)}, u32[]{:S(2)}, u32[]{:S(2)}) %collective-permute-start.10) | collective-permute-done | bytes 163872 | tf_op jit(solution)/shard_map/ppermute | solution.py:363
  77.2 1.3 %collective-permute-done.11 = bf16[32,2560]{1,0:T(8,128)(2,1)S(1)} collective-permute-done((bf16[32,2560]{1,0:T(8,128)(2,1)S(1)}, bf16[32,2560]{1,0:T(8,128)(2,1)S(1)}, u32[]{:S(2)}, u32[]{:S(2)}) %collective-permute-start.11) | collective-permute-done | bytes 163872 | tf_op jit(solution)/shard_map/ppermute | solution.py:363
  78.5 0.8 %fusion.2 = bf16[1,32,5120]{2,1,0:T(8,128)(2,1)} fusion(f32[1,32,2560]{2,1,0:T(8,128)S(1)} %add_bitcast_fusion, f32[1,32,2560]{2,1,0:T(8,128)S(1)} %add_bitcast_fusion.1, bf16[1,32,5120]{2,1,0:T(8,128)(2,1)S(1)} %copy-done.1, f32[5120]{0:T(1024)S(1)} %convert_element_type.45, f32[5120]{0:T(1024)S(1)} %bitcast.17), kind=kLoop, calls=%fused_computation.3 | loop fusion | flops 983040 | bytes 1351680 | tf_op jit(solution)/shard_map/convert_element_type | solution.py:420
  (29 shorter events, 0.7 us)
Async XLA Ops:
  31.6 15.6 %collective-permute-start.5 = (bf16[512,5120]{1,0:T(8,128)(2,1)}, bf16[512,5120]{1,0:T(8,128)(2,1)}, u32[]{:S(2)}, u32[]{:S(2)}) collective-permute-start(bf16[512,5120]{1,0:T(8,128)(2,1)} %refs_4_.3), channel_id=1, source_target_pairs={{0,1},{1,0},{2,3},{3,2},{4,5},{5,4},{6,7},{7,6},{8,9},{9,8},{10,11... | collective-permute-start | bytes 15728648 | tf_op jit(solution)/shard_map/ppermute | solution.py:363
  34.8 0.7 copy-start
  38.4 2.0 %collective-permute-start.1 = (bf16[3,128,128]{2,1,0:T(8,128)(2,1)S(1)}, bf16[3,128,128]{2,1,0:T(8,128)(2,1)S(1)}, u32[]{:S(2)}, u32[]{:S(2)}) collective-permute-start(bf16[3,128,128]{2,1,0:T(8,128)(2,1)S(1)} %get-tuple-element.23), channel_id=1, source_target_pairs={{0,1},{1,0},{2,3},{3,2},{4,5},{5,4},{6,7},{7,6},{8,9},{9,8},{10,11... | collective-permute-start | bytes 294920 | tf_op jit(solution)/shard_map/ppermute | solution.py:239
  40.2 3.9 %collective-permute-start = (bf16[1,128,128]{2,1,0:T(8,128)(2,1)S(1)}, bf16[1,128,128]{2,1,0:T(8,128)(2,1)S(1)}, u32[]{:S(2)}, u32[]{:S(2)}) collective-permute-start(bf16[1,128,128]{2,1,0:T(8,128)(2,1)S(1)} %get-tuple-element.21), channel_id=1, source_target_pairs={{0,1},{1,0},{2,3},{3,2},{4,5},{5,4},{6,7},{7,6},{8,9},{9,8},{10,11... | collective-permute-start | bytes 98312 | tf_op jit(solution)/shard_map/ppermute | solution.py:239
  40.4 5.9 %collective-permute-start.4 = (bf16[2,128,128]{2,1,0:T(8,128)(2,1)S(1)}, bf16[2,128,128]{2,1,0:T(8,128)(2,1)S(1)}, u32[]{:S(2)}, u32[]{:S(2)}) collective-permute-start(bf16[2,128,128]{2,1,0:T(8,128)(2,1)S(1)} %pad_maximum_fusion.2), channel_id=1, source_target_pairs={{0,24},{8,16},{16,8},{24,0},{1,25},{9,17},{17,9},{25,1},{2,26},{10... | collective-permute-start | bytes 196616 | tf_op jit(solution)/shard_map/ppermute | solution.py:239
  41.3 5.4 %collective-permute-start.3 = (bf16[2,128,128]{2,1,0:T(8,128)(2,1)S(1)}, bf16[2,128,128]{2,1,0:T(8,128)(2,1)S(1)}, u32[]{:S(2)}, u32[]{:S(2)}) collective-permute-start(bf16[2,128,128]{2,1,0:T(8,128)(2,1)S(1)} %pad_maximum_fusion.1), channel_id=1, source_target_pairs={{0,16},{8,24},{16,0},{24,8},{1,17},{9,25},{17,1},{25,9},{2,18},{10... | collective-permute-start | bytes 196616 | tf_op jit(solution)/shard_map/ppermute | solution.py:239
  42.8 4.3 %collective-permute-start.2 = (bf16[2,128,128]{2,1,0:T(8,128)(2,1)S(1)}, bf16[2,128,128]{2,1,0:T(8,128)(2,1)S(1)}, u32[]{:S(2)}, u32[]{:S(2)}) collective-permute-start(bf16[2,128,128]{2,1,0:T(8,128)(2,1)S(1)} %pad_maximum_fusion), channel_id=1, source_target_pairs={{0,8},{8,0},{16,24},{24,16},{1,9},{9,1},{17,25},{25,17},{2,10},{10... | collective-permute-start | bytes 196616 | tf_op jit(solution)/shard_map/ppermute | solution.py:239
  44.1 8.8 %copy-start.2 = (bf16[5120]{0:T(1024)(128)(2,1)S(1)}, bf16[5120]{0:T(1024)(128)(2,1)}, u32[]{:S(2)}) copy-start(bf16[5120]{0:T(1024)(128)(2,1)} %param.18) | copy-start | bytes 30724
  52.0 8.0 %collective-permute-start.6 = (bf16[32,2560]{1,0:T(8,128)(2,1)S(1)}, bf16[32,2560]{1,0:T(8,128)(2,1)S(1)}, u32[]{:S(2)}, u32[]{:S(2)}) collective-permute-start(bf16[32,2560]{1,0:T(8,128)(2,1)S(1)} %get-tuple-element.27), channel_id=1, source_target_pairs={{0,2},{1,3},{2,0},{3,1},{4,6},{5,7},{6,4},{7,5},{8,10},{9,11},{10,... | collective-permute-start | bytes 491528 | tf_op jit(solution)/shard_map/ppermute | solution.py:363
  53.0 25.5 %copy-start.1 = (bf16[1,32,5120]{2,1,0:T(8,128)(2,1)S(1)}, bf16[1,32,5120]{2,1,0:T(8,128)(2,1)}, u32[]{:S(2)}) copy-start(bf16[1,32,5120]{2,1,0:T(8,128)(2,1)} %param.11) | copy-start | bytes 983044
  57.9 12.5 %collective-permute-start.9 = (bf16[32,2560]{1,0:T(8,128)(2,1)S(1)}, bf16[32,2560]{1,0:T(8,128)(2,1)S(1)}, u32[]{:S(2)}, u32[]{:S(2)}) collective-permute-start(bf16[32,2560]{1,0:T(8,128)(2,1)S(1)} %get-tuple-element.32), channel_id=1, source_target_pairs={{0,2},{1,3},{2,0},{3,1},{4,6},{5,7},{6,4},{7,5},{8,10},{9,11},{10,... | collective-permute-start | bytes 491528 | tf_op jit(solution)/shard_map/ppermute | solution.py:363
  59.9 13.6 %collective-permute-start.7 = (bf16[32,2560]{1,0:T(8,128)(2,1)S(1)}, bf16[32,2560]{1,0:T(8,128)(2,1)S(1)}, u32[]{:S(2)}, u32[]{:S(2)}) collective-permute-start(bf16[32,2560]{1,0:T(8,128)(2,1)S(1)} %get-tuple-element.28), channel_id=1, source_target_pairs={{0,2},{1,3},{2,0},{3,1},{4,6},{5,7},{6,4},{7,5},{8,10},{9,11},{10,... | collective-permute-start | bytes 491528 | tf_op jit(solution)/shard_map/ppermute | solution.py:363
  60.1 13.4 %collective-permute-start.8 = (bf16[32,2560]{1,0:T(8,128)(2,1)S(1)}, bf16[32,2560]{1,0:T(8,128)(2,1)S(1)}, u32[]{:S(2)}, u32[]{:S(2)}) collective-permute-start(bf16[32,2560]{1,0:T(8,128)(2,1)S(1)} %add_convert_fusion.1), channel_id=1, source_target_pairs={{0,4},{1,5},{2,6},{3,7},{4,0},{5,1},{6,2},{7,3},{8,12},{9,13},{10,... | collective-permute-start | bytes 491528 | tf_op jit(solution)/shard_map/ppermute | solution.py:363
  70.3 6.8 %collective-permute-start.10 = (bf16[32,2560]{1,0:T(8,128)(2,1)S(1)}, bf16[32,2560]{1,0:T(8,128)(2,1)S(1)}, u32[]{:S(2)}, u32[]{:S(2)}) collective-permute-start(bf16[32,2560]{1,0:T(8,128)(2,1)S(1)} %get-tuple-element.33), channel_id=1, source_target_pairs={{0,2},{1,3},{2,0},{3,1},{4,6},{5,7},{6,4},{7,5},{8,10},{9,11},{10,... | collective-permute-start | bytes 491528 | tf_op jit(solution)/shard_map/ppermute | solution.py:363
  70.4 8.1 %collective-permute-start.11 = (bf16[32,2560]{1,0:T(8,128)(2,1)S(1)}, bf16[32,2560]{1,0:T(8,128)(2,1)S(1)}, u32[]{:S(2)}, u32[]{:S(2)}) collective-permute-start(bf16[32,2560]{1,0:T(8,128)(2,1)S(1)} %add_convert_fusion), channel_id=1, source_target_pairs={{0,4},{1,5},{2,6},{3,7},{4,0},{5,1},{6,2},{7,3},{8,12},{9,13},{10,... | collective-permute-start | bytes 491528 | tf_op jit(solution)/shard_map/ppermute | solution.py:363

commit v7 on v5

--- a/solution.py
+++ b/solution.py
@@ -101,34 +101,57 @@
                 out_ref[here, cols] = (summed / total).astype(jnp.bfloat16)
 
 
-def projection_kernel(chips, sources, index_ref, *refs):
-    own_ref, other_ref = refs[sources : sources + 2]
-    outs = refs[sources + 2 : -1]
-    gathered_ref = refs[-1]
+def projection_kernel(chips, sources, first, index_ref, *refs):
+    weights = refs[sources : sources + 2]
+    outs = refs[sources + 2 : -4]
+    gathered_ref, result_ref, held_ref, sems = refs[-4:]
     shift = index_ref[0]
     slot = index_ref[1]
     _, half, part = refs[0].shape
     rows = half // chips
-    width = own_ref.shape[0]
-
-    @pl.when(pl.program_id(0) == 0)
-    def _():
-        for d in range(sources):
-            for parity in range(2):
-                first = pl.multiple_of(parity * width + (slot ^ d) * part, part)
-                for j in range(chips):
-                    here = pl.ds(pl.multiple_of((shift ^ j) * rows, rows), rows)
-                    gathered_ref[j * rows : (j + 1) * rows, pl.ds(first, part)] = refs[d][parity, here, :]
-
-    result = jnp.dot(gathered_ref[:, :width], own_ref[...], preferred_element_type=jnp.float32)
-    result += jnp.dot(gathered_ref[:, width:], other_ref[...], preferred_element_type=jnp.float32)
-    for j in range(chips):
-        outs[j][...] = result[j * rows : (j + 1) * rows].astype(outs[j].dtype)
-
-
-def spread_norm_kernel(n, frames, query_ref, key_ref, value_ref, gain_query_ref, gain_key_ref, out_ref):
+    width = weights[0].shape[0]
+    columns = outs[0].shape[1]
+    copies = [
+        pltpu.make_async_copy(weights[i].at[:, pl.ds(first, columns)], held_ref.at[i], sems.at[i])
+        for i in range(2)
+    ]
+    for copy in copies:
+        copy.start()
+    for d in range(sources):
+        for parity in range(2):
+            place = pl.multiple_of(parity * width + (slot ^ d) * part, part)
+            for j in range(chips):
+                here = pl.ds(pl.multiple_of((shift ^ j) * rows, rows), rows)
+                gathered_ref[j * rows : (j + 1) * rows, pl.ds(place, part)] = refs[d][parity, here, :]
+    tile = columns // 2
+    copies[0].wait()
+    for start in range(0, columns, tile):
+        cols = slice(start, start + tile)
+        result_ref[:, cols] = jnp.dot(
+            gathered_ref[:, :width], held_ref[0, :, cols], preferred_element_type=jnp.float32
+        )
+    copies[1].wait()
+    for start in range(0, columns, tile):
+        cols = slice(start, start + tile)
+        result = result_ref[:, cols] + jnp.dot(
+            gathered_ref[:, width:], held_ref[1, :, cols], preferred_element_type=jnp.float32
+        )
+        for j in range(chips):
+            outs[j][:, cols] = result[j * rows : (j + 1) * rows].astype(outs[j].dtype)
+
+
+def spread_value_kernel(n, frames, value_ref, out_ref):
+    part = value_ref.shape[1] // (n * frames)
+    for s in range(n):
+        for f in range(frames):
+            first = (s * frames + f) * part
+            out_ref[f * n + s] = value_ref[:, first : first + part]
+
+
+def spread_norm_kernel(n, frames, order_ref, query_ref, key_ref, gain_query_ref, gain_key_ref, out_ref, hidden_ref):
     features = query_ref.shape[1]
     part = features // (n * frames)
+    rows = query_ref.shape[0]
     query_inverse = inverse_rms(query_ref[...])
     key_inverse = inverse_rms(key_ref[...])
     for s in range(n):
@@ -138,11 +161,15 @@
             query = query_ref[:, cols].astype(jnp.float32) * query_inverse * gain_query_ref[:, cols]
             key = key_ref[:, cols].astype(jnp.float32) * key_inverse * gain_key_ref[:, cols]
             out_ref[f * n + s, :, :part] = query.astype(jnp.bfloat16)
-            out_ref[f * n + s, :, part : 2 * part] = key.astype(jnp.bfloat16)
-            out_ref[f * n + s, :, 2 * part :] = value_ref[:, cols]
-
-
-def spread_attention_kernel(n, frames, picked, index_ref, order_ref, rows_ref, mine_ref, given_ref, both):
+            out_ref[f * n + s, :, part:] = key.astype(jnp.bfloat16)
+    for g in range(frames):
+        for f in range(frames):
+            hidden_ref[g : g + 1, f * n * rows : (f + 1) * n * rows] = jnp.full(
+                (1, n * rows), jnp.where(order_ref[f] <= order_ref[g], 0.0, -1e30), jnp.float32
+            )
+
+
+def spread_attention_kernel(n, frames, picked, index_ref, hidden_ref, rows_ref, value_ref, mine_ref, given_ref, both):
     slot = index_ref[0]
     core = index_ref[1]
     rows = rows_ref.shape[1]
@@ -153,17 +180,10 @@
     for h in range(part // HD):
         cols = slice(h * HD, (h + 1) * HD)
         keys = rows_ref[:, :, part + h * HD : part + (h + 1) * HD].reshape(-1, HD)
-        values = rows_ref[:, :, 2 * part + h * HD : 2 * part + (h + 1) * HD].reshape(-1, HD)
+        values = value_ref[:, :, cols].reshape(-1, HD)
         for place, distance in enumerate(picked):
             frame = slot ^ distance
-            rank = order_ref[frame]
-            hidden = jnp.concatenate(
-                [
-                    jnp.full((1, frame_rows), jnp.where(order_ref[f] <= rank, 0.0, -1e30), jnp.float32)
-                    for f in range(frames)
-                ],
-                axis=1,
-            )
+            hidden = hidden_ref[pl.ds(frame, 1), :]
             for start in range(0, frame_rows, step):
                 query = rows_ref[pl.ds(frame * n + start // rows, step // rows), :, cols]
                 scores = lax.dot_general(
@@ -197,13 +217,30 @@
     frame_rows = n * rows
     vmem = pl.BlockSpec(memory_space=VMEM)
     smem = pl.BlockSpec(memory_space=SMEM)
-    sends = pl.pallas_call(
+    values = pl.pallas_call(
+        functools.partial(spread_value_kernel, n, frames),
+        out_shape=jax.ShapeDtypeStruct((n * frames, rows, part), jnp.bfloat16),
+        in_specs=[vmem],
+        out_specs=vmem,
+        cost_estimate=pl.CostEstimate(
+            flops=0, bytes_accessed=4 * rows * features, transcendentals=0
+        ),
+        name="values",
+    )(value_rows)
+    values = lax.all_to_all(values, ("frame", "seq"), split_axis=0, concat_axis=0, tiled=True)
+    sends, hidden = pl.pallas_call(
         functools.partial(spread_norm_kernel, n, frames),
-        out_shape=jax.ShapeDtypeStruct((n * frames, rows, 3 * part), jnp.bfloat16),
-        in_specs=[vmem] * 5,
-        out_specs=vmem,
+        out_shape=[
+            jax.ShapeDtypeStruct((n * frames, rows, 2 * part), jnp.bfloat16),
+            jax.ShapeDtypeStruct((frames, frames * frame_rows), jnp.float32),
+        ],
+        in_specs=[smem] + [vmem] * 4,
+        out_specs=[vmem] * 2,
+        cost_estimate=pl.CostEstimate(
+            flops=16 * rows * features, bytes_accessed=8 * rows * features, transcendentals=0
+        ),
         name="norm",
-    )(query_rows, key_rows, value_rows, gain_query.reshape(1, features), gain_key.reshape(1, features))
+    )(slot_order, query_rows, key_rows, gain_query.reshape(1, features), gain_key.reshape(1, features))
     held = lax.all_to_all(sends, ("frame", "seq"), split_axis=0, concat_axis=0, tiled=True)
     keys = frames * frame_rows
     me = lax.axis_index("seq").astype(jnp.int32)
@@ -215,7 +252,7 @@
         return pl.pallas_call(
             functools.partial(spread_attention_kernel, n, frames, picked),
             out_shape=[jax.ShapeDtypeStruct((count, frame_rows // 2, part), jnp.bfloat16)] * 2,
-            in_specs=[smem, smem, vmem],
+            in_specs=[smem, vmem, vmem, vmem],
             out_specs=[vmem] * 2,
             scratch_shapes=[pltpu.VMEM((2, count, frame_rows // 2, part), jnp.bfloat16)],
             compiler_params=pltpu.CompilerParams(vmem_limit_bytes=8 * 2**20 + 6 * 128 * keys * 4),
@@ -225,7 +262,7 @@
                 transcendentals=count * frame_rows * keys * (part // HD),
             ),
             name=name,
-        )(index, slot_order, held)
+        )(index, hidden, held, values)
 
     def across(value, axis, distance):
         size = n if axis == "seq" else frames
@@ -367,23 +404,25 @@
 
     cuts = 2
     columns = model // cuts
-    tile = columns // 2
     sources = len(attended)
     halves = []
     for cut in range(cuts):
-        weight_spec = pl.BlockSpec((width, tile), lambda i, first=2 * cut: (0, first + i))
         partial_sums = pl.pallas_call(
-            functools.partial(projection_kernel, chips, sources),
-            grid=(columns // tile,),
+            functools.partial(projection_kernel, chips, sources, cut * columns),
             out_shape=[
                 jax.ShapeDtypeStruct((rows, columns), jnp.bfloat16 if j % 2 else jnp.float32)
                 for j in range(chips)
             ],
             in_specs=[pl.BlockSpec(memory_space=SMEM)]
-            + [pl.BlockSpec(block.shape, lambda i: (0, 0, 0)) for block in attended]
-            + [weight_spec, weight_spec],
-            out_specs=[pl.BlockSpec((rows, tile), lambda i: (0, i))] * chips,
-            scratch_shapes=[pltpu.VMEM((half, 2 * width), jnp.bfloat16)],
+            + [pl.BlockSpec(memory_space=VMEM)] * sources
+            + [pl.BlockSpec(memory_space=pl.ANY)] * 2,
+            out_specs=[pl.BlockSpec(memory_space=VMEM)] * chips,
+            scratch_shapes=[
+                pltpu.VMEM((half, 2 * width), jnp.bfloat16),
+                pltpu.VMEM((half, columns), jnp.float32),
+                pltpu.VMEM((2, width, columns), jnp.bfloat16),
+                pltpu.SemaphoreType.DMA((2,)),
+            ],
             compiler_params=pltpu.CompilerParams(vmem_limit_bytes=48 * 2**20),
             cost_estimate=pl.CostEstimate(
                 flops=4 * half * width * columns,

time: 72.9 us -> 81.1 us (1.11)
  waiting for transfers between devices: 36 us -> 38.8 us
  starting transfers between devices: 17.7 us -> 20.3 us
  Pallas kernels: 12.8 us -> 15.2 us
    all_to_all x0 -> x1, waiting for transfers between devices: none -> 8.25 us  [spread_attention(): lax.all_to_all(values, ('frame', 'seq'), split_axis=0, concat_axis=0, til...]
    all_to_all x0 -> x1, starting transfers between devices: none -> 6.96 us  [spread_attention(): lax.all_to_all(values, ('frame', 'seq'), split_axis=0, concat_axis=0, til...]
    all_to_all x1, waiting for transfers between devices: 18.7 us -> 12.9 us  [spread_attention(): lax.all_to_all(sends, ('frame', 'seq'), split_axis=0, concat_axis=0, tile...]
    all_to_all x1, starting transfers between devices: 6.96 us -> 2.6 us  [spread_attention(): lax.all_to_all(sends, ('frame', 'seq'), split_axis=0, concat_axis=0, tile...]
    pallas_call x2 -> x3, Pallas kernels: 6.29 us -> 8.92 us  [the longest x2 7.22 us: shards(): pl.pallas_call(functools.partial(projection_kernel, chips, sources, cut *...]
  transfers between devices with their start and end apart: 13 -> 14, of which waited for: 8 -> 9; matrix products, arithmetic and copies ran while one was open for 3% -> 3% of each run, Pallas kernels for 13% -> 14%
where the time goes in v7:
time: 81.1 us; the launch traced here: 80.6 us
  waiting for transfers between devices  38.8 us (48%)
  starting transfers between devices  20.3 us (25%)
  Pallas kernels  15.2 us (19%)
  other arithmetic  2.1 us (3%)
  between operations  2.09 us (3%)
  local copies, waits for them, and re-layouts  2.07 us (3%)
    ppermute x7, waiting for transfers between devices, across(): return lax.ppermute(value, axis, [(i, i ^ distance) for i in range(n)])  15 us
    all_to_all x1, waiting for transfers between devices, spread_attention(): lax.all_to_all(sends, ('frame', 'seq'), split_axis=0, concat_axis=0, tile...  12.9 us
    all_to_all x1, waiting for transfers between devices, spread_attention(): lax.all_to_all(values, ('frame', 'seq'), split_axis=0, concat_axis=0, til...  8.25 us
    pallas_call x2, Pallas kernels, shards(): pl.pallas_call(functools.partial(projection_kernel, chips, sources, cut *...  7.22 us
    all_to_all x1, starting transfers between devices, spread_attention(): lax.all_to_all(values, ('frame', 'seq'), split_axis=0, concat_axis=0, til...  6.96 us
    ppermute x7, starting transfers between devices, across(): return lax.ppermute(value, axis, [(i, i ^ distance) for i in range(n)])  6.46 us
    ppermute x5, starting transfers between devices, across(): return lax.ppermute(value, axis, [(i, i ^ distance) for i in range(size)])  4.31 us
    pallas_call x2, Pallas kernels, attend(): pl.pallas_call(functools.partial(spread_attention_kernel, n, frames, pick...  4.18 us
  transfers between devices with their start and end apart: 14, of which 9 were waited for; matrix products, arithmetic and copies ran while one was open for 3% of the time, Pallas kernels for 14%

profile of v7, /device:TPU:0, one launch (start us, length us, event | category | flops | bytes accessed | tf_op | source)
XLA Modules:
  0.0 80.6 jit_solution(17712147480764317394)
XLA Ops:
  0.5 1.7 %values.1 = bf16[32,32,128]{2,1,0:T(8,128)(2,1)} custom-call(bf16[32,4096]{1,0:T(8,128)(2,1)} %bitcast.16), custom_call_target="tpu_custom_call" | custom-call | bytes 524288 | tf_op jit(solution)/shard_map/values/pallas_call | solution.py:220
  2.2 7.0 %all-to-all-start.1 = ((bf16[32,32,128]{2,1,0:T(8,128)(2,1)}), bf16[32,32,128]{2,1,0:T(8,128)(2,1)S(1)}, u32[]{:S(2)}, u32[]{:S(2)}) async-start(bf16[32,32,128]{2,1,0:T(8,128)(2,1)} %values.1), calls=%async_computation.1 | async-start | bytes 524288 | tf_op jit(solution)/shard_map/all_to_all | solution.py:230
  9.1 2.1 %norm.1 = (bf16[32,32,256]{2,1,0:T(8,128)(2,1)}, f32[4,1024]{1,0:T(4,128)}) custom-call(s32[4]{0:T(128)} %order_ref.1, bf16[32,4096]{1,0:T(8,128)(2,1)} %bitcast.14, bf16[32,4096]{1,0:T(8,128)(2,1)} %bitcast.15, f32[1,4096]{1,0:T(1,128)} %bitcast.18, f32[1,4096]{1,0:T(1,128)} %bitcast.19), custom_call_target="tpu_custom_call" | custom-call | flops 2097152 | bytes 1048576 | tf_op jit(solution)/shard_map/norm/pallas_call | solution.py:231
  11.3 8.2 %all-to-all-done.1.value_ref = bf16[32,32,128]{2,1,0:T(8,128)(2,1)S(1)} async-done(((bf16[32,32,128]{2,1,0:T(8,128)(2,1)}), bf16[32,32,128]{2,1,0:T(8,128)(2,1)S(1)}, u32[]{:S(2)}, u32[]{:S(2)}) %all-to-all-start.1) | async-done | bytes 262176 | tf_op jit(solution)/shard_map/all_to_all | solution.py:230
  19.5 2.6 %all-to-all-start = ((bf16[32,32,256]{2,1,0:T(8,128)(2,1)}), bf16[32,32,256]{2,1,0:T(8,128)(2,1)S(1)}, u32[]{:S(2)}, u32[]{:S(2)}) async-start(bf16[32,32,256]{2,1,0:T(8,128)(2,1)} %get-tuple-element.22), calls=%async_computation | async-start | bytes 1048576 | tf_op jit(solution)/shard_map/all_to_all | solution.py:244
  22.1 1.3 %dynamic_slice.8 = s32[1]{0:T(128)} dynamic-slice(s32[4]{0:T(128)} %param.20, s32[]{:T(128)S(6)} %select_n.19), dynamic_slice_sizes={1} | dynamic-slice | bytes 12 | tf_op jit(solution)/shard_map/jit(dynamic_index_in_dim)/dynamic_slice | solution.py:448
  25.5 12.9 %all-to-all-done.rows_ref = bf16[32,32,256]{2,1,0:T(8,128)(2,1)S(1)} async-done(((bf16[32,32,256]{2,1,0:T(8,128)(2,1)}), bf16[32,32,256]{2,1,0:T(8,128)(2,1)S(1)}, u32[]{:S(2)}, u32[]{:S(2)}) %all-to-all-start) | async-done | bytes 524320 | tf_op jit(solution)/shard_map/all_to_all | solution.py:244
  38.5 0.7 copy-done
  39.2 2.8 %attention_far.1 = (bf16[3,128,128]{2,1,0:T(8,128)(2,1)S(1)}, bf16[3,128,128]{2,1,0:T(8,128)(2,1)S(1)}) custom-call(s32[2]{0:T(128)S(1)} %pad_add_fusion.1.index_ref, f32[4,1024]{1,0:T(4,128)S(1)} %copy-done, bf16[32,32,256]{2,1,0:T(8,128)(2,1)S(1)} %all-to-all-done.rows_ref, bf16[32,32,128]{2,1,0:T(8,128)(2,1)S(1)} %all-to-all-done.1.value_ref), custom_call_target="tpu_custom_call" | custom-call | flops 402653184 | bytes 1048576 | tf_op jit(solution)/shard_map/attention_far/pallas_call | solution.py:252
  42.0 1.4 %attention_near.1 = (bf16[1,128,128]{2,1,0:T(8,128)(2,1)S(1)}, bf16[1,128,128]{2,1,0:T(8,128)(2,1)S(1)}) custom-call(s32[2]{0:T(128)S(1)} %pad_add_fusion.1.index_ref, f32[4,1024]{1,0:T(4,128)S(1)} %copy-done, bf16[32,32,256]{2,1,0:T(8,128)(2,1)S(1)} %all-to-all-done.rows_ref, bf16[32,32,128]{2,1,0:T(8,128)(2,1)S(1)} %all-to-all-done.1.value_ref), custom_call_target="tpu_custom_call" | custom-call | flops 134217728 | bytes 1048576 | tf_op jit(solution)/shard_map/attention_near/pallas_call | solution.py:252
  44.7 1.4 %collective-permute-start.3 = (bf16[2,128,128]{2,1,0:T(8,128)(2,1)S(1)}, bf16[2,128,128]{2,1,0:T(8,128)(2,1)S(1)}, u32[]{:S(2)}, u32[]{:S(2)}) collective-permute-start(bf16[2,128,128]{2,1,0:T(8,128)(2,1)S(1)} %pad_maximum_fusion.1), channel_id=1, source_target_pairs={{0,16},{8,24},{16,0},{24,8},{1,17},{9,25},{17,1},{25,9},{2,18},{10... | collective-permute-start | bytes 196616 | tf_op jit(solution)/shard_map/ppermute | solution.py:269
  46.1 1.7 %collective-permute-start.2 = (bf16[2,128,128]{2,1,0:T(8,128)(2,1)S(1)}, bf16[2,128,128]{2,1,0:T(8,128)(2,1)S(1)}, u32[]{:S(2)}, u32[]{:S(2)}) collective-permute-start(bf16[2,128,128]{2,1,0:T(8,128)(2,1)S(1)} %pad_maximum_fusion), channel_id=1, source_target_pairs={{0,8},{8,0},{16,24},{24,16},{1,9},{9,1},{17,25},{25,17},{2,10},{10... | collective-permute-start | bytes 196616 | tf_op jit(solution)/shard_map/ppermute | solution.py:269
  47.8 2.2 %collective-permute-done.4.refs_3_ = bf16[2,128,128]{2,1,0:T(8,128)(2,1)S(1)} collective-permute-done((bf16[2,128,128]{2,1,0:T(8,128)(2,1)S(1)}, bf16[2,128,128]{2,1,0:T(8,128)(2,1)S(1)}, u32[]{:S(2)}, u32[]{:S(2)}) %collective-permute-start.4) | collective-permute-done | bytes 65568 | tf_op jit(solution)/shard_map/ppermute | solution.py:269
  50.4 3.6 %projection_0.1 = (f32[32,2560]{1,0:T(8,128)S(1)}, bf16[32,2560]{1,0:T(8,128)(2,1)S(1)}, f32[32,2560]{1,0:T(8,128)S(1)}, bf16[32,2560]{1,0:T(8,128)(2,1)S(1)}) custom-call(s32[2]{0:T(128)S(1)} %pad_add_fusion.index_ref, bf16[2,128,128]{2,1,0:T(8,128)(2,1)S(1)} %constant_dynamic-update-slice_fusion.refs_0_, ...), custom_call_target="tpu_custom_call" | custom-call | flops 671088640 | bytes 5898240 | tf_op jit(solution)/shard_map/projection_0/pallas_call | solution.py:410
  54.5 0.9 %dynamic-slice_convert_fusion = f32[1,5120]{1,0:T(1,128)S(1)} fusion(bf16[64,5120]{1,0:T(8,128)(2,1)} %param.19, s32[]{:T(128)S(6)} %select_n.20), kind=kLoop, calls=%fused_computation.11 | loop fusion | flops 5120 | bytes 30724 | tf_op jit(solution)/shard_map/mul | solution.py:451
  55.4 3.6 %projection_1.1 = (f32[32,2560]{1,0:T(8,128)S(1)}, bf16[32,2560]{1,0:T(8,128)(2,1)S(1)}, f32[32,2560]{1,0:T(8,128)S(1)}, bf16[32,2560]{1,0:T(8,128)(2,1)S(1)}) custom-call(s32[2]{0:T(128)S(1)} %pad_add_fusion.index_ref, bf16[2,128,128]{2,1,0:T(8,128)(2,1)S(1)} %constant_dynamic-update-slice_fusion.refs_0_, ...), custom_call_target="tpu_custom_call" | custom-call | flops 671088640 | bytes 5898240 | tf_op jit(solution)/shard_map/projection_1/pallas_call | solution.py:410
  59.0 1.7 %collective-permute-start.9 = (bf16[32,2560]{1,0:T(8,128)(2,1)S(1)}, bf16[32,2560]{1,0:T(8,128)(2,1)S(1)}, u32[]{:S(2)}, u32[]{:S(2)}) collective-permute-start(bf16[32,2560]{1,0:T(8,128)(2,1)S(1)} %get-tuple-element.34), channel_id=1, source_target_pairs={{0,2},{1,3},{2,0},{3,1},{4,6},{5,7},{6,4},{7,5},{8,10},{9,11},{10,... | collective-permute-start | bytes 491528 | tf_op jit(solution)/shard_map/ppermute | solution.py:393
  61.1 1.3 %collective-permute-start.8 = (bf16[32,2560]{1,0:T(8,128)(2,1)S(1)}, bf16[32,2560]{1,0:T(8,128)(2,1)S(1)}, u32[]{:S(2)}, u32[]{:S(2)}) collective-permute-start(bf16[32,2560]{1,0:T(8,128)(2,1)S(1)} %add_convert_fusion.1), channel_id=1, source_target_pairs={{0,4},{1,5},{2,6},{3,7},{4,0},{5,1},{6,2},{7,3},{8,12},{9,13},{10,... | collective-permute-start | bytes 491528 | tf_op jit(solution)/shard_map/ppermute | solution.py:393
  62.5 9.0 %collective-permute-done.9 = bf16[32,2560]{1,0:T(8,128)(2,1)S(1)} collective-permute-done((bf16[32,2560]{1,0:T(8,128)(2,1)S(1)}, bf16[32,2560]{1,0:T(8,128)(2,1)S(1)}, u32[]{:S(2)}, u32[]{:S(2)}) %collective-permute-start.9) | collective-permute-done | bytes 163872 | tf_op jit(solution)/shard_map/ppermute | solution.py:393
  71.5 2.2 %collective-permute-start.11 = (bf16[32,2560]{1,0:T(8,128)(2,1)S(1)}, bf16[32,2560]{1,0:T(8,128)(2,1)S(1)}, u32[]{:S(2)}, u32[]{:S(2)}) collective-permute-start(bf16[32,2560]{1,0:T(8,128)(2,1)S(1)} %add_convert_fusion), channel_id=1, source_target_pairs={{0,4},{1,5},{2,6},{3,7},{4,0},{5,1},{6,2},{7,3},{8,12},{9,13},{10,... | collective-permute-start | bytes 491528 | tf_op jit(solution)/shard_map/ppermute | solution.py:393
  73.7 0.9 %collective-permute-done.7 = bf16[32,2560]{1,0:T(8,128)(2,1)S(1)} collective-permute-done((bf16[32,2560]{1,0:T(8,128)(2,1)S(1)}, bf16[32,2560]{1,0:T(8,128)(2,1)S(1)}, u32[]{:S(2)}, u32[]{:S(2)}) %collective-permute-start.7) | collective-permute-done | bytes 163872 | tf_op jit(solution)/shard_map/ppermute | solution.py:393
  74.7 3.6 %collective-permute-done.10 = bf16[32,2560]{1,0:T(8,128)(2,1)S(1)} collective-permute-done((bf16[32,2560]{1,0:T(8,128)(2,1)S(1)}, bf16[32,2560]{1,0:T(8,128)(2,1)S(1)}, u32[]{:S(2)}, u32[]{:S(2)}) %collective-permute-start.10) | collective-permute-done | bytes 163872 | tf_op jit(solution)/shard_map/ppermute | solution.py:393
  78.3 1.4 %collective-permute-done.11 = bf16[32,2560]{1,0:T(8,128)(2,1)S(1)} collective-permute-done((bf16[32,2560]{1,0:T(8,128)(2,1)S(1)}, bf16[32,2560]{1,0:T(8,128)(2,1)S(1)}, u32[]{:S(2)}, u32[]{:S(2)}) %collective-permute-start.11) | collective-permute-done | bytes 163872 | tf_op jit(solution)/shard_map/ppermute | solution.py:393
  79.7 0.8 %fusion.2 = bf16[1,32,5120]{2,1,0:T(8,128)(2,1)} fusion(f32[1,32,2560]{2,1,0:T(8,128)S(1)} %add_bitcast_fusion, f32[1,32,2560]{2,1,0:T(8,128)S(1)} %add_bitcast_fusion.1, bf16[1,32,5120]{2,1,0:T(8,128)(2,1)S(1)} %copy-done.1, f32[5120]{0:T(1024)S(1)} %convert_element_type.45, f32[5120]{0:T(1024)S(1)} %bitcast.17), kind=kLoop, calls=%fused_computation.3 | loop fusion | flops 983040 | bytes 1351680 | tf_op jit(solution)/shard_map/convert_element_type | solution.py:452
  (33 shorter events, 3.3 us)
Async XLA Ops:
  0.0 50.4 %collective-permute-start.5 = (bf16[512,5120]{1,0:T(8,128)(2,1)}, bf16[512,5120]{1,0:T(8,128)(2,1)}, u32[]{:S(2)}, u32[]{:S(2)}) collective-permute-start(bf16[512,5120]{1,0:T(8,128)(2,1)} %refs_4_.3), channel_id=1, source_target_pairs={{0,1},{1,0},{2,3},{3,2},{4,5},{5,4},{6,7},{7,6},{8,9},{9,8},{10,11... | collective-permute-start | bytes 15728648 | tf_op jit(solution)/shard_map/ppermute | solution.py:393
  2.2 17.4 %all-to-all-start.1 = ((bf16[32,32,128]{2,1,0:T(8,128)(2,1)}), bf16[32,32,128]{2,1,0:T(8,128)(2,1)S(1)}, u32[]{:S(2)}, u32[]{:S(2)}) async-start(bf16[32,32,128]{2,1,0:T(8,128)(2,1)} %values.1), calls=%async_computation.1 | async-start | bytes 524288 | tf_op jit(solution)/shard_map/all_to_all | solution.py:230
  19.5 19.0 %all-to-all-start = ((bf16[32,32,256]{2,1,0:T(8,128)(2,1)}), bf16[32,32,256]{2,1,0:T(8,128)(2,1)S(1)}, u32[]{:S(2)}, u32[]{:S(2)}) async-start(bf16[32,32,256]{2,1,0:T(8,128)(2,1)} %get-tuple-element.22), calls=%async_computation | async-start | bytes 1048576 | tf_op jit(solution)/shard_map/all_to_all | solution.py:244
  38.5 0.7 copy-start
  42.0 2.1 %collective-permute-start.1 = (bf16[3,128,128]{2,1,0:T(8,128)(2,1)S(1)}, bf16[3,128,128]{2,1,0:T(8,128)(2,1)S(1)}, u32[]{:S(2)}, u32[]{:S(2)}) collective-permute-start(bf16[3,128,128]{2,1,0:T(8,128)(2,1)S(1)} %get-tuple-element.26), channel_id=1, source_target_pairs={{0,1},{1,0},{2,3},{3,2},{4,5},{5,4},{6,7},{7,6},{8,9},{9,8},{10,11... | collective-permute-start | bytes 294920 | tf_op jit(solution)/shard_map/ppermute | solution.py:269
  43.5 4.3 %collective-permute-start = (bf16[1,128,128]{2,1,0:T(8,128)(2,1)S(1)}, bf16[1,128,128]{2,1,0:T(8,128)(2,1)S(1)}, u32[]{:S(2)}, u32[]{:S(2)}) collective-permute-start(bf16[1,128,128]{2,1,0:T(8,128)(2,1)S(1)} %get-tuple-element.24), channel_id=1, source_target_pairs={{0,1},{1,0},{2,3},{3,2},{4,5},{5,4},{6,7},{7,6},{8,9},{9,8},{10,11... | collective-permute-start | bytes 98312 | tf_op jit(solution)/shard_map/ppermute | solution.py:269
  44.1 5.9 %collective-permute-start.4 = (bf16[2,128,128]{2,1,0:T(8,128)(2,1)S(1)}, bf16[2,128,128]{2,1,0:T(8,128)(2,1)S(1)}, u32[]{:S(2)}, u32[]{:S(2)}) collective-permute-start(bf16[2,128,128]{2,1,0:T(8,128)(2,1)S(1)} %pad_maximum_fusion.2), channel_id=1, source_target_pairs={{0,24},{8,16},{16,8},{24,0},{1,25},{9,17},{17,9},{25,1},{2,26},{10... | collective-permute-start | bytes 196616 | tf_op jit(solution)/shard_map/ppermute | solution.py:269
  44.7 5.5 %collective-permute-start.3 = (bf16[2,128,128]{2,1,0:T(8,128)(2,1)S(1)}, bf16[2,128,128]{2,1,0:T(8,128)(2,1)S(1)}, u32[]{:S(2)}, u32[]{:S(2)}) collective-permute-start(bf16[2,128,128]{2,1,0:T(8,128)(2,1)S(1)} %pad_maximum_fusion.1), channel_id=1, source_target_pairs={{0,16},{8,24},{16,0},{24,8},{1,17},{9,25},{17,1},{25,9},{2,18},{10... | collective-permute-start | bytes 196616 | tf_op jit(solution)/shard_map/ppermute | solution.py:269
  46.1 4.3 %collective-permute-start.2 = (bf16[2,128,128]{2,1,0:T(8,128)(2,1)S(1)}, bf16[2,128,128]{2,1,0:T(8,128)(2,1)S(1)}, u32[]{:S(2)}, u32[]{:S(2)}) collective-permute-start(bf16[2,128,128]{2,1,0:T(8,128)(2,1)S(1)} %pad_maximum_fusion), channel_id=1, source_target_pairs={{0,8},{8,0},{16,24},{24,16},{1,9},{9,1},{17,25},{25,17},{2,10},{10... | collective-permute-start | bytes 196616 | tf_op jit(solution)/shard_map/ppermute | solution.py:269
  47.8 7.6 %copy-start.2 = (bf16[5120]{0:T(1024)(128)(2,1)S(1)}, bf16[5120]{0:T(1024)(128)(2,1)}, u32[]{:S(2)}) copy-start(bf16[5120]{0:T(1024)(128)(2,1)} %param.18) | copy-start | bytes 30724
  54.0 6.7 %collective-permute-start.6 = (bf16[32,2560]{1,0:T(8,128)(2,1)S(1)}, bf16[32,2560]{1,0:T(8,128)(2,1)S(1)}, u32[]{:S(2)}, u32[]{:S(2)}) collective-permute-start(bf16[32,2560]{1,0:T(8,128)(2,1)S(1)} %get-tuple-element.29), channel_id=1, source_target_pairs={{0,2},{1,3},{2,0},{3,1},{4,6},{5,7},{6,4},{7,5},{8,10},{9,11},{10,... | collective-permute-start | bytes 491528 | tf_op jit(solution)/shard_map/ppermute | solution.py:393
  55.4 24.4 %copy-start.1 = (bf16[1,32,5120]{2,1,0:T(8,128)(2,1)S(1)}, bf16[1,32,5120]{2,1,0:T(8,128)(2,1)}, u32[]{:S(2)}) copy-start(bf16[1,32,5120]{2,1,0:T(8,128)(2,1)} %param.11) | copy-start | bytes 983044
  59.0 12.5 %collective-permute-start.9 = (bf16[32,2560]{1,0:T(8,128)(2,1)S(1)}, bf16[32,2560]{1,0:T(8,128)(2,1)S(1)}, u32[]{:S(2)}, u32[]{:S(2)}) collective-permute-start(bf16[32,2560]{1,0:T(8,128)(2,1)S(1)} %get-tuple-element.34), channel_id=1, source_target_pairs={{0,2},{1,3},{2,0},{3,1},{4,6},{5,7},{6,4},{7,5},{8,10},{9,11},{10,... | collective-permute-start | bytes 491528 | tf_op jit(solution)/shard_map/ppermute | solution.py:393
  60.7 13.9 %collective-permute-start.7 = (bf16[32,2560]{1,0:T(8,128)(2,1)S(1)}, bf16[32,2560]{1,0:T(8,128)(2,1)S(1)}, u32[]{:S(2)}, u32[]{:S(2)}) collective-permute-start(bf16[32,2560]{1,0:T(8,128)(2,1)S(1)} %get-tuple-element.30), channel_id=1, source_target_pairs={{0,2},{1,3},{2,0},{3,1},{4,6},{5,7},{6,4},{7,5},{8,10},{9,11},{10,... | collective-permute-start | bytes 491528 | tf_op jit(solution)/shard_map/ppermute | solution.py:393
  61.1 13.5 %collective-permute-start.8 = (bf16[32,2560]{1,0:T(8,128)(2,1)S(1)}, bf16[32,2560]{1,0:T(8,128)(2,1)S(1)}, u32[]{:S(2)}, u32[]{:S(2)}) collective-permute-start(bf16[32,2560]{1,0:T(8,128)(2,1)S(1)} %add_convert_fusion.1), channel_id=1, source_target_pairs={{0,4},{1,5},{2,6},{3,7},{4,0},{5,1},{6,2},{7,3},{8,12},{9,13},{10,... | collective-permute-start | bytes 491528 | tf_op jit(solution)/shard_map/ppermute | solution.py:393
  71.5 6.8 %collective-permute-start.10 = (bf16[32,2560]{1,0:T(8,128)(2,1)S(1)}, bf16[32,2560]{1,0:T(8,128)(2,1)S(1)}, u32[]{:S(2)}, u32[]{:S(2)}) collective-permute-start(bf16[32,2560]{1,0:T(8,128)(2,1)S(1)} %get-tuple-element.35), channel_id=1, source_target_pairs={{0,2},{1,3},{2,0},{3,1},{4,6},{5,7},{6,4},{7,5},{8,10},{9,11},{10,... | collective-permute-start | bytes 491528 | tf_op jit(solution)/shard_map/ppermute | solution.py:393
  71.5 8.2 %collective-permute-start.11 = (bf16[32,2560]{1,0:T(8,128)(2,1)S(1)}, bf16[32,2560]{1,0:T(8,128)(2,1)S(1)}, u32[]{:S(2)}, u32[]{:S(2)}) collective-permute-start(bf16[32,2560]{1,0:T(8,128)(2,1)S(1)} %add_convert_fusion), channel_id=1, source_target_pairs={{0,4},{1,5},{2,6},{3,7},{4,0},{5,1},{6,2},{7,3},{8,12},{9,13},{10,... | collective-permute-start | bytes 491528 | tf_op jit(solution)/shard_map/ppermute | solution.py:393

commit v8 on v5

--- a/solution.py
+++ b/solution.py
@@ -101,7 +101,28 @@
                 out_ref[here, cols] = (summed / total).astype(jnp.bfloat16)
 
 
-def projection_kernel(chips, sources, index_ref, *refs):
+def stage_kernel(weight_ref, out_ref, sem):
+    copy = pltpu.make_async_copy(weight_ref, out_ref, sem)
+    copy.start()
+    copy.wait()
+
+
+def stage(weight, name):
+    return pl.pallas_call(
+        stage_kernel,
+        out_shape=pltpu.VMEM(weight.shape, weight.dtype),
+        in_specs=[pl.BlockSpec(memory_space=pl.ANY)],
+        out_specs=pl.BlockSpec(memory_space=VMEM),
+        scratch_shapes=[pltpu.SemaphoreType.DMA],
+        compiler_params=pltpu.CompilerParams(vmem_limit_bytes=16 * 2**20),
+        cost_estimate=pl.CostEstimate(
+            flops=0, bytes_accessed=4 * weight.size, transcendentals=0
+        ),
+        name=name,
+    )(weight)
+
+
+def projection_kernel(chips, sources, first, index_ref, *refs):
     own_ref, other_ref = refs[sources : sources + 2]
     outs = refs[sources + 2 : -1]
     gathered_ref = refs[-1]
@@ -110,20 +131,20 @@
     _, half, part = refs[0].shape
     rows = half // chips
     width = own_ref.shape[0]
-
-    @pl.when(pl.program_id(0) == 0)
-    def _():
-        for d in range(sources):
-            for parity in range(2):
-                first = pl.multiple_of(parity * width + (slot ^ d) * part, part)
-                for j in range(chips):
-                    here = pl.ds(pl.multiple_of((shift ^ j) * rows, rows), rows)
-                    gathered_ref[j * rows : (j + 1) * rows, pl.ds(first, part)] = refs[d][parity, here, :]
-
-    result = jnp.dot(gathered_ref[:, :width], own_ref[...], preferred_element_type=jnp.float32)
-    result += jnp.dot(gathered_ref[:, width:], other_ref[...], preferred_element_type=jnp.float32)
-    for j in range(chips):
-        outs[j][...] = result[j * rows : (j + 1) * rows].astype(outs[j].dtype)
+    columns = outs[0].shape[1]
+    for d in range(sources):
+        for parity in range(2):
+            place = pl.multiple_of(parity * width + (slot ^ d) * part, part)
+            for j in range(chips):
+                here = pl.ds(pl.multiple_of((shift ^ j) * rows, rows), rows)
+                gathered_ref[j * rows : (j + 1) * rows, pl.ds(place, part)] = refs[d][parity, here, :]
+    tile = columns // 5
+    for start in range(0, columns, tile):
+        cols = slice(first + start, first + start + tile)
+        result = jnp.dot(gathered_ref[:, :width], own_ref[:, cols], preferred_element_type=jnp.float32)
+        result += jnp.dot(gathered_ref[:, width:], other_ref[:, cols], preferred_element_type=jnp.float32)
+        for j in range(chips):
+            outs[j][:, start : start + tile] = result[j * rows : (j + 1) * rows].astype(outs[j].dtype)
 
 
 def spread_norm_kernel(n, frames, query_ref, key_ref, value_ref, gain_query_ref, gain_key_ref, out_ref):
@@ -142,7 +163,7 @@
             out_ref[f * n + s, :, 2 * part :] = value_ref[:, cols]
 
 
-def spread_attention_kernel(n, frames, picked, index_ref, order_ref, rows_ref, mine_ref, given_ref, both):
+def spread_attention_kernel(n, frames, picked, index_ref, rows_ref, mine_ref, given_ref, both):
     slot = index_ref[0]
     core = index_ref[1]
     rows = rows_ref.shape[1]
@@ -156,10 +177,10 @@
         values = rows_ref[:, :, 2 * part + h * HD : 2 * part + (h + 1) * HD].reshape(-1, HD)
         for place, distance in enumerate(picked):
             frame = slot ^ distance
-            rank = order_ref[frame]
+            rank = index_ref[2 + frame]
             hidden = jnp.concatenate(
                 [
-                    jnp.full((1, frame_rows), jnp.where(order_ref[f] <= rank, 0.0, -1e30), jnp.float32)
+                    jnp.full((1, frame_rows), jnp.where(index_ref[2 + f] <= rank, 0.0, -1e30), jnp.float32)
                     for f in range(frames)
                 ],
                 axis=1,
@@ -188,7 +209,7 @@
     given_ref[...] = both[core ^ 1]
 
 
-def spread_attention(query_rows, key_rows, value_rows, gain_query, gain_key, slot_order):
+def spread_attention(query_rows, key_rows, value_rows, gain_query, gain_key, slot_order, weights):
     n = lax.axis_size("seq")
     frames = lax.axis_size("frame")
     rows, features = query_rows.shape
@@ -208,14 +229,15 @@
     keys = frames * frame_rows
     me = lax.axis_index("seq").astype(jnp.int32)
     slot = lax.axis_index("frame").astype(jnp.int32)
-    index = jnp.stack([slot, me % 2])
+    index = jnp.concatenate([jnp.stack([slot, me % 2]), slot_order])
+    index = lax.optimization_barrier((index, *weights))[0]
 
     def attend(picked, name):
         count = len(picked)
         return pl.pallas_call(
             functools.partial(spread_attention_kernel, n, frames, picked),
             out_shape=[jax.ShapeDtypeStruct((count, frame_rows // 2, part), jnp.bfloat16)] * 2,
-            in_specs=[smem, smem, vmem],
+            in_specs=[smem, vmem],
             out_specs=[vmem] * 2,
             scratch_shapes=[pltpu.VMEM((2, count, frame_rows // 2, part), jnp.bfloat16)],
             compiler_params=pltpu.CompilerParams(vmem_limit_bytes=8 * 2**20 + 6 * 128 * keys * 4),
@@ -225,7 +247,7 @@
                 transcendentals=count * frame_rows * keys * (part // HD),
             ),
             name=name,
-        )(index, slot_order, held)
+        )(index, held)
 
     def across(value, axis, distance):
         size = n if axis == "seq" else frames
@@ -242,7 +264,7 @@
     return [found[d] for d in range(frames)]
 
 
-def gathered_attention(query_rows, key_rows, value_rows, gain_query, gain_key, slot_order):
+def gathered_attention(query_rows, key_rows, value_rows, gain_query, gain_key, slot_order, weights):
     n = lax.axis_size("seq")
     frames = lax.axis_size("frame")
     chips = n // 2
@@ -358,40 +380,38 @@
     def after(value, *earlier):
         return lax.optimization_barrier((value, *earlier))[0]
 
-    other_weight = across(out_weight, "seq", 1)
+    weights = [
+        stage(out_weight, "stage_own"),
+        stage(across(out_weight, "seq", 1), "stage_other"),
+    ]
     spread = (width // HD) % frames == 0
     attended = (spread_attention if spread else gathered_attention)(
-        query_rows[0], key_rows[0], value_rows[0], gain_query, gain_key, slot_order
+        query_rows[0], key_rows[0], value_rows[0], gain_query, gain_key, slot_order, weights
     )
     index = jnp.stack([me // 2, slot]) if spread else jnp.zeros((2,), jnp.int32)
 
     cuts = 2
     columns = model // cuts
-    tile = columns // 2
     sources = len(attended)
     halves = []
     for cut in range(cuts):
-        weight_spec = pl.BlockSpec((width, tile), lambda i, first=2 * cut: (0, first + i))
         partial_sums = pl.pallas_call(
-            functools.partial(projection_kernel, chips, sources),
-            grid=(columns // tile,),
+            functools.partial(projection_kernel, chips, sources, cut * columns),
             out_shape=[
                 jax.ShapeDtypeStruct((rows, columns), jnp.bfloat16 if j % 2 else jnp.float32)
                 for j in range(chips)
             ],
-            in_specs=[pl.BlockSpec(memory_space=SMEM)]
-            + [pl.BlockSpec(block.shape, lambda i: (0, 0, 0)) for block in attended]
-            + [weight_spec, weight_spec],
-            out_specs=[pl.BlockSpec((rows, tile), lambda i: (0, i))] * chips,
+            in_specs=[pl.BlockSpec(memory_space=SMEM)] + [pl.BlockSpec(memory_space=VMEM)] * (sources + 2),
+            out_specs=[pl.BlockSpec(memory_space=VMEM)] * chips,
             scratch_shapes=[pltpu.VMEM((half, 2 * width), jnp.bfloat16)],
-            compiler_params=pltpu.CompilerParams(vmem_limit_bytes=48 * 2**20),
+            compiler_params=pltpu.CompilerParams(vmem_limit_bytes=16 * 2**20),
             cost_estimate=pl.CostEstimate(
                 flops=4 * half * width * columns,
                 bytes_accessed=4 * width * columns + 8 * rows * columns,
                 transcendentals=0,
             ),
             name=f"projection_{cut}",
-        )(index, *attended, out_weight, other_weight)
+        )(index, *attended, *weights)
         sums = {j: part for j, part in enumerate(partial_sums)}
         bit = 1
         while bit < chips:

time: 72.9 us -> 73.6 us (level)
  local copies, waits for them, and re-layouts: 1.95 us -> 12.8 us
  waiting for transfers between devices: 36 us -> 26.1 us
    unnamed x7 -> x19, local copies, waits for them, and re-layouts: 0.67 us -> 12.2 us
    all_to_all x1, waiting for transfers between devices: 18.7 us -> 9.19 us  [spread_attention(): lax.all_to_all(sends, ('frame', 'seq'), split_axis=0, concat_axis=0, tile...]
    pallas_call x2 -> x4, Pallas kernels: 6.29 us -> 5.76 us  [the longest x2 2.91 us: shards(): pl.pallas_call(functools.partial(projection_kernel, chips, sources, cut *...]
  transfers between devices with their start and end apart: 13 -> 13, of which waited for: 8 -> 8; matrix products, arithmetic and copies ran while one was open for 3% -> 3% of each run, Pallas kernels for 13% -> 11%
where the time goes in v8:
time: 73.6 us; the launch traced here: 73.2 us
  waiting for transfers between devices  26.1 us (35%)
  starting transfers between devices  17.8 us (24%)
  local copies, waits for them, and re-layouts  12.8 us (17%)
  Pallas kernels  12.3 us (17%)
  other arithmetic  2.1 us (3%)
  between operations  2.09 us (3%)
    ppermute x7, waiting for transfers between devices, across(): return lax.ppermute(value, axis, [(i, i ^ distance) for i in range(n)])  14.4 us
    unnamed x19, local copies, waits for them, and re-layouts  12.2 us
    all_to_all x1, waiting for transfers between devices, spread_attention(): lax.all_to_all(sends, ('frame', 'seq'), split_axis=0, concat_axis=0, tile...  9.19 us
    all_to_all x1, starting transfers between devices, spread_attention(): lax.all_to_all(sends, ('frame', 'seq'), split_axis=0, concat_axis=0, tile...  6.96 us
    ppermute x7, starting transfers between devices, across(): return lax.ppermute(value, axis, [(i, i ^ distance) for i in range(n)])  6.51 us
    ppermute x5, starting transfers between devices, across(): return lax.ppermute(value, axis, [(i, i ^ distance) for i in range(size)])  4.3 us
    pallas_call x2, Pallas kernels, attend(): pl.pallas_call(functools.partial(spread_attention_kernel, n, frames, pick...  4.2 us
    pallas_call x2, Pallas kernels, shards(): pl.pallas_call(functools.partial(projection_kernel, chips, sources, cut *...  2.91 us
  transfers between devices with their start and end apart: 13, of which 8 were waited for; matrix products, arithmetic and copies ran while one was open for 3% of the time, Pallas kernels for 11%

profile of v8, /device:TPU:0, one launch (start us, length us, event | category | flops | bytes accessed | tf_op | source)
XLA Modules:
  0.0 73.2 jit_solution(12825107305863528277)
XLA Ops:
  0.5 2.3 %norm.1 = bf16[32,32,384]{2,1,0:T(8,128)(2,1)} custom-call(bf16[32,4096]{1,0:T(8,128)(2,1)} %bitcast.14, bf16[32,4096]{1,0:T(8,128)(2,1)} %bitcast.15, bf16[32,4096]{1,0:T(8,128)(2,1)} %bitcast.16, f32[1,4096]{1,0:T(1,128)} %bitcast.18, f32[1,4096]{1,0:T(1,128)} %bitcast.19), custom_call_target="tpu_custom_call" | custom-call | tf_op jit(solution)/shard_map/norm/pallas_call | solution.py:221
  2.8 7.0 %all-to-all-start = ((bf16[32,32,384]{2,1,0:T(8,128)(2,1)}), bf16[32,32,384]{2,1,0:T(8,128)(2,1)S(1)}, u32[]{:S(2)}, u32[]{:S(2)}) async-start(bf16[32,32,384]{2,1,0:T(8,128)(2,1)} %norm.1), calls=%async_computation | async-start | bytes 1572864 | tf_op jit(solution)/shard_map/all_to_all | solution.py:228
  9.8 2.5 %copy-done.4 = bf16[512,5120]{1,0:T(8,128)(2,1)S(1)} copy-done((bf16[512,5120]{1,0:T(8,128)(2,1)S(1)}, bf16[512,5120]{1,0:T(8,128)(2,1)}, u32[]{:S(2)}) %copy-start.4) | copy-done | bytes 5242904
  12.6 2.3 %copy-done = bf16[512,5120]{1,0:T(8,128)(2,1)} copy-done((bf16[512,5120]{1,0:T(8,128)(2,1)}, bf16[512,5120]{1,0:T(8,128)(2,1)S(1)}, u32[]{:S(2)}) %copy-start) | copy-done | bytes 5242904
  17.6 2.5 %stage_other.1.refs_5_ = bf16[512,5120]{1,0:T(8,128)(2,1)S(1)} custom-call(bf16[512,5120]{1,0:T(8,128)(2,1)} %collective-permute-done.weight_ref), custom_call_target="tpu_custom_call" | custom-call | bytes 10485760 | tf_op jit(solution)/shard_map/stage_other/pallas_call | solution.py:111
  20.1 2.4 %copy-done.2 = bf16[512,5120]{1,0:T(8,128)(2,1)} copy-done((bf16[512,5120]{1,0:T(8,128)(2,1)}, bf16[512,5120]{1,0:T(8,128)(2,1)S(1)}, u32[]{:S(2)}) %copy-start.2) | copy-done | bytes 5242904
  22.5 9.2 %all-to-all-done.rows_ref = bf16[32,32,384]{2,1,0:T(8,128)(2,1)S(1)} async-done(((bf16[32,32,384]{2,1,0:T(8,128)(2,1)}), bf16[32,32,384]{2,1,0:T(8,128)(2,1)S(1)}, u32[]{:S(2)}, u32[]{:S(2)}) %all-to-all-start) | async-done | bytes 786464 | tf_op jit(solution)/shard_map/all_to_all | solution.py:228
  31.7 2.8 %attention_far.1 = (bf16[3,128,128]{2,1,0:T(8,128)(2,1)S(1)}, bf16[3,128,128]{2,1,0:T(8,128)(2,1)S(1)}) custom-call(s32[6]{0:T(128)S(1)} %pad_add_fusion.1.index_ref, bf16[32,32,384]{2,1,0:T(8,128)(2,1)S(1)} %all-to-all-done.rows_ref), custom_call_target="tpu_custom_call" | custom-call | flops 402653184 | bytes 1048576 | tf_op jit(solution)/shard_map/attention_far/pallas_call | solution.py:237
  34.6 1.4 %attention_near.1 = (bf16[1,128,128]{2,1,0:T(8,128)(2,1)S(1)}, bf16[1,128,128]{2,1,0:T(8,128)(2,1)S(1)}) custom-call(s32[6]{0:T(128)S(1)} %pad_add_fusion.1.index_ref, bf16[32,32,384]{2,1,0:T(8,128)(2,1)S(1)} %all-to-all-done.rows_ref), custom_call_target="tpu_custom_call" | custom-call | flops 134217728 | bytes 1048576 | tf_op jit(solution)/shard_map/attention_near/pallas_call | solution.py:237
  37.2 1.4 %collective-permute-start.4 = (bf16[2,128,128]{2,1,0:T(8,128)(2,1)S(1)}, bf16[2,128,128]{2,1,0:T(8,128)(2,1)S(1)}, u32[]{:S(2)}, u32[]{:S(2)}) collective-permute-start(bf16[2,128,128]{2,1,0:T(8,128)(2,1)S(1)} %pad_maximum_fusion.1), channel_id=1, source_target_pairs={{0,16},{8,24},{16,0},{24,8},{1,17},{9,25},{17,1},{25,9},{2,18},{10... | collective-permute-start | bytes 196616 | tf_op jit(solution)/shard_map/ppermute | solution.py:254
  38.6 1.7 %collective-permute-start.3 = (bf16[2,128,128]{2,1,0:T(8,128)(2,1)S(1)}, bf16[2,128,128]{2,1,0:T(8,128)(2,1)S(1)}, u32[]{:S(2)}, u32[]{:S(2)}) collective-permute-start(bf16[2,128,128]{2,1,0:T(8,128)(2,1)S(1)} %pad_maximum_fusion), channel_id=1, source_target_pairs={{0,8},{8,0},{16,24},{24,16},{1,9},{9,1},{17,25},{25,17},{2,10},{10... | collective-permute-start | bytes 196616 | tf_op jit(solution)/shard_map/ppermute | solution.py:254
  40.3 2.2 %collective-permute-done.5.refs_3_ = bf16[2,128,128]{2,1,0:T(8,128)(2,1)S(1)} collective-permute-done((bf16[2,128,128]{2,1,0:T(8,128)(2,1)S(1)}, bf16[2,128,128]{2,1,0:T(8,128)(2,1)S(1)}, u32[]{:S(2)}, u32[]{:S(2)}) %collective-permute-start.5) | collective-permute-done | bytes 65568 | tf_op jit(solution)/shard_map/ppermute | solution.py:254
  42.9 2.5 %copy-done.1 = bf16[512,5120]{1,0:T(8,128)(2,1)S(1)} copy-done((bf16[512,5120]{1,0:T(8,128)(2,1)S(1)}, bf16[512,5120]{1,0:T(8,128)(2,1)}, u32[]{:S(2)}) %copy-start.1) | copy-done | bytes 5242904
  45.4 2.5 %copy-done.3 = bf16[512,5120]{1,0:T(8,128)(2,1)S(1)} copy-done((bf16[512,5120]{1,0:T(8,128)(2,1)S(1)}, bf16[512,5120]{1,0:T(8,128)(2,1)}, u32[]{:S(2)}) %copy-start.3) | copy-done | bytes 5242904
  47.9 1.5 %projection_0.1 = (f32[32,2560]{1,0:T(8,128)S(1)}, bf16[32,2560]{1,0:T(8,128)(2,1)S(1)}, f32[32,2560]{1,0:T(8,128)S(1)}, bf16[32,2560]{1,0:T(8,128)(2,1)S(1)}) custom-call(s32[2]{0:T(128)S(1)} %pad_add_fusion.index_ref, bf16[2,128,128]{2,1,0:T(8,128)(2,1)S(1)} %constant_dynamic-update-slice_fusion.refs_0_, ...), custom_call_target="tpu_custom_call" | custom-call | flops 671088640 | bytes 5898240 | tf_op jit(solution)/shard_map/projection_0/pallas_call | solution.py:398
  49.6 0.9 %dynamic-slice_convert_fusion = f32[1,5120]{1,0:T(1,128)S(1)} fusion(bf16[64,5120]{1,0:T(8,128)(2,1)} %param.19, s32[]{:T(128)S(6)} %select_n.20), kind=kLoop, calls=%fused_computation.11 | loop fusion | flops 5120 | bytes 30724 | tf_op jit(solution)/shard_map/mul | solution.py:432
  50.5 1.5 %projection_1.1 = (f32[32,2560]{1,0:T(8,128)S(1)}, bf16[32,2560]{1,0:T(8,128)(2,1)S(1)}, f32[32,2560]{1,0:T(8,128)S(1)}, bf16[32,2560]{1,0:T(8,128)(2,1)S(1)}) custom-call(s32[2]{0:T(128)S(1)} %pad_add_fusion.index_ref, bf16[2,128,128]{2,1,0:T(8,128)(2,1)S(1)} %constant_dynamic-update-slice_fusion.refs_0_, ...), custom_call_target="tpu_custom_call" | custom-call | flops 671088640 | bytes 5898240 | tf_op jit(solution)/shard_map/projection_1/pallas_call | solution.py:398
  52.0 1.9 %collective-permute-start.9 = (bf16[32,2560]{1,0:T(8,128)(2,1)S(1)}, bf16[32,2560]{1,0:T(8,128)(2,1)S(1)}, u32[]{:S(2)}, u32[]{:S(2)}) collective-permute-start(bf16[32,2560]{1,0:T(8,128)(2,1)S(1)} %get-tuple-element.32), channel_id=1, source_target_pairs={{0,2},{1,3},{2,0},{3,1},{4,6},{5,7},{6,4},{7,5},{8,10},{9,11},{10,... | collective-permute-start | bytes 491528 | tf_op jit(solution)/shard_map/ppermute | solution.py:378
  53.9 1.9 %collective-permute-done.6 = bf16[32,2560]{1,0:T(8,128)(2,1)S(1)} collective-permute-done((bf16[32,2560]{1,0:T(8,128)(2,1)S(1)}, bf16[32,2560]{1,0:T(8,128)(2,1)S(1)}, u32[]{:S(2)}, u32[]{:S(2)}) %collective-permute-start.6) | collective-permute-done | bytes 163872 | tf_op jit(solution)/shard_map/ppermute | solution.py:378
  55.8 1.7 %collective-permute-start.8 = (bf16[32,2560]{1,0:T(8,128)(2,1)S(1)}, bf16[32,2560]{1,0:T(8,128)(2,1)S(1)}, u32[]{:S(2)}, u32[]{:S(2)}) collective-permute-start(bf16[32,2560]{1,0:T(8,128)(2,1)S(1)} %add_convert_fusion.1), channel_id=1, source_target_pairs={{0,4},{1,5},{2,6},{3,7},{4,0},{5,1},{6,2},{7,3},{8,12},{9,13},{10,... | collective-permute-start | bytes 491528 | tf_op jit(solution)/shard_map/ppermute | solution.py:378
  57.5 4.2 %collective-permute-done.9 = bf16[32,2560]{1,0:T(8,128)(2,1)S(1)} collective-permute-done((bf16[32,2560]{1,0:T(8,128)(2,1)S(1)}, bf16[32,2560]{1,0:T(8,128)(2,1)S(1)}, u32[]{:S(2)}, u32[]{:S(2)}) %collective-permute-start.9) | collective-permute-done | bytes 163872 | tf_op jit(solution)/shard_map/ppermute | solution.py:378
  61.8 2.2 %collective-permute-start.11 = (bf16[32,2560]{1,0:T(8,128)(2,1)S(1)}, bf16[32,2560]{1,0:T(8,128)(2,1)S(1)}, u32[]{:S(2)}, u32[]{:S(2)}) collective-permute-start(bf16[32,2560]{1,0:T(8,128)(2,1)S(1)} %add_convert_fusion), channel_id=1, source_target_pairs={{0,4},{1,5},{2,6},{3,7},{4,0},{5,1},{6,2},{7,3},{8,12},{9,13},{10,... | collective-permute-start | bytes 491528 | tf_op jit(solution)/shard_map/ppermute | solution.py:378
  64.0 4.7 %collective-permute-done.7 = bf16[32,2560]{1,0:T(8,128)(2,1)S(1)} collective-permute-done((bf16[32,2560]{1,0:T(8,128)(2,1)S(1)}, bf16[32,2560]{1,0:T(8,128)(2,1)S(1)}, u32[]{:S(2)}, u32[]{:S(2)}) %collective-permute-start.7) | collective-permute-done | bytes 163872 | tf_op jit(solution)/shard_map/ppermute | solution.py:378
  68.8 3.5 %collective-permute-done.10 = bf16[32,2560]{1,0:T(8,128)(2,1)S(1)} collective-permute-done((bf16[32,2560]{1,0:T(8,128)(2,1)S(1)}, bf16[32,2560]{1,0:T(8,128)(2,1)S(1)}, u32[]{:S(2)}, u32[]{:S(2)}) %collective-permute-start.10) | collective-permute-done | bytes 163872 | tf_op jit(solution)/shard_map/ppermute | solution.py:378
  (44 shorter events, 4.6 us)
Async XLA Ops:
  0.0 17.6 %collective-permute-start = (bf16[512,5120]{1,0:T(8,128)(2,1)}, bf16[512,5120]{1,0:T(8,128)(2,1)}, u32[]{:S(2)}, u32[]{:S(2)}) collective-permute-start(bf16[512,5120]{1,0:T(8,128)(2,1)} %weight_ref.1), channel_id=1, source_target_pairs={{0,1},{1,0},{2,3},{3,2},{4,5},{5,4},{6,7},{7,6},{8,9},{9,8},{10,11... | collective-permute-start | bytes 15728648 | tf_op jit(solution)/shard_map/ppermute | solution.py:378
  2.8 28.9 %all-to-all-start = ((bf16[32,32,384]{2,1,0:T(8,128)(2,1)}), bf16[32,32,384]{2,1,0:T(8,128)(2,1)S(1)}, u32[]{:S(2)}, u32[]{:S(2)}) async-start(bf16[32,32,384]{2,1,0:T(8,128)(2,1)} %norm.1), calls=%async_computation | async-start | bytes 1572864 | tf_op jit(solution)/shard_map/all_to_all | solution.py:228
  9.7 2.5 %copy-start.4 = (bf16[512,5120]{1,0:T(8,128)(2,1)S(1)}, bf16[512,5120]{1,0:T(8,128)(2,1)}, u32[]{:S(2)}) copy-start(bf16[512,5120]{1,0:T(8,128)(2,1)} %weight_ref.1) | copy-start | bytes 15728644
  12.2 2.7 %copy-start.8 = (s32[4]{0:T(128)S(1)}, s32[4]{0:T(128)}, u32[]{:S(2)}) copy-start(s32[4]{0:T(128)} %param.20) | copy-start | bytes 52
  12.2 5.3 %copy-start.7 = (s32[4]{0:T(128)S(1)}, s32[4]{0:T(128)}, u32[]{:S(2)}) copy-start(s32[4]{0:T(128)} %param.21) | copy-start | bytes 52
  12.6 2.3 %copy-start = (bf16[512,5120]{1,0:T(8,128)(2,1)}, bf16[512,5120]{1,0:T(8,128)(2,1)S(1)}, u32[]{:S(2)}) copy-start(bf16[512,5120]{1,0:T(8,128)(2,1)S(1)} %stage_own.1.refs_4_) | copy-start | bytes 15728644
  20.1 2.4 %copy-start.2 = (bf16[512,5120]{1,0:T(8,128)(2,1)}, bf16[512,5120]{1,0:T(8,128)(2,1)S(1)}, u32[]{:S(2)}) copy-start(bf16[512,5120]{1,0:T(8,128)(2,1)S(1)} %stage_other.1.refs_5_) | copy-start | bytes 15728644
  34.5 2.1 %collective-permute-start.2 = (bf16[3,128,128]{2,1,0:T(8,128)(2,1)S(1)}, bf16[3,128,128]{2,1,0:T(8,128)(2,1)S(1)}, u32[]{:S(2)}, u32[]{:S(2)}) collective-permute-start(bf16[3,128,128]{2,1,0:T(8,128)(2,1)S(1)} %get-tuple-element.24), channel_id=1, source_target_pairs={{0,1},{1,0},{2,3},{3,2},{4,5},{5,4},{6,7},{7,6},{8,9},{9,8},{10,11... | collective-permute-start | bytes 294920 | tf_op jit(solution)/shard_map/ppermute | solution.py:254
  36.0 4.3 %collective-permute-start.1 = (bf16[1,128,128]{2,1,0:T(8,128)(2,1)S(1)}, bf16[1,128,128]{2,1,0:T(8,128)(2,1)S(1)}, u32[]{:S(2)}, u32[]{:S(2)}) collective-permute-start(bf16[1,128,128]{2,1,0:T(8,128)(2,1)S(1)} %get-tuple-element.22), channel_id=1, source_target_pairs={{0,1},{1,0},{2,3},{3,2},{4,5},{5,4},{6,7},{7,6},{8,9},{9,8},{10,11... | collective-permute-start | bytes 98312 | tf_op jit(solution)/shard_map/ppermute | solution.py:254
  36.6 5.9 %collective-permute-start.5 = (bf16[2,128,128]{2,1,0:T(8,128)(2,1)S(1)}, bf16[2,128,128]{2,1,0:T(8,128)(2,1)S(1)}, u32[]{:S(2)}, u32[]{:S(2)}) collective-permute-start(bf16[2,128,128]{2,1,0:T(8,128)(2,1)S(1)} %pad_maximum_fusion.2), channel_id=1, source_target_pairs={{0,24},{8,16},{16,8},{24,0},{1,25},{9,17},{17,9},{25,1},{2,26},{10... | collective-permute-start | bytes 196616 | tf_op jit(solution)/shard_map/ppermute | solution.py:254
  37.2 5.5 %collective-permute-start.4 = (bf16[2,128,128]{2,1,0:T(8,128)(2,1)S(1)}, bf16[2,128,128]{2,1,0:T(8,128)(2,1)S(1)}, u32[]{:S(2)}, u32[]{:S(2)}) collective-permute-start(bf16[2,128,128]{2,1,0:T(8,128)(2,1)S(1)} %pad_maximum_fusion.1), channel_id=1, source_target_pairs={{0,16},{8,24},{16,0},{24,8},{1,17},{9,25},{17,1},{25,9},{2,18},{10... | collective-permute-start | bytes 196616 | tf_op jit(solution)/shard_map/ppermute | solution.py:254
  38.6 4.3 %collective-permute-start.3 = (bf16[2,128,128]{2,1,0:T(8,128)(2,1)S(1)}, bf16[2,128,128]{2,1,0:T(8,128)(2,1)S(1)}, u32[]{:S(2)}, u32[]{:S(2)}) collective-permute-start(bf16[2,128,128]{2,1,0:T(8,128)(2,1)S(1)} %pad_maximum_fusion), channel_id=1, source_target_pairs={{0,8},{8,0},{16,24},{24,16},{1,9},{9,1},{17,25},{25,17},{2,10},{10... | collective-permute-start | bytes 196616 | tf_op jit(solution)/shard_map/ppermute | solution.py:254
  40.3 10.2 %copy-start.6 = (bf16[5120]{0:T(1024)(128)(2,1)S(1)}, bf16[5120]{0:T(1024)(128)(2,1)}, u32[]{:S(2)}) copy-start(bf16[5120]{0:T(1024)(128)(2,1)} %param.18) | copy-start | bytes 30724
  42.9 2.5 %copy-start.1 = (bf16[512,5120]{1,0:T(8,128)(2,1)S(1)}, bf16[512,5120]{1,0:T(8,128)(2,1)}, u32[]{:S(2)}) copy-start(bf16[512,5120]{1,0:T(8,128)(2,1)} %copy-done) | copy-start | bytes 15728644
  45.4 2.5 %copy-start.3 = (bf16[512,5120]{1,0:T(8,128)(2,1)S(1)}, bf16[512,5120]{1,0:T(8,128)(2,1)}, u32[]{:S(2)}) copy-start(bf16[512,5120]{1,0:T(8,128)(2,1)} %copy-done.2) | copy-start | bytes 15728644
  49.3 6.5 %collective-permute-start.6 = (bf16[32,2560]{1,0:T(8,128)(2,1)S(1)}, bf16[32,2560]{1,0:T(8,128)(2,1)S(1)}, u32[]{:S(2)}, u32[]{:S(2)}) collective-permute-start(bf16[32,2560]{1,0:T(8,128)(2,1)S(1)} %get-tuple-element.27), channel_id=1, source_target_pairs={{0,2},{1,3},{2,0},{3,1},{4,6},{5,7},{6,4},{7,5},{8,10},{9,11},{10,... | collective-permute-start | bytes 491528 | tf_op jit(solution)/shard_map/ppermute | solution.py:378
  50.5 21.8 %copy-start.5 = (bf16[1,32,5120]{2,1,0:T(8,128)(2,1)S(1)}, bf16[1,32,5120]{2,1,0:T(8,128)(2,1)}, u32[]{:S(2)}) copy-start(bf16[1,32,5120]{2,1,0:T(8,128)(2,1)} %param.11) | copy-start | bytes 983044
  52.0 9.8 %collective-permute-start.9 = (bf16[32,2560]{1,0:T(8,128)(2,1)S(1)}, bf16[32,2560]{1,0:T(8,128)(2,1)S(1)}, u32[]{:S(2)}, u32[]{:S(2)}) collective-permute-start(bf16[32,2560]{1,0:T(8,128)(2,1)S(1)} %get-tuple-element.32), channel_id=1, source_target_pairs={{0,2},{1,3},{2,0},{3,1},{4,6},{5,7},{6,4},{7,5},{8,10},{9,11},{10,... | collective-permute-start | bytes 491528 | tf_op jit(solution)/shard_map/ppermute | solution.py:378
  55.8 12.9 %collective-permute-start.7 = (bf16[32,2560]{1,0:T(8,128)(2,1)S(1)}, bf16[32,2560]{1,0:T(8,128)(2,1)S(1)}, u32[]{:S(2)}, u32[]{:S(2)}) collective-permute-start(bf16[32,2560]{1,0:T(8,128)(2,1)S(1)} %get-tuple-element.28), channel_id=1, source_target_pairs={{0,2},{1,3},{2,0},{3,1},{4,6},{5,7},{6,4},{7,5},{8,10},{9,11},{10,... | collective-permute-start | bytes 491528 | tf_op jit(solution)/shard_map/ppermute | solution.py:378
  55.8 12.9 %collective-permute-start.8 = (bf16[32,2560]{1,0:T(8,128)(2,1)S(1)}, bf16[32,2560]{1,0:T(8,128)(2,1)S(1)}, u32[]{:S(2)}, u32[]{:S(2)}) collective-permute-start(bf16[32,2560]{1,0:T(8,128)(2,1)S(1)} %add_convert_fusion.1), channel_id=1, source_target_pairs={{0,4},{1,5},{2,6},{3,7},{4,0},{5,1},{6,2},{7,3},{8,12},{9,13},{10,... | collective-permute-start | bytes 491528 | tf_op jit(solution)/shard_map/ppermute | solution.py:378
  61.7 10.5 %collective-permute-start.10 = (bf16[32,2560]{1,0:T(8,128)(2,1)S(1)}, bf16[32,2560]{1,0:T(8,128)(2,1)S(1)}, u32[]{:S(2)}, u32[]{:S(2)}) collective-permute-start(bf16[32,2560]{1,0:T(8,128)(2,1)S(1)} %get-tuple-element.33), channel_id=1, source_target_pairs={{0,2},{1,3},{2,0},{3,1},{4,6},{5,7},{6,4},{7,5},{8,10},{9,11},{10,... | collective-permute-start | bytes 491528 | tf_op jit(solution)/shard_map/ppermute | solution.py:378
  61.8 10.5 %collective-permute-start.11 = (bf16[32,2560]{1,0:T(8,128)(2,1)S(1)}, bf16[32,2560]{1,0:T(8,128)(2,1)S(1)}, u32[]{:S(2)}, u32[]{:S(2)}) collective-permute-start(bf16[32,2560]{1,0:T(8,128)(2,1)S(1)} %add_convert_fusion), channel_id=1, source_target_pairs={{0,4},{1,5},{2,6},{3,7},{4,0},{5,1},{6,2},{7,3},{8,12},{9,13},{10,... | collective-permute-start | bytes 491528 | tf_op jit(solution)/shard_map/ppermute | solution.py:378

commit v9 on v8

--- a/solution.py
+++ b/solution.py
@@ -411,7 +411,7 @@
                 transcendentals=0,
             ),
             name=f"projection_{cut}",
-        )(index, *attended, *weights)
+        )(index, *attended, *[pltpu.with_memory_space_constraint(w, VMEM) for w in weights])
         sums = {j: part for j, part in enumerate(partial_sums)}
         bit = 1
         while bit < chips:

time: 73.6 us -> 73.6 us (level)
  no operation moved by 1% of the time
where the time goes in v9:
time: 73.6 us; the launch traced here: 73.2 us
  waiting for transfers between devices  26.1 us (35%)
  starting transfers between devices  17.8 us (24%)
  local copies, waits for them, and re-layouts  12.8 us (17%)
  Pallas kernels  12.3 us (17%)
  other arithmetic  2.1 us (3%)
  between operations  2.09 us (3%)
    ppermute x7, waiting for transfers between devices, across(): return lax.ppermute(value, axis, [(i, i ^ distance) for i in range(n)])  14.4 us
    unnamed x19, local copies, waits for them, and re-layouts  12.2 us
    all_to_all x1, waiting for transfers between devices, spread_attention(): lax.all_to_all(sends, ('frame', 'seq'), split_axis=0, concat_axis=0, tile...  9.19 us
    all_to_all x1, starting transfers between devices, spread_attention(): lax.all_to_all(sends, ('frame', 'seq'), split_axis=0, concat_axis=0, tile...  6.96 us
    ppermute x7, starting transfers between devices, across(): return lax.ppermute(value, axis, [(i, i ^ distance) for i in range(n)])  6.51 us
    ppermute x5, starting transfers between devices, across(): return lax.ppermute(value, axis, [(i, i ^ distance) for i in range(size)])  4.3 us
    pallas_call x2, Pallas kernels, attend(): pl.pallas_call(functools.partial(spread_attention_kernel, n, frames, pick...  4.2 us
    pallas_call x2, Pallas kernels, shards(): pl.pallas_call(functools.partial(projection_kernel, chips, sources, cut *...  2.91 us
  transfers between devices with their start and end apart: 13, of which 8 were waited for; matrix products, arithmetic and copies ran while one was open for 3% of the time, Pallas kernels for 11%

profile of v9, /device:TPU:0, one launch (start us, length us, event | category | flops | bytes accessed | tf_op | source)
XLA Modules:
  0.0 73.2 jit_solution(12825107305863528277)
XLA Ops:
  0.5 2.3 %norm.1 = bf16[32,32,384]{2,1,0:T(8,128)(2,1)} custom-call(bf16[32,4096]{1,0:T(8,128)(2,1)} %bitcast.14, bf16[32,4096]{1,0:T(8,128)(2,1)} %bitcast.15, bf16[32,4096]{1,0:T(8,128)(2,1)} %bitcast.16, f32[1,4096]{1,0:T(1,128)} %bitcast.18, f32[1,4096]{1,0:T(1,128)} %bitcast.19), custom_call_target="tpu_custom_call" | custom-call | tf_op jit(solution)/shard_map/norm/pallas_call | solution.py:221
  2.8 7.0 %all-to-all-start = ((bf16[32,32,384]{2,1,0:T(8,128)(2,1)}), bf16[32,32,384]{2,1,0:T(8,128)(2,1)S(1)}, u32[]{:S(2)}, u32[]{:S(2)}) async-start(bf16[32,32,384]{2,1,0:T(8,128)(2,1)} %norm.1), calls=%async_computation | async-start | bytes 1572864 | tf_op jit(solution)/shard_map/all_to_all | solution.py:228
  9.8 2.5 %copy-done.4 = bf16[512,5120]{1,0:T(8,128)(2,1)S(1)} copy-done((bf16[512,5120]{1,0:T(8,128)(2,1)S(1)}, bf16[512,5120]{1,0:T(8,128)(2,1)}, u32[]{:S(2)}) %copy-start.4) | copy-done | bytes 5242904
  12.6 2.3 %copy-done = bf16[512,5120]{1,0:T(8,128)(2,1)} copy-done((bf16[512,5120]{1,0:T(8,128)(2,1)}, bf16[512,5120]{1,0:T(8,128)(2,1)S(1)}, u32[]{:S(2)}) %copy-start) | copy-done | bytes 5242904
  17.6 2.5 %stage_other.1.refs_5_ = bf16[512,5120]{1,0:T(8,128)(2,1)S(1)} custom-call(bf16[512,5120]{1,0:T(8,128)(2,1)} %collective-permute-done.weight_ref), custom_call_target="tpu_custom_call" | custom-call | bytes 10485760 | tf_op jit(solution)/shard_map/stage_other/pallas_call | solution.py:111
  20.1 2.4 %copy-done.2 = bf16[512,5120]{1,0:T(8,128)(2,1)} copy-done((bf16[512,5120]{1,0:T(8,128)(2,1)}, bf16[512,5120]{1,0:T(8,128)(2,1)S(1)}, u32[]{:S(2)}) %copy-start.2) | copy-done | bytes 5242904
  22.5 9.2 %all-to-all-done.rows_ref = bf16[32,32,384]{2,1,0:T(8,128)(2,1)S(1)} async-done(((bf16[32,32,384]{2,1,0:T(8,128)(2,1)}), bf16[32,32,384]{2,1,0:T(8,128)(2,1)S(1)}, u32[]{:S(2)}, u32[]{:S(2)}) %all-to-all-start) | async-done | bytes 786464 | tf_op jit(solution)/shard_map/all_to_all | solution.py:228
  31.7 2.8 %attention_far.1 = (bf16[3,128,128]{2,1,0:T(8,128)(2,1)S(1)}, bf16[3,128,128]{2,1,0:T(8,128)(2,1)S(1)}) custom-call(s32[6]{0:T(128)S(1)} %pad_add_fusion.1.index_ref, bf16[32,32,384]{2,1,0:T(8,128)(2,1)S(1)} %all-to-all-done.rows_ref), custom_call_target="tpu_custom_call" | custom-call | flops 402653184 | bytes 1048576 | tf_op jit(solution)/shard_map/attention_far/pallas_call | solution.py:237
  34.6 1.4 %attention_near.1 = (bf16[1,128,128]{2,1,0:T(8,128)(2,1)S(1)}, bf16[1,128,128]{2,1,0:T(8,128)(2,1)S(1)}) custom-call(s32[6]{0:T(128)S(1)} %pad_add_fusion.1.index_ref, bf16[32,32,384]{2,1,0:T(8,128)(2,1)S(1)} %all-to-all-done.rows_ref), custom_call_target="tpu_custom_call" | custom-call | flops 134217728 | bytes 1048576 | tf_op jit(solution)/shard_map/attention_near/pallas_call | solution.py:237
  37.2 1.4 %collective-permute-start.4 = (bf16[2,128,128]{2,1,0:T(8,128)(2,1)S(1)}, bf16[2,128,128]{2,1,0:T(8,128)(2,1)S(1)}, u32[]{:S(2)}, u32[]{:S(2)}) collective-permute-start(bf16[2,128,128]{2,1,0:T(8,128)(2,1)S(1)} %pad_maximum_fusion.1), channel_id=1, source_target_pairs={{0,16},{8,24},{16,0},{24,8},{1,17},{9,25},{17,1},{25,9},{2,18},{10... | collective-permute-start | bytes 196616 | tf_op jit(solution)/shard_map/ppermute | solution.py:254
  38.6 1.7 %collective-permute-start.3 = (bf16[2,128,128]{2,1,0:T(8,128)(2,1)S(1)}, bf16[2,128,128]{2,1,0:T(8,128)(2,1)S(1)}, u32[]{:S(2)}, u32[]{:S(2)}) collective-permute-start(bf16[2,128,128]{2,1,0:T(8,128)(2,1)S(1)} %pad_maximum_fusion), channel_id=1, source_target_pairs={{0,8},{8,0},{16,24},{24,16},{1,9},{9,1},{17,25},{25,17},{2,10},{10... | collective-permute-start | bytes 196616 | tf_op jit(solution)/shard_map/ppermute | solution.py:254
  40.3 2.2 %collective-permute-done.5.refs_3_ = bf16[2,128,128]{2,1,0:T(8,128)(2,1)S(1)} collective-permute-done((bf16[2,128,128]{2,1,0:T(8,128)(2,1)S(1)}, bf16[2,128,128]{2,1,0:T(8,128)(2,1)S(1)}, u32[]{:S(2)}, u32[]{:S(2)}) %collective-permute-start.5) | collective-permute-done | bytes 65568 | tf_op jit(solution)/shard_map/ppermute | solution.py:254
  42.9 2.5 %copy-done.1 = bf16[512,5120]{1,0:T(8,128)(2,1)S(1)} copy-done((bf16[512,5120]{1,0:T(8,128)(2,1)S(1)}, bf16[512,5120]{1,0:T(8,128)(2,1)}, u32[]{:S(2)}) %copy-start.1) | copy-done | bytes 5242904
  45.4 2.5 %copy-done.3 = bf16[512,5120]{1,0:T(8,128)(2,1)S(1)} copy-done((bf16[512,5120]{1,0:T(8,128)(2,1)S(1)}, bf16[512,5120]{1,0:T(8,128)(2,1)}, u32[]{:S(2)}) %copy-start.3) | copy-done | bytes 5242904
  47.9 1.5 %projection_0.1 = (f32[32,2560]{1,0:T(8,128)S(1)}, bf16[32,2560]{1,0:T(8,128)(2,1)S(1)}, f32[32,2560]{1,0:T(8,128)S(1)}, bf16[32,2560]{1,0:T(8,128)(2,1)S(1)}) custom-call(s32[2]{0:T(128)S(1)} %pad_add_fusion.index_ref, bf16[2,128,128]{2,1,0:T(8,128)(2,1)S(1)} %constant_dynamic-update-slice_fusion.refs_0_, ...), custom_call_target="tpu_custom_call" | custom-call | flops 671088640 | bytes 5898240 | tf_op jit(solution)/shard_map/projection_0/pallas_call | solution.py:398
  49.6 0.9 %dynamic-slice_convert_fusion = f32[1,5120]{1,0:T(1,128)S(1)} fusion(bf16[64,5120]{1,0:T(8,128)(2,1)} %param.19, s32[]{:T(128)S(6)} %select_n.20), kind=kLoop, calls=%fused_computation.11 | loop fusion | flops 5120 | bytes 30724 | tf_op jit(solution)/shard_map/mul | solution.py:432
  50.5 1.5 %projection_1.1 = (f32[32,2560]{1,0:T(8,128)S(1)}, bf16[32,2560]{1,0:T(8,128)(2,1)S(1)}, f32[32,2560]{1,0:T(8,128)S(1)}, bf16[32,2560]{1,0:T(8,128)(2,1)S(1)}) custom-call(s32[2]{0:T(128)S(1)} %pad_add_fusion.index_ref, bf16[2,128,128]{2,1,0:T(8,128)(2,1)S(1)} %constant_dynamic-update-slice_fusion.refs_0_, ...), custom_call_target="tpu_custom_call" | custom-call | flops 671088640 | bytes 5898240 | tf_op jit(solution)/shard_map/projection_1/pallas_call | solution.py:398
  52.0 1.9 %collective-permute-start.9 = (bf16[32,2560]{1,0:T(8,128)(2,1)S(1)}, bf16[32,2560]{1,0:T(8,128)(2,1)S(1)}, u32[]{:S(2)}, u32[]{:S(2)}) collective-permute-start(bf16[32,2560]{1,0:T(8,128)(2,1)S(1)} %get-tuple-element.32), channel_id=1, source_target_pairs={{0,2},{1,3},{2,0},{3,1},{4,6},{5,7},{6,4},{7,5},{8,10},{9,11},{10,... | collective-permute-start | bytes 491528 | tf_op jit(solution)/shard_map/ppermute | solution.py:378
  53.9 1.9 %collective-permute-done.6 = bf16[32,2560]{1,0:T(8,128)(2,1)S(1)} collective-permute-done((bf16[32,2560]{1,0:T(8,128)(2,1)S(1)}, bf16[32,2560]{1,0:T(8,128)(2,1)S(1)}, u32[]{:S(2)}, u32[]{:S(2)}) %collective-permute-start.6) | collective-permute-done | bytes 163872 | tf_op jit(solution)/shard_map/ppermute | solution.py:378
  55.8 1.7 %collective-permute-start.8 = (bf16[32,2560]{1,0:T(8,128)(2,1)S(1)}, bf16[32,2560]{1,0:T(8,128)(2,1)S(1)}, u32[]{:S(2)}, u32[]{:S(2)}) collective-permute-start(bf16[32,2560]{1,0:T(8,128)(2,1)S(1)} %add_convert_fusion.1), channel_id=1, source_target_pairs={{0,4},{1,5},{2,6},{3,7},{4,0},{5,1},{6,2},{7,3},{8,12},{9,13},{10,... | collective-permute-start | bytes 491528 | tf_op jit(solution)/shard_map/ppermute | solution.py:378
  57.5 4.2 %collective-permute-done.9 = bf16[32,2560]{1,0:T(8,128)(2,1)S(1)} collective-permute-done((bf16[32,2560]{1,0:T(8,128)(2,1)S(1)}, bf16[32,2560]{1,0:T(8,128)(2,1)S(1)}, u32[]{:S(2)}, u32[]{:S(2)}) %collective-permute-start.9) | collective-permute-done | bytes 163872 | tf_op jit(solution)/shard_map/ppermute | solution.py:378
  61.8 2.2 %collective-permute-start.11 = (bf16[32,2560]{1,0:T(8,128)(2,1)S(1)}, bf16[32,2560]{1,0:T(8,128)(2,1)S(1)}, u32[]{:S(2)}, u32[]{:S(2)}) collective-permute-start(bf16[32,2560]{1,0:T(8,128)(2,1)S(1)} %add_convert_fusion), channel_id=1, source_target_pairs={{0,4},{1,5},{2,6},{3,7},{4,0},{5,1},{6,2},{7,3},{8,12},{9,13},{10,... | collective-permute-start | bytes 491528 | tf_op jit(solution)/shard_map/ppermute | solution.py:378
  64.0 4.7 %collective-permute-done.7 = bf16[32,2560]{1,0:T(8,128)(2,1)S(1)} collective-permute-done((bf16[32,2560]{1,0:T(8,128)(2,1)S(1)}, bf16[32,2560]{1,0:T(8,128)(2,1)S(1)}, u32[]{:S(2)}, u32[]{:S(2)}) %collective-permute-start.7) | collective-permute-done | bytes 163872 | tf_op jit(solution)/shard_map/ppermute | solution.py:378
  68.8 3.5 %collective-permute-done.10 = bf16[32,2560]{1,0:T(8,128)(2,1)S(1)} collective-permute-done((bf16[32,2560]{1,0:T(8,128)(2,1)S(1)}, bf16[32,2560]{1,0:T(8,128)(2,1)S(1)}, u32[]{:S(2)}, u32[]{:S(2)}) %collective-permute-start.10) | collective-permute-done | bytes 163872 | tf_op jit(solution)/shard_map/ppermute | solution.py:378
  (44 shorter events, 4.6 us)
Async XLA Ops:
  0.0 17.6 %collective-permute-start = (bf16[512,5120]{1,0:T(8,128)(2,1)}, bf16[512,5120]{1,0:T(8,128)(2,1)}, u32[]{:S(2)}, u32[]{:S(2)}) collective-permute-start(bf16[512,5120]{1,0:T(8,128)(2,1)} %weight_ref.1), channel_id=1, source_target_pairs={{0,1},{1,0},{2,3},{3,2},{4,5},{5,4},{6,7},{7,6},{8,9},{9,8},{10,11... | collective-permute-start | bytes 15728648 | tf_op jit(solution)/shard_map/ppermute | solution.py:378
  2.8 28.9 %all-to-all-start = ((bf16[32,32,384]{2,1,0:T(8,128)(2,1)}), bf16[32,32,384]{2,1,0:T(8,128)(2,1)S(1)}, u32[]{:S(2)}, u32[]{:S(2)}) async-start(bf16[32,32,384]{2,1,0:T(8,128)(2,1)} %norm.1), calls=%async_computation | async-start | bytes 1572864 | tf_op jit(solution)/shard_map/all_to_all | solution.py:228
  9.7 2.5 %copy-start.4 = (bf16[512,5120]{1,0:T(8,128)(2,1)S(1)}, bf16[512,5120]{1,0:T(8,128)(2,1)}, u32[]{:S(2)}) copy-start(bf16[512,5120]{1,0:T(8,128)(2,1)} %weight_ref.1) | copy-start | bytes 15728644
  12.2 2.7 %copy-start.8 = (s32[4]{0:T(128)S(1)}, s32[4]{0:T(128)}, u32[]{:S(2)}) copy-start(s32[4]{0:T(128)} %param.20) | copy-start | bytes 52
  12.2 5.3 %copy-start.7 = (s32[4]{0:T(128)S(1)}, s32[4]{0:T(128)}, u32[]{:S(2)}) copy-start(s32[4]{0:T(128)} %param.21) | copy-start | bytes 52
  12.6 2.3 %copy-start = (bf16[512,5120]{1,0:T(8,128)(2,1)}, bf16[512,5120]{1,0:T(8,128)(2,1)S(1)}, u32[]{:S(2)}) copy-start(bf16[512,5120]{1,0:T(8,128)(2,1)S(1)} %stage_own.1.refs_4_) | copy-start | bytes 15728644
  20.1 2.4 %copy-start.2 = (bf16[512,5120]{1,0:T(8,128)(2,1)}, bf16[512,5120]{1,0:T(8,128)(2,1)S(1)}, u32[]{:S(2)}) copy-start(bf16[512,5120]{1,0:T(8,128)(2,1)S(1)} %stage_other.1.refs_5_) | copy-start | bytes 15728644
  34.5 2.1 %collective-permute-start.2 = (bf16[3,128,128]{2,1,0:T(8,128)(2,1)S(1)}, bf16[3,128,128]{2,1,0:T(8,128)(2,1)S(1)}, u32[]{:S(2)}, u32[]{:S(2)}) collective-permute-start(bf16[3,128,128]{2,1,0:T(8,128)(2,1)S(1)} %get-tuple-element.24), channel_id=1, source_target_pairs={{0,1},{1,0},{2,3},{3,2},{4,5},{5,4},{6,7},{7,6},{8,9},{9,8},{10,11... | collective-permute-start | bytes 294920 | tf_op jit(solution)/shard_map/ppermute | solution.py:254
  36.0 4.3 %collective-permute-start.1 = (bf16[1,128,128]{2,1,0:T(8,128)(2,1)S(1)}, bf16[1,128,128]{2,1,0:T(8,128)(2,1)S(1)}, u32[]{:S(2)}, u32[]{:S(2)}) collective-permute-start(bf16[1,128,128]{2,1,0:T(8,128)(2,1)S(1)} %get-tuple-element.22), channel_id=1, source_target_pairs={{0,1},{1,0},{2,3},{3,2},{4,5},{5,4},{6,7},{7,6},{8,9},{9,8},{10,11... | collective-permute-start | bytes 98312 | tf_op jit(solution)/shard_map/ppermute | solution.py:254
  36.6 5.9 %collective-permute-start.5 = (bf16[2,128,128]{2,1,0:T(8,128)(2,1)S(1)}, bf16[2,128,128]{2,1,0:T(8,128)(2,1)S(1)}, u32[]{:S(2)}, u32[]{:S(2)}) collective-permute-start(bf16[2,128,128]{2,1,0:T(8,128)(2,1)S(1)} %pad_maximum_fusion.2), channel_id=1, source_target_pairs={{0,24},{8,16},{16,8},{24,0},{1,25},{9,17},{17,9},{25,1},{2,26},{10... | collective-permute-start | bytes 196616 | tf_op jit(solution)/shard_map/ppermute | solution.py:254
  37.2 5.5 %collective-permute-start.4 = (bf16[2,128,128]{2,1,0:T(8,128)(2,1)S(1)}, bf16[2,128,128]{2,1,0:T(8,128)(2,1)S(1)}, u32[]{:S(2)}, u32[]{:S(2)}) collective-permute-start(bf16[2,128,128]{2,1,0:T(8,128)(2,1)S(1)} %pad_maximum_fusion.1), channel_id=1, source_target_pairs={{0,16},{8,24},{16,0},{24,8},{1,17},{9,25},{17,1},{25,9},{2,18},{10... | collective-permute-start | bytes 196616 | tf_op jit(solution)/shard_map/ppermute | solution.py:254
  38.6 4.3 %collective-permute-start.3 = (bf16[2,128,128]{2,1,0:T(8,128)(2,1)S(1)}, bf16[2,128,128]{2,1,0:T(8,128)(2,1)S(1)}, u32[]{:S(2)}, u32[]{:S(2)}) collective-permute-start(bf16[2,128,128]{2,1,0:T(8,128)(2,1)S(1)} %pad_maximum_fusion), channel_id=1, source_target_pairs={{0,8},{8,0},{16,24},{24,16},{1,9},{9,1},{17,25},{25,17},{2,10},{10... | collective-permute-start | bytes 196616 | tf_op jit(solution)/shard_map/ppermute | solution.py:254
  40.3 10.2 %copy-start.6 = (bf16[5120]{0:T(1024)(128)(2,1)S(1)}, bf16[5120]{0:T(1024)(128)(2,1)}, u32[]{:S(2)}) copy-start(bf16[5120]{0:T(1024)(128)(2,1)} %param.18) | copy-start | bytes 30724
  42.9 2.5 %copy-start.1 = (bf16[512,5120]{1,0:T(8,128)(2,1)S(1)}, bf16[512,5120]{1,0:T(8,128)(2,1)}, u32[]{:S(2)}) copy-start(bf16[512,5120]{1,0:T(8,128)(2,1)} %copy-done) | copy-start | bytes 15728644
  45.4 2.5 %copy-start.3 = (bf16[512,5120]{1,0:T(8,128)(2,1)S(1)}, bf16[512,5120]{1,0:T(8,128)(2,1)}, u32[]{:S(2)}) copy-start(bf16[512,5120]{1,0:T(8,128)(2,1)} %copy-done.2) | copy-start | bytes 15728644
  49.3 6.5 %collective-permute-start.6 = (bf16[32,2560]{1,0:T(8,128)(2,1)S(1)}, bf16[32,2560]{1,0:T(8,128)(2,1)S(1)}, u32[]{:S(2)}, u32[]{:S(2)}) collective-permute-start(bf16[32,2560]{1,0:T(8,128)(2,1)S(1)} %get-tuple-element.27), channel_id=1, source_target_pairs={{0,2},{1,3},{2,0},{3,1},{4,6},{5,7},{6,4},{7,5},{8,10},{9,11},{10,... | collective-permute-start | bytes 491528 | tf_op jit(solution)/shard_map/ppermute | solution.py:378
  50.5 21.8 %copy-start.5 = (bf16[1,32,5120]{2,1,0:T(8,128)(2,1)S(1)}, bf16[1,32,5120]{2,1,0:T(8,128)(2,1)}, u32[]{:S(2)}) copy-start(bf16[1,32,5120]{2,1,0:T(8,128)(2,1)} %param.11) | copy-start | bytes 983044
  52.0 9.8 %collective-permute-start.9 = (bf16[32,2560]{1,0:T(8,128)(2,1)S(1)}, bf16[32,2560]{1,0:T(8,128)(2,1)S(1)}, u32[]{:S(2)}, u32[]{:S(2)}) collective-permute-start(bf16[32,2560]{1,0:T(8,128)(2,1)S(1)} %get-tuple-element.32), channel_id=1, source_target_pairs={{0,2},{1,3},{2,0},{3,1},{4,6},{5,7},{6,4},{7,5},{8,10},{9,11},{10,... | collective-permute-start | bytes 491528 | tf_op jit(solution)/shard_map/ppermute | solution.py:378
  55.8 12.9 %collective-permute-start.7 = (bf16[32,2560]{1,0:T(8,128)(2,1)S(1)}, bf16[32,2560]{1,0:T(8,128)(2,1)S(1)}, u32[]{:S(2)}, u32[]{:S(2)}) collective-permute-start(bf16[32,2560]{1,0:T(8,128)(2,1)S(1)} %get-tuple-element.28), channel_id=1, source_target_pairs={{0,2},{1,3},{2,0},{3,1},{4,6},{5,7},{6,4},{7,5},{8,10},{9,11},{10,... | collective-permute-start | bytes 491528 | tf_op jit(solution)/shard_map/ppermute | solution.py:378
  55.8 12.9 %collective-permute-start.8 = (bf16[32,2560]{1,0:T(8,128)(2,1)S(1)}, bf16[32,2560]{1,0:T(8,128)(2,1)S(1)}, u32[]{:S(2)}, u32[]{:S(2)}) collective-permute-start(bf16[32,2560]{1,0:T(8,128)(2,1)S(1)} %add_convert_fusion.1), channel_id=1, source_target_pairs={{0,4},{1,5},{2,6},{3,7},{4,0},{5,1},{6,2},{7,3},{8,12},{9,13},{10,... | collective-permute-start | bytes 491528 | tf_op jit(solution)/shard_map/ppermute | solution.py:378
  61.7 10.5 %collective-permute-start.10 = (bf16[32,2560]{1,0:T(8,128)(2,1)S(1)}, bf16[32,2560]{1,0:T(8,128)(2,1)S(1)}, u32[]{:S(2)}, u32[]{:S(2)}) collective-permute-start(bf16[32,2560]{1,0:T(8,128)(2,1)S(1)} %get-tuple-element.33), channel_id=1, source_target_pairs={{0,2},{1,3},{2,0},{3,1},{4,6},{5,7},{6,4},{7,5},{8,10},{9,11},{10,... | collective-permute-start | bytes 491528 | tf_op jit(solution)/shard_map/ppermute | solution.py:378
  61.8 10.5 %collective-permute-start.11 = (bf16[32,2560]{1,0:T(8,128)(2,1)S(1)}, bf16[32,2560]{1,0:T(8,128)(2,1)S(1)}, u32[]{:S(2)}, u32[]{:S(2)}) collective-permute-start(bf16[32,2560]{1,0:T(8,128)(2,1)S(1)} %add_convert_fusion), channel_id=1, source_target_pairs={{0,4},{1,5},{2,6},{3,7},{4,0},{5,1},{6,2},{7,3},{8,12},{9,13},{10,... | collective-permute-start | bytes 491528 | tf_op jit(solution)/shard_map/ppermute | solution.py:378

commit v10 on v5

--- a/solution.py
+++ b/solution.py
@@ -142,24 +142,24 @@
             out_ref[f * n + s, :, 2 * part :] = value_ref[:, cols]
 
 
-def spread_attention_kernel(n, frames, picked, index_ref, order_ref, rows_ref, mine_ref, given_ref, both):
+def spread_attention_kernel(n, frames, picked, index_ref, rows_ref, mine_ref, given_ref, both):
     slot = index_ref[0]
     core = index_ref[1]
     rows = rows_ref.shape[1]
     part = mine_ref.shape[2]
     frame_rows = n * rows
     factor = (HD ** (-0.5)) * LOG2E
-    step = min(frame_rows, 128)
+    step = min(frame_rows, 256)
     for h in range(part // HD):
         cols = slice(h * HD, (h + 1) * HD)
         keys = rows_ref[:, :, part + h * HD : part + (h + 1) * HD].reshape(-1, HD)
         values = rows_ref[:, :, 2 * part + h * HD : 2 * part + (h + 1) * HD].reshape(-1, HD)
         for place, distance in enumerate(picked):
             frame = slot ^ distance
-            rank = order_ref[frame]
+            rank = index_ref[2 + frame]
             hidden = jnp.concatenate(
                 [
-                    jnp.full((1, frame_rows), jnp.where(order_ref[f] <= rank, 0.0, -1e30), jnp.float32)
+                    jnp.full((1, frame_rows), jnp.where(index_ref[2 + f] <= rank, 0.0, -1e30), jnp.float32)
                     for f in range(frames)
                 ],
                 axis=1,
@@ -208,14 +208,14 @@
     keys = frames * frame_rows
     me = lax.axis_index("seq").astype(jnp.int32)
     slot = lax.axis_index("frame").astype(jnp.int32)
-    index = jnp.stack([slot, me % 2])
+    index = jnp.concatenate([jnp.stack([slot, me % 2]), slot_order])
 
     def attend(picked, name):
         count = len(picked)
         return pl.pallas_call(
             functools.partial(spread_attention_kernel, n, frames, picked),
             out_shape=[jax.ShapeDtypeStruct((count, frame_rows // 2, part), jnp.bfloat16)] * 2,
-            in_specs=[smem, smem, vmem],
+            in_specs=[smem, vmem],
             out_specs=[vmem] * 2,
             scratch_shapes=[pltpu.VMEM((2, count, frame_rows // 2, part), jnp.bfloat16)],
             compiler_params=pltpu.CompilerParams(vmem_limit_bytes=8 * 2**20 + 6 * 128 * keys * 4),
@@ -225,7 +225,7 @@
                 transcendentals=count * frame_rows * keys * (part // HD),
             ),
             name=name,
-        )(index, slot_order, held)
+        )(index, held)
 
     def across(value, axis, distance):
         size = n if axis == "seq" else frames
@@ -239,7 +239,7 @@
     found = {0: jnp.concatenate([near_mine, near_got], axis=0)}
     for place, d in enumerate(far):
         found[d] = across(jnp.stack([far_mine[place], far_got[place]]), "frame", d)
-    return [found[d] for d in range(frames)]
+    return [found[d] for d in range(frames)], held
 
 
 def gathered_attention(query_rows, key_rows, value_rows, gain_query, gain_key, slot_order):
@@ -326,7 +326,7 @@
         ),
         name="attention",
     )(slot_array, slot_order, *queries, *pieces)
-    return [jnp.stack([even, across(odd, "seq", 1)])]
+    return [jnp.stack([even, across(odd, "seq", 1)])], halves[1]
 
 
 def shards(
@@ -358,11 +358,11 @@
     def after(value, *earlier):
         return lax.optimization_barrier((value, *earlier))[0]
 
-    other_weight = across(out_weight, "seq", 1)
     spread = (width // HD) % frames == 0
-    attended = (spread_attention if spread else gathered_attention)(
+    attended, travelled = (spread_attention if spread else gathered_attention)(
         query_rows[0], key_rows[0], value_rows[0], gain_query, gain_key, slot_order
     )
+    other_weight = across(after(out_weight, travelled), "seq", 1)
     index = jnp.stack([me // 2, slot]) if spread else jnp.zeros((2,), jnp.int32)
 
     cuts = 2

time: 72.9 us -> 76 us (1.043)
  blocking collectives: 0 us -> 29.3 us
  waiting for transfers between devices: 36 us -> 18.5 us
  starting transfers between devices: 17.7 us -> 10.2 us
  Pallas kernels: 12.8 us -> 12 us
    all_to_all x0 -> x1, blocking collectives: none -> 29.3 us  [spread_attention(): lax.all_to_all(sends, ('frame', 'seq'), split_axis=0, concat_axis=0, tile...]
    all_to_all x1 -> x0, waiting for transfers between devices: 18.7 us -> none  [spread_attention(): lax.all_to_all(sends, ('frame', 'seq'), split_axis=0, concat_axis=0, tile...]
    all_to_all x1 -> x0, starting transfers between devices: 6.96 us -> none  [spread_attention(): lax.all_to_all(sends, ('frame', 'seq'), split_axis=0, concat_axis=0, tile...]
    ppermute x5, waiting for transfers between devices: 2.59 us -> 3.71 us  [across(): return lax.ppermute(value, axis, [(i, i ^ distance) for i in range(size)])]
    pallas_call x2, Pallas kernels: 4.18 us -> 3.37 us  [attend(): pl.pallas_call(functools.partial(spread_attention_kernel, n, frames, pick...]
  transfers between devices with their start and end apart: 13 -> 12, of which waited for: 8 -> 8; matrix products, arithmetic and copies ran while one was open for 3% -> 4% of each run, Pallas kernels for 13% -> 9%
where the time goes in v10:
time: 76 us; the launch traced here: 75.7 us
  blocking collectives  29.3 us (39%)
  waiting for transfers between devices  18.5 us (24%)
  Pallas kernels  12 us (16%)
  starting transfers between devices  10.2 us (13%)
  other arithmetic  2.74 us (4%)
  between operations  1.83 us (2%)
  local copies, waits for them, and re-layouts  1.28 us (2%)
    all_to_all x1, blocking collectives, spread_attention(): lax.all_to_all(sends, ('frame', 'seq'), split_axis=0, concat_axis=0, tile...  29.3 us
    ppermute x7, waiting for transfers between devices, across(): return lax.ppermute(value, axis, [(i, i ^ distance) for i in range(n)])  14.8 us
    pallas_call x2, Pallas kernels, shards(): pl.pallas_call(functools.partial(projection_kernel, chips, sources), grid...  6.29 us
    ppermute x7, starting transfers between devices, across(): return lax.ppermute(value, axis, [(i, i ^ distance) for i in range(n)])  5.87 us
    ppermute x5, starting transfers between devices, across(): return lax.ppermute(value, axis, [(i, i ^ distance) for i in range(size)])  4.33 us
    ppermute x5, waiting for transfers between devices, across(): return lax.ppermute(value, axis, [(i, i ^ distance) for i in range(size)])  3.71 us
    pallas_call x2, Pallas kernels, attend(): pl.pallas_call(functools.partial(spread_attention_kernel, n, frames, pick...  3.37 us
    pallas_call x1, Pallas kernels, spread_attention(): pl.pallas_call(functools.partial(spread_norm_kernel, n, frames), out_shap...  2.3 us
  transfers between devices with their start and end apart: 12, of which 8 were waited for; matrix products, arithmetic and copies ran while one was open for 4% of the time, Pallas kernels for 9%

profile of v10, /device:TPU:0, one launch (start us, length us, event | category | flops | bytes accessed | tf_op | source)
XLA Modules:
  0.0 75.7 jit_solution(6542517632121293251)
XLA Ops:
  0.0 2.3 %norm.1 = bf16[32,32,384]{2,1,0:T(8,128)(2,1)} custom-call(bf16[32,4096]{1,0:T(8,128)(2,1)} %bitcast.14, bf16[32,4096]{1,0:T(8,128)(2,1)} %bitcast.15, bf16[32,4096]{1,0:T(8,128)(2,1)} %bitcast.16, f32[1,4096]{1,0:T(1,128)} %bitcast.18, f32[1,4096]{1,0:T(1,128)} %bitcast.19), custom_call_target="tpu_custom_call" | custom-call | tf_op jit(solution)/shard_map/norm/pallas_call | solution.py:200
  2.3 29.3 %all_to_all.5.rows_ref = bf16[32,32,384]{2,1,0:T(8,128)(2,1)S(1)} all-to-all(bf16[32,32,384]{2,1,0:T(8,128)(2,1)} %norm.1), channel_id=1, replica_groups=mesh['frame'=4,'seq'=8] {'frame','seq'}, dimensions={0} | all-to-all | bytes 1572864 | tf_op jit(solution)/shard_map/all_to_all | solution.py:207
  31.6 1.2 %dynamic_slice.8 = s32[1]{0:T(128)} dynamic-slice(s32[4]{0:T(128)} %param.20, s32[]{:T(128)S(6)} %select_n.19), dynamic_slice_sizes={1} | dynamic-slice | bytes 12 | tf_op jit(solution)/shard_map/jit(dynamic_index_in_dim)/dynamic_slice | solution.py:409
  34.6 0.7 pad_add_fusion.1.index_ref
  35.3 2.2 %attention_far.1 = (bf16[3,128,128]{2,1,0:T(8,128)(2,1)S(1)}, bf16[3,128,128]{2,1,0:T(8,128)(2,1)S(1)}) custom-call(s32[6]{0:T(128)S(1)} %pad_add_fusion.1.index_ref, bf16[32,32,384]{2,1,0:T(8,128)(2,1)S(1)} %all_to_all.5.rows_ref), custom_call_target="tpu_custom_call" | custom-call | flops 402653184 | bytes 1048576 | tf_op jit(solution)/shard_map/attention_far/pallas_call | solution.py:215
  37.5 0.6 collective-permute-start.1
  38.1 1.2 %attention_near.1 = (bf16[1,128,128]{2,1,0:T(8,128)(2,1)S(1)}, bf16[1,128,128]{2,1,0:T(8,128)(2,1)S(1)}) custom-call(s32[6]{0:T(128)S(1)} %pad_add_fusion.1.index_ref, bf16[32,32,384]{2,1,0:T(8,128)(2,1)S(1)} %all_to_all.5.rows_ref), custom_call_target="tpu_custom_call" | custom-call | flops 134217728 | bytes 1048576 | tf_op jit(solution)/shard_map/attention_near/pallas_call | solution.py:215
  39.4 1.0 %collective-permute-done.1 = bf16[3,128,128]{2,1,0:T(8,128)(2,1)S(1)} collective-permute-done((bf16[3,128,128]{2,1,0:T(8,128)(2,1)S(1)}, bf16[3,128,128]{2,1,0:T(8,128)(2,1)S(1)}, u32[]{:S(2)}, u32[]{:S(2)}) %collective-permute-start.1) | collective-permute-done | bytes 98336 | tf_op jit(solution)/shard_map/ppermute | solution.py:232
  40.4 0.6 collective-permute-start.4
  41.0 1.5 %collective-permute-start.3 = (bf16[2,128,128]{2,1,0:T(8,128)(2,1)S(1)}, bf16[2,128,128]{2,1,0:T(8,128)(2,1)S(1)}, u32[]{:S(2)}, u32[]{:S(2)}) collective-permute-start(bf16[2,128,128]{2,1,0:T(8,128)(2,1)S(1)} %pad_maximum_fusion.1), channel_id=1, source_target_pairs={{0,16},{8,24},{16,0},{24,8},{1,17},{9,25},{17,1},{25,9},{2,18},{10... | collective-permute-start | bytes 196616 | tf_op jit(solution)/shard_map/ppermute | solution.py:232
  42.5 1.6 %collective-permute-start.2 = (bf16[2,128,128]{2,1,0:T(8,128)(2,1)S(1)}, bf16[2,128,128]{2,1,0:T(8,128)(2,1)S(1)}, u32[]{:S(2)}, u32[]{:S(2)}) collective-permute-start(bf16[2,128,128]{2,1,0:T(8,128)(2,1)S(1)} %pad_maximum_fusion), channel_id=1, source_target_pairs={{0,8},{8,0},{16,24},{24,16},{1,9},{9,1},{17,25},{25,17},{2,10},{10... | collective-permute-start | bytes 196616 | tf_op jit(solution)/shard_map/ppermute | solution.py:232
  44.1 2.2 %collective-permute-done.4.refs_3_ = bf16[2,128,128]{2,1,0:T(8,128)(2,1)S(1)} collective-permute-done((bf16[2,128,128]{2,1,0:T(8,128)(2,1)S(1)}, bf16[2,128,128]{2,1,0:T(8,128)(2,1)S(1)}, u32[]{:S(2)}, u32[]{:S(2)}) %collective-permute-start.4) | collective-permute-done | bytes 65568 | tf_op jit(solution)/shard_map/ppermute | solution.py:232
  46.5 0.3 collective-permute-done.2.refs_1_
  46.8 3.1 %projection_0.1 = (f32[32,2560]{1,0:T(8,128)S(1)}, bf16[32,2560]{1,0:T(8,128)(2,1)S(1)}, f32[32,2560]{1,0:T(8,128)S(1)}, bf16[32,2560]{1,0:T(8,128)(2,1)S(1)}) custom-call(s32[2]{0:T(128)S(1)} %pad_add_fusion.index_ref, bf16[2,128,128]{2,1,0:T(8,128)(2,1)S(1)} %constant_dynamic-update-slice_fusion.refs_0_, ...), custom_call_target="tpu_custom_call" | custom-call | flops 671088640 | bytes 5898240 | tf_op jit(solution)/shard_map/projection_0/pallas_call | solution.py:375
  50.1 0.9 %dynamic-slice_convert_fusion = f32[1,5120]{1,0:T(1,128)S(1)} fusion(bf16[64,5120]{1,0:T(8,128)(2,1)} %param.19, s32[]{:T(128)S(6)} %select_n.20), kind=kLoop, calls=%fused_computation.11 | loop fusion | flops 5120 | bytes 30724 | tf_op jit(solution)/shard_map/mul | solution.py:412
  51.0 3.2 %projection_1.1 = (f32[32,2560]{1,0:T(8,128)S(1)}, bf16[32,2560]{1,0:T(8,128)(2,1)S(1)}, f32[32,2560]{1,0:T(8,128)S(1)}, bf16[32,2560]{1,0:T(8,128)(2,1)S(1)}) custom-call(s32[2]{0:T(128)S(1)} %pad_add_fusion.index_ref, bf16[2,128,128]{2,1,0:T(8,128)(2,1)S(1)} %constant_dynamic-update-slice_fusion.refs_0_, ...), custom_call_target="tpu_custom_call" | custom-call | flops 671088640 | bytes 5898240 | tf_op jit(solution)/shard_map/projection_1/pallas_call | solution.py:375
  54.2 2.0 %collective-permute-start.9 = (bf16[32,2560]{1,0:T(8,128)(2,1)S(1)}, bf16[32,2560]{1,0:T(8,128)(2,1)S(1)}, u32[]{:S(2)}, u32[]{:S(2)}) collective-permute-start(bf16[32,2560]{1,0:T(8,128)(2,1)S(1)} %get-tuple-element.32), channel_id=1, source_target_pairs={{0,2},{1,3},{2,0},{3,1},{4,6},{5,7},{6,4},{7,5},{8,10},{9,11},{10,... | collective-permute-start | bytes 491528 | tf_op jit(solution)/shard_map/ppermute | solution.py:356
  56.4 1.6 %collective-permute-start.8 = (bf16[32,2560]{1,0:T(8,128)(2,1)S(1)}, bf16[32,2560]{1,0:T(8,128)(2,1)S(1)}, u32[]{:S(2)}, u32[]{:S(2)}) collective-permute-start(bf16[32,2560]{1,0:T(8,128)(2,1)S(1)} %add_convert_fusion.1), channel_id=1, source_target_pairs={{0,4},{1,5},{2,6},{3,7},{4,0},{5,1},{6,2},{7,3},{8,12},{9,13},{10,... | collective-permute-start | bytes 491528 | tf_op jit(solution)/shard_map/ppermute | solution.py:356
  57.9 8.8 %collective-permute-done.9 = bf16[32,2560]{1,0:T(8,128)(2,1)S(1)} collective-permute-done((bf16[32,2560]{1,0:T(8,128)(2,1)S(1)}, bf16[32,2560]{1,0:T(8,128)(2,1)S(1)}, u32[]{:S(2)}, u32[]{:S(2)}) %collective-permute-start.9) | collective-permute-done | bytes 163872 | tf_op jit(solution)/shard_map/ppermute | solution.py:356
  66.7 2.1 %collective-permute-start.11 = (bf16[32,2560]{1,0:T(8,128)(2,1)S(1)}, bf16[32,2560]{1,0:T(8,128)(2,1)S(1)}, u32[]{:S(2)}, u32[]{:S(2)}) collective-permute-start(bf16[32,2560]{1,0:T(8,128)(2,1)S(1)} %add_convert_fusion), channel_id=1, source_target_pairs={{0,4},{1,5},{2,6},{3,7},{4,0},{5,1},{6,2},{7,3},{8,12},{9,13},{10,... | collective-permute-start | bytes 491528 | tf_op jit(solution)/shard_map/ppermute | solution.py:356
  68.8 1.0 %collective-permute-done.7 = bf16[32,2560]{1,0:T(8,128)(2,1)S(1)} collective-permute-done((bf16[32,2560]{1,0:T(8,128)(2,1)S(1)}, bf16[32,2560]{1,0:T(8,128)(2,1)S(1)}, u32[]{:S(2)}, u32[]{:S(2)}) %collective-permute-start.7) | collective-permute-done | bytes 163872 | tf_op jit(solution)/shard_map/ppermute | solution.py:356
  69.9 3.7 %collective-permute-done.10 = bf16[32,2560]{1,0:T(8,128)(2,1)S(1)} collective-permute-done((bf16[32,2560]{1,0:T(8,128)(2,1)S(1)}, bf16[32,2560]{1,0:T(8,128)(2,1)S(1)}, u32[]{:S(2)}, u32[]{:S(2)}) %collective-permute-start.10) | collective-permute-done | bytes 163872 | tf_op jit(solution)/shard_map/ppermute | solution.py:356
  73.5 1.3 %collective-permute-done.11 = bf16[32,2560]{1,0:T(8,128)(2,1)S(1)} collective-permute-done((bf16[32,2560]{1,0:T(8,128)(2,1)S(1)}, bf16[32,2560]{1,0:T(8,128)(2,1)S(1)}, u32[]{:S(2)}, u32[]{:S(2)}) %collective-permute-start.11) | collective-permute-done | bytes 163872 | tf_op jit(solution)/shard_map/ppermute | solution.py:356
  74.9 0.8 %fusion.2 = bf16[1,32,5120]{2,1,0:T(8,128)(2,1)} fusion(f32[1,32,2560]{2,1,0:T(8,128)S(1)} %add_bitcast_fusion, f32[1,32,2560]{2,1,0:T(8,128)S(1)} %add_bitcast_fusion.1, bf16[1,32,5120]{2,1,0:T(8,128)(2,1)S(1)} %copy-done, f32[5120]{0:T(1024)S(1)} %convert_element_type.45, f32[5120]{0:T(1024)S(1)} %bitcast.17), kind=kLoop, calls=%fused_computation.3 | loop fusion | flops 983040 | bytes 1351680 | tf_op jit(solution)/shard_map/convert_element_type | solution.py:413
  (27 shorter events, 0.8 us)
Async XLA Ops:
  31.6 15.3 %collective-permute-start.5 = (bf16[512,5120]{1,0:T(8,128)(2,1)}, bf16[512,5120]{1,0:T(8,128)(2,1)}, u32[]{:S(2)}, u32[]{:S(2)}) collective-permute-start(bf16[512,5120]{1,0:T(8,128)(2,1)} %refs_4_.3), channel_id=1, source_target_pairs={{0,1},{1,0},{2,3},{3,2},{4,5},{5,4},{6,7},{7,6},{8,9},{9,8},{10,11... | collective-permute-start | bytes 15728648 | tf_op jit(solution)/shard_map/ppermute | solution.py:356
  37.5 2.9 %collective-permute-start.1 = (bf16[3,128,128]{2,1,0:T(8,128)(2,1)S(1)}, bf16[3,128,128]{2,1,0:T(8,128)(2,1)S(1)}, u32[]{:S(2)}, u32[]{:S(2)}) collective-permute-start(bf16[3,128,128]{2,1,0:T(8,128)(2,1)S(1)} %get-tuple-element.23), channel_id=1, source_target_pairs={{0,1},{1,0},{2,3},{3,2},{4,5},{5,4},{6,7},{7,6},{8,9},{9,8},{10,11... | collective-permute-start | bytes 294920 | tf_op jit(solution)/shard_map/ppermute | solution.py:232
  39.3 4.8 %collective-permute-start = (bf16[1,128,128]{2,1,0:T(8,128)(2,1)S(1)}, bf16[1,128,128]{2,1,0:T(8,128)(2,1)S(1)}, u32[]{:S(2)}, u32[]{:S(2)}) collective-permute-start(bf16[1,128,128]{2,1,0:T(8,128)(2,1)S(1)} %get-tuple-element.21), channel_id=1, source_target_pairs={{0,1},{1,0},{2,3},{3,2},{4,5},{5,4},{6,7},{7,6},{8,9},{9,8},{10,11... | collective-permute-start | bytes 98312 | tf_op jit(solution)/shard_map/ppermute | solution.py:232
  40.4 5.9 %collective-permute-start.4 = (bf16[2,128,128]{2,1,0:T(8,128)(2,1)S(1)}, bf16[2,128,128]{2,1,0:T(8,128)(2,1)S(1)}, u32[]{:S(2)}, u32[]{:S(2)}) collective-permute-start(bf16[2,128,128]{2,1,0:T(8,128)(2,1)S(1)} %pad_maximum_fusion.2), channel_id=1, source_target_pairs={{0,24},{8,16},{16,8},{24,0},{1,25},{9,17},{17,9},{25,1},{2,26},{10... | collective-permute-start | bytes 196616 | tf_op jit(solution)/shard_map/ppermute | solution.py:232
  41.0 5.5 %collective-permute-start.3 = (bf16[2,128,128]{2,1,0:T(8,128)(2,1)S(1)}, bf16[2,128,128]{2,1,0:T(8,128)(2,1)S(1)}, u32[]{:S(2)}, u32[]{:S(2)}) collective-permute-start(bf16[2,128,128]{2,1,0:T(8,128)(2,1)S(1)} %pad_maximum_fusion.1), channel_id=1, source_target_pairs={{0,16},{8,24},{16,0},{24,8},{1,17},{9,25},{17,1},{25,9},{2,18},{10... | collective-permute-start | bytes 196616 | tf_op jit(solution)/shard_map/ppermute | solution.py:232
  42.5 4.3 %collective-permute-start.2 = (bf16[2,128,128]{2,1,0:T(8,128)(2,1)S(1)}, bf16[2,128,128]{2,1,0:T(8,128)(2,1)S(1)}, u32[]{:S(2)}, u32[]{:S(2)}) collective-permute-start(bf16[2,128,128]{2,1,0:T(8,128)(2,1)S(1)} %pad_maximum_fusion), channel_id=1, source_target_pairs={{0,8},{8,0},{16,24},{24,16},{1,9},{9,1},{17,25},{25,17},{2,10},{10... | collective-permute-start | bytes 196616 | tf_op jit(solution)/shard_map/ppermute | solution.py:232
  44.1 6.9 %copy-start.1 = (bf16[5120]{0:T(1024)(128)(2,1)S(1)}, bf16[5120]{0:T(1024)(128)(2,1)}, u32[]{:S(2)}) copy-start(bf16[5120]{0:T(1024)(128)(2,1)} %param.18) | copy-start | bytes 30724
  50.0 6.3 %collective-permute-start.6 = (bf16[32,2560]{1,0:T(8,128)(2,1)S(1)}, bf16[32,2560]{1,0:T(8,128)(2,1)S(1)}, u32[]{:S(2)}, u32[]{:S(2)}) collective-permute-start(bf16[32,2560]{1,0:T(8,128)(2,1)S(1)} %get-tuple-element.27), channel_id=1, source_target_pairs={{0,2},{1,3},{2,0},{3,1},{4,6},{5,7},{6,4},{7,5},{8,10},{9,11},{10,... | collective-permute-start | bytes 491528 | tf_op jit(solution)/shard_map/ppermute | solution.py:356
  51.0 23.8 %copy-start = (bf16[1,32,5120]{2,1,0:T(8,128)(2,1)S(1)}, bf16[1,32,5120]{2,1,0:T(8,128)(2,1)}, u32[]{:S(2)}) copy-start(bf16[1,32,5120]{2,1,0:T(8,128)(2,1)} %param.11) | copy-start | bytes 983044
  54.2 12.5 %collective-permute-start.9 = (bf16[32,2560]{1,0:T(8,128)(2,1)S(1)}, bf16[32,2560]{1,0:T(8,128)(2,1)S(1)}, u32[]{:S(2)}, u32[]{:S(2)}) collective-permute-start(bf16[32,2560]{1,0:T(8,128)(2,1)S(1)} %get-tuple-element.32), channel_id=1, source_target_pairs={{0,2},{1,3},{2,0},{3,1},{4,6},{5,7},{6,4},{7,5},{8,10},{9,11},{10,... | collective-permute-start | bytes 491528 | tf_op jit(solution)/shard_map/ppermute | solution.py:356
  56.2 13.6 %collective-permute-start.7 = (bf16[32,2560]{1,0:T(8,128)(2,1)S(1)}, bf16[32,2560]{1,0:T(8,128)(2,1)S(1)}, u32[]{:S(2)}, u32[]{:S(2)}) collective-permute-start(bf16[32,2560]{1,0:T(8,128)(2,1)S(1)} %get-tuple-element.28), channel_id=1, source_target_pairs={{0,2},{1,3},{2,0},{3,1},{4,6},{5,7},{6,4},{7,5},{8,10},{9,11},{10,... | collective-permute-start | bytes 491528 | tf_op jit(solution)/shard_map/ppermute | solution.py:356
  56.4 13.5 %collective-permute-start.8 = (bf16[32,2560]{1,0:T(8,128)(2,1)S(1)}, bf16[32,2560]{1,0:T(8,128)(2,1)S(1)}, u32[]{:S(2)}, u32[]{:S(2)}) collective-permute-start(bf16[32,2560]{1,0:T(8,128)(2,1)S(1)} %add_convert_fusion.1), channel_id=1, source_target_pairs={{0,4},{1,5},{2,6},{3,7},{4,0},{5,1},{6,2},{7,3},{8,12},{9,13},{10,... | collective-permute-start | bytes 491528 | tf_op jit(solution)/shard_map/ppermute | solution.py:356
  66.7 6.8 %collective-permute-start.10 = (bf16[32,2560]{1,0:T(8,128)(2,1)S(1)}, bf16[32,2560]{1,0:T(8,128)(2,1)S(1)}, u32[]{:S(2)}, u32[]{:S(2)}) collective-permute-start(bf16[32,2560]{1,0:T(8,128)(2,1)S(1)} %get-tuple-element.33), channel_id=1, source_target_pairs={{0,2},{1,3},{2,0},{3,1},{4,6},{5,7},{6,4},{7,5},{8,10},{9,11},{10,... | collective-permute-start | bytes 491528 | tf_op jit(solution)/shard_map/ppermute | solution.py:356
  66.7 8.1 %collective-permute-start.11 = (bf16[32,2560]{1,0:T(8,128)(2,1)S(1)}, bf16[32,2560]{1,0:T(8,128)(2,1)S(1)}, u32[]{:S(2)}, u32[]{:S(2)}) collective-permute-start(bf16[32,2560]{1,0:T(8,128)(2,1)S(1)} %add_convert_fusion), channel_id=1, source_target_pairs={{0,4},{1,5},{2,6},{3,7},{4,0},{5,1},{6,2},{7,3},{8,12},{9,13},{10,... | collective-permute-start | bytes 491528 | tf_op jit(solution)/shard_map/ppermute | solution.py:356

commit v11 on v10

--- a/solution.py
+++ b/solution.py
@@ -239,7 +239,7 @@
     found = {0: jnp.concatenate([near_mine, near_got], axis=0)}
     for place, d in enumerate(far):
         found[d] = across(jnp.stack([far_mine[place], far_got[place]]), "frame", d)
-    return [found[d] for d in range(frames)], held
+    return [found[d] for d in range(frames)]
 
 
 def gathered_attention(query_rows, key_rows, value_rows, gain_query, gain_key, slot_order):
@@ -326,7 +326,7 @@
         ),
         name="attention",
     )(slot_array, slot_order, *queries, *pieces)
-    return [jnp.stack([even, across(odd, "seq", 1)])], halves[1]
+    return [jnp.stack([even, across(odd, "seq", 1)])]
 
 
 def shards(
@@ -358,11 +358,11 @@
     def after(value, *earlier):
         return lax.optimization_barrier((value, *earlier))[0]
 
+    other_weight = across(out_weight, "seq", 1)
     spread = (width // HD) % frames == 0
-    attended, travelled = (spread_attention if spread else gathered_attention)(
+    attended = (spread_attention if spread else gathered_attention)(
         query_rows[0], key_rows[0], value_rows[0], gain_query, gain_key, slot_order
     )
-    other_weight = across(after(out_weight, travelled), "seq", 1)
     index = jnp.stack([me // 2, slot]) if spread else jnp.zeros((2,), jnp.int32)
 
     cuts = 2

time: 76 us -> 71.4 us (0.939)
  blocking collectives: 29.3 us -> 0 us
  waiting for transfers between devices: 18.5 us -> 35.3 us
  starting transfers between devices: 10.2 us -> 17.7 us
    all_to_all x1 -> x0, blocking collectives: 29.3 us -> none  [spread_attention(): lax.all_to_all(sends, ('frame', 'seq'), split_axis=0, concat_axis=0, tile...]
    all_to_all x0 -> x1, waiting for transfers between devices: none -> 18 us  [spread_attention(): lax.all_to_all(sends, ('frame', 'seq'), split_axis=0, concat_axis=0, tile...]
    all_to_all x0 -> x1, starting transfers between devices: none -> 6.96 us  [spread_attention(): lax.all_to_all(sends, ('frame', 'seq'), split_axis=0, concat_axis=0, tile...]
    ppermute x5, waiting for transfers between devices: 3.71 us -> 2.59 us  [across(): return lax.ppermute(value, axis, [(i, i ^ distance) for i in range(size)])]
  transfers between devices with their start and end apart: 12 -> 13, of which waited for: 8 -> 8; matrix products, arithmetic and copies ran while one was open for 4% -> 4% of each run, Pallas kernels for 9% -> 12%
where the time goes in v11:
time: 71.4 us; the launch traced here: 71.1 us
  waiting for transfers between devices  35.3 us (49%)
  starting transfers between devices  17.7 us (25%)
  Pallas kernels  12 us (17%)
  other arithmetic  2.75 us (4%)
  between operations  2.09 us (3%)
  local copies, waits for them, and re-layouts  1.31 us (2%)
    all_to_all x1, waiting for transfers between devices, spread_attention(): lax.all_to_all(sends, ('frame', 'seq'), split_axis=0, concat_axis=0, tile...  18 us
    ppermute x7, waiting for transfers between devices, across(): return lax.ppermute(value, axis, [(i, i ^ distance) for i in range(n)])  14.7 us
    all_to_all x1, starting transfers between devices, spread_attention(): lax.all_to_all(sends, ('frame', 'seq'), split_axis=0, concat_axis=0, tile...  6.96 us
    ppermute x7, starting transfers between devices, across(): return lax.ppermute(value, axis, [(i, i ^ distance) for i in range(n)])  6.44 us
    pallas_call x2, Pallas kernels, shards(): pl.pallas_call(functools.partial(projection_kernel, chips, sources), grid...  6.28 us
    ppermute x5, starting transfers between devices, across(): return lax.ppermute(value, axis, [(i, i ^ distance) for i in range(size)])  4.31 us
    pallas_call x2, Pallas kernels, attend(): pl.pallas_call(functools.partial(spread_attention_kernel, n, frames, pick...  3.37 us
    ppermute x5, waiting for transfers between devices, across(): return lax.ppermute(value, axis, [(i, i ^ distance) for i in range(size)])  2.59 us
  transfers between devices with their start and end apart: 13, of which 8 were waited for; matrix products, arithmetic and copies ran while one was open for 4% of the time, Pallas kernels for 12%

profile of v11, /device:TPU:0, one launch (start us, length us, event | category | flops | bytes accessed | tf_op | source)
XLA Modules:
  0.0 71.1 jit_solution(1187073051622837248)
XLA Ops:
  0.0 0.5 collective-permute-start.5
  0.5 2.3 %norm.1 = bf16[32,32,384]{2,1,0:T(8,128)(2,1)} custom-call(bf16[32,4096]{1,0:T(8,128)(2,1)} %bitcast.14, bf16[32,4096]{1,0:T(8,128)(2,1)} %bitcast.15, bf16[32,4096]{1,0:T(8,128)(2,1)} %bitcast.16, f32[1,4096]{1,0:T(1,128)} %bitcast.18, f32[1,4096]{1,0:T(1,128)} %bitcast.19), custom_call_target="tpu_custom_call" | custom-call | tf_op jit(solution)/shard_map/norm/pallas_call | solution.py:200
  2.8 7.0 %all-to-all-start = ((bf16[32,32,384]{2,1,0:T(8,128)(2,1)}), bf16[32,32,384]{2,1,0:T(8,128)(2,1)S(1)}, u32[]{:S(2)}, u32[]{:S(2)}) async-start(bf16[32,32,384]{2,1,0:T(8,128)(2,1)} %norm.1), calls=%async_computation | async-start | bytes 1572864 | tf_op jit(solution)/shard_map/all_to_all | solution.py:207
  9.7 1.3 %dynamic_slice.8 = s32[1]{0:T(128)} dynamic-slice(s32[4]{0:T(128)} %param.20, s32[]{:T(128)S(6)} %select_n.19), dynamic_slice_sizes={1} | dynamic-slice | bytes 12 | tf_op jit(solution)/shard_map/jit(dynamic_index_in_dim)/dynamic_slice | solution.py:409
  13.0 0.7 %pad_add_fusion.1.index_ref = s32[6]{0:T(128)S(1)} fusion(s32[4]{0:T(128)} %param.21, s32[1]{0:T(128)} %bitcast.4, s32[1]{0:T(128)} %bitcast.3), kind=kLoop, calls=%fused_computation.15 | loop fusion | flops 12 | bytes 48 | tf_op jit(solution)/shard_map/concatenate | solution.py:211
  13.7 18.0 %all-to-all-done.rows_ref = bf16[32,32,384]{2,1,0:T(8,128)(2,1)S(1)} async-done(((bf16[32,32,384]{2,1,0:T(8,128)(2,1)}), bf16[32,32,384]{2,1,0:T(8,128)(2,1)S(1)}, u32[]{:S(2)}, u32[]{:S(2)}) %all-to-all-start) | async-done | bytes 786464 | tf_op jit(solution)/shard_map/all_to_all | solution.py:207
  31.7 2.2 %attention_far.1 = (bf16[3,128,128]{2,1,0:T(8,128)(2,1)S(1)}, bf16[3,128,128]{2,1,0:T(8,128)(2,1)S(1)}) custom-call(s32[6]{0:T(128)S(1)} %pad_add_fusion.1.index_ref, bf16[32,32,384]{2,1,0:T(8,128)(2,1)S(1)} %all-to-all-done.rows_ref), custom_call_target="tpu_custom_call" | custom-call | flops 402653184 | bytes 1048576 | tf_op jit(solution)/shard_map/attention_far/pallas_call | solution.py:215
  33.9 1.2 %attention_near.1 = (bf16[1,128,128]{2,1,0:T(8,128)(2,1)S(1)}, bf16[1,128,128]{2,1,0:T(8,128)(2,1)S(1)}) custom-call(s32[6]{0:T(128)S(1)} %pad_add_fusion.1.index_ref, bf16[32,32,384]{2,1,0:T(8,128)(2,1)S(1)} %all-to-all-done.rows_ref), custom_call_target="tpu_custom_call" | custom-call | flops 134217728 | bytes 1048576 | tf_op jit(solution)/shard_map/attention_near/pallas_call | solution.py:215
  35.2 0.6 collective-permute-start
  35.8 0.6 collective-permute-start.4
  36.4 1.4 %collective-permute-start.3 = (bf16[2,128,128]{2,1,0:T(8,128)(2,1)S(1)}, bf16[2,128,128]{2,1,0:T(8,128)(2,1)S(1)}, u32[]{:S(2)}, u32[]{:S(2)}) collective-permute-start(bf16[2,128,128]{2,1,0:T(8,128)(2,1)S(1)} %pad_maximum_fusion.1), channel_id=1, source_target_pairs={{0,16},{8,24},{16,0},{24,8},{1,17},{9,25},{17,1},{25,9},{2,18},{10... | collective-permute-start | bytes 196616 | tf_op jit(solution)/shard_map/ppermute | solution.py:232
  37.8 1.7 %collective-permute-start.2 = (bf16[2,128,128]{2,1,0:T(8,128)(2,1)S(1)}, bf16[2,128,128]{2,1,0:T(8,128)(2,1)S(1)}, u32[]{:S(2)}, u32[]{:S(2)}) collective-permute-start(bf16[2,128,128]{2,1,0:T(8,128)(2,1)S(1)} %pad_maximum_fusion), channel_id=1, source_target_pairs={{0,8},{8,0},{16,24},{24,16},{1,9},{9,1},{17,25},{25,17},{2,10},{10... | collective-permute-start | bytes 196616 | tf_op jit(solution)/shard_map/ppermute | solution.py:232
  39.5 2.2 %collective-permute-done.4.refs_3_ = bf16[2,128,128]{2,1,0:T(8,128)(2,1)S(1)} collective-permute-done((bf16[2,128,128]{2,1,0:T(8,128)(2,1)S(1)}, bf16[2,128,128]{2,1,0:T(8,128)(2,1)S(1)}, u32[]{:S(2)}, u32[]{:S(2)}) %collective-permute-start.4) | collective-permute-done | bytes 65568 | tf_op jit(solution)/shard_map/ppermute | solution.py:232
  42.1 3.1 %projection_0.1 = (f32[32,2560]{1,0:T(8,128)S(1)}, bf16[32,2560]{1,0:T(8,128)(2,1)S(1)}, f32[32,2560]{1,0:T(8,128)S(1)}, bf16[32,2560]{1,0:T(8,128)(2,1)S(1)}) custom-call(s32[2]{0:T(128)S(1)} %pad_add_fusion.index_ref, bf16[2,128,128]{2,1,0:T(8,128)(2,1)S(1)} %constant_dynamic-update-slice_fusion.refs_0_, ...), custom_call_target="tpu_custom_call" | custom-call | flops 671088640 | bytes 5898240 | tf_op jit(solution)/shard_map/projection_0/pallas_call | solution.py:375
  45.5 0.9 %dynamic-slice_convert_fusion = f32[1,5120]{1,0:T(1,128)S(1)} fusion(bf16[64,5120]{1,0:T(8,128)(2,1)} %param.19, s32[]{:T(128)S(6)} %select_n.20), kind=kLoop, calls=%fused_computation.11 | loop fusion | flops 5120 | bytes 30724 | tf_op jit(solution)/shard_map/mul | solution.py:412
  46.4 3.2 %projection_1.1 = (f32[32,2560]{1,0:T(8,128)S(1)}, bf16[32,2560]{1,0:T(8,128)(2,1)S(1)}, f32[32,2560]{1,0:T(8,128)S(1)}, bf16[32,2560]{1,0:T(8,128)(2,1)S(1)}) custom-call(s32[2]{0:T(128)S(1)} %pad_add_fusion.index_ref, bf16[2,128,128]{2,1,0:T(8,128)(2,1)S(1)} %constant_dynamic-update-slice_fusion.refs_0_, ...), custom_call_target="tpu_custom_call" | custom-call | flops 671088640 | bytes 5898240 | tf_op jit(solution)/shard_map/projection_1/pallas_call | solution.py:375
  49.6 1.9 %collective-permute-start.9 = (bf16[32,2560]{1,0:T(8,128)(2,1)S(1)}, bf16[32,2560]{1,0:T(8,128)(2,1)S(1)}, u32[]{:S(2)}, u32[]{:S(2)}) collective-permute-start(bf16[32,2560]{1,0:T(8,128)(2,1)S(1)} %get-tuple-element.30), channel_id=1, source_target_pairs={{0,2},{1,3},{2,0},{3,1},{4,6},{5,7},{6,4},{7,5},{8,10},{9,11},{10,... | collective-permute-start | bytes 491528 | tf_op jit(solution)/shard_map/ppermute | solution.py:356
  51.7 1.6 %collective-permute-start.8 = (bf16[32,2560]{1,0:T(8,128)(2,1)S(1)}, bf16[32,2560]{1,0:T(8,128)(2,1)S(1)}, u32[]{:S(2)}, u32[]{:S(2)}) collective-permute-start(bf16[32,2560]{1,0:T(8,128)(2,1)S(1)} %add_convert_fusion.1), channel_id=1, source_target_pairs={{0,4},{1,5},{2,6},{3,7},{4,0},{5,1},{6,2},{7,3},{8,12},{9,13},{10,... | collective-permute-start | bytes 491528 | tf_op jit(solution)/shard_map/ppermute | solution.py:356
  53.3 8.8 %collective-permute-done.9 = bf16[32,2560]{1,0:T(8,128)(2,1)S(1)} collective-permute-done((bf16[32,2560]{1,0:T(8,128)(2,1)S(1)}, bf16[32,2560]{1,0:T(8,128)(2,1)S(1)}, u32[]{:S(2)}, u32[]{:S(2)}) %collective-permute-start.9) | collective-permute-done | bytes 163872 | tf_op jit(solution)/shard_map/ppermute | solution.py:356
  62.1 2.1 %collective-permute-start.11 = (bf16[32,2560]{1,0:T(8,128)(2,1)S(1)}, bf16[32,2560]{1,0:T(8,128)(2,1)S(1)}, u32[]{:S(2)}, u32[]{:S(2)}) collective-permute-start(bf16[32,2560]{1,0:T(8,128)(2,1)S(1)} %add_convert_fusion), channel_id=1, source_target_pairs={{0,4},{1,5},{2,6},{3,7},{4,0},{5,1},{6,2},{7,3},{8,12},{9,13},{10,... | collective-permute-start | bytes 491528 | tf_op jit(solution)/shard_map/ppermute | solution.py:356
  64.2 1.2 %collective-permute-done.7 = bf16[32,2560]{1,0:T(8,128)(2,1)S(1)} collective-permute-done((bf16[32,2560]{1,0:T(8,128)(2,1)S(1)}, bf16[32,2560]{1,0:T(8,128)(2,1)S(1)}, u32[]{:S(2)}, u32[]{:S(2)}) %collective-permute-start.7) | collective-permute-done | bytes 163872 | tf_op jit(solution)/shard_map/ppermute | solution.py:356
  65.4 3.5 %collective-permute-done.10 = bf16[32,2560]{1,0:T(8,128)(2,1)S(1)} collective-permute-done((bf16[32,2560]{1,0:T(8,128)(2,1)S(1)}, bf16[32,2560]{1,0:T(8,128)(2,1)S(1)}, u32[]{:S(2)}, u32[]{:S(2)}) %collective-permute-start.10) | collective-permute-done | bytes 163872 | tf_op jit(solution)/shard_map/ppermute | solution.py:356
  68.9 1.3 %collective-permute-done.11 = bf16[32,2560]{1,0:T(8,128)(2,1)S(1)} collective-permute-done((bf16[32,2560]{1,0:T(8,128)(2,1)S(1)}, bf16[32,2560]{1,0:T(8,128)(2,1)S(1)}, u32[]{:S(2)}, u32[]{:S(2)}) %collective-permute-start.11) | collective-permute-done | bytes 163872 | tf_op jit(solution)/shard_map/ppermute | solution.py:356
  70.3 0.8 %fusion.2 = bf16[1,32,5120]{2,1,0:T(8,128)(2,1)} fusion(f32[1,32,2560]{2,1,0:T(8,128)S(1)} %add_bitcast_fusion, f32[1,32,2560]{2,1,0:T(8,128)S(1)} %add_bitcast_fusion.1, bf16[1,32,5120]{2,1,0:T(8,128)(2,1)S(1)} %copy-done, f32[5120]{0:T(1024)S(1)} %convert_element_type.45, f32[5120]{0:T(1024)S(1)} %bitcast.17), kind=kLoop, calls=%fused_computation.3 | loop fusion | flops 983040 | bytes 1351680 | tf_op jit(solution)/shard_map/convert_element_type | solution.py:413
  (28 shorter events, 1.3 us)
Async XLA Ops:
  0.0 42.1 %collective-permute-start.5 = (bf16[512,5120]{1,0:T(8,128)(2,1)}, bf16[512,5120]{1,0:T(8,128)(2,1)}, u32[]{:S(2)}, u32[]{:S(2)}) collective-permute-start(bf16[512,5120]{1,0:T(8,128)(2,1)} %refs_4_.3), channel_id=1, source_target_pairs={{0,1},{1,0},{2,3},{3,2},{4,5},{5,4},{6,7},{7,6},{8,9},{9,8},{10,11... | collective-permute-start | bytes 15728648 | tf_op jit(solution)/shard_map/ppermute | solution.py:356
  2.8 28.9 %all-to-all-start = ((bf16[32,32,384]{2,1,0:T(8,128)(2,1)}), bf16[32,32,384]{2,1,0:T(8,128)(2,1)S(1)}, u32[]{:S(2)}, u32[]{:S(2)}) async-start(bf16[32,32,384]{2,1,0:T(8,128)(2,1)} %norm.1), calls=%async_computation | async-start | bytes 1572864 | tf_op jit(solution)/shard_map/all_to_all | solution.py:207
  33.9 1.9 %collective-permute-start.1 = (bf16[3,128,128]{2,1,0:T(8,128)(2,1)S(1)}, bf16[3,128,128]{2,1,0:T(8,128)(2,1)S(1)}, u32[]{:S(2)}, u32[]{:S(2)}) collective-permute-start(bf16[3,128,128]{2,1,0:T(8,128)(2,1)S(1)} %get-tuple-element.22), channel_id=1, source_target_pairs={{0,1},{1,0},{2,3},{3,2},{4,5},{5,4},{6,7},{7,6},{8,9},{9,8},{10,11... | collective-permute-start | bytes 294920 | tf_op jit(solution)/shard_map/ppermute | solution.py:232
  35.2 4.3 %collective-permute-start = (bf16[1,128,128]{2,1,0:T(8,128)(2,1)S(1)}, bf16[1,128,128]{2,1,0:T(8,128)(2,1)S(1)}, u32[]{:S(2)}, u32[]{:S(2)}) collective-permute-start(bf16[1,128,128]{2,1,0:T(8,128)(2,1)S(1)} %get-tuple-element.20), channel_id=1, source_target_pairs={{0,1},{1,0},{2,3},{3,2},{4,5},{5,4},{6,7},{7,6},{8,9},{9,8},{10,11... | collective-permute-start | bytes 98312 | tf_op jit(solution)/shard_map/ppermute | solution.py:232
  35.8 5.9 %collective-permute-start.4 = (bf16[2,128,128]{2,1,0:T(8,128)(2,1)S(1)}, bf16[2,128,128]{2,1,0:T(8,128)(2,1)S(1)}, u32[]{:S(2)}, u32[]{:S(2)}) collective-permute-start(bf16[2,128,128]{2,1,0:T(8,128)(2,1)S(1)} %pad_maximum_fusion.2), channel_id=1, source_target_pairs={{0,24},{8,16},{16,8},{24,0},{1,25},{9,17},{17,9},{25,1},{2,26},{10... | collective-permute-start | bytes 196616 | tf_op jit(solution)/shard_map/ppermute | solution.py:232
  36.4 5.5 %collective-permute-start.3 = (bf16[2,128,128]{2,1,0:T(8,128)(2,1)S(1)}, bf16[2,128,128]{2,1,0:T(8,128)(2,1)S(1)}, u32[]{:S(2)}, u32[]{:S(2)}) collective-permute-start(bf16[2,128,128]{2,1,0:T(8,128)(2,1)S(1)} %pad_maximum_fusion.1), channel_id=1, source_target_pairs={{0,16},{8,24},{16,0},{24,8},{1,17},{9,25},{17,1},{25,9},{2,18},{10... | collective-permute-start | bytes 196616 | tf_op jit(solution)/shard_map/ppermute | solution.py:232
  37.8 4.3 %collective-permute-start.2 = (bf16[2,128,128]{2,1,0:T(8,128)(2,1)S(1)}, bf16[2,128,128]{2,1,0:T(8,128)(2,1)S(1)}, u32[]{:S(2)}, u32[]{:S(2)}) collective-permute-start(bf16[2,128,128]{2,1,0:T(8,128)(2,1)S(1)} %pad_maximum_fusion), channel_id=1, source_target_pairs={{0,8},{8,0},{16,24},{24,16},{1,9},{9,1},{17,25},{25,17},{2,10},{10... | collective-permute-start | bytes 196616 | tf_op jit(solution)/shard_map/ppermute | solution.py:232
  39.5 6.9 %copy-start.1 = (bf16[5120]{0:T(1024)(128)(2,1)S(1)}, bf16[5120]{0:T(1024)(128)(2,1)}, u32[]{:S(2)}) copy-start(bf16[5120]{0:T(1024)(128)(2,1)} %param.18) | copy-start | bytes 30724
  45.2 6.3 %collective-permute-start.6 = (bf16[32,2560]{1,0:T(8,128)(2,1)S(1)}, bf16[32,2560]{1,0:T(8,128)(2,1)S(1)}, u32[]{:S(2)}, u32[]{:S(2)}) collective-permute-start(bf16[32,2560]{1,0:T(8,128)(2,1)S(1)} %get-tuple-element.25), channel_id=1, source_target_pairs={{0,2},{1,3},{2,0},{3,1},{4,6},{5,7},{6,4},{7,5},{8,10},{9,11},{10,... | collective-permute-start | bytes 491528 | tf_op jit(solution)/shard_map/ppermute | solution.py:356
  46.4 23.9 %copy-start = (bf16[1,32,5120]{2,1,0:T(8,128)(2,1)S(1)}, bf16[1,32,5120]{2,1,0:T(8,128)(2,1)}, u32[]{:S(2)}) copy-start(bf16[1,32,5120]{2,1,0:T(8,128)(2,1)} %param.11) | copy-start | bytes 983044
  49.6 12.5 %collective-permute-start.9 = (bf16[32,2560]{1,0:T(8,128)(2,1)S(1)}, bf16[32,2560]{1,0:T(8,128)(2,1)S(1)}, u32[]{:S(2)}, u32[]{:S(2)}) collective-permute-start(bf16[32,2560]{1,0:T(8,128)(2,1)S(1)} %get-tuple-element.30), channel_id=1, source_target_pairs={{0,2},{1,3},{2,0},{3,1},{4,6},{5,7},{6,4},{7,5},{8,10},{9,11},{10,... | collective-permute-start | bytes 491528 | tf_op jit(solution)/shard_map/ppermute | solution.py:356
  51.5 13.9 %collective-permute-start.7 = (bf16[32,2560]{1,0:T(8,128)(2,1)S(1)}, bf16[32,2560]{1,0:T(8,128)(2,1)S(1)}, u32[]{:S(2)}, u32[]{:S(2)}) collective-permute-start(bf16[32,2560]{1,0:T(8,128)(2,1)S(1)} %get-tuple-element.26), channel_id=1, source_target_pairs={{0,2},{1,3},{2,0},{3,1},{4,6},{5,7},{6,4},{7,5},{8,10},{9,11},{10,... | collective-permute-start | bytes 491528 | tf_op jit(solution)/shard_map/ppermute | solution.py:356
  51.7 13.6 %collective-permute-start.8 = (bf16[32,2560]{1,0:T(8,128)(2,1)S(1)}, bf16[32,2560]{1,0:T(8,128)(2,1)S(1)}, u32[]{:S(2)}, u32[]{:S(2)}) collective-permute-start(bf16[32,2560]{1,0:T(8,128)(2,1)S(1)} %add_convert_fusion.1), channel_id=1, source_target_pairs={{0,4},{1,5},{2,6},{3,7},{4,0},{5,1},{6,2},{7,3},{8,12},{9,13},{10,... | collective-permute-start | bytes 491528 | tf_op jit(solution)/shard_map/ppermute | solution.py:356
  62.1 6.8 %collective-permute-start.10 = (bf16[32,2560]{1,0:T(8,128)(2,1)S(1)}, bf16[32,2560]{1,0:T(8,128)(2,1)S(1)}, u32[]{:S(2)}, u32[]{:S(2)}) collective-permute-start(bf16[32,2560]{1,0:T(8,128)(2,1)S(1)} %get-tuple-element.31), channel_id=1, source_target_pairs={{0,2},{1,3},{2,0},{3,1},{4,6},{5,7},{6,4},{7,5},{8,10},{9,11},{10,... | collective-permute-start | bytes 491528 | tf_op jit(solution)/shard_map/ppermute | solution.py:356
  62.1 8.1 %collective-permute-start.11 = (bf16[32,2560]{1,0:T(8,128)(2,1)S(1)}, bf16[32,2560]{1,0:T(8,128)(2,1)S(1)}, u32[]{:S(2)}, u32[]{:S(2)}) collective-permute-start(bf16[32,2560]{1,0:T(8,128)(2,1)S(1)} %add_convert_fusion), channel_id=1, source_target_pairs={{0,4},{1,5},{2,6},{3,7},{4,0},{5,1},{6,2},{7,3},{8,12},{9,13},{10,... | collective-permute-start | bytes 491528 | tf_op jit(solution)/shard_map/ppermute | solution.py:356

commit v12 on v11

--- a/solution.py
+++ b/solution.py
@@ -365,6 +365,10 @@
     )
     index = jnp.stack([me // 2, slot]) if spread else jnp.zeros((2,), jnp.int32)
 
+    level = lax.dynamic_index_in_dim(noise_level, slot, keepdims=False)
+    gate_row = lax.dynamic_index_in_dim(gate_table, level, keepdims=True).astype(jnp.float32)
+    index, gate_row = lax.optimization_barrier((index, gate_row))
+
     cuts = 2
     columns = model // cuts
     tile = columns // 2
@@ -406,8 +410,6 @@
         halves.append(sums[0])
     projected = jnp.concatenate(halves, axis=1)
 
-    level = lax.dynamic_index_in_dim(noise_level, slot, keepdims=False)
-    gate_row = lax.dynamic_index_in_dim(gate_table, level, keepdims=True).astype(jnp.float32)
     bias = out_bias.astype(jnp.float32)[None, :]
     mixed = tokens[0].astype(jnp.float32) + gate_row * (projected + bias)
     return mixed.astype(jnp.bfloat16)[None]

time: 71.4 us -> 70.5 us (0.987)
  waiting for transfers between devices: 35.3 us -> 34.4 us
    all_to_all x1, waiting for transfers between devices: 18 us -> 17 us  [spread_attention(): lax.all_to_all(sends, ('frame', 'seq'), split_axis=0, concat_axis=0, tile...]
    convert_element_type x0 -> x1, other arithmetic: none -> 0.9 us  [shards(): lax.dynamic_index_in_dim(gate_table, level, keepdims=True)]
    mul x1 -> x0, other arithmetic: 0.9 us -> none  [shards(): mixed = tokens[0].astype(jnp.float32) + gate_row * (projected + bias)]
  transfers between devices with their start and end apart: 13 -> 13, of which waited for: 8 -> 9; matrix products, arithmetic and copies ran while one was open for 4% -> 5% of each run, Pallas kernels for 12% -> 13%
where the time goes in v12:
time: 70.5 us; the launch traced here: 70.2 us
  waiting for transfers between devices  34.4 us (49%)
  starting transfers between devices  17.6 us (25%)
  Pallas kernels  12 us (17%)
  other arithmetic  2.76 us (4%)
  between operations  2.07 us (3%)
  local copies, waits for them, and re-layouts  1.3 us (2%)
    all_to_all x1, waiting for transfers between devices, spread_attention(): lax.all_to_all(sends, ('frame', 'seq'), split_axis=0, concat_axis=0, tile...  17 us
    ppermute x7, waiting for transfers between devices, across(): return lax.ppermute(value, axis, [(i, i ^ distance) for i in range(n)])  14.8 us
    all_to_all x1, starting transfers between devices, spread_attention(): lax.all_to_all(sends, ('frame', 'seq'), split_axis=0, concat_axis=0, tile...  6.96 us
    ppermute x7, starting transfers between devices, across(): return lax.ppermute(value, axis, [(i, i ^ distance) for i in range(n)])  6.38 us
    pallas_call x2, Pallas kernels, shards(): pl.pallas_call(functools.partial(projection_kernel, chips, sources), grid...  6.29 us
    ppermute x5, starting transfers between devices, across(): return lax.ppermute(value, axis, [(i, i ^ distance) for i in range(size)])  4.31 us
    pallas_call x2, Pallas kernels, attend(): pl.pallas_call(functools.partial(spread_attention_kernel, n, frames, pick...  3.37 us
    ppermute x5, waiting for transfers between devices, across(): return lax.ppermute(value, axis, [(i, i ^ distance) for i in range(size)])  2.59 us
  transfers between devices with their start and end apart: 13, of which 9 were waited for; matrix products, arithmetic and copies ran while one was open for 5% of the time, Pallas kernels for 13%

profile of v12, /device:TPU:0, one launch (start us, length us, event | category | flops | bytes accessed | tf_op | source)
XLA Modules:
  0.0 70.2 jit_solution(3507187958609895202)
XLA Ops:
  0.0 0.5 collective-permute-start.5
  0.5 2.3 %norm.1 = bf16[32,32,384]{2,1,0:T(8,128)(2,1)} custom-call(bf16[32,4096]{1,0:T(8,128)(2,1)} %bitcast.14, bf16[32,4096]{1,0:T(8,128)(2,1)} %bitcast.15, bf16[32,4096]{1,0:T(8,128)(2,1)} %bitcast.16, f32[1,4096]{1,0:T(1,128)} %bitcast.18, f32[1,4096]{1,0:T(1,128)} %bitcast.19), custom_call_target="tpu_custom_call" | custom-call | tf_op jit(solution)/shard_map/norm/pallas_call | solution.py:200
  2.8 7.0 %all-to-all-start = ((bf16[32,32,384]{2,1,0:T(8,128)(2,1)}), bf16[32,32,384]{2,1,0:T(8,128)(2,1)S(1)}, u32[]{:S(2)}, u32[]{:S(2)}) async-start(bf16[32,32,384]{2,1,0:T(8,128)(2,1)} %norm.1), calls=%async_computation | async-start | bytes 1572864 | tf_op jit(solution)/shard_map/all_to_all | solution.py:207
  9.7 1.3 %dynamic_slice.8 = s32[1]{0:T(128)} dynamic-slice(s32[4]{0:T(128)} %param.20, s32[]{:T(128)S(6)} %select_n.20), dynamic_slice_sizes={1} | dynamic-slice | bytes 12 | tf_op jit(solution)/shard_map/jit(dynamic_index_in_dim)/dynamic_slice | solution.py:368
  13.0 0.9 %dynamic-slice_convert_fusion = f32[1,5120]{1,0:T(1,128)S(1)} fusion(bf16[64,5120]{1,0:T(8,128)(2,1)} %param.19, s32[]{:T(128)S(6)} %select_n.21), kind=kLoop, calls=%fused_computation.11 | loop fusion | flops 5120 | bytes 30724 | tf_op jit(solution)/shard_map/convert_element_type | solution.py:369
  13.9 0.7 %pad_add_fusion.1.index_ref = s32[6]{0:T(128)S(1)} fusion(s32[4]{0:T(128)} %param.21, s32[1]{0:T(128)} %bitcast.4, s32[1]{0:T(128)} %bitcast.1), kind=kLoop, calls=%fused_computation.15 | loop fusion | flops 12 | bytes 48 | tf_op jit(solution)/shard_map/concatenate | solution.py:211
  14.6 17.0 %all-to-all-done.rows_ref = bf16[32,32,384]{2,1,0:T(8,128)(2,1)S(1)} async-done(((bf16[32,32,384]{2,1,0:T(8,128)(2,1)}), bf16[32,32,384]{2,1,0:T(8,128)(2,1)S(1)}, u32[]{:S(2)}, u32[]{:S(2)}) %all-to-all-start) | async-done | bytes 786464 | tf_op jit(solution)/shard_map/all_to_all | solution.py:207
  31.7 2.2 %attention_far.1 = (bf16[3,128,128]{2,1,0:T(8,128)(2,1)S(1)}, bf16[3,128,128]{2,1,0:T(8,128)(2,1)S(1)}) custom-call(s32[6]{0:T(128)S(1)} %pad_add_fusion.1.index_ref, bf16[32,32,384]{2,1,0:T(8,128)(2,1)S(1)} %all-to-all-done.rows_ref), custom_call_target="tpu_custom_call" | custom-call | flops 402653184 | bytes 1048576 | tf_op jit(solution)/shard_map/attention_far/pallas_call | solution.py:215
  33.9 1.2 %attention_near.1 = (bf16[1,128,128]{2,1,0:T(8,128)(2,1)S(1)}, bf16[1,128,128]{2,1,0:T(8,128)(2,1)S(1)}) custom-call(s32[6]{0:T(128)S(1)} %pad_add_fusion.1.index_ref, bf16[32,32,384]{2,1,0:T(8,128)(2,1)S(1)} %all-to-all-done.rows_ref), custom_call_target="tpu_custom_call" | custom-call | flops 134217728 | bytes 1048576 | tf_op jit(solution)/shard_map/attention_near/pallas_call | solution.py:215
  35.2 0.6 collective-permute-start
  35.8 0.6 collective-permute-start.4
  36.4 1.4 %collective-permute-start.3 = (bf16[2,128,128]{2,1,0:T(8,128)(2,1)S(1)}, bf16[2,128,128]{2,1,0:T(8,128)(2,1)S(1)}, u32[]{:S(2)}, u32[]{:S(2)}) collective-permute-start(bf16[2,128,128]{2,1,0:T(8,128)(2,1)S(1)} %pad_maximum_fusion.1), channel_id=1, source_target_pairs={{0,16},{8,24},{16,0},{24,8},{1,17},{9,25},{17,1},{25,9},{2,18},{10... | collective-permute-start | bytes 196616 | tf_op jit(solution)/shard_map/ppermute | solution.py:232
  37.8 1.7 %collective-permute-start.2 = (bf16[2,128,128]{2,1,0:T(8,128)(2,1)S(1)}, bf16[2,128,128]{2,1,0:T(8,128)(2,1)S(1)}, u32[]{:S(2)}, u32[]{:S(2)}) collective-permute-start(bf16[2,128,128]{2,1,0:T(8,128)(2,1)S(1)} %pad_maximum_fusion), channel_id=1, source_target_pairs={{0,8},{8,0},{16,24},{24,16},{1,9},{9,1},{17,25},{25,17},{2,10},{10... | collective-permute-start | bytes 196616 | tf_op jit(solution)/shard_map/ppermute | solution.py:232
  39.5 2.2 %collective-permute-done.4.refs_3_ = bf16[2,128,128]{2,1,0:T(8,128)(2,1)S(1)} collective-permute-done((bf16[2,128,128]{2,1,0:T(8,128)(2,1)S(1)}, bf16[2,128,128]{2,1,0:T(8,128)(2,1)S(1)}, u32[]{:S(2)}, u32[]{:S(2)}) %collective-permute-start.4) | collective-permute-done | bytes 65568 | tf_op jit(solution)/shard_map/ppermute | solution.py:232
  42.1 3.1 %projection_0.1 = (f32[32,2560]{1,0:T(8,128)S(1)}, bf16[32,2560]{1,0:T(8,128)(2,1)S(1)}, f32[32,2560]{1,0:T(8,128)S(1)}, bf16[32,2560]{1,0:T(8,128)(2,1)S(1)}) custom-call(s32[2]{0:T(128)S(1)} %pad_add_fusion.index_ref, bf16[2,128,128]{2,1,0:T(8,128)(2,1)S(1)} %constant_dynamic-update-slice_fusion.refs_0_, ...), custom_call_target="tpu_custom_call" | custom-call | flops 671088640 | bytes 5898240 | tf_op jit(solution)/shard_map/projection_0/pallas_call | solution.py:379
  45.5 3.2 %projection_1.1 = (f32[32,2560]{1,0:T(8,128)S(1)}, bf16[32,2560]{1,0:T(8,128)(2,1)S(1)}, f32[32,2560]{1,0:T(8,128)S(1)}, bf16[32,2560]{1,0:T(8,128)(2,1)S(1)}) custom-call(s32[2]{0:T(128)S(1)} %pad_add_fusion.index_ref, bf16[2,128,128]{2,1,0:T(8,128)(2,1)S(1)} %constant_dynamic-update-slice_fusion.refs_0_, ...), custom_call_target="tpu_custom_call" | custom-call | flops 671088640 | bytes 5898240 | tf_op jit(solution)/shard_map/projection_1/pallas_call | solution.py:379
  48.7 1.9 %collective-permute-start.9 = (bf16[32,2560]{1,0:T(8,128)(2,1)S(1)}, bf16[32,2560]{1,0:T(8,128)(2,1)S(1)}, u32[]{:S(2)}, u32[]{:S(2)}) collective-permute-start(bf16[32,2560]{1,0:T(8,128)(2,1)S(1)} %get-tuple-element.34), channel_id=1, source_target_pairs={{0,2},{1,3},{2,0},{3,1},{4,6},{5,7},{6,4},{7,5},{8,10},{9,11},{10,... | collective-permute-start | bytes 491528 | tf_op jit(solution)/shard_map/ppermute | solution.py:356
  50.9 1.5 %collective-permute-start.8 = (bf16[32,2560]{1,0:T(8,128)(2,1)S(1)}, bf16[32,2560]{1,0:T(8,128)(2,1)S(1)}, u32[]{:S(2)}, u32[]{:S(2)}) collective-permute-start(bf16[32,2560]{1,0:T(8,128)(2,1)S(1)} %add_convert_fusion.1), channel_id=1, source_target_pairs={{0,4},{1,5},{2,6},{3,7},{4,0},{5,1},{6,2},{7,3},{8,12},{9,13},{10,... | collective-permute-start | bytes 491528 | tf_op jit(solution)/shard_map/ppermute | solution.py:356
  52.5 8.6 %collective-permute-done.9 = bf16[32,2560]{1,0:T(8,128)(2,1)S(1)} collective-permute-done((bf16[32,2560]{1,0:T(8,128)(2,1)S(1)}, bf16[32,2560]{1,0:T(8,128)(2,1)S(1)}, u32[]{:S(2)}, u32[]{:S(2)}) %collective-permute-start.9) | collective-permute-done | bytes 163872 | tf_op jit(solution)/shard_map/ppermute | solution.py:356
  61.2 2.1 %collective-permute-start.11 = (bf16[32,2560]{1,0:T(8,128)(2,1)S(1)}, bf16[32,2560]{1,0:T(8,128)(2,1)S(1)}, u32[]{:S(2)}, u32[]{:S(2)}) collective-permute-start(bf16[32,2560]{1,0:T(8,128)(2,1)S(1)} %add_convert_fusion), channel_id=1, source_target_pairs={{0,4},{1,5},{2,6},{3,7},{4,0},{5,1},{6,2},{7,3},{8,12},{9,13},{10,... | collective-permute-start | bytes 491528 | tf_op jit(solution)/shard_map/ppermute | solution.py:356
  63.3 1.4 %collective-permute-done.7 = bf16[32,2560]{1,0:T(8,128)(2,1)S(1)} collective-permute-done((bf16[32,2560]{1,0:T(8,128)(2,1)S(1)}, bf16[32,2560]{1,0:T(8,128)(2,1)S(1)}, u32[]{:S(2)}, u32[]{:S(2)}) %collective-permute-start.7) | collective-permute-done | bytes 163872 | tf_op jit(solution)/shard_map/ppermute | solution.py:356
  64.7 3.2 %collective-permute-done.10 = bf16[32,2560]{1,0:T(8,128)(2,1)S(1)} collective-permute-done((bf16[32,2560]{1,0:T(8,128)(2,1)S(1)}, bf16[32,2560]{1,0:T(8,128)(2,1)S(1)}, u32[]{:S(2)}, u32[]{:S(2)}) %collective-permute-start.10) | collective-permute-done | bytes 163872 | tf_op jit(solution)/shard_map/ppermute | solution.py:356
  68.0 1.3 %collective-permute-done.11 = bf16[32,2560]{1,0:T(8,128)(2,1)S(1)} collective-permute-done((bf16[32,2560]{1,0:T(8,128)(2,1)S(1)}, bf16[32,2560]{1,0:T(8,128)(2,1)S(1)}, u32[]{:S(2)}, u32[]{:S(2)}) %collective-permute-start.11) | collective-permute-done | bytes 163872 | tf_op jit(solution)/shard_map/ppermute | solution.py:356
  69.3 0.8 %fusion.2 = bf16[1,32,5120]{2,1,0:T(8,128)(2,1)} fusion(f32[1,32,2560]{2,1,0:T(8,128)S(1)} %add_bitcast_fusion, f32[1,32,2560]{2,1,0:T(8,128)S(1)} %add_bitcast_fusion.1, bf16[1,32,5120]{2,1,0:T(8,128)(2,1)S(1)} %copy-done, f32[5120]{0:T(1024)S(1)} %convert_element_type.48, f32[5120]{0:T(1024)S(1)} %bitcast.17), kind=kLoop, calls=%fused_computation.3 | loop fusion | flops 983040 | bytes 1351680 | tf_op jit(solution)/shard_map/convert_element_type | solution.py:415
  (28 shorter events, 1.4 us)
Async XLA Ops:
  0.0 42.1 %collective-permute-start.5 = (bf16[512,5120]{1,0:T(8,128)(2,1)}, bf16[512,5120]{1,0:T(8,128)(2,1)}, u32[]{:S(2)}, u32[]{:S(2)}) collective-permute-start(bf16[512,5120]{1,0:T(8,128)(2,1)} %refs_4_.3), channel_id=1, source_target_pairs={{0,1},{1,0},{2,3},{3,2},{4,5},{5,4},{6,7},{7,6},{8,9},{9,8},{10,11... | collective-permute-start | bytes 15728648 | tf_op jit(solution)/shard_map/ppermute | solution.py:356
  2.8 28.9 %all-to-all-start = ((bf16[32,32,384]{2,1,0:T(8,128)(2,1)}), bf16[32,32,384]{2,1,0:T(8,128)(2,1)S(1)}, u32[]{:S(2)}, u32[]{:S(2)}) async-start(bf16[32,32,384]{2,1,0:T(8,128)(2,1)} %norm.1), calls=%async_computation | async-start | bytes 1572864 | tf_op jit(solution)/shard_map/all_to_all | solution.py:207
  33.9 1.9 %collective-permute-start.1 = (bf16[3,128,128]{2,1,0:T(8,128)(2,1)S(1)}, bf16[3,128,128]{2,1,0:T(8,128)(2,1)S(1)}, u32[]{:S(2)}, u32[]{:S(2)}) collective-permute-start(bf16[3,128,128]{2,1,0:T(8,128)(2,1)S(1)} %get-tuple-element.26), channel_id=1, source_target_pairs={{0,1},{1,0},{2,3},{3,2},{4,5},{5,4},{6,7},{7,6},{8,9},{9,8},{10,11... | collective-permute-start | bytes 294920 | tf_op jit(solution)/shard_map/ppermute | solution.py:232
  35.2 4.3 %collective-permute-start = (bf16[1,128,128]{2,1,0:T(8,128)(2,1)S(1)}, bf16[1,128,128]{2,1,0:T(8,128)(2,1)S(1)}, u32[]{:S(2)}, u32[]{:S(2)}) collective-permute-start(bf16[1,128,128]{2,1,0:T(8,128)(2,1)S(1)} %get-tuple-element.24), channel_id=1, source_target_pairs={{0,1},{1,0},{2,3},{3,2},{4,5},{5,4},{6,7},{7,6},{8,9},{9,8},{10,11... | collective-permute-start | bytes 98312 | tf_op jit(solution)/shard_map/ppermute | solution.py:232
  35.8 5.9 %collective-permute-start.4 = (bf16[2,128,128]{2,1,0:T(8,128)(2,1)S(1)}, bf16[2,128,128]{2,1,0:T(8,128)(2,1)S(1)}, u32[]{:S(2)}, u32[]{:S(2)}) collective-permute-start(bf16[2,128,128]{2,1,0:T(8,128)(2,1)S(1)} %pad_maximum_fusion.2), channel_id=1, source_target_pairs={{0,24},{8,16},{16,8},{24,0},{1,25},{9,17},{17,9},{25,1},{2,26},{10... | collective-permute-start | bytes 196616 | tf_op jit(solution)/shard_map/ppermute | solution.py:232
  36.4 5.5 %collective-permute-start.3 = (bf16[2,128,128]{2,1,0:T(8,128)(2,1)S(1)}, bf16[2,128,128]{2,1,0:T(8,128)(2,1)S(1)}, u32[]{:S(2)}, u32[]{:S(2)}) collective-permute-start(bf16[2,128,128]{2,1,0:T(8,128)(2,1)S(1)} %pad_maximum_fusion.1), channel_id=1, source_target_pairs={{0,16},{8,24},{16,0},{24,8},{1,17},{9,25},{17,1},{25,9},{2,18},{10... | collective-permute-start | bytes 196616 | tf_op jit(solution)/shard_map/ppermute | solution.py:232
  37.8 4.3 %collective-permute-start.2 = (bf16[2,128,128]{2,1,0:T(8,128)(2,1)S(1)}, bf16[2,128,128]{2,1,0:T(8,128)(2,1)S(1)}, u32[]{:S(2)}, u32[]{:S(2)}) collective-permute-start(bf16[2,128,128]{2,1,0:T(8,128)(2,1)S(1)} %pad_maximum_fusion), channel_id=1, source_target_pairs={{0,8},{8,0},{16,24},{24,16},{1,9},{9,1},{17,25},{25,17},{2,10},{10... | collective-permute-start | bytes 196616 | tf_op jit(solution)/shard_map/ppermute | solution.py:232
  39.5 6.0 %copy-start.1 = (bf16[5120]{0:T(1024)(128)(2,1)S(1)}, bf16[5120]{0:T(1024)(128)(2,1)}, u32[]{:S(2)}) copy-start(bf16[5120]{0:T(1024)(128)(2,1)} %param.18) | copy-start | bytes 30724
  45.2 5.6 %collective-permute-start.6 = (bf16[32,2560]{1,0:T(8,128)(2,1)S(1)}, bf16[32,2560]{1,0:T(8,128)(2,1)S(1)}, u32[]{:S(2)}, u32[]{:S(2)}) collective-permute-start(bf16[32,2560]{1,0:T(8,128)(2,1)S(1)} %get-tuple-element.29), channel_id=1, source_target_pairs={{0,2},{1,3},{2,0},{3,1},{4,6},{5,7},{6,4},{7,5},{8,10},{9,11},{10,... | collective-permute-start | bytes 491528 | tf_op jit(solution)/shard_map/ppermute | solution.py:356
  45.5 23.8 %copy-start = (bf16[1,32,5120]{2,1,0:T(8,128)(2,1)S(1)}, bf16[1,32,5120]{2,1,0:T(8,128)(2,1)}, u32[]{:S(2)}) copy-start(bf16[1,32,5120]{2,1,0:T(8,128)(2,1)} %param.11) | copy-start | bytes 983044
  48.7 12.4 %collective-permute-start.9 = (bf16[32,2560]{1,0:T(8,128)(2,1)S(1)}, bf16[32,2560]{1,0:T(8,128)(2,1)S(1)}, u32[]{:S(2)}, u32[]{:S(2)}) collective-permute-start(bf16[32,2560]{1,0:T(8,128)(2,1)S(1)} %get-tuple-element.34), channel_id=1, source_target_pairs={{0,2},{1,3},{2,0},{3,1},{4,6},{5,7},{6,4},{7,5},{8,10},{9,11},{10,... | collective-permute-start | bytes 491528 | tf_op jit(solution)/shard_map/ppermute | solution.py:356
  50.8 13.9 %collective-permute-start.7 = (bf16[32,2560]{1,0:T(8,128)(2,1)S(1)}, bf16[32,2560]{1,0:T(8,128)(2,1)S(1)}, u32[]{:S(2)}, u32[]{:S(2)}) collective-permute-start(bf16[32,2560]{1,0:T(8,128)(2,1)S(1)} %get-tuple-element.30), channel_id=1, source_target_pairs={{0,2},{1,3},{2,0},{3,1},{4,6},{5,7},{6,4},{7,5},{8,10},{9,11},{10,... | collective-permute-start | bytes 491528 | tf_op jit(solution)/shard_map/ppermute | solution.py:356
  50.9 13.7 %collective-permute-start.8 = (bf16[32,2560]{1,0:T(8,128)(2,1)S(1)}, bf16[32,2560]{1,0:T(8,128)(2,1)S(1)}, u32[]{:S(2)}, u32[]{:S(2)}) collective-permute-start(bf16[32,2560]{1,0:T(8,128)(2,1)S(1)} %add_convert_fusion.1), channel_id=1, source_target_pairs={{0,4},{1,5},{2,6},{3,7},{4,0},{5,1},{6,2},{7,3},{8,12},{9,13},{10,... | collective-permute-start | bytes 491528 | tf_op jit(solution)/shard_map/ppermute | solution.py:356
  61.1 6.8 %collective-permute-start.10 = (bf16[32,2560]{1,0:T(8,128)(2,1)S(1)}, bf16[32,2560]{1,0:T(8,128)(2,1)S(1)}, u32[]{:S(2)}, u32[]{:S(2)}) collective-permute-start(bf16[32,2560]{1,0:T(8,128)(2,1)S(1)} %get-tuple-element.35), channel_id=1, source_target_pairs={{0,2},{1,3},{2,0},{3,1},{4,6},{5,7},{6,4},{7,5},{8,10},{9,11},{10,... | collective-permute-start | bytes 491528 | tf_op jit(solution)/shard_map/ppermute | solution.py:356
  61.2 8.1 %collective-permute-start.11 = (bf16[32,2560]{1,0:T(8,128)(2,1)S(1)}, bf16[32,2560]{1,0:T(8,128)(2,1)S(1)}, u32[]{:S(2)}, u32[]{:S(2)}) collective-permute-start(bf16[32,2560]{1,0:T(8,128)(2,1)S(1)} %add_convert_fusion), channel_id=1, source_target_pairs={{0,4},{1,5},{2,6},{3,7},{4,0},{5,1},{6,2},{7,3},{8,12},{9,13},{10,... | collective-permute-start | bytes 491528 | tf_op jit(solution)/shard_map/ppermute | solution.py:356

commit v13 on v12

--- a/solution.py
+++ b/solution.py
@@ -210,7 +210,7 @@
     slot = lax.axis_index("frame").astype(jnp.int32)
     index = jnp.concatenate([jnp.stack([slot, me % 2]), slot_order])
 
-    def attend(picked, name):
+    def attend(picked, index, name):
         count = len(picked)
         return pl.pallas_call(
             functools.partial(spread_attention_kernel, n, frames, picked),
@@ -232,9 +232,9 @@
         return lax.ppermute(value, axis, [(i, i ^ distance) for i in range(size)])
 
     far = list(range(frames - 1, 0, -1))
-    far_mine, far_given = attend(far, "attention_far")
+    far_mine, far_given = attend(far, index, "attention_far")
     far_got = across(far_given, "seq", 1)
-    near_mine, near_given = attend([0], "attention_near")
+    near_mine, near_given = attend([0], lax.optimization_barrier((index, far_got))[0], "attention_near")
     near_got = across(near_given, "seq", 1)
     found = {0: jnp.concatenate([near_mine, near_got], axis=0)}
     for place, d in enumerate(far):

time: 70.5 us -> 69.7 us (0.989)
  waiting for transfers between devices: 34.4 us -> 32.1 us
  starting transfers between devices: 17.6 us -> 19.2 us
    ppermute x7, waiting for transfers between devices: 14.8 us -> 12.3 us  [across(): return lax.ppermute(value, axis, [(i, i ^ distance) for i in range(n)])]
    ppermute x7, starting transfers between devices: 6.38 us -> 8.47 us  [across(): return lax.ppermute(value, axis, [(i, i ^ distance) for i in range(n)])]
  transfers between devices with their start and end apart: 13 -> 13, of which waited for: 9 -> 8; matrix products, arithmetic and copies ran while one was open for 5% -> 5% of each run, Pallas kernels for 13% -> 13%
where the time goes in v13:
time: 69.7 us; the launch traced here: 69.4 us
  waiting for transfers between devices  32.1 us (46%)
  starting transfers between devices  19.2 us (28%)
  Pallas kernels  12 us (17%)
  other arithmetic  2.76 us (4%)
  between operations  2.08 us (3%)
  local copies, waits for them, and re-layouts  1.3 us (2%)
    all_to_all x1, waiting for transfers between devices, spread_attention(): lax.all_to_all(sends, ('frame', 'seq'), split_axis=0, concat_axis=0, tile...  17 us
    ppermute x7, waiting for transfers between devices, across(): return lax.ppermute(value, axis, [(i, i ^ distance) for i in range(n)])  12.3 us
    ppermute x7, starting transfers between devices, across(): return lax.ppermute(value, axis, [(i, i ^ distance) for i in range(n)])  8.47 us
    all_to_all x1, starting transfers between devices, spread_attention(): lax.all_to_all(sends, ('frame', 'seq'), split_axis=0, concat_axis=0, tile...  6.96 us
    pallas_call x2, Pallas kernels, shards(): pl.pallas_call(functools.partial(projection_kernel, chips, sources), grid...  6.29 us
    ppermute x5, starting transfers between devices, across(): return lax.ppermute(value, axis, [(i, i ^ distance) for i in range(size)])  3.82 us
    pallas_call x2, Pallas kernels, attend(): pl.pallas_call(functools.partial(spread_attention_kernel, n, frames, pick...  3.37 us
    ppermute x5, waiting for transfers between devices, across(): return lax.ppermute(value, axis, [(i, i ^ distance) for i in range(size)])  2.7 us
  transfers between devices with their start and end apart: 13, of which 8 were waited for; matrix products, arithmetic and copies ran while one was open for 5% of the time, Pallas kernels for 13%

profile of v13, /device:TPU:0, one launch (start us, length us, event | category | flops | bytes accessed | tf_op | source)
XLA Modules:
  0.0 69.4 jit_solution(7814370814290802085)
XLA Ops:
  0.0 0.5 collective-permute-start.5
  0.5 2.3 %norm.1 = bf16[32,32,384]{2,1,0:T(8,128)(2,1)} custom-call(bf16[32,4096]{1,0:T(8,128)(2,1)} %bitcast.14, bf16[32,4096]{1,0:T(8,128)(2,1)} %bitcast.15, bf16[32,4096]{1,0:T(8,128)(2,1)} %bitcast.16, f32[1,4096]{1,0:T(1,128)} %bitcast.18, f32[1,4096]{1,0:T(1,128)} %bitcast.19), custom_call_target="tpu_custom_call" | custom-call | tf_op jit(solution)/shard_map/norm/pallas_call | solution.py:200
  2.8 7.0 %all-to-all-start = ((bf16[32,32,384]{2,1,0:T(8,128)(2,1)}), bf16[32,32,384]{2,1,0:T(8,128)(2,1)S(1)}, u32[]{:S(2)}, u32[]{:S(2)}) async-start(bf16[32,32,384]{2,1,0:T(8,128)(2,1)} %norm.1), calls=%async_computation | async-start | bytes 1572864 | tf_op jit(solution)/shard_map/all_to_all | solution.py:207
  9.7 1.3 %dynamic_slice.8 = s32[1]{0:T(128)} dynamic-slice(s32[4]{0:T(128)} %param.20, s32[]{:T(128)S(6)} %select_n.20), dynamic_slice_sizes={1} | dynamic-slice | bytes 12 | tf_op jit(solution)/shard_map/jit(dynamic_index_in_dim)/dynamic_slice | solution.py:368
  13.0 0.9 %dynamic-slice_convert_fusion = f32[1,5120]{1,0:T(1,128)S(1)} fusion(bf16[64,5120]{1,0:T(8,128)(2,1)} %param.19, s32[]{:T(128)S(6)} %select_n.21), kind=kLoop, calls=%fused_computation.11 | loop fusion | flops 5120 | bytes 30724 | tf_op jit(solution)/shard_map/convert_element_type | solution.py:369
  13.9 0.7 %pad_add_fusion.1.index_ref = s32[6]{0:T(128)S(1)} fusion(s32[4]{0:T(128)} %param.21, s32[1]{0:T(128)} %bitcast.4, s32[1]{0:T(128)} %bitcast.1), kind=kLoop, calls=%fused_computation.15 | loop fusion | flops 12 | bytes 48 | tf_op jit(solution)/shard_map/concatenate | solution.py:211
  14.6 17.0 %all-to-all-done.rows_ref = bf16[32,32,384]{2,1,0:T(8,128)(2,1)S(1)} async-done(((bf16[32,32,384]{2,1,0:T(8,128)(2,1)}), bf16[32,32,384]{2,1,0:T(8,128)(2,1)S(1)}, u32[]{:S(2)}, u32[]{:S(2)}) %all-to-all-start) | async-done | bytes 786464 | tf_op jit(solution)/shard_map/all_to_all | solution.py:207
  31.7 2.2 %attention_far.1 = (bf16[3,128,128]{2,1,0:T(8,128)(2,1)S(1)}, bf16[3,128,128]{2,1,0:T(8,128)(2,1)S(1)}) custom-call(s32[6]{0:T(128)S(1)} %pad_add_fusion.1.index_ref, bf16[32,32,384]{2,1,0:T(8,128)(2,1)S(1)} %all-to-all-done.rows_ref), custom_call_target="tpu_custom_call" | custom-call | flops 402653184 | bytes 1048576 | tf_op jit(solution)/shard_map/attention_far/pallas_call | solution.py:215
  34.0 1.3 %collective-permute-done = bf16[3,128,128]{2,1,0:T(8,128)(2,1)S(1)} collective-permute-done((bf16[3,128,128]{2,1,0:T(8,128)(2,1)S(1)}, bf16[3,128,128]{2,1,0:T(8,128)(2,1)S(1)}, u32[]{:S(2)}, u32[]{:S(2)}) %collective-permute-start) | collective-permute-done | bytes 98336 | tf_op jit(solution)/shard_map/ppermute | solution.py:232
  35.3 0.6 collective-permute-start.4
  35.9 1.5 %collective-permute-start.3 = (bf16[2,128,128]{2,1,0:T(8,128)(2,1)S(1)}, bf16[2,128,128]{2,1,0:T(8,128)(2,1)S(1)}, u32[]{:S(2)}, u32[]{:S(2)}) collective-permute-start(bf16[2,128,128]{2,1,0:T(8,128)(2,1)S(1)} %pad_maximum_fusion.1), channel_id=1, source_target_pairs={{0,16},{8,24},{16,0},{24,8},{1,17},{9,25},{17,1},{25,9},{2,18},{10... | collective-permute-start | bytes 196616 | tf_op jit(solution)/shard_map/ppermute | solution.py:232
  37.4 1.6 %collective-permute-start.2 = (bf16[2,128,128]{2,1,0:T(8,128)(2,1)S(1)}, bf16[2,128,128]{2,1,0:T(8,128)(2,1)S(1)}, u32[]{:S(2)}, u32[]{:S(2)}) collective-permute-start(bf16[2,128,128]{2,1,0:T(8,128)(2,1)S(1)} %pad_maximum_fusion), channel_id=1, source_target_pairs={{0,8},{8,0},{16,24},{24,16},{1,9},{9,1},{17,25},{25,17},{2,10},{10... | collective-permute-start | bytes 196616 | tf_op jit(solution)/shard_map/ppermute | solution.py:232
  39.0 1.2 %attention_near.1 = (bf16[1,128,128]{2,1,0:T(8,128)(2,1)S(1)}, bf16[1,128,128]{2,1,0:T(8,128)(2,1)S(1)}) custom-call(s32[6]{0:T(128)S(1)} %pad_add_fusion.1.index_ref, bf16[32,32,384]{2,1,0:T(8,128)(2,1)S(1)} %all-to-all-done.rows_ref), custom_call_target="tpu_custom_call" | custom-call | flops 134217728 | bytes 1048576 | tf_op jit(solution)/shard_map/attention_near/pallas_call | solution.py:215
  40.2 1.2 %collective-permute-done.1 = bf16[1,128,128]{2,1,0:T(8,128)(2,1)S(1)} collective-permute-done((bf16[1,128,128]{2,1,0:T(8,128)(2,1)S(1)}, bf16[1,128,128]{2,1,0:T(8,128)(2,1)S(1)}, u32[]{:S(2)}, u32[]{:S(2)}) %collective-permute-start.1) | collective-permute-done | bytes 32800 | tf_op jit(solution)/shard_map/ppermute | solution.py:232
  41.7 3.1 %projection_0.1 = (f32[32,2560]{1,0:T(8,128)S(1)}, bf16[32,2560]{1,0:T(8,128)(2,1)S(1)}, f32[32,2560]{1,0:T(8,128)S(1)}, bf16[32,2560]{1,0:T(8,128)(2,1)S(1)}) custom-call(s32[2]{0:T(128)S(1)} %pad_add_fusion.index_ref, bf16[2,128,128]{2,1,0:T(8,128)(2,1)S(1)} %constant_dynamic-update-slice_fusion.refs_0_, ...), custom_call_target="tpu_custom_call" | custom-call | flops 671088640 | bytes 5898240 | tf_op jit(solution)/shard_map/projection_0/pallas_call | solution.py:379
  45.0 3.2 %projection_1.1 = (f32[32,2560]{1,0:T(8,128)S(1)}, bf16[32,2560]{1,0:T(8,128)(2,1)S(1)}, f32[32,2560]{1,0:T(8,128)S(1)}, bf16[32,2560]{1,0:T(8,128)(2,1)S(1)}) custom-call(s32[2]{0:T(128)S(1)} %pad_add_fusion.index_ref, bf16[2,128,128]{2,1,0:T(8,128)(2,1)S(1)} %constant_dynamic-update-slice_fusion.refs_0_, ...), custom_call_target="tpu_custom_call" | custom-call | flops 671088640 | bytes 5898240 | tf_op jit(solution)/shard_map/projection_1/pallas_call | solution.py:379
  48.2 2.0 %collective-permute-start.9 = (bf16[32,2560]{1,0:T(8,128)(2,1)S(1)}, bf16[32,2560]{1,0:T(8,128)(2,1)S(1)}, u32[]{:S(2)}, u32[]{:S(2)}) collective-permute-start(bf16[32,2560]{1,0:T(8,128)(2,1)S(1)} %get-tuple-element.36), channel_id=1, source_target_pairs={{0,2},{1,3},{2,0},{3,1},{4,6},{5,7},{6,4},{7,5},{8,10},{9,11},{10,... | collective-permute-start | bytes 491528 | tf_op jit(solution)/shard_map/ppermute | solution.py:356
  50.2 0.9 %collective-permute-done.6 = bf16[32,2560]{1,0:T(8,128)(2,1)S(1)} collective-permute-done((bf16[32,2560]{1,0:T(8,128)(2,1)S(1)}, bf16[32,2560]{1,0:T(8,128)(2,1)S(1)}, u32[]{:S(2)}, u32[]{:S(2)}) %collective-permute-start.6) | collective-permute-done | bytes 163872 | tf_op jit(solution)/shard_map/ppermute | solution.py:356
  51.3 0.8 %collective-permute-start.8 = (bf16[32,2560]{1,0:T(8,128)(2,1)S(1)}, bf16[32,2560]{1,0:T(8,128)(2,1)S(1)}, u32[]{:S(2)}, u32[]{:S(2)}) collective-permute-start(bf16[32,2560]{1,0:T(8,128)(2,1)S(1)} %add_convert_fusion.1), channel_id=1, source_target_pairs={{0,4},{1,5},{2,6},{3,7},{4,0},{5,1},{6,2},{7,3},{8,12},{9,13},{10,... | collective-permute-start | bytes 491528 | tf_op jit(solution)/shard_map/ppermute | solution.py:356
  52.1 5.7 %collective-permute-done.9 = bf16[32,2560]{1,0:T(8,128)(2,1)S(1)} collective-permute-done((bf16[32,2560]{1,0:T(8,128)(2,1)S(1)}, bf16[32,2560]{1,0:T(8,128)(2,1)S(1)}, u32[]{:S(2)}, u32[]{:S(2)}) %collective-permute-start.9) | collective-permute-done | bytes 163872 | tf_op jit(solution)/shard_map/ppermute | solution.py:356
  57.8 4.9 %collective-permute-start.11 = (bf16[32,2560]{1,0:T(8,128)(2,1)S(1)}, bf16[32,2560]{1,0:T(8,128)(2,1)S(1)}, u32[]{:S(2)}, u32[]{:S(2)}) collective-permute-start(bf16[32,2560]{1,0:T(8,128)(2,1)S(1)} %add_convert_fusion), channel_id=1, source_target_pairs={{0,4},{1,5},{2,6},{3,7},{4,0},{5,1},{6,2},{7,3},{8,12},{9,13},{10,... | collective-permute-start | bytes 491528 | tf_op jit(solution)/shard_map/ppermute | solution.py:356
  62.7 1.3 %collective-permute-done.7 = bf16[32,2560]{1,0:T(8,128)(2,1)S(1)} collective-permute-done((bf16[32,2560]{1,0:T(8,128)(2,1)S(1)}, bf16[32,2560]{1,0:T(8,128)(2,1)S(1)}, u32[]{:S(2)}, u32[]{:S(2)}) %collective-permute-start.7) | collective-permute-done | bytes 163872 | tf_op jit(solution)/shard_map/ppermute | solution.py:356
  64.2 4.4 %collective-permute-done.10 = bf16[32,2560]{1,0:T(8,128)(2,1)S(1)} collective-permute-done((bf16[32,2560]{1,0:T(8,128)(2,1)S(1)}, bf16[32,2560]{1,0:T(8,128)(2,1)S(1)}, u32[]{:S(2)}, u32[]{:S(2)}) %collective-permute-start.10) | collective-permute-done | bytes 163872 | tf_op jit(solution)/shard_map/ppermute | solution.py:356
  68.6 0.8 %fusion.2 = bf16[1,32,5120]{2,1,0:T(8,128)(2,1)} fusion(f32[1,32,2560]{2,1,0:T(8,128)S(1)} %add_bitcast_fusion, f32[1,32,2560]{2,1,0:T(8,128)S(1)} %add_bitcast_fusion.1, bf16[1,32,5120]{2,1,0:T(8,128)(2,1)S(1)} %copy-done, f32[5120]{0:T(1024)S(1)} %convert_element_type.48, f32[5120]{0:T(1024)S(1)} %bitcast.17), kind=kLoop, calls=%fused_computation.3 | loop fusion | flops 983040 | bytes 1351680 | tf_op jit(solution)/shard_map/convert_element_type | solution.py:415
  (28 shorter events, 1.0 us)
Async XLA Ops:
  0.0 41.7 %collective-permute-start.5 = (bf16[512,5120]{1,0:T(8,128)(2,1)}, bf16[512,5120]{1,0:T(8,128)(2,1)}, u32[]{:S(2)}, u32[]{:S(2)}) collective-permute-start(bf16[512,5120]{1,0:T(8,128)(2,1)} %refs_4_.3), channel_id=1, source_target_pairs={{0,1},{1,0},{2,3},{3,2},{4,5},{5,4},{6,7},{7,6},{8,9},{9,8},{10,11... | collective-permute-start | bytes 15728648 | tf_op jit(solution)/shard_map/ppermute | solution.py:356
  2.8 28.9 %all-to-all-start = ((bf16[32,32,384]{2,1,0:T(8,128)(2,1)}), bf16[32,32,384]{2,1,0:T(8,128)(2,1)S(1)}, u32[]{:S(2)}, u32[]{:S(2)}) async-start(bf16[32,32,384]{2,1,0:T(8,128)(2,1)} %norm.1), calls=%async_computation | async-start | bytes 1572864 | tf_op jit(solution)/shard_map/all_to_all | solution.py:207
  33.9 1.4 %collective-permute-start = (bf16[3,128,128]{2,1,0:T(8,128)(2,1)S(1)}, bf16[3,128,128]{2,1,0:T(8,128)(2,1)S(1)}, u32[]{:S(2)}, u32[]{:S(2)}) collective-permute-start(bf16[3,128,128]{2,1,0:T(8,128)(2,1)S(1)} %get-tuple-element.24), channel_id=1, source_target_pairs={{0,1},{1,0},{2,3},{3,2},{4,5},{5,4},{6,7},{7,6},{8,9},{9,8},{10,11... | collective-permute-start | bytes 294920 | tf_op jit(solution)/shard_map/ppermute | solution.py:232
  35.3 6.2 %collective-permute-start.4 = (bf16[2,128,128]{2,1,0:T(8,128)(2,1)S(1)}, bf16[2,128,128]{2,1,0:T(8,128)(2,1)S(1)}, u32[]{:S(2)}, u32[]{:S(2)}) collective-permute-start(bf16[2,128,128]{2,1,0:T(8,128)(2,1)S(1)} %pad_maximum_fusion.2), channel_id=1, source_target_pairs={{0,24},{8,16},{16,8},{24,0},{1,25},{9,17},{17,9},{25,1},{2,26},{10... | collective-permute-start | bytes 196616 | tf_op jit(solution)/shard_map/ppermute | solution.py:232
  35.9 5.6 %collective-permute-start.3 = (bf16[2,128,128]{2,1,0:T(8,128)(2,1)S(1)}, bf16[2,128,128]{2,1,0:T(8,128)(2,1)S(1)}, u32[]{:S(2)}, u32[]{:S(2)}) collective-permute-start(bf16[2,128,128]{2,1,0:T(8,128)(2,1)S(1)} %pad_maximum_fusion.1), channel_id=1, source_target_pairs={{0,16},{8,24},{16,0},{24,8},{1,17},{9,25},{17,1},{25,9},{2,18},{10... | collective-permute-start | bytes 196616 | tf_op jit(solution)/shard_map/ppermute | solution.py:232
  37.4 4.3 %collective-permute-start.2 = (bf16[2,128,128]{2,1,0:T(8,128)(2,1)S(1)}, bf16[2,128,128]{2,1,0:T(8,128)(2,1)S(1)}, u32[]{:S(2)}, u32[]{:S(2)}) collective-permute-start(bf16[2,128,128]{2,1,0:T(8,128)(2,1)S(1)} %pad_maximum_fusion), channel_id=1, source_target_pairs={{0,8},{8,0},{16,24},{24,16},{1,9},{9,1},{17,25},{25,17},{2,10},{10... | collective-permute-start | bytes 196616 | tf_op jit(solution)/shard_map/ppermute | solution.py:232
  40.2 1.3 %collective-permute-start.1 = (bf16[1,128,128]{2,1,0:T(8,128)(2,1)S(1)}, bf16[1,128,128]{2,1,0:T(8,128)(2,1)S(1)}, u32[]{:S(2)}, u32[]{:S(2)}) collective-permute-start(bf16[1,128,128]{2,1,0:T(8,128)(2,1)S(1)} %get-tuple-element.27), channel_id=1, source_target_pairs={{0,1},{1,0},{2,3},{3,2},{4,5},{5,4},{6,7},{7,6},{8,9},{9,8},{10,11... | collective-permute-start | bytes 98312 | tf_op jit(solution)/shard_map/ppermute | solution.py:232
  41.4 3.5 %copy-start.1 = (bf16[5120]{0:T(1024)(128)(2,1)S(1)}, bf16[5120]{0:T(1024)(128)(2,1)}, u32[]{:S(2)}) copy-start(bf16[5120]{0:T(1024)(128)(2,1)} %param.18) | copy-start | bytes 30724
  44.8 6.3 %collective-permute-start.6 = (bf16[32,2560]{1,0:T(8,128)(2,1)S(1)}, bf16[32,2560]{1,0:T(8,128)(2,1)S(1)}, u32[]{:S(2)}, u32[]{:S(2)}) collective-permute-start(bf16[32,2560]{1,0:T(8,128)(2,1)S(1)} %get-tuple-element.31), channel_id=1, source_target_pairs={{0,2},{1,3},{2,0},{3,1},{4,6},{5,7},{6,4},{7,5},{8,10},{9,11},{10,... | collective-permute-start | bytes 491528 | tf_op jit(solution)/shard_map/ppermute | solution.py:356
  45.0 23.6 %copy-start = (bf16[1,32,5120]{2,1,0:T(8,128)(2,1)S(1)}, bf16[1,32,5120]{2,1,0:T(8,128)(2,1)}, u32[]{:S(2)}) copy-start(bf16[1,32,5120]{2,1,0:T(8,128)(2,1)} %param.11) | copy-start | bytes 983044
  48.2 9.6 %collective-permute-start.9 = (bf16[32,2560]{1,0:T(8,128)(2,1)S(1)}, bf16[32,2560]{1,0:T(8,128)(2,1)S(1)}, u32[]{:S(2)}, u32[]{:S(2)}) collective-permute-start(bf16[32,2560]{1,0:T(8,128)(2,1)S(1)} %get-tuple-element.36), channel_id=1, source_target_pairs={{0,2},{1,3},{2,0},{3,1},{4,6},{5,7},{6,4},{7,5},{8,10},{9,11},{10,... | collective-permute-start | bytes 491528 | tf_op jit(solution)/shard_map/ppermute | solution.py:356
  51.1 13.0 %collective-permute-start.7 = (bf16[32,2560]{1,0:T(8,128)(2,1)S(1)}, bf16[32,2560]{1,0:T(8,128)(2,1)S(1)}, u32[]{:S(2)}, u32[]{:S(2)}) collective-permute-start(bf16[32,2560]{1,0:T(8,128)(2,1)S(1)} %get-tuple-element.32), channel_id=1, source_target_pairs={{0,2},{1,3},{2,0},{3,1},{4,6},{5,7},{6,4},{7,5},{8,10},{9,11},{10,... | collective-permute-start | bytes 491528 | tf_op jit(solution)/shard_map/ppermute | solution.py:356
  51.3 12.8 %collective-permute-start.8 = (bf16[32,2560]{1,0:T(8,128)(2,1)S(1)}, bf16[32,2560]{1,0:T(8,128)(2,1)S(1)}, u32[]{:S(2)}, u32[]{:S(2)}) collective-permute-start(bf16[32,2560]{1,0:T(8,128)(2,1)S(1)} %add_convert_fusion.1), channel_id=1, source_target_pairs={{0,4},{1,5},{2,6},{3,7},{4,0},{5,1},{6,2},{7,3},{8,12},{9,13},{10,... | collective-permute-start | bytes 491528 | tf_op jit(solution)/shard_map/ppermute | solution.py:356
  57.8 10.8 %collective-permute-start.10 = (bf16[32,2560]{1,0:T(8,128)(2,1)S(1)}, bf16[32,2560]{1,0:T(8,128)(2,1)S(1)}, u32[]{:S(2)}, u32[]{:S(2)}) collective-permute-start(bf16[32,2560]{1,0:T(8,128)(2,1)S(1)} %get-tuple-element.37), channel_id=1, source_target_pairs={{0,2},{1,3},{2,0},{3,1},{4,6},{5,7},{6,4},{7,5},{8,10},{9,11},{10,... | collective-permute-start | bytes 491528 | tf_op jit(solution)/shard_map/ppermute | solution.py:356
  57.8 10.7 %collective-permute-start.11 = (bf16[32,2560]{1,0:T(8,128)(2,1)S(1)}, bf16[32,2560]{1,0:T(8,128)(2,1)S(1)}, u32[]{:S(2)}, u32[]{:S(2)}) collective-permute-start(bf16[32,2560]{1,0:T(8,128)(2,1)S(1)} %add_convert_fusion), channel_id=1, source_target_pairs={{0,4},{1,5},{2,6},{3,7},{4,0},{5,1},{6,2},{7,3},{8,12},{9,13},{10,... | collective-permute-start | bytes 491528 | tf_op jit(solution)/shard_map/ppermute | solution.py:356

commit v14 on v13

--- a/solution.py
+++ b/solution.py
@@ -369,13 +369,12 @@
     gate_row = lax.dynamic_index_in_dim(gate_table, level, keepdims=True).astype(jnp.float32)
     index, gate_row = lax.optimization_barrier((index, gate_row))
 
-    cuts = 2
-    columns = model // cuts
-    tile = columns // 2
+    fifth = model // 5
     sources = len(attended)
     halves = []
-    for cut in range(cuts):
-        weight_spec = pl.BlockSpec((width, tile), lambda i, first=2 * cut: (0, first + i))
+    for cut, (begin, columns) in enumerate(((0, 3 * fifth), (3 * fifth, 2 * fifth))):
+        tile = columns // 2
+        weight_spec = pl.BlockSpec((width, tile), lambda i, first=begin // tile: (0, first + i))
         partial_sums = pl.pallas_call(
             functools.partial(projection_kernel, chips, sources),
             grid=(columns // tile,),

time: 69.7 us -> 70.8 us (1.016)
  waiting for transfers between devices: 32.1 us -> 35.3 us
  starting transfers between devices: 19.2 us -> 17.1 us
    ppermute x7, waiting for transfers between devices: 12.3 us -> 15.5 us  [across(): return lax.ppermute(value, axis, [(i, i ^ distance) for i in range(n)])]
    ppermute x7, starting transfers between devices: 8.47 us -> 6.37 us  [across(): return lax.ppermute(value, axis, [(i, i ^ distance) for i in range(n)])]
  transfers between devices with their start and end apart: 13 -> 13, of which waited for: 8 -> 8; matrix products, arithmetic and copies ran while one was open for 5% -> 4% of each run, Pallas kernels for 13% -> 13%
where the time goes in v14:
time: 70.8 us; the launch traced here: 70.5 us
  waiting for transfers between devices  35.3 us (50%)
  starting transfers between devices  17.1 us (24%)
  Pallas kernels  12 us (17%)
  other arithmetic  2.74 us (4%)
  between operations  2.08 us (3%)
  local copies, waits for them, and re-layouts  1.3 us (2%)
    all_to_all x1, waiting for transfers between devices, spread_attention(): lax.all_to_all(sends, ('frame', 'seq'), split_axis=0, concat_axis=0, tile...  17 us
    ppermute x7, waiting for transfers between devices, across(): return lax.ppermute(value, axis, [(i, i ^ distance) for i in range(n)])  15.5 us
    all_to_all x1, starting transfers between devices, spread_attention(): lax.all_to_all(sends, ('frame', 'seq'), split_axis=0, concat_axis=0, tile...  6.96 us
    ppermute x7, starting transfers between devices, across(): return lax.ppermute(value, axis, [(i, i ^ distance) for i in range(n)])  6.37 us
    pallas_call x2, Pallas kernels, shards(): pl.pallas_call(functools.partial(projection_kernel, chips, sources), grid...  6.3 us
    ppermute x5, starting transfers between devices, across(): return lax.ppermute(value, axis, [(i, i ^ distance) for i in range(size)])  3.82 us
    pallas_call x2, Pallas kernels, attend(): pl.pallas_call(functools.partial(spread_attention_kernel, n, frames, pick...  3.37 us
    ppermute x5, waiting for transfers between devices, across(): return lax.ppermute(value, axis, [(i, i ^ distance) for i in range(size)])  2.7 us
  transfers between devices with their start and end apart: 13, of which 8 were waited for; matrix products, arithmetic and copies ran while one was open for 4% of the time, Pallas kernels for 13%

profile of v14, /device:TPU:0, one launch (start us, length us, event | category | flops | bytes accessed | tf_op | source)
XLA Modules:
  0.0 70.5 jit_solution(9489690121278457213)
XLA Ops:
  0.0 0.5 collective-permute-start.5
  0.5 2.3 %norm.1 = bf16[32,32,384]{2,1,0:T(8,128)(2,1)} custom-call(bf16[32,4096]{1,0:T(8,128)(2,1)} %bitcast.14, bf16[32,4096]{1,0:T(8,128)(2,1)} %bitcast.15, bf16[32,4096]{1,0:T(8,128)(2,1)} %bitcast.16, f32[1,4096]{1,0:T(1,128)} %bitcast.18, f32[1,4096]{1,0:T(1,128)} %bitcast.19), custom_call_target="tpu_custom_call" | custom-call | tf_op jit(solution)/shard_map/norm/pallas_call | solution.py:200
  2.8 7.0 %all-to-all-start = ((bf16[32,32,384]{2,1,0:T(8,128)(2,1)}), bf16[32,32,384]{2,1,0:T(8,128)(2,1)S(1)}, u32[]{:S(2)}, u32[]{:S(2)}) async-start(bf16[32,32,384]{2,1,0:T(8,128)(2,1)} %norm.1), calls=%async_computation | async-start | bytes 1572864 | tf_op jit(solution)/shard_map/all_to_all | solution.py:207
  9.7 1.3 %dynamic_slice.8 = s32[1]{0:T(128)} dynamic-slice(s32[4]{0:T(128)} %param.20, s32[]{:T(128)S(6)} %select_n.20), dynamic_slice_sizes={1} | dynamic-slice | bytes 12 | tf_op jit(solution)/shard_map/jit(dynamic_index_in_dim)/dynamic_slice | solution.py:368
  13.0 0.9 %dynamic-slice_convert_fusion = f32[1,5120]{1,0:T(1,128)S(1)} fusion(bf16[64,5120]{1,0:T(8,128)(2,1)} %param.19, s32[]{:T(128)S(6)} %select_n.21), kind=kLoop, calls=%fused_computation.11 | loop fusion | flops 5120 | bytes 30724 | tf_op jit(solution)/shard_map/convert_element_type | solution.py:369
  13.9 0.7 %pad_add_fusion.1.index_ref = s32[6]{0:T(128)S(1)} fusion(s32[4]{0:T(128)} %param.21, s32[1]{0:T(128)} %bitcast.4, s32[1]{0:T(128)} %bitcast.1), kind=kLoop, calls=%fused_computation.15 | loop fusion | flops 12 | bytes 48 | tf_op jit(solution)/shard_map/concatenate | solution.py:211
  14.6 17.0 %all-to-all-done.rows_ref = bf16[32,32,384]{2,1,0:T(8,128)(2,1)S(1)} async-done(((bf16[32,32,384]{2,1,0:T(8,128)(2,1)}), bf16[32,32,384]{2,1,0:T(8,128)(2,1)S(1)}, u32[]{:S(2)}, u32[]{:S(2)}) %all-to-all-start) | async-done | bytes 786464 | tf_op jit(solution)/shard_map/all_to_all | solution.py:207
  31.7 2.2 %attention_far.1 = (bf16[3,128,128]{2,1,0:T(8,128)(2,1)S(1)}, bf16[3,128,128]{2,1,0:T(8,128)(2,1)S(1)}) custom-call(s32[6]{0:T(128)S(1)} %pad_add_fusion.1.index_ref, bf16[32,32,384]{2,1,0:T(8,128)(2,1)S(1)} %all-to-all-done.rows_ref), custom_call_target="tpu_custom_call" | custom-call | flops 402653184 | bytes 1048576 | tf_op jit(solution)/shard_map/attention_far/pallas_call | solution.py:215
  34.0 1.3 %collective-permute-done = bf16[3,128,128]{2,1,0:T(8,128)(2,1)S(1)} collective-permute-done((bf16[3,128,128]{2,1,0:T(8,128)(2,1)S(1)}, bf16[3,128,128]{2,1,0:T(8,128)(2,1)S(1)}, u32[]{:S(2)}, u32[]{:S(2)}) %collective-permute-start) | collective-permute-done | bytes 98336 | tf_op jit(solution)/shard_map/ppermute | solution.py:232
  35.3 0.6 collective-permute-start.4
  35.9 1.5 %collective-permute-start.3 = (bf16[2,128,128]{2,1,0:T(8,128)(2,1)S(1)}, bf16[2,128,128]{2,1,0:T(8,128)(2,1)S(1)}, u32[]{:S(2)}, u32[]{:S(2)}) collective-permute-start(bf16[2,128,128]{2,1,0:T(8,128)(2,1)S(1)} %pad_maximum_fusion.1), channel_id=1, source_target_pairs={{0,16},{8,24},{16,0},{24,8},{1,17},{9,25},{17,1},{25,9},{2,18},{10... | collective-permute-start | bytes 196616 | tf_op jit(solution)/shard_map/ppermute | solution.py:232
  37.4 1.6 %collective-permute-start.2 = (bf16[2,128,128]{2,1,0:T(8,128)(2,1)S(1)}, bf16[2,128,128]{2,1,0:T(8,128)(2,1)S(1)}, u32[]{:S(2)}, u32[]{:S(2)}) collective-permute-start(bf16[2,128,128]{2,1,0:T(8,128)(2,1)S(1)} %pad_maximum_fusion), channel_id=1, source_target_pairs={{0,8},{8,0},{16,24},{24,16},{1,9},{9,1},{17,25},{25,17},{2,10},{10... | collective-permute-start | bytes 196616 | tf_op jit(solution)/shard_map/ppermute | solution.py:232
  39.0 1.2 %attention_near.1 = (bf16[1,128,128]{2,1,0:T(8,128)(2,1)S(1)}, bf16[1,128,128]{2,1,0:T(8,128)(2,1)S(1)}) custom-call(s32[6]{0:T(128)S(1)} %pad_add_fusion.1.index_ref, bf16[32,32,384]{2,1,0:T(8,128)(2,1)S(1)} %all-to-all-done.rows_ref), custom_call_target="tpu_custom_call" | custom-call | flops 134217728 | bytes 1048576 | tf_op jit(solution)/shard_map/attention_near/pallas_call | solution.py:215
  40.2 1.2 %collective-permute-done.1 = bf16[1,128,128]{2,1,0:T(8,128)(2,1)S(1)} collective-permute-done((bf16[1,128,128]{2,1,0:T(8,128)(2,1)S(1)}, bf16[1,128,128]{2,1,0:T(8,128)(2,1)S(1)}, u32[]{:S(2)}, u32[]{:S(2)}) %collective-permute-start.1) | collective-permute-done | bytes 32800 | tf_op jit(solution)/shard_map/ppermute | solution.py:232
  41.7 2.7 %projection_1.1 = (f32[32,2048]{1,0:T(8,128)S(1)}, bf16[32,2048]{1,0:T(8,128)(2,1)S(1)}, f32[32,2048]{1,0:T(8,128)S(1)}, bf16[32,2048]{1,0:T(8,128)(2,1)S(1)}) custom-call(s32[2]{0:T(128)S(1)} %pad_add_fusion.index_ref, bf16[2,128,128]{2,1,0:T(8,128)(2,1)S(1)} %constant_dynamic-update-slice_fusion.refs_0_, ...), custom_call_target="tpu_custom_call" | custom-call | flops 536870912 | bytes 4718592 | tf_op jit(solution)/shard_map/projection_1/pallas_call | solution.py:378
  44.6 3.6 %projection_0.1 = (f32[32,3072]{1,0:T(8,128)S(1)}, bf16[32,3072]{1,0:T(8,128)(2,1)S(1)}, f32[32,3072]{1,0:T(8,128)S(1)}, bf16[32,3072]{1,0:T(8,128)(2,1)S(1)}) custom-call(s32[2]{0:T(128)S(1)} %pad_add_fusion.index_ref, bf16[2,128,128]{2,1,0:T(8,128)(2,1)S(1)} %constant_dynamic-update-slice_fusion.refs_0_, ...), custom_call_target="tpu_custom_call" | custom-call | flops 805306368 | bytes 7077888 | tf_op jit(solution)/shard_map/projection_0/pallas_call | solution.py:378
  48.2 2.0 %collective-permute-start.6 = (bf16[32,3072]{1,0:T(8,128)(2,1)S(1)}, bf16[32,3072]{1,0:T(8,128)(2,1)S(1)}, u32[]{:S(2)}, u32[]{:S(2)}) collective-permute-start(bf16[32,3072]{1,0:T(8,128)(2,1)S(1)} %get-tuple-element.31), channel_id=1, source_target_pairs={{0,2},{1,3},{2,0},{3,1},{4,6},{5,7},{6,4},{7,5},{8,10},{9,11},{10,... | collective-permute-start | bytes 589832 | tf_op jit(solution)/shard_map/ppermute | solution.py:356
  50.3 1.6 %collective-permute-start.11 = (bf16[32,2048]{1,0:T(8,128)(2,1)S(1)}, bf16[32,2048]{1,0:T(8,128)(2,1)S(1)}, u32[]{:S(2)}, u32[]{:S(2)}) collective-permute-start(bf16[32,2048]{1,0:T(8,128)(2,1)S(1)} %add_convert_fusion.1), channel_id=1, source_target_pairs={{0,4},{1,5},{2,6},{3,7},{4,0},{5,1},{6,2},{7,3},{8,12},{9,13},{10,... | collective-permute-start | bytes 393224 | tf_op jit(solution)/shard_map/ppermute | solution.py:356
  51.9 7.0 %collective-permute-done.6 = bf16[32,3072]{1,0:T(8,128)(2,1)S(1)} collective-permute-done((bf16[32,3072]{1,0:T(8,128)(2,1)S(1)}, bf16[32,3072]{1,0:T(8,128)(2,1)S(1)}, u32[]{:S(2)}, u32[]{:S(2)}) %collective-permute-start.6) | collective-permute-done | bytes 196640 | tf_op jit(solution)/shard_map/ppermute | solution.py:356
  58.9 2.1 %collective-permute-start.8 = (bf16[32,3072]{1,0:T(8,128)(2,1)S(1)}, bf16[32,3072]{1,0:T(8,128)(2,1)S(1)}, u32[]{:S(2)}, u32[]{:S(2)}) collective-permute-start(bf16[32,3072]{1,0:T(8,128)(2,1)S(1)} %add_convert_fusion), channel_id=1, source_target_pairs={{0,4},{1,5},{2,6},{3,7},{4,0},{5,1},{6,2},{7,3},{8,12},{9,13},{10,... | collective-permute-start | bytes 589832 | tf_op jit(solution)/shard_map/ppermute | solution.py:356
  61.0 2.0 %collective-permute-done.10 = bf16[32,2048]{1,0:T(8,128)(2,1)S(1)} collective-permute-done((bf16[32,2048]{1,0:T(8,128)(2,1)S(1)}, bf16[32,2048]{1,0:T(8,128)(2,1)S(1)}, u32[]{:S(2)}, u32[]{:S(2)}) %collective-permute-start.10) | collective-permute-done | bytes 131104 | tf_op jit(solution)/shard_map/ppermute | solution.py:356
  63.1 5.0 %collective-permute-done.7 = bf16[32,3072]{1,0:T(8,128)(2,1)S(1)} collective-permute-done((bf16[32,3072]{1,0:T(8,128)(2,1)S(1)}, bf16[32,3072]{1,0:T(8,128)(2,1)S(1)}, u32[]{:S(2)}, u32[]{:S(2)}) %collective-permute-start.7) | collective-permute-done | bytes 196640 | tf_op jit(solution)/shard_map/ppermute | solution.py:356
  68.1 1.5 %collective-permute-done.8 = bf16[32,3072]{1,0:T(8,128)(2,1)S(1)} collective-permute-done((bf16[32,3072]{1,0:T(8,128)(2,1)S(1)}, bf16[32,3072]{1,0:T(8,128)(2,1)S(1)}, u32[]{:S(2)}, u32[]{:S(2)}) %collective-permute-start.8) | collective-permute-done | bytes 196640 | tf_op jit(solution)/shard_map/ppermute | solution.py:356
  69.7 0.8 %fusion.2 = bf16[1,32,5120]{2,1,0:T(8,128)(2,1)} fusion(f32[1,32,2048]{2,1,0:T(8,128)S(1)} %add_bitcast_fusion.1, f32[1,32,3072]{2,1,0:T(8,128)S(1)} %add_bitcast_fusion, bf16[1,32,5120]{2,1,0:T(8,128)(2,1)S(1)} %copy-done, f32[5120]{0:T(1024)S(1)} %convert_element_type.48, f32[5120]{0:T(1024)S(1)} %bitcast.17), kind=kLoop, calls=%fused_computation.3 | loop fusion | flops 983040 | bytes 1351680 | tf_op jit(solution)/shard_map/convert_element_type | solution.py:414
  (28 shorter events, 0.9 us)
Async XLA Ops:
  0.0 41.7 %collective-permute-start.5 = (bf16[512,5120]{1,0:T(8,128)(2,1)}, bf16[512,5120]{1,0:T(8,128)(2,1)}, u32[]{:S(2)}, u32[]{:S(2)}) collective-permute-start(bf16[512,5120]{1,0:T(8,128)(2,1)} %refs_4_.3), channel_id=1, source_target_pairs={{0,1},{1,0},{2,3},{3,2},{4,5},{5,4},{6,7},{7,6},{8,9},{9,8},{10,11... | collective-permute-start | bytes 15728648 | tf_op jit(solution)/shard_map/ppermute | solution.py:356
  2.8 28.9 %all-to-all-start = ((bf16[32,32,384]{2,1,0:T(8,128)(2,1)}), bf16[32,32,384]{2,1,0:T(8,128)(2,1)S(1)}, u32[]{:S(2)}, u32[]{:S(2)}) async-start(bf16[32,32,384]{2,1,0:T(8,128)(2,1)} %norm.1), calls=%async_computation | async-start | bytes 1572864 | tf_op jit(solution)/shard_map/all_to_all | solution.py:207
  33.9 1.4 %collective-permute-start = (bf16[3,128,128]{2,1,0:T(8,128)(2,1)S(1)}, bf16[3,128,128]{2,1,0:T(8,128)(2,1)S(1)}, u32[]{:S(2)}, u32[]{:S(2)}) collective-permute-start(bf16[3,128,128]{2,1,0:T(8,128)(2,1)S(1)} %get-tuple-element.24), channel_id=1, source_target_pairs={{0,1},{1,0},{2,3},{3,2},{4,5},{5,4},{6,7},{7,6},{8,9},{9,8},{10,11... | collective-permute-start | bytes 294920 | tf_op jit(solution)/shard_map/ppermute | solution.py:232
  35.3 6.2 %collective-permute-start.4 = (bf16[2,128,128]{2,1,0:T(8,128)(2,1)S(1)}, bf16[2,128,128]{2,1,0:T(8,128)(2,1)S(1)}, u32[]{:S(2)}, u32[]{:S(2)}) collective-permute-start(bf16[2,128,128]{2,1,0:T(8,128)(2,1)S(1)} %pad_maximum_fusion.2), channel_id=1, source_target_pairs={{0,24},{8,16},{16,8},{24,0},{1,25},{9,17},{17,9},{25,1},{2,26},{10... | collective-permute-start | bytes 196616 | tf_op jit(solution)/shard_map/ppermute | solution.py:232
  35.9 5.6 %collective-permute-start.3 = (bf16[2,128,128]{2,1,0:T(8,128)(2,1)S(1)}, bf16[2,128,128]{2,1,0:T(8,128)(2,1)S(1)}, u32[]{:S(2)}, u32[]{:S(2)}) collective-permute-start(bf16[2,128,128]{2,1,0:T(8,128)(2,1)S(1)} %pad_maximum_fusion.1), channel_id=1, source_target_pairs={{0,16},{8,24},{16,0},{24,8},{1,17},{9,25},{17,1},{25,9},{2,18},{10... | collective-permute-start | bytes 196616 | tf_op jit(solution)/shard_map/ppermute | solution.py:232
  37.4 4.3 %collective-permute-start.2 = (bf16[2,128,128]{2,1,0:T(8,128)(2,1)S(1)}, bf16[2,128,128]{2,1,0:T(8,128)(2,1)S(1)}, u32[]{:S(2)}, u32[]{:S(2)}) collective-permute-start(bf16[2,128,128]{2,1,0:T(8,128)(2,1)S(1)} %pad_maximum_fusion), channel_id=1, source_target_pairs={{0,8},{8,0},{16,24},{24,16},{1,9},{9,1},{17,25},{25,17},{2,10},{10... | collective-permute-start | bytes 196616 | tf_op jit(solution)/shard_map/ppermute | solution.py:232
  40.2 1.3 %collective-permute-start.1 = (bf16[1,128,128]{2,1,0:T(8,128)(2,1)S(1)}, bf16[1,128,128]{2,1,0:T(8,128)(2,1)S(1)}, u32[]{:S(2)}, u32[]{:S(2)}) collective-permute-start(bf16[1,128,128]{2,1,0:T(8,128)(2,1)S(1)} %get-tuple-element.27), channel_id=1, source_target_pairs={{0,1},{1,0},{2,3},{3,2},{4,5},{5,4},{6,7},{7,6},{8,9},{9,8},{10,11... | collective-permute-start | bytes 98312 | tf_op jit(solution)/shard_map/ppermute | solution.py:232
  41.4 3.1 %copy-start.1 = (bf16[5120]{0:T(1024)(128)(2,1)S(1)}, bf16[5120]{0:T(1024)(128)(2,1)}, u32[]{:S(2)}) copy-start(bf16[5120]{0:T(1024)(128)(2,1)} %param.18) | copy-start | bytes 30724
  44.4 5.8 %collective-permute-start.9 = (bf16[32,2048]{1,0:T(8,128)(2,1)S(1)}, bf16[32,2048]{1,0:T(8,128)(2,1)S(1)}, u32[]{:S(2)}, u32[]{:S(2)}) collective-permute-start(bf16[32,2048]{1,0:T(8,128)(2,1)S(1)} %get-tuple-element.36), channel_id=1, source_target_pairs={{0,2},{1,3},{2,0},{3,1},{4,6},{5,7},{6,4},{7,5},{8,10},{9,11},{10,... | collective-permute-start | bytes 393224 | tf_op jit(solution)/shard_map/ppermute | solution.py:356
  44.6 25.1 %copy-start = (bf16[1,32,5120]{2,1,0:T(8,128)(2,1)S(1)}, bf16[1,32,5120]{2,1,0:T(8,128)(2,1)}, u32[]{:S(2)}) copy-start(bf16[1,32,5120]{2,1,0:T(8,128)(2,1)} %param.11) | copy-start | bytes 983044
  48.2 10.7 %collective-permute-start.6 = (bf16[32,3072]{1,0:T(8,128)(2,1)S(1)}, bf16[32,3072]{1,0:T(8,128)(2,1)S(1)}, u32[]{:S(2)}, u32[]{:S(2)}) collective-permute-start(bf16[32,3072]{1,0:T(8,128)(2,1)S(1)} %get-tuple-element.31), channel_id=1, source_target_pairs={{0,2},{1,3},{2,0},{3,1},{4,6},{5,7},{6,4},{7,5},{8,10},{9,11},{10,... | collective-permute-start | bytes 589832 | tf_op jit(solution)/shard_map/ppermute | solution.py:356
  50.2 12.9 %collective-permute-start.10 = (bf16[32,2048]{1,0:T(8,128)(2,1)S(1)}, bf16[32,2048]{1,0:T(8,128)(2,1)S(1)}, u32[]{:S(2)}, u32[]{:S(2)}) collective-permute-start(bf16[32,2048]{1,0:T(8,128)(2,1)S(1)} %get-tuple-element.37), channel_id=1, source_target_pairs={{0,2},{1,3},{2,0},{3,1},{4,6},{5,7},{6,4},{7,5},{8,10},{9,11},{10,... | collective-permute-start | bytes 393224 | tf_op jit(solution)/shard_map/ppermute | solution.py:356
  50.3 12.7 %collective-permute-start.11 = (bf16[32,2048]{1,0:T(8,128)(2,1)S(1)}, bf16[32,2048]{1,0:T(8,128)(2,1)S(1)}, u32[]{:S(2)}, u32[]{:S(2)}) collective-permute-start(bf16[32,2048]{1,0:T(8,128)(2,1)S(1)} %add_convert_fusion.1), channel_id=1, source_target_pairs={{0,4},{1,5},{2,6},{3,7},{4,0},{5,1},{6,2},{7,3},{8,12},{9,13},{10,... | collective-permute-start | bytes 393224 | tf_op jit(solution)/shard_map/ppermute | solution.py:356
  58.8 9.3 %collective-permute-start.7 = (bf16[32,3072]{1,0:T(8,128)(2,1)S(1)}, bf16[32,3072]{1,0:T(8,128)(2,1)S(1)}, u32[]{:S(2)}, u32[]{:S(2)}) collective-permute-start(bf16[32,3072]{1,0:T(8,128)(2,1)S(1)} %get-tuple-element.32), channel_id=1, source_target_pairs={{0,2},{1,3},{2,0},{3,1},{4,6},{5,7},{6,4},{7,5},{8,10},{9,11},{10,... | collective-permute-start | bytes 589832 | tf_op jit(solution)/shard_map/ppermute | solution.py:356
  58.9 10.7 %collective-permute-start.8 = (bf16[32,3072]{1,0:T(8,128)(2,1)S(1)}, bf16[32,3072]{1,0:T(8,128)(2,1)S(1)}, u32[]{:S(2)}, u32[]{:S(2)}) collective-permute-start(bf16[32,3072]{1,0:T(8,128)(2,1)S(1)} %add_convert_fusion), channel_id=1, source_target_pairs={{0,4},{1,5},{2,6},{3,7},{4,0},{5,1},{6,2},{7,3},{8,12},{9,13},{10,... | collective-permute-start | bytes 589832 | tf_op jit(solution)/shard_map/ppermute | solution.py:356

commit v15 on v13

--- a/solution.py
+++ b/solution.py
@@ -239,7 +239,7 @@
     found = {0: jnp.concatenate([near_mine, near_got], axis=0)}
     for place, d in enumerate(far):
         found[d] = across(jnp.stack([far_mine[place], far_got[place]]), "frame", d)
-    return [found[d] for d in range(frames)]
+    return [found[d] for d in range(frames)], sends
 
 
 def gathered_attention(query_rows, key_rows, value_rows, gain_query, gain_key, slot_order):
@@ -326,7 +326,7 @@
         ),
         name="attention",
     )(slot_array, slot_order, *queries, *pieces)
-    return [jnp.stack([even, across(odd, "seq", 1)])]
+    return [jnp.stack([even, across(odd, "seq", 1)])], sends[0]
 
 
 def shards(
@@ -358,11 +358,11 @@
     def after(value, *earlier):
         return lax.optimization_barrier((value, *earlier))[0]
 
-    other_weight = across(out_weight, "seq", 1)
     spread = (width // HD) % frames == 0
-    attended = (spread_attention if spread else gathered_attention)(
+    attended, normed = (spread_attention if spread else gathered_attention)(
         query_rows[0], key_rows[0], value_rows[0], gain_query, gain_key, slot_order
     )
+    other_weight = across(after(out_weight, normed), "seq", 1)
     index = jnp.stack([me // 2, slot]) if spread else jnp.zeros((2,), jnp.int32)
 
     level = lax.dynamic_index_in_dim(noise_level, slot, keepdims=False)

time: 69.7 us -> 69.7 us (level)
  transfers between devices with their start and end apart: 13 -> 13, of which waited for: 8 -> 8; matrix products, arithmetic and copies ran while one was open for 5% -> 5% of each run, Pallas kernels for 13% -> 9%
where the time goes in v15:
time: 69.7 us; the launch traced here: 69.4 us
  waiting for transfers between devices  32.1 us (46%)
  starting transfers between devices  19.2 us (28%)
  Pallas kernels  12 us (17%)
  other arithmetic  2.76 us (4%)
  between operations  2.08 us (3%)
  local copies, waits for them, and re-layouts  1.3 us (2%)
    all_to_all x1, waiting for transfers between devices, spread_attention(): lax.all_to_all(sends, ('frame', 'seq'), split_axis=0, concat_axis=0, tile...  17 us
    ppermute x7, waiting for transfers between devices, across(): return lax.ppermute(value, axis, [(i, i ^ distance) for i in range(n)])  12.3 us
    ppermute x7, starting transfers between devices, across(): return lax.ppermute(value, axis, [(i, i ^ distance) for i in range(n)])  8.47 us
    all_to_all x1, starting transfers between devices, spread_attention(): lax.all_to_all(sends, ('frame', 'seq'), split_axis=0, concat_axis=0, tile...  6.96 us
    pallas_call x2, Pallas kernels, shards(): pl.pallas_call(functools.partial(projection_kernel, chips, sources), grid...  6.29 us
    ppermute x5, starting transfers between devices, across(): return lax.ppermute(value, axis, [(i, i ^ distance) for i in range(size)])  3.82 us
    pallas_call x2, Pallas kernels, attend(): pl.pallas_call(functools.partial(spread_attention_kernel, n, frames, pick...  3.37 us
    ppermute x5, waiting for transfers between devices, across(): return lax.ppermute(value, axis, [(i, i ^ distance) for i in range(size)])  2.7 us
  transfers between devices with their start and end apart: 13, of which 8 were waited for; matrix products, arithmetic and copies ran while one was open for 5% of the time, Pallas kernels for 9%

profile of v15, /device:TPU:0, one launch (start us, length us, event | category | flops | bytes accessed | tf_op | source)
XLA Modules:
  0.0 69.4 jit_solution(7307335292711779124)
XLA Ops:
  0.0 2.3 %norm.1 = bf16[32,32,384]{2,1,0:T(8,128)(2,1)} custom-call(bf16[32,4096]{1,0:T(8,128)(2,1)} %bitcast.14, bf16[32,4096]{1,0:T(8,128)(2,1)} %bitcast.15, bf16[32,4096]{1,0:T(8,128)(2,1)} %bitcast.16, f32[1,4096]{1,0:T(1,128)} %bitcast.18, f32[1,4096]{1,0:T(1,128)} %bitcast.19), custom_call_target="tpu_custom_call" | custom-call | tf_op jit(solution)/shard_map/norm/pallas_call | solution.py:200
  2.3 0.5 collective-permute-start.5
  2.8 7.0 %all-to-all-start = ((bf16[32,32,384]{2,1,0:T(8,128)(2,1)}), bf16[32,32,384]{2,1,0:T(8,128)(2,1)S(1)}, u32[]{:S(2)}, u32[]{:S(2)}) async-start(bf16[32,32,384]{2,1,0:T(8,128)(2,1)} %norm.1), calls=%async_computation | async-start | bytes 1572864 | tf_op jit(solution)/shard_map/all_to_all | solution.py:207
  9.7 1.3 %dynamic_slice.8 = s32[1]{0:T(128)} dynamic-slice(s32[4]{0:T(128)} %param.20, s32[]{:T(128)S(6)} %select_n.20), dynamic_slice_sizes={1} | dynamic-slice | bytes 12 | tf_op jit(solution)/shard_map/jit(dynamic_index_in_dim)/dynamic_slice | solution.py:368
  13.0 0.9 %dynamic-slice_convert_fusion = f32[1,5120]{1,0:T(1,128)S(1)} fusion(bf16[64,5120]{1,0:T(8,128)(2,1)} %param.19, s32[]{:T(128)S(6)} %select_n.21), kind=kLoop, calls=%fused_computation.11 | loop fusion | flops 5120 | bytes 30724 | tf_op jit(solution)/shard_map/convert_element_type | solution.py:369
  13.9 0.7 %pad_add_fusion.1.index_ref = s32[6]{0:T(128)S(1)} fusion(s32[4]{0:T(128)} %param.21, s32[1]{0:T(128)} %bitcast.4, s32[1]{0:T(128)} %bitcast.1), kind=kLoop, calls=%fused_computation.15 | loop fusion | flops 12 | bytes 48 | tf_op jit(solution)/shard_map/concatenate | solution.py:211
  14.6 17.0 %all-to-all-done.rows_ref = bf16[32,32,384]{2,1,0:T(8,128)(2,1)S(1)} async-done(((bf16[32,32,384]{2,1,0:T(8,128)(2,1)}), bf16[32,32,384]{2,1,0:T(8,128)(2,1)S(1)}, u32[]{:S(2)}, u32[]{:S(2)}) %all-to-all-start) | async-done | bytes 786464 | tf_op jit(solution)/shard_map/all_to_all | solution.py:207
  31.7 2.2 %attention_far.1 = (bf16[3,128,128]{2,1,0:T(8,128)(2,1)S(1)}, bf16[3,128,128]{2,1,0:T(8,128)(2,1)S(1)}) custom-call(s32[6]{0:T(128)S(1)} %pad_add_fusion.1.index_ref, bf16[32,32,384]{2,1,0:T(8,128)(2,1)S(1)} %all-to-all-done.rows_ref), custom_call_target="tpu_custom_call" | custom-call | flops 402653184 | bytes 1048576 | tf_op jit(solution)/shard_map/attention_far/pallas_call | solution.py:215
  34.0 1.3 %collective-permute-done = bf16[3,128,128]{2,1,0:T(8,128)(2,1)S(1)} collective-permute-done((bf16[3,128,128]{2,1,0:T(8,128)(2,1)S(1)}, bf16[3,128,128]{2,1,0:T(8,128)(2,1)S(1)}, u32[]{:S(2)}, u32[]{:S(2)}) %collective-permute-start) | collective-permute-done | bytes 98336 | tf_op jit(solution)/shard_map/ppermute | solution.py:232
  35.3 0.6 collective-permute-start.4
  35.9 1.5 %collective-permute-start.3 = (bf16[2,128,128]{2,1,0:T(8,128)(2,1)S(1)}, bf16[2,128,128]{2,1,0:T(8,128)(2,1)S(1)}, u32[]{:S(2)}, u32[]{:S(2)}) collective-permute-start(bf16[2,128,128]{2,1,0:T(8,128)(2,1)S(1)} %pad_maximum_fusion.1), channel_id=1, source_target_pairs={{0,16},{8,24},{16,0},{24,8},{1,17},{9,25},{17,1},{25,9},{2,18},{10... | collective-permute-start | bytes 196616 | tf_op jit(solution)/shard_map/ppermute | solution.py:232
  37.4 1.6 %collective-permute-start.2 = (bf16[2,128,128]{2,1,0:T(8,128)(2,1)S(1)}, bf16[2,128,128]{2,1,0:T(8,128)(2,1)S(1)}, u32[]{:S(2)}, u32[]{:S(2)}) collective-permute-start(bf16[2,128,128]{2,1,0:T(8,128)(2,1)S(1)} %pad_maximum_fusion), channel_id=1, source_target_pairs={{0,8},{8,0},{16,24},{24,16},{1,9},{9,1},{17,25},{25,17},{2,10},{10... | collective-permute-start | bytes 196616 | tf_op jit(solution)/shard_map/ppermute | solution.py:232
  39.0 1.2 %attention_near.1 = (bf16[1,128,128]{2,1,0:T(8,128)(2,1)S(1)}, bf16[1,128,128]{2,1,0:T(8,128)(2,1)S(1)}) custom-call(s32[6]{0:T(128)S(1)} %pad_add_fusion.1.index_ref, bf16[32,32,384]{2,1,0:T(8,128)(2,1)S(1)} %all-to-all-done.rows_ref), custom_call_target="tpu_custom_call" | custom-call | flops 134217728 | bytes 1048576 | tf_op jit(solution)/shard_map/attention_near/pallas_call | solution.py:215
  40.2 1.2 %collective-permute-done.1 = bf16[1,128,128]{2,1,0:T(8,128)(2,1)S(1)} collective-permute-done((bf16[1,128,128]{2,1,0:T(8,128)(2,1)S(1)}, bf16[1,128,128]{2,1,0:T(8,128)(2,1)S(1)}, u32[]{:S(2)}, u32[]{:S(2)}) %collective-permute-start.1) | collective-permute-done | bytes 32800 | tf_op jit(solution)/shard_map/ppermute | solution.py:232
  41.7 3.1 %projection_0.1 = (f32[32,2560]{1,0:T(8,128)S(1)}, bf16[32,2560]{1,0:T(8,128)(2,1)S(1)}, f32[32,2560]{1,0:T(8,128)S(1)}, bf16[32,2560]{1,0:T(8,128)(2,1)S(1)}) custom-call(s32[2]{0:T(128)S(1)} %pad_add_fusion.index_ref, bf16[2,128,128]{2,1,0:T(8,128)(2,1)S(1)} %constant_dynamic-update-slice_fusion.refs_0_, ...), custom_call_target="tpu_custom_call" | custom-call | flops 671088640 | bytes 5898240 | tf_op jit(solution)/shard_map/projection_0/pallas_call | solution.py:379
  45.0 3.2 %projection_1.1 = (f32[32,2560]{1,0:T(8,128)S(1)}, bf16[32,2560]{1,0:T(8,128)(2,1)S(1)}, f32[32,2560]{1,0:T(8,128)S(1)}, bf16[32,2560]{1,0:T(8,128)(2,1)S(1)}) custom-call(s32[2]{0:T(128)S(1)} %pad_add_fusion.index_ref, bf16[2,128,128]{2,1,0:T(8,128)(2,1)S(1)} %constant_dynamic-update-slice_fusion.refs_0_, ...), custom_call_target="tpu_custom_call" | custom-call | flops 671088640 | bytes 5898240 | tf_op jit(solution)/shard_map/projection_1/pallas_call | solution.py:379
  48.2 2.0 %collective-permute-start.9 = (bf16[32,2560]{1,0:T(8,128)(2,1)S(1)}, bf16[32,2560]{1,0:T(8,128)(2,1)S(1)}, u32[]{:S(2)}, u32[]{:S(2)}) collective-permute-start(bf16[32,2560]{1,0:T(8,128)(2,1)S(1)} %get-tuple-element.38), channel_id=1, source_target_pairs={{0,2},{1,3},{2,0},{3,1},{4,6},{5,7},{6,4},{7,5},{8,10},{9,11},{10,... | collective-permute-start | bytes 491528 | tf_op jit(solution)/shard_map/ppermute | solution.py:356
  50.2 0.9 %collective-permute-done.6 = bf16[32,2560]{1,0:T(8,128)(2,1)S(1)} collective-permute-done((bf16[32,2560]{1,0:T(8,128)(2,1)S(1)}, bf16[32,2560]{1,0:T(8,128)(2,1)S(1)}, u32[]{:S(2)}, u32[]{:S(2)}) %collective-permute-start.6) | collective-permute-done | bytes 163872 | tf_op jit(solution)/shard_map/ppermute | solution.py:356
  51.3 0.8 %collective-permute-start.8 = (bf16[32,2560]{1,0:T(8,128)(2,1)S(1)}, bf16[32,2560]{1,0:T(8,128)(2,1)S(1)}, u32[]{:S(2)}, u32[]{:S(2)}) collective-permute-start(bf16[32,2560]{1,0:T(8,128)(2,1)S(1)} %add_convert_fusion.1), channel_id=1, source_target_pairs={{0,4},{1,5},{2,6},{3,7},{4,0},{5,1},{6,2},{7,3},{8,12},{9,13},{10,... | collective-permute-start | bytes 491528 | tf_op jit(solution)/shard_map/ppermute | solution.py:356
  52.1 5.7 %collective-permute-done.9 = bf16[32,2560]{1,0:T(8,128)(2,1)S(1)} collective-permute-done((bf16[32,2560]{1,0:T(8,128)(2,1)S(1)}, bf16[32,2560]{1,0:T(8,128)(2,1)S(1)}, u32[]{:S(2)}, u32[]{:S(2)}) %collective-permute-start.9) | collective-permute-done | bytes 163872 | tf_op jit(solution)/shard_map/ppermute | solution.py:356
  57.8 4.9 %collective-permute-start.11 = (bf16[32,2560]{1,0:T(8,128)(2,1)S(1)}, bf16[32,2560]{1,0:T(8,128)(2,1)S(1)}, u32[]{:S(2)}, u32[]{:S(2)}) collective-permute-start(bf16[32,2560]{1,0:T(8,128)(2,1)S(1)} %add_convert_fusion), channel_id=1, source_target_pairs={{0,4},{1,5},{2,6},{3,7},{4,0},{5,1},{6,2},{7,3},{8,12},{9,13},{10,... | collective-permute-start | bytes 491528 | tf_op jit(solution)/shard_map/ppermute | solution.py:356
  62.7 1.3 %collective-permute-done.7 = bf16[32,2560]{1,0:T(8,128)(2,1)S(1)} collective-permute-done((bf16[32,2560]{1,0:T(8,128)(2,1)S(1)}, bf16[32,2560]{1,0:T(8,128)(2,1)S(1)}, u32[]{:S(2)}, u32[]{:S(2)}) %collective-permute-start.7) | collective-permute-done | bytes 163872 | tf_op jit(solution)/shard_map/ppermute | solution.py:356
  64.2 4.4 %collective-permute-done.10 = bf16[32,2560]{1,0:T(8,128)(2,1)S(1)} collective-permute-done((bf16[32,2560]{1,0:T(8,128)(2,1)S(1)}, bf16[32,2560]{1,0:T(8,128)(2,1)S(1)}, u32[]{:S(2)}, u32[]{:S(2)}) %collective-permute-start.10) | collective-permute-done | bytes 163872 | tf_op jit(solution)/shard_map/ppermute | solution.py:356
  68.6 0.8 %fusion.2 = bf16[1,32,5120]{2,1,0:T(8,128)(2,1)} fusion(f32[1,32,2560]{2,1,0:T(8,128)S(1)} %add_bitcast_fusion, f32[1,32,2560]{2,1,0:T(8,128)S(1)} %add_bitcast_fusion.1, bf16[1,32,5120]{2,1,0:T(8,128)(2,1)S(1)} %copy-done, f32[5120]{0:T(1024)S(1)} %convert_element_type.48, f32[5120]{0:T(1024)S(1)} %bitcast.17), kind=kLoop, calls=%fused_computation.3 | loop fusion | flops 983040 | bytes 1351680 | tf_op jit(solution)/shard_map/convert_element_type | solution.py:415
  (28 shorter events, 1.0 us)
Async XLA Ops:
  2.3 39.4 %collective-permute-start.5 = (bf16[512,5120]{1,0:T(8,128)(2,1)}, bf16[512,5120]{1,0:T(8,128)(2,1)}, u32[]{:S(2)}, u32[]{:S(2)}) collective-permute-start(bf16[512,5120]{1,0:T(8,128)(2,1)} %refs_4_.3), channel_id=1, source_target_pairs={{0,1},{1,0},{2,3},{3,2},{4,5},{5,4},{6,7},{7,6},{8,9},{9,8},{10,11... | collective-permute-start | bytes 15728648 | tf_op jit(solution)/shard_map/ppermute | solution.py:356
  2.8 28.9 %all-to-all-start = ((bf16[32,32,384]{2,1,0:T(8,128)(2,1)}), bf16[32,32,384]{2,1,0:T(8,128)(2,1)S(1)}, u32[]{:S(2)}, u32[]{:S(2)}) async-start(bf16[32,32,384]{2,1,0:T(8,128)(2,1)} %norm.1), calls=%async_computation | async-start | bytes 1572864 | tf_op jit(solution)/shard_map/all_to_all | solution.py:207
  33.9 1.4 %collective-permute-start = (bf16[3,128,128]{2,1,0:T(8,128)(2,1)S(1)}, bf16[3,128,128]{2,1,0:T(8,128)(2,1)S(1)}, u32[]{:S(2)}, u32[]{:S(2)}) collective-permute-start(bf16[3,128,128]{2,1,0:T(8,128)(2,1)S(1)} %get-tuple-element.25), channel_id=1, source_target_pairs={{0,1},{1,0},{2,3},{3,2},{4,5},{5,4},{6,7},{7,6},{8,9},{9,8},{10,11... | collective-permute-start | bytes 294920 | tf_op jit(solution)/shard_map/ppermute | solution.py:232
  35.3 6.2 %collective-permute-start.4 = (bf16[2,128,128]{2,1,0:T(8,128)(2,1)S(1)}, bf16[2,128,128]{2,1,0:T(8,128)(2,1)S(1)}, u32[]{:S(2)}, u32[]{:S(2)}) collective-permute-start(bf16[2,128,128]{2,1,0:T(8,128)(2,1)S(1)} %pad_maximum_fusion.2), channel_id=1, source_target_pairs={{0,24},{8,16},{16,8},{24,0},{1,25},{9,17},{17,9},{25,1},{2,26},{10... | collective-permute-start | bytes 196616 | tf_op jit(solution)/shard_map/ppermute | solution.py:232
  35.9 5.6 %collective-permute-start.3 = (bf16[2,128,128]{2,1,0:T(8,128)(2,1)S(1)}, bf16[2,128,128]{2,1,0:T(8,128)(2,1)S(1)}, u32[]{:S(2)}, u32[]{:S(2)}) collective-permute-start(bf16[2,128,128]{2,1,0:T(8,128)(2,1)S(1)} %pad_maximum_fusion.1), channel_id=1, source_target_pairs={{0,16},{8,24},{16,0},{24,8},{1,17},{9,25},{17,1},{25,9},{2,18},{10... | collective-permute-start | bytes 196616 | tf_op jit(solution)/shard_map/ppermute | solution.py:232
  37.4 4.3 %collective-permute-start.2 = (bf16[2,128,128]{2,1,0:T(8,128)(2,1)S(1)}, bf16[2,128,128]{2,1,0:T(8,128)(2,1)S(1)}, u32[]{:S(2)}, u32[]{:S(2)}) collective-permute-start(bf16[2,128,128]{2,1,0:T(8,128)(2,1)S(1)} %pad_maximum_fusion), channel_id=1, source_target_pairs={{0,8},{8,0},{16,24},{24,16},{1,9},{9,1},{17,25},{25,17},{2,10},{10... | collective-permute-start | bytes 196616 | tf_op jit(solution)/shard_map/ppermute | solution.py:232
  40.2 1.3 %collective-permute-start.1 = (bf16[1,128,128]{2,1,0:T(8,128)(2,1)S(1)}, bf16[1,128,128]{2,1,0:T(8,128)(2,1)S(1)}, u32[]{:S(2)}, u32[]{:S(2)}) collective-permute-start(bf16[1,128,128]{2,1,0:T(8,128)(2,1)S(1)} %get-tuple-element.28), channel_id=1, source_target_pairs={{0,1},{1,0},{2,3},{3,2},{4,5},{5,4},{6,7},{7,6},{8,9},{9,8},{10,11... | collective-permute-start | bytes 98312 | tf_op jit(solution)/shard_map/ppermute | solution.py:232
  41.4 3.5 %copy-start.1 = (bf16[5120]{0:T(1024)(128)(2,1)S(1)}, bf16[5120]{0:T(1024)(128)(2,1)}, u32[]{:S(2)}) copy-start(bf16[5120]{0:T(1024)(128)(2,1)} %param.18) | copy-start | bytes 30724
  44.8 6.3 %collective-permute-start.6 = (bf16[32,2560]{1,0:T(8,128)(2,1)S(1)}, bf16[32,2560]{1,0:T(8,128)(2,1)S(1)}, u32[]{:S(2)}, u32[]{:S(2)}) collective-permute-start(bf16[32,2560]{1,0:T(8,128)(2,1)S(1)} %get-tuple-element.33), channel_id=1, source_target_pairs={{0,2},{1,3},{2,0},{3,1},{4,6},{5,7},{6,4},{7,5},{8,10},{9,11},{10,... | collective-permute-start | bytes 491528 | tf_op jit(solution)/shard_map/ppermute | solution.py:356
  45.0 23.6 %copy-start = (bf16[1,32,5120]{2,1,0:T(8,128)(2,1)S(1)}, bf16[1,32,5120]{2,1,0:T(8,128)(2,1)}, u32[]{:S(2)}) copy-start(bf16[1,32,5120]{2,1,0:T(8,128)(2,1)} %param.11) | copy-start | bytes 983044
  48.2 9.6 %collective-permute-start.9 = (bf16[32,2560]{1,0:T(8,128)(2,1)S(1)}, bf16[32,2560]{1,0:T(8,128)(2,1)S(1)}, u32[]{:S(2)}, u32[]{:S(2)}) collective-permute-start(bf16[32,2560]{1,0:T(8,128)(2,1)S(1)} %get-tuple-element.38), channel_id=1, source_target_pairs={{0,2},{1,3},{2,0},{3,1},{4,6},{5,7},{6,4},{7,5},{8,10},{9,11},{10,... | collective-permute-start | bytes 491528 | tf_op jit(solution)/shard_map/ppermute | solution.py:356
  51.1 13.0 %collective-permute-start.7 = (bf16[32,2560]{1,0:T(8,128)(2,1)S(1)}, bf16[32,2560]{1,0:T(8,128)(2,1)S(1)}, u32[]{:S(2)}, u32[]{:S(2)}) collective-permute-start(bf16[32,2560]{1,0:T(8,128)(2,1)S(1)} %get-tuple-element.34), channel_id=1, source_target_pairs={{0,2},{1,3},{2,0},{3,1},{4,6},{5,7},{6,4},{7,5},{8,10},{9,11},{10,... | collective-permute-start | bytes 491528 | tf_op jit(solution)/shard_map/ppermute | solution.py:356
  51.3 12.8 %collective-permute-start.8 = (bf16[32,2560]{1,0:T(8,128)(2,1)S(1)}, bf16[32,2560]{1,0:T(8,128)(2,1)S(1)}, u32[]{:S(2)}, u32[]{:S(2)}) collective-permute-start(bf16[32,2560]{1,0:T(8,128)(2,1)S(1)} %add_convert_fusion.1), channel_id=1, source_target_pairs={{0,4},{1,5},{2,6},{3,7},{4,0},{5,1},{6,2},{7,3},{8,12},{9,13},{10,... | collective-permute-start | bytes 491528 | tf_op jit(solution)/shard_map/ppermute | solution.py:356
  57.8 10.8 %collective-permute-start.10 = (bf16[32,2560]{1,0:T(8,128)(2,1)S(1)}, bf16[32,2560]{1,0:T(8,128)(2,1)S(1)}, u32[]{:S(2)}, u32[]{:S(2)}) collective-permute-start(bf16[32,2560]{1,0:T(8,128)(2,1)S(1)} %get-tuple-element.39), channel_id=1, source_target_pairs={{0,2},{1,3},{2,0},{3,1},{4,6},{5,7},{6,4},{7,5},{8,10},{9,11},{10,... | collective-permute-start | bytes 491528 | tf_op jit(solution)/shard_map/ppermute | solution.py:356
  57.8 10.7 %collective-permute-start.11 = (bf16[32,2560]{1,0:T(8,128)(2,1)S(1)}, bf16[32,2560]{1,0:T(8,128)(2,1)S(1)}, u32[]{:S(2)}, u32[]{:S(2)}) collective-permute-start(bf16[32,2560]{1,0:T(8,128)(2,1)S(1)} %add_convert_fusion), channel_id=1, source_target_pairs={{0,4},{1,5},{2,6},{3,7},{4,0},{5,1},{6,2},{7,3},{8,12},{9,13},{10,... | collective-permute-start | bytes 491528 | tf_op jit(solution)/shard_map/ppermute | solution.py:356

commit v16 on v13

--- a/solution.py
+++ b/solution.py
@@ -396,19 +396,21 @@
             ),
             name=f"projection_{cut}",
         )(index, *attended, out_weight, other_weight)
-        sums = {j: part for j, part in enumerate(partial_sums)}
-        bit = 1
-        while bit < chips:
-            leaving = sorted((j for j in sums if j & bit), reverse=True)
-            earlier = ()
-            for j in leaving:
+        halves.append({j: part for j, part in enumerate(partial_sums)})
+    bit = 1
+    while bit < chips:
+        leaving = sorted((j for j in halves[0] if j & bit), reverse=True)
+        earlier = []
+        for j in leaving:
+            found = []
+            for sums in halves:
                 leaves = after(sums.pop(j).astype(jnp.bfloat16), *earlier)
                 arrived = across(leaves, "seq", 2 * bit)
                 sums[j ^ bit] = sums[j ^ bit].astype(jnp.float32) + arrived.astype(jnp.float32)
-                earlier = (arrived,)
-            bit *= 2
-        halves.append(sums[0])
-    projected = jnp.concatenate(halves, axis=1)
+                found.append(arrived)
+            earlier = found
+        bit *= 2
+    projected = jnp.concatenate([sums[0] for sums in halves], axis=1)
 
     bias = out_bias.astype(jnp.float32)[None, :]
     mixed = tokens[0].astype(jnp.float32) + gate_row * (projected + bias)

time: 69.7 us -> 70.7 us (1.014)
  waiting for transfers between devices: 32.1 us -> 34.7 us
  starting transfers between devices: 19.2 us -> 17.5 us
    ppermute x7, starting transfers between devices: 8.47 us -> 6.61 us  [across(): return lax.ppermute(value, axis, [(i, i ^ distance) for i in range(n)])]
    ppermute x5, waiting for transfers between devices: 2.7 us -> 4.17 us  [across(): return lax.ppermute(value, axis, [(i, i ^ distance) for i in range(size)])]
    ppermute x7, waiting for transfers between devices: 12.3 us -> 13.5 us  [across(): return lax.ppermute(value, axis, [(i, i ^ distance) for i in range(n)])]
  transfers between devices with their start and end apart: 13 -> 13, of which waited for: 8 -> 9; matrix products, arithmetic and copies ran while one was open for 5% -> 4% of each run, Pallas kernels for 13% -> 13%
where the time goes in v16:
time: 70.7 us; the launch traced here: 70.4 us
  waiting for transfers between devices  34.7 us (49%)
  starting transfers between devices  17.5 us (25%)
  Pallas kernels  12 us (17%)
  other arithmetic  2.75 us (4%)
  between operations  2.09 us (3%)
  local copies, waits for them, and re-layouts  1.3 us (2%)
    all_to_all x1, waiting for transfers between devices, spread_attention(): lax.all_to_all(sends, ('frame', 'seq'), split_axis=0, concat_axis=0, tile...  17 us
    ppermute x7, waiting for transfers between devices, across(): return lax.ppermute(value, axis, [(i, i ^ distance) for i in range(n)])  13.5 us
    all_to_all x1, starting transfers between devices, spread_attention(): lax.all_to_all(sends, ('frame', 'seq'), split_axis=0, concat_axis=0, tile...  6.96 us
    ppermute x7, starting transfers between devices, across(): return lax.ppermute(value, axis, [(i, i ^ distance) for i in range(n)])  6.61 us
    pallas_call x2, Pallas kernels, shards(): pl.pallas_call(functools.partial(projection_kernel, chips, sources), grid...  6.29 us
    ppermute x5, waiting for transfers between devices, across(): return lax.ppermute(value, axis, [(i, i ^ distance) for i in range(size)])  4.17 us
    ppermute x5, starting transfers between devices, across(): return lax.ppermute(value, axis, [(i, i ^ distance) for i in range(size)])  3.97 us
    pallas_call x2, Pallas kernels, attend(): pl.pallas_call(functools.partial(spread_attention_kernel, n, frames, pick...  3.37 us
  transfers between devices with their start and end apart: 13, of which 9 were waited for; matrix products, arithmetic and copies ran while one was open for 4% of the time, Pallas kernels for 13%

profile of v16, /device:TPU:0, one launch (start us, length us, event | category | flops | bytes accessed | tf_op | source)
XLA Modules:
  0.0 70.4 jit_solution(9283599206718885942)
XLA Ops:
  0.5 2.3 %norm.1 = bf16[32,32,384]{2,1,0:T(8,128)(2,1)} custom-call(bf16[32,4096]{1,0:T(8,128)(2,1)} %bitcast.14, bf16[32,4096]{1,0:T(8,128)(2,1)} %bitcast.15, bf16[32,4096]{1,0:T(8,128)(2,1)} %bitcast.16, f32[1,4096]{1,0:T(1,128)} %bitcast.18, f32[1,4096]{1,0:T(1,128)} %bitcast.19), custom_call_target="tpu_custom_call" | custom-call | tf_op jit(solution)/shard_map/norm/pallas_call | solution.py:200
  2.8 7.0 %all-to-all-start = ((bf16[32,32,384]{2,1,0:T(8,128)(2,1)}), bf16[32,32,384]{2,1,0:T(8,128)(2,1)S(1)}, u32[]{:S(2)}, u32[]{:S(2)}) async-start(bf16[32,32,384]{2,1,0:T(8,128)(2,1)} %norm.1), calls=%async_computation | async-start | bytes 1572864 | tf_op jit(solution)/shard_map/all_to_all | solution.py:207
  9.7 1.3 %dynamic_slice.8 = s32[1]{0:T(128)} dynamic-slice(s32[4]{0:T(128)} %param.20, s32[]{:T(128)S(6)} %select_n.20), dynamic_slice_sizes={1} | dynamic-slice | bytes 12 | tf_op jit(solution)/shard_map/jit(dynamic_index_in_dim)/dynamic_slice | solution.py:368
  13.0 0.9 %dynamic-slice_convert_fusion = f32[1,5120]{1,0:T(1,128)S(1)} fusion(bf16[64,5120]{1,0:T(8,128)(2,1)} %param.19, s32[]{:T(128)S(6)} %select_n.21), kind=kLoop, calls=%fused_computation.11 | loop fusion | flops 5120 | bytes 30724 | tf_op jit(solution)/shard_map/convert_element_type | solution.py:369
  13.9 0.7 %pad_add_fusion.1.index_ref = s32[6]{0:T(128)S(1)} fusion(s32[4]{0:T(128)} %param.21, s32[1]{0:T(128)} %bitcast.4, s32[1]{0:T(128)} %bitcast.1), kind=kLoop, calls=%fused_computation.15 | loop fusion | flops 12 | bytes 48 | tf_op jit(solution)/shard_map/concatenate | solution.py:211
  14.6 17.0 %all-to-all-done.rows_ref = bf16[32,32,384]{2,1,0:T(8,128)(2,1)S(1)} async-done(((bf16[32,32,384]{2,1,0:T(8,128)(2,1)}), bf16[32,32,384]{2,1,0:T(8,128)(2,1)S(1)}, u32[]{:S(2)}, u32[]{:S(2)}) %all-to-all-start) | async-done | bytes 786464 | tf_op jit(solution)/shard_map/all_to_all | solution.py:207
  31.7 2.2 %attention_far.1 = (bf16[3,128,128]{2,1,0:T(8,128)(2,1)S(1)}, bf16[3,128,128]{2,1,0:T(8,128)(2,1)S(1)}) custom-call(s32[6]{0:T(128)S(1)} %pad_add_fusion.1.index_ref, bf16[32,32,384]{2,1,0:T(8,128)(2,1)S(1)} %all-to-all-done.rows_ref), custom_call_target="tpu_custom_call" | custom-call | flops 402653184 | bytes 1048576 | tf_op jit(solution)/shard_map/attention_far/pallas_call | solution.py:215
  34.0 1.3 %collective-permute-done = bf16[3,128,128]{2,1,0:T(8,128)(2,1)S(1)} collective-permute-done((bf16[3,128,128]{2,1,0:T(8,128)(2,1)S(1)}, bf16[3,128,128]{2,1,0:T(8,128)(2,1)S(1)}, u32[]{:S(2)}, u32[]{:S(2)}) %collective-permute-start) | collective-permute-done | bytes 98336 | tf_op jit(solution)/shard_map/ppermute | solution.py:232
  35.2 1.2 %attention_near.1 = (bf16[1,128,128]{2,1,0:T(8,128)(2,1)S(1)}, bf16[1,128,128]{2,1,0:T(8,128)(2,1)S(1)}) custom-call(s32[6]{0:T(128)S(1)} %pad_add_fusion.1.index_ref, bf16[32,32,384]{2,1,0:T(8,128)(2,1)S(1)} %all-to-all-done.rows_ref), custom_call_target="tpu_custom_call" | custom-call | flops 134217728 | bytes 1048576 | tf_op jit(solution)/shard_map/attention_near/pallas_call | solution.py:215
  36.7 0.8 %collective-permute-start.2 = (bf16[2,128,128]{2,1,0:T(8,128)(2,1)S(1)}, bf16[2,128,128]{2,1,0:T(8,128)(2,1)S(1)}, u32[]{:S(2)}, u32[]{:S(2)}) collective-permute-start(bf16[2,128,128]{2,1,0:T(8,128)(2,1)S(1)} %pad_maximum_fusion), channel_id=1, source_target_pairs={{0,8},{8,0},{16,24},{24,16},{1,9},{9,1},{17,25},{25,17},{2,10},{10... | collective-permute-start | bytes 196616 | tf_op jit(solution)/shard_map/ppermute | solution.py:232
  38.1 2.3 %collective-permute-start.4 = (bf16[2,128,128]{2,1,0:T(8,128)(2,1)S(1)}, bf16[2,128,128]{2,1,0:T(8,128)(2,1)S(1)}, u32[]{:S(2)}, u32[]{:S(2)}) collective-permute-start(bf16[2,128,128]{2,1,0:T(8,128)(2,1)S(1)} %pad_maximum_fusion.2), channel_id=1, source_target_pairs={{0,24},{8,16},{16,8},{24,0},{1,25},{9,17},{17,9},{25,1},{2,26},{10... | collective-permute-start | bytes 196616 | tf_op jit(solution)/shard_map/ppermute | solution.py:232
  41.1 1.4 %collective-permute-done.3.refs_2_ = bf16[2,128,128]{2,1,0:T(8,128)(2,1)S(1)} collective-permute-done((bf16[2,128,128]{2,1,0:T(8,128)(2,1)S(1)}, bf16[2,128,128]{2,1,0:T(8,128)(2,1)S(1)}, u32[]{:S(2)}, u32[]{:S(2)}) %collective-permute-start.3) | collective-permute-done | bytes 65568 | tf_op jit(solution)/shard_map/ppermute | solution.py:232
  42.5 0.8 %collective-permute-done.4.refs_3_ = bf16[2,128,128]{2,1,0:T(8,128)(2,1)S(1)} collective-permute-done((bf16[2,128,128]{2,1,0:T(8,128)(2,1)S(1)}, bf16[2,128,128]{2,1,0:T(8,128)(2,1)S(1)}, u32[]{:S(2)}, u32[]{:S(2)}) %collective-permute-start.4) | collective-permute-done | bytes 65568 | tf_op jit(solution)/shard_map/ppermute | solution.py:232
  43.3 3.1 %projection_1.1 = (f32[32,2560]{1,0:T(8,128)S(1)}, bf16[32,2560]{1,0:T(8,128)(2,1)S(1)}, f32[32,2560]{1,0:T(8,128)S(1)}, bf16[32,2560]{1,0:T(8,128)(2,1)S(1)}) custom-call(s32[2]{0:T(128)S(1)} %pad_add_fusion.index_ref, bf16[2,128,128]{2,1,0:T(8,128)(2,1)S(1)} %constant_dynamic-update-slice_fusion.refs_0_, ...), custom_call_target="tpu_custom_call" | custom-call | flops 671088640 | bytes 5898240 | tf_op jit(solution)/shard_map/projection_1/pallas_call | solution.py:379
  46.5 3.2 %projection_0.1 = (f32[32,2560]{1,0:T(8,128)S(1)}, bf16[32,2560]{1,0:T(8,128)(2,1)S(1)}, f32[32,2560]{1,0:T(8,128)S(1)}, bf16[32,2560]{1,0:T(8,128)(2,1)S(1)}) custom-call(s32[2]{0:T(128)S(1)} %pad_add_fusion.index_ref, bf16[2,128,128]{2,1,0:T(8,128)(2,1)S(1)} %constant_dynamic-update-slice_fusion.refs_0_, ...), custom_call_target="tpu_custom_call" | custom-call | flops 671088640 | bytes 5898240 | tf_op jit(solution)/shard_map/projection_0/pallas_call | solution.py:379
  49.7 2.1 %collective-permute-start.6 = (bf16[32,2560]{1,0:T(8,128)(2,1)S(1)}, bf16[32,2560]{1,0:T(8,128)(2,1)S(1)}, u32[]{:S(2)}, u32[]{:S(2)}) collective-permute-start(bf16[32,2560]{1,0:T(8,128)(2,1)S(1)} %get-tuple-element.31), channel_id=1, source_target_pairs={{0,2},{1,3},{2,0},{3,1},{4,6},{5,7},{6,4},{7,5},{8,10},{9,11},{10,... | collective-permute-start | bytes 491528 | tf_op jit(solution)/shard_map/ppermute | solution.py:356
  51.8 0.9 %collective-permute-done.7 = bf16[32,2560]{1,0:T(8,128)(2,1)S(1)} collective-permute-done((bf16[32,2560]{1,0:T(8,128)(2,1)S(1)}, bf16[32,2560]{1,0:T(8,128)(2,1)S(1)}, u32[]{:S(2)}, u32[]{:S(2)}) %collective-permute-start.7) | collective-permute-done | bytes 163872 | tf_op jit(solution)/shard_map/ppermute | solution.py:356
  52.7 4.3 %collective-permute-done.6 = bf16[32,2560]{1,0:T(8,128)(2,1)S(1)} collective-permute-done((bf16[32,2560]{1,0:T(8,128)(2,1)S(1)}, bf16[32,2560]{1,0:T(8,128)(2,1)S(1)}, u32[]{:S(2)}, u32[]{:S(2)}) %collective-permute-start.6) | collective-permute-done | bytes 163872 | tf_op jit(solution)/shard_map/ppermute | solution.py:356
  57.1 1.3 %collective-permute-start.10 = (bf16[32,2560]{1,0:T(8,128)(2,1)S(1)}, bf16[32,2560]{1,0:T(8,128)(2,1)S(1)}, u32[]{:S(2)}, u32[]{:S(2)}) collective-permute-start(bf16[32,2560]{1,0:T(8,128)(2,1)S(1)} %get-tuple-element.37), channel_id=1, source_target_pairs={{0,2},{1,3},{2,0},{3,1},{4,6},{5,7},{6,4},{7,5},{8,10},{9,11},{10,... | collective-permute-start | bytes 491528 | tf_op jit(solution)/shard_map/ppermute | solution.py:356
  58.4 1.1 %collective-permute-start.9 = (bf16[32,2560]{1,0:T(8,128)(2,1)S(1)}, bf16[32,2560]{1,0:T(8,128)(2,1)S(1)}, u32[]{:S(2)}, u32[]{:S(2)}) collective-permute-start(bf16[32,2560]{1,0:T(8,128)(2,1)S(1)} %add_convert_fusion.1), channel_id=1, source_target_pairs={{0,4},{1,5},{2,6},{3,7},{4,0},{5,1},{6,2},{7,3},{8,12},{9,13},{10,... | collective-permute-start | bytes 491528 | tf_op jit(solution)/shard_map/ppermute | solution.py:356
  59.5 1.6 %collective-permute-start.8 = (bf16[32,2560]{1,0:T(8,128)(2,1)S(1)}, bf16[32,2560]{1,0:T(8,128)(2,1)S(1)}, u32[]{:S(2)}, u32[]{:S(2)}) collective-permute-start(bf16[32,2560]{1,0:T(8,128)(2,1)S(1)} %get-tuple-element.33), channel_id=1, source_target_pairs={{0,2},{1,3},{2,0},{3,1},{4,6},{5,7},{6,4},{7,5},{8,10},{9,11},{10,... | collective-permute-start | bytes 491528 | tf_op jit(solution)/shard_map/ppermute | solution.py:356
  61.1 6.1 %collective-permute-done.10 = bf16[32,2560]{1,0:T(8,128)(2,1)S(1)} collective-permute-done((bf16[32,2560]{1,0:T(8,128)(2,1)S(1)}, bf16[32,2560]{1,0:T(8,128)(2,1)S(1)}, u32[]{:S(2)}, u32[]{:S(2)}) %collective-permute-start.10) | collective-permute-done | bytes 163872 | tf_op jit(solution)/shard_map/ppermute | solution.py:356
  67.2 2.3 %collective-permute-done.8 = bf16[32,2560]{1,0:T(8,128)(2,1)S(1)} collective-permute-done((bf16[32,2560]{1,0:T(8,128)(2,1)S(1)}, bf16[32,2560]{1,0:T(8,128)(2,1)S(1)}, u32[]{:S(2)}, u32[]{:S(2)}) %collective-permute-start.8) | collective-permute-done | bytes 163872 | tf_op jit(solution)/shard_map/ppermute | solution.py:356
  69.5 0.8 %fusion.2 = bf16[1,32,5120]{2,1,0:T(8,128)(2,1)} fusion(f32[1,32,2560]{2,1,0:T(8,128)S(1)} %add_bitcast_fusion, f32[1,32,2560]{2,1,0:T(8,128)S(1)} %add_bitcast_fusion.1, bf16[1,32,5120]{2,1,0:T(8,128)(2,1)S(1)} %copy-done, f32[5120]{0:T(1024)S(1)} %convert_element_type.48, f32[5120]{0:T(1024)S(1)} %bitcast.17), kind=kLoop, calls=%fused_computation.3 | loop fusion | flops 983040 | bytes 1351680 | tf_op jit(solution)/shard_map/convert_element_type | solution.py:417
  (28 shorter events, 2.5 us)
Async XLA Ops:
  0.0 43.3 %collective-permute-start.5 = (bf16[512,5120]{1,0:T(8,128)(2,1)}, bf16[512,5120]{1,0:T(8,128)(2,1)}, u32[]{:S(2)}, u32[]{:S(2)}) collective-permute-start(bf16[512,5120]{1,0:T(8,128)(2,1)} %refs_4_.3), channel_id=1, source_target_pairs={{0,1},{1,0},{2,3},{3,2},{4,5},{5,4},{6,7},{7,6},{8,9},{9,8},{10,11... | collective-permute-start | bytes 15728648 | tf_op jit(solution)/shard_map/ppermute | solution.py:356
  2.8 28.9 %all-to-all-start = ((bf16[32,32,384]{2,1,0:T(8,128)(2,1)}), bf16[32,32,384]{2,1,0:T(8,128)(2,1)S(1)}, u32[]{:S(2)}, u32[]{:S(2)}) async-start(bf16[32,32,384]{2,1,0:T(8,128)(2,1)} %norm.1), calls=%async_computation | async-start | bytes 1572864 | tf_op jit(solution)/shard_map/all_to_all | solution.py:207
  33.9 1.4 %collective-permute-start = (bf16[3,128,128]{2,1,0:T(8,128)(2,1)S(1)}, bf16[3,128,128]{2,1,0:T(8,128)(2,1)S(1)}, u32[]{:S(2)}, u32[]{:S(2)}) collective-permute-start(bf16[3,128,128]{2,1,0:T(8,128)(2,1)S(1)} %get-tuple-element.24), channel_id=1, source_target_pairs={{0,1},{1,0},{2,3},{3,2},{4,5},{5,4},{6,7},{7,6},{8,9},{9,8},{10,11... | collective-permute-start | bytes 294920 | tf_op jit(solution)/shard_map/ppermute | solution.py:232
  36.4 3.9 %collective-permute-start.1 = (bf16[1,128,128]{2,1,0:T(8,128)(2,1)S(1)}, bf16[1,128,128]{2,1,0:T(8,128)(2,1)S(1)}, u32[]{:S(2)}, u32[]{:S(2)}) collective-permute-start(bf16[1,128,128]{2,1,0:T(8,128)(2,1)S(1)} %get-tuple-element.27), channel_id=1, source_target_pairs={{0,1},{1,0},{2,3},{3,2},{4,5},{5,4},{6,7},{7,6},{8,9},{9,8},{10,11... | collective-permute-start | bytes 98312 | tf_op jit(solution)/shard_map/ppermute | solution.py:232
  36.7 4.4 %collective-permute-start.2 = (bf16[2,128,128]{2,1,0:T(8,128)(2,1)S(1)}, bf16[2,128,128]{2,1,0:T(8,128)(2,1)S(1)}, u32[]{:S(2)}, u32[]{:S(2)}) collective-permute-start(bf16[2,128,128]{2,1,0:T(8,128)(2,1)S(1)} %pad_maximum_fusion), channel_id=1, source_target_pairs={{0,8},{8,0},{16,24},{24,16},{1,9},{9,1},{17,25},{25,17},{2,10},{10... | collective-permute-start | bytes 196616 | tf_op jit(solution)/shard_map/ppermute | solution.py:232
  37.5 5.0 %collective-permute-start.3 = (bf16[2,128,128]{2,1,0:T(8,128)(2,1)S(1)}, bf16[2,128,128]{2,1,0:T(8,128)(2,1)S(1)}, u32[]{:S(2)}, u32[]{:S(2)}) collective-permute-start(bf16[2,128,128]{2,1,0:T(8,128)(2,1)S(1)} %pad_maximum_fusion.1), channel_id=1, source_target_pairs={{0,16},{8,24},{16,0},{24,8},{1,17},{9,25},{17,1},{25,9},{2,18},{10... | collective-permute-start | bytes 196616 | tf_op jit(solution)/shard_map/ppermute | solution.py:232
  38.1 5.2 %collective-permute-start.4 = (bf16[2,128,128]{2,1,0:T(8,128)(2,1)S(1)}, bf16[2,128,128]{2,1,0:T(8,128)(2,1)S(1)}, u32[]{:S(2)}, u32[]{:S(2)}) collective-permute-start(bf16[2,128,128]{2,1,0:T(8,128)(2,1)S(1)} %pad_maximum_fusion.2), channel_id=1, source_target_pairs={{0,24},{8,16},{16,8},{24,0},{1,25},{9,17},{17,9},{25,1},{2,26},{10... | collective-permute-start | bytes 196616 | tf_op jit(solution)/shard_map/ppermute | solution.py:232
  40.4 6.1 %copy-start.1 = (bf16[5120]{0:T(1024)(128)(2,1)S(1)}, bf16[5120]{0:T(1024)(128)(2,1)}, u32[]{:S(2)}) copy-start(bf16[5120]{0:T(1024)(128)(2,1)} %param.18) | copy-start | bytes 30724
  46.4 6.2 %collective-permute-start.7 = (bf16[32,2560]{1,0:T(8,128)(2,1)S(1)}, bf16[32,2560]{1,0:T(8,128)(2,1)S(1)}, u32[]{:S(2)}, u32[]{:S(2)}) collective-permute-start(bf16[32,2560]{1,0:T(8,128)(2,1)S(1)} %get-tuple-element.32), channel_id=1, source_target_pairs={{0,2},{1,3},{2,0},{3,1},{4,6},{5,7},{6,4},{7,5},{8,10},{9,11},{10,... | collective-permute-start | bytes 491528 | tf_op jit(solution)/shard_map/ppermute | solution.py:356
  46.5 23.0 %copy-start = (bf16[1,32,5120]{2,1,0:T(8,128)(2,1)S(1)}, bf16[1,32,5120]{2,1,0:T(8,128)(2,1)}, u32[]{:S(2)}) copy-start(bf16[1,32,5120]{2,1,0:T(8,128)(2,1)} %param.11) | copy-start | bytes 983044
  49.7 7.4 %collective-permute-start.6 = (bf16[32,2560]{1,0:T(8,128)(2,1)S(1)}, bf16[32,2560]{1,0:T(8,128)(2,1)S(1)}, u32[]{:S(2)}, u32[]{:S(2)}) collective-permute-start(bf16[32,2560]{1,0:T(8,128)(2,1)S(1)} %get-tuple-element.31), channel_id=1, source_target_pairs={{0,2},{1,3},{2,0},{3,1},{4,6},{5,7},{6,4},{7,5},{8,10},{9,11},{10,... | collective-permute-start | bytes 491528 | tf_op jit(solution)/shard_map/ppermute | solution.py:356
  52.7 8.4 %collective-permute-start.11 = (bf16[32,2560]{1,0:T(8,128)(2,1)S(1)}, bf16[32,2560]{1,0:T(8,128)(2,1)S(1)}, u32[]{:S(2)}, u32[]{:S(2)}) collective-permute-start(bf16[32,2560]{1,0:T(8,128)(2,1)S(1)} %add_convert_fusion), channel_id=1, source_target_pairs={{0,4},{1,5},{2,6},{3,7},{4,0},{5,1},{6,2},{7,3},{8,12},{9,13},{10,... | collective-permute-start | bytes 491528 | tf_op jit(solution)/shard_map/ppermute | solution.py:356
  57.1 10.1 %collective-permute-start.10 = (bf16[32,2560]{1,0:T(8,128)(2,1)S(1)}, bf16[32,2560]{1,0:T(8,128)(2,1)S(1)}, u32[]{:S(2)}, u32[]{:S(2)}) collective-permute-start(bf16[32,2560]{1,0:T(8,128)(2,1)S(1)} %get-tuple-element.37), channel_id=1, source_target_pairs={{0,2},{1,3},{2,0},{3,1},{4,6},{5,7},{6,4},{7,5},{8,10},{9,11},{10,... | collective-permute-start | bytes 491528 | tf_op jit(solution)/shard_map/ppermute | solution.py:356
  58.4 8.8 %collective-permute-start.9 = (bf16[32,2560]{1,0:T(8,128)(2,1)S(1)}, bf16[32,2560]{1,0:T(8,128)(2,1)S(1)}, u32[]{:S(2)}, u32[]{:S(2)}) collective-permute-start(bf16[32,2560]{1,0:T(8,128)(2,1)S(1)} %add_convert_fusion.1), channel_id=1, source_target_pairs={{0,4},{1,5},{2,6},{3,7},{4,0},{5,1},{6,2},{7,3},{8,12},{9,13},{10,... | collective-permute-start | bytes 491528 | tf_op jit(solution)/shard_map/ppermute | solution.py:356
  59.5 10.0 %collective-permute-start.8 = (bf16[32,2560]{1,0:T(8,128)(2,1)S(1)}, bf16[32,2560]{1,0:T(8,128)(2,1)S(1)}, u32[]{:S(2)}, u32[]{:S(2)}) collective-permute-start(bf16[32,2560]{1,0:T(8,128)(2,1)S(1)} %get-tuple-element.33), channel_id=1, source_target_pairs={{0,2},{1,3},{2,0},{3,1},{4,6},{5,7},{6,4},{7,5},{8,10},{9,11},{10,... | collective-permute-start | bytes 491528 | tf_op jit(solution)/shard_map/ppermute | solution.py:356
